TPU v7x, 32 devices: a whole 2x2x4 slice. The times are simulated.
32 devices in a mesh: gx: 8 (over y, x, core), gy: 4 (over z).
Axes of the slice: x: 2, y: 2, z: 4, core: 2. Of those that a mesh axis runs over, the one named last changes fastest.
Arguments:
- source: float32 [64, 64, 512], P('gx', 'gy'), may hold values from -6 to 6
- face_coef: bfloat16 [3, 64, 64, 512], P(None, 'gx', 'gy'), may hold values from 0.25 to 4
Outputs:
- potential: float32 [64, 64, 512], P('gx', 'gy')
All inputs are finite; a program needn't handle non-finite values.
Results may differ from a plain program's by a relative error of at most 0.0003.
Values sent between devices are 32-bit elements; how exact they have to be, the bound alone decides.
No kernel may reach another device: no remote copies, remote signals or barrier semaphores. Data moves between devices by JAX's collectives and lax.ppermute only.
A program may use at most 64 MiB of HBM per device.

v0:
```python
import math

import jax
import jax.numpy as jnp
from jax import lax
from jax.sharding import PartitionSpec as P

LEVELS = 3
SWEEPS = 2


MASS = 0.002


def with_halo(block, sides, width):
    for axis, dim in sides:
        count = lax.axis_size(axis)
        forward = [(i, i + 1) for i in range(count - 1)]
        forward.append((count - 1, 0))
        backward = [(target, source) for source, target in forward]
        low = lax.ppermute(
            lax.slice_in_dim(block, block.shape[dim] - width, None, axis=dim), axis, forward
        )
        high = lax.ppermute(lax.slice_in_dim(block, 0, width, axis=dim), axis, backward)
        block = jnp.concatenate([low, block, high], axis=dim)
    return block


def shifted(block, axis, distance):
    devices = range(lax.axis_size(axis))
    route = [((i - distance) % len(devices), i) for i in devices]
    return lax.ppermute(block, axis, route)


def coarsen(couplings):
    east_face = couplings[0][1::2]
    east_face = (
        east_face[:, 0::2, 0::2]
        + east_face[:, 1::2, 0::2]
        + east_face[:, 0::2, 1::2]
        + east_face[:, 1::2, 1::2]
    )
    north_face = couplings[1][:, 1::2]
    north_face = (
        north_face[0::2, :, 0::2]
        + north_face[1::2, :, 0::2]
        + north_face[0::2, :, 1::2]
        + north_face[1::2, :, 1::2]
    )
    upper_face = couplings[2][:, :, 1::2]
    upper_face = (
        upper_face[0::2, 0::2]
        + upper_face[1::2, 0::2]
        + upper_face[0::2, 1::2]
        + upper_face[1::2, 1::2]
    )
    return jnp.stack((east_face, north_face, upper_face)) * 0.0625


def restrict(residual):
    dims = residual.shape
    return residual.reshape(dims[0] // 2, 2, dims[1] // 2, 2, dims[2] // 2, 2).mean(axis=(1, 3, 5))


def prolong(correction):
    return jnp.repeat(jnp.repeat(jnp.repeat(correction, 2, 0), 2, 1), 2, 2)


def pad_single(potential):
    return with_halo(potential, (("gx", 0), ("gy", 1)), 1)


def lower_tables(couplings):
    previous_rows = shifted(couplings[0][-1:], "gx", 1)
    previous_cols = shifted(couplings[1][:, -1:], "gy", 1)
    east_back = jnp.concatenate((previous_rows, couplings[0][:-1]), axis=0)
    north_back = jnp.concatenate((previous_cols, couplings[1][:, :-1]), axis=1)
    upper_back = jnp.roll(couplings[2], 1, 2)
    diagonal = (
        MASS + couplings[0] + east_back + couplings[1] + north_back + couplings[2] + upper_back
    )
    return (
        (couplings[0], couplings[1], couplings[2]),
        (east_back, north_back, upper_back),
        diagonal,
    )


def region_parity(local_dims, extent):
    row_ids = (
        lax.axis_index("gx") * local_dims[0]
        - extent
        + jnp.arange(local_dims[0] + 2 * extent, dtype=jnp.int32)
    )
    col_ids = (
        lax.axis_index("gy") * local_dims[1]
        - extent
        + jnp.arange(local_dims[1] + 2 * extent, dtype=jnp.int32)
    )
    depth_ids = jnp.arange(local_dims[2], dtype=jnp.int32)
    return (row_ids[:, None, None] + col_ids[None, :, None] + depth_ids[None, None, :]) % 2


def neighbour_terms(padded, offset, couplings, lagged):
    row_count = couplings[0].shape[0]
    col_count = couplings[0].shape[1]
    centre = padded[offset : offset + row_count, offset : offset + col_count]
    summed = (
        couplings[0] * padded[offset + 1 : offset + 1 + row_count, offset : offset + col_count]
        + lagged[0] * padded[offset - 1 : offset - 1 + row_count, offset : offset + col_count]
    )
    summed = (
        summed
        + couplings[1] * padded[offset : offset + row_count, offset + 1 : offset + 1 + col_count]
        + lagged[1] * padded[offset : offset + row_count, offset - 1 : offset - 1 + col_count]
    )
    summed = summed + couplings[2] * jnp.roll(centre, -1, 2) + lagged[2] * jnp.roll(centre, 1, 2)
    return (centre, summed)


def relax_colour(padded, offset, tables, right_side, parity, colour):
    centre, summed = neighbour_terms(padded, offset, tables[0], tables[1])
    return jnp.where(parity == colour, (right_side + summed) / tables[2], centre)


def hartley_table(row_ids, col_ids, length):
    angles = (row_ids[:, None] * col_ids[None, :] % length).astype(jnp.float32) * (
        2.0 * math.pi / length
    )
    return jnp.cos(angles) + jnp.sin(angles)


def eigenvalues(row_ids, col_ids, depth_ids, lengths, averages):
    parts_list = []
    for axis_index, wave_ids in enumerate((row_ids, col_ids, depth_ids)):
        wave = wave_ids.astype(jnp.float32) * (2.0 * math.pi / lengths[axis_index])
        parts_list.append(2.0 * averages[axis_index] * (1.0 - jnp.cos(wave)))
    return (
        MASS
        + parts_list[0][:, None, None]
        + parts_list[1][None, :, None]
        + parts_list[2][None, None, :]
    )


def coarse_solve(right_side, averages):
    local_rows, local_cols, depth_count = right_side.shape
    total_rows = local_rows * lax.axis_size("gx")
    total_cols = local_cols * lax.axis_size("gy")
    row_ids = lax.axis_index("gx") * local_rows + jnp.arange(local_rows, dtype=jnp.int32)
    col_ids = lax.axis_index("gy") * local_cols + jnp.arange(local_cols, dtype=jnp.int32)
    depth_ids = jnp.arange(depth_count, dtype=jnp.int32)
    depth_table = hartley_table(depth_ids, depth_ids, depth_count)
    lengths = (total_rows, total_cols, depth_count)
    normaliser = float(total_rows * total_cols * depth_count)

    def along_depth(values):
        return jnp.einsum("abz,zk->abk", values, depth_table, precision=lax.Precision.HIGHEST)

    gathered = lax.all_gather(
        lax.all_gather(right_side, "gy", axis=1, tiled=True), "gx", axis=0, tiled=True
    )
    all_rows = jnp.arange(total_rows, dtype=jnp.int32)
    all_cols = jnp.arange(total_cols, dtype=jnp.int32)
    spectrum = along_depth(gathered)
    spectrum = jnp.einsum(
        "ij,jbz->ibz",
        hartley_table(all_rows, all_rows, total_rows),
        spectrum,
        precision=lax.Precision.HIGHEST,
    )
    spectrum = jnp.einsum(
        "ij,ajz->aiz",
        hartley_table(all_cols, all_cols, total_cols),
        spectrum,
        precision=lax.Precision.HIGHEST,
    )
    spectrum = spectrum / (
        eigenvalues(all_rows, all_cols, depth_ids, lengths, averages) * normaliser
    )
    own_part = jnp.einsum(
        "ij,jbz->ibz",
        hartley_table(row_ids, all_rows, total_rows),
        spectrum,
        precision=lax.Precision.HIGHEST,
    )
    own_part = jnp.einsum(
        "ij,ajz->aiz",
        hartley_table(col_ids, all_cols, total_cols),
        own_part,
        precision=lax.Precision.HIGHEST,
    )
    return along_depth(own_part)


def multigrid_cycle(right_side, face_list, averages, level_index):
    if level_index == LEVELS - 1:
        return coarse_solve(right_side, averages)
    couplings = face_list[level_index]
    inner_parity = region_parity(right_side.shape, 0)
    inner_tables = lower_tables(couplings)

    def sweep_all(potential):
        for sweep_index in range(SWEEPS):
            for colour in (0, 1):
                potential = relax_colour(
                    pad_single(potential), 1, inner_tables, right_side, inner_parity, colour
                )
        return potential

    potential = sweep_all(jnp.zeros_like(right_side))
    centre, summed = neighbour_terms(pad_single(potential), 1, inner_tables[0], inner_tables[1])
    residual = right_side - (inner_tables[2] * centre - summed)
    correction = multigrid_cycle(restrict(residual), face_list, averages, level_index + 1)
    potential = potential + prolong(correction)
    return sweep_all(potential)


def shards(source, face_coef):
    face_list = [face_coef.astype(jnp.float32)]
    for level_index in range(LEVELS - 1):
        face_list.append(coarsen(face_list[-1]))
    coarsest = face_list[-1]
    cell_count = coarsest[0].size * lax.axis_size("gx") * lax.axis_size("gy")
    averages = lax.psum(jnp.sum(coarsest, axis=(1, 2, 3)), ("gx", "gy")) / cell_count
    return multigrid_cycle(source, face_list, averages, 0)


def solution(mesh):
    return jax.shard_map(
        shards,
        mesh=mesh,
        in_specs=(P("gx", "gy", None), P(None, "gx", "gy", None)),
        out_specs=P("gx", "gy", None),
        check_vma=False,
    )
```

profile of v0, /device:TPU:0, one launch (start us, length us, event | category | flops | bytes accessed | tf_op | source)
XLA Modules:
  0.0 310.4 jit_solution(13600069066482494750)
XLA Ops:
  0.0 3.3 %collective-permute-start = (f32[1,16,512]{2,1,0:T(8,128)S(1)}, f32[1,16,512]{2,1,0:T(8,128)S(1)}, u32[]{:S(2)}, u32[]{:S(2)}) collective-permute-start(f32[1,16,512]{2,1,0:T(8,128)S(1)} %broadcast.225), channel_id=1, source_target_pairs={{4,0},{8,4},{12,8},{16,12},{20,16},{24,20},{28,24},{0,28},{5,1},{9... | collective-permute-start | bytes 98312 | tf_op jit(solution)/shard_map/ppermute | solution.py:24
  3.3 2.6 collective-permute-start.22
  14.7 4.5 %slice.971 = f32[8,16,256]{2,1,0:T(8,128)S(1)} slice(f32[8,16,512]{2,1,0:T(8,128)S(1)} %get-tuple-element.8), slice={[0:8:1], [0:16:1], [1:512:2]} | slice | bytes 262144 | tf_op jit(solution)/shard_map/slice | solution.py:50
  28.6 39.5 %psum.7 = f32[3]{0:T(128)S(1)} all-reduce(f32[3]{0:T(128)S(1)} %fusion.238), channel_id=1, replica_groups=mesh['gx'=8,'gy'=4] {'gx','gy'}, use_global_device_ids=true, to_apply=%region_3.4 | all-reduce | flops 3 | bytes 24 | tf_op jit(solution)/shard_map/psum | solution.py:225
  71.8 3.6 %collective-permute-start.3 = (f32[10,1,512]{2,1,0:T(1,128)S(1)}, f32[10,1,512]{2,1,0:T(1,128)S(1)}, u32[]{:S(2)}, u32[]{:S(2)}) collective-permute-start(f32[10,1,512]{2,1,0:T(1,128)S(1)} %get-tuple-element.26), channel_id=1, source_target_pairs={{1,0},{2,1},{3,2},{0,3},{5,4},{6,5},{7,6},{4,7},{9,8},{10,9},{11,1... | collective-permute-start | bytes 61448 | tf_op jit(solution)/shard_map/ppermute | solution.py:24
  77.2 3.6 %collective-permute-start.25 = (f32[6,1,256]{2,1,0:T(1,128)S(1)}, f32[6,1,256]{2,1,0:T(1,128)S(1)}, u32[]{:S(2)}, u32[]{:S(2)}) collective-permute-start(f32[6,1,256]{2,1,0:T(1,128)S(1)} %get-tuple-element.95), channel_id=1, source_target_pairs={{1,0},{2,1},{3,2},{0,3},{5,4},{6,5},{7,6},{4,7},{9,8},{10,9},{11,1... | collective-permute-start | bytes 18440 | tf_op jit(solution)/shard_map/ppermute | solution.py:24
  84.1 3.0 collective-permute-done.7
  90.9 2.2 collective-permute-done.9
  95.3 2.7 collective-permute-done.11
  105.9 2.7 collective-permute-done.15
  108.7 2.0 collective-permute-start.17
  116.5 2.7 collective-permute-done.19
  125.3 18.1 %reshape.182 = f32[4,2,8,2,256,2]{5,4,3,2,1,0:T(8,128)} reshape(f32[8,16,512]{2,1,0:T(8,128)S(1)} %fusion.64) | data formatting | bytes 524288 | tf_op jit(solution)/shard_map/reshape | solution.py:62
  143.5 7.0 %reduce_sum.27 = f32[4,8,256]{2,1,0:T(8,128)S(1)} reduce(f32[4,2,8,2,256,2]{5,4,3,2,1,0:T(8,128)} %reshape.182, f32[]{:T(128)} %constant.118.clone.1), dimensions={1,3,5}, to_apply=%region_0.0 | reduce | flops 57344 | bytes 294916 | tf_op jit(solution)/shard_map/reduce_sum | solution.py:62
  152.0 2.7 collective-permute-done.29
  154.7 2.0 collective-permute-start.30
  158.4 3.8 %collective-permute-done.31 = f32[6,1,256]{2,1,0:T(1,128)S(1)} collective-permute-done((f32[6,1,256]{2,1,0:T(1,128)S(1)}, f32[6,1,256]{2,1,0:T(1,128)S(1)}, u32[]{:S(2)}, u32[]{:S(2)}) %collective-permute-start.31) | collective-permute-done | bytes 6176 | tf_op jit(solution)/shard_map/ppermute | solution.py:21
  163.7 2.7 collective-permute-done.33
  173.4 2.7 collective-permute-done.37
  183.2 2.7 collective-permute-done.41
  191.5 3.4 %reshape.183 = f32[2,2,4,2,128,2]{5,4,3,2,1,0:T(8,128)} reshape(f32[4,8,256]{2,1,0:T(8,128)S(1)} %fusion.189) | data formatting | bytes 65536 | tf_op jit(solution)/shard_map/reshape | solution.py:62
  196.8 13.1 %all_gather.6 = f32[2,16,128]{2,0,1:T(2,128)S(1)} all-gather(f32[2,4,128]{2,0,1:T(2,128)S(1)} %copy.720), channel_id=1, replica_groups=mesh['gx'=8,'gy'=4] {'gy'}, dimensions={1}, use_global_device_ids=true | all-gather | bytes 20480 | tf_op jit(solution)/shard_map/all_gather | solution.py:161
  209.9 10.0 %all_gather.7 = f32[16,16,128]{2,1,0:T(8,128)S(1)} all-gather(f32[2,16,128]{2,1,0:T(8,128)S(1)} %copy.721), channel_id=1, replica_groups=mesh['gx'=8,'gy'=4] {'gx'}, dimensions={0}, use_global_device_ids=true | all-gather | bytes 147456 | tf_op jit(solution)/shard_map/all_gather | solution.py:160
  225.5 2.6 collective-permute-done.45
  235.3 2.7 collective-permute-done.49
  245.0 2.7 collective-permute-done.53
  254.8 2.7 collective-permute-done.57
  265.1 2.2 copy.730
  269.0 2.7 collective-permute-done.61
  279.6 2.7 collective-permute-done.65
  290.2 2.7 collective-permute-done.69
  300.8 2.7 collective-permute-done.73
  (308 shorter events, 143.3 us)
Async XLA Ops:
  0.0 71.3 %collective-permute-start = (f32[1,16,512]{2,1,0:T(8,128)S(1)}, f32[1,16,512]{2,1,0:T(8,128)S(1)}, u32[]{:S(2)}, u32[]{:S(2)}) collective-permute-start(f32[1,16,512]{2,1,0:T(8,128)S(1)} %broadcast.225), channel_id=1, source_target_pairs={{4,0},{8,4},{12,8},{16,12},{20,16},{24,20},{28,24},{0,28},{5,1},{9... | collective-permute-start | bytes 98312 | tf_op jit(solution)/shard_map/ppermute | solution.py:24
  3.3 68.0 %collective-permute-start.2 = (f32[1,16,512]{2,1,0:T(8,128)S(1)}, f32[1,16,512]{2,1,0:T(8,128)S(1)}, u32[]{:S(2)}, u32[]{:S(2)}) collective-permute-start(f32[1,16,512]{2,1,0:T(8,128)S(1)} %broadcast.225), channel_id=1, source_target_pairs={{0,4},{4,8},{8,12},{12,16},{16,20},{20,24},{24,28},{28,0},{1,5},{5... | collective-permute-start | bytes 98312 | tf_op jit(solution)/shard_map/ppermute | solution.py:21
  3.3 68.4 %collective-permute-start.22 = (f32[1,8,256]{2,1,0:T(8,128)S(1)}, f32[1,8,256]{2,1,0:T(8,128)S(1)}, u32[]{:S(2)}, u32[]{:S(2)}) collective-permute-start(f32[1,8,256]{2,1,0:T(8,128)S(1)} %broadcast.227), channel_id=1, source_target_pairs={{4,0},{8,4},{12,8},{16,12},{20,16},{24,20},{28,24},{0,28},{5,1},{9... | collective-permute-start | bytes 24584 | tf_op jit(solution)/shard_map/ppermute | solution.py:24
  6.0 69.4 %collective-permute-start.24 = (f32[1,8,256]{2,1,0:T(8,128)S(1)}, f32[1,8,256]{2,1,0:T(8,128)S(1)}, u32[]{:S(2)}, u32[]{:S(2)}) collective-permute-start(f32[1,8,256]{2,1,0:T(8,128)S(1)} %broadcast.227), channel_id=1, source_target_pairs={{0,4},{4,8},{8,12},{12,16},{16,20},{20,24},{24,28},{28,0},{1,5},{5... | collective-permute-start | bytes 24584 | tf_op jit(solution)/shard_map/ppermute | solution.py:21
  7.2 68.2 %collective-permute-start.4 = (f32[8,1,512]{2,0,1:T(8,128)S(1)}, f32[8,1,512]{2,0,1:T(8,128)S(1)}, u32[]{:S(2)}, u32[]{:S(2)}) collective-permute-start(f32[8,1,512]{2,0,1:T(8,128)S(1)} %copy.718), channel_id=1, source_target_pairs={{3,0},{0,1},{1,2},{2,3},{7,4},{4,5},{5,6},{6,7},{11,8},{8,9},{9,10... | collective-permute-start | bytes 49160 | tf_op jit(solution)/shard_map/ppermute | solution.py:32
  71.3 6.0 %collective-permute-start.1 = (f32[1,16,512]{2,1,0:T(8,128)S(1)}, f32[1,16,512]{2,1,0:T(8,128)S(1)}, u32[]{:S(2)}, u32[]{:S(2)}) collective-permute-start(f32[1,16,512]{2,1,0:T(8,128)S(1)} %slice_bitcast_fusion.7), channel_id=1, source_target_pairs={{28,0},{0,4},{4,8},{8,12},{12,16},{16,20},{20,24},{24,28},{29,1},{... | collective-permute-start | bytes 98312 | tf_op jit(solution)/shard_map/ppermute | solution.py:32
  71.3 79.1 %collective-permute-start.26 = (f32[4,1,256]{2,1,0:T(1,128)S(1)}, f32[4,1,256]{2,1,0:T(1,128)S(1)}, u32[]{:S(2)}, u32[]{:S(2)}) collective-permute-start(f32[4,1,256]{2,1,0:T(1,128)S(1)} %slice.1193), channel_id=1, source_target_pairs={{3,0},{0,1},{1,2},{2,3},{7,4},{4,5},{5,6},{6,7},{11,8},{8,9},{9,10... | collective-permute-start | bytes 12296 | tf_op jit(solution)/shard_map/ppermute | solution.py:32
  71.8 9.0 %collective-permute-start.3 = (f32[10,1,512]{2,1,0:T(1,128)S(1)}, f32[10,1,512]{2,1,0:T(1,128)S(1)}, u32[]{:S(2)}, u32[]{:S(2)}) collective-permute-start(f32[10,1,512]{2,1,0:T(1,128)S(1)} %get-tuple-element.26), channel_id=1, source_target_pairs={{1,0},{2,1},{3,2},{0,3},{5,4},{6,5},{7,6},{4,7},{9,8},{10,9},{11,1... | collective-permute-start | bytes 61448 | tf_op jit(solution)/shard_map/ppermute | solution.py:24
  75.4 5.6 %collective-permute-start.5 = (f32[10,1,512]{2,1,0:T(1,128)S(1)}, f32[10,1,512]{2,1,0:T(1,128)S(1)}, u32[]{:S(2)}, u32[]{:S(2)}) collective-permute-start(f32[10,1,512]{2,1,0:T(1,128)S(1)} %get-tuple-element.27), channel_id=1, source_target_pairs={{0,1},{1,2},{2,3},{3,0},{4,5},{5,6},{6,7},{7,4},{8,9},{9,10},{10,1... | collective-permute-start | bytes 61448 | tf_op jit(solution)/shard_map/ppermute | solution.py:21
  75.4 75.1 %collective-permute-start.23 = (f32[1,8,256]{2,1,0:T(8,128)S(1)}, f32[1,8,256]{2,1,0:T(8,128)S(1)}, u32[]{:S(2)}, u32[]{:S(2)}) collective-permute-start(f32[1,8,256]{2,1,0:T(8,128)S(1)} %slice_bitcast_fusion.9), channel_id=1, source_target_pairs={{28,0},{0,4},{4,8},{8,12},{12,16},{16,20},{20,24},{24,28},{29,1},{... | collective-permute-start | bytes 24584 | tf_op jit(solution)/shard_map/ppermute | solution.py:32
  77.2 73.2 %collective-permute-start.25 = (f32[6,1,256]{2,1,0:T(1,128)S(1)}, f32[6,1,256]{2,1,0:T(1,128)S(1)}, u32[]{:S(2)}, u32[]{:S(2)}) collective-permute-start(f32[6,1,256]{2,1,0:T(1,128)S(1)} %get-tuple-element.95), channel_id=1, source_target_pairs={{1,0},{2,1},{3,2},{0,3},{5,4},{6,5},{7,6},{4,7},{9,8},{10,9},{11,1... | collective-permute-start | bytes 18440 | tf_op jit(solution)/shard_map/ppermute | solution.py:24
  82.5 4.6 %collective-permute-start.7 = (f32[1,16,512]{2,1,0:T(8,128)S(1)}, f32[1,16,512]{2,1,0:T(8,128)S(1)}, u32[]{:S(2)}, u32[]{:S(2)}) collective-permute-start(f32[1,16,512]{2,1,0:T(8,128)S(1)} %get-tuple-element.74), channel_id=1, source_target_pairs={{0,4},{4,8},{8,12},{12,16},{16,20},{20,24},{24,28},{28,0},{1,5},{5... | collective-permute-start | bytes 98312 | tf_op jit(solution)/shard_map/ppermute | solution.py:21
  87.5 5.6 %collective-permute-start.9 = (f32[10,1,512]{2,1,0:T(1,128)S(1)}, f32[10,1,512]{2,1,0:T(1,128)S(1)}, u32[]{:S(2)}, u32[]{:S(2)}) collective-permute-start(f32[10,1,512]{2,1,0:T(1,128)S(1)} %get-tuple-element.25), channel_id=1, source_target_pairs={{0,1},{1,2},{2,3},{3,0},{4,5},{5,6},{6,7},{7,4},{8,9},{9,10},{10,1... | collective-permute-start | bytes 61448 | tf_op jit(solution)/shard_map/ppermute | solution.py:21
  93.7 4.3 %collective-permute-start.11 = (f32[1,16,512]{2,1,0:T(8,128)S(1)}, f32[1,16,512]{2,1,0:T(8,128)S(1)}, u32[]{:S(2)}, u32[]{:S(2)}) collective-permute-start(f32[1,16,512]{2,1,0:T(8,128)S(1)} %get-tuple-element.68), channel_id=1, source_target_pairs={{0,4},{4,8},{8,12},{12,16},{16,20},{20,24},{24,28},{28,0},{1,5},{5... | collective-permute-start | bytes 98312 | tf_op jit(solution)/shard_map/ppermute | solution.py:21
  98.1 5.6 %collective-permute-start.13 = (f32[10,1,512]{2,1,0:T(1,128)S(1)}, f32[10,1,512]{2,1,0:T(1,128)S(1)}, u32[]{:S(2)}, u32[]{:S(2)}) collective-permute-start(f32[10,1,512]{2,1,0:T(1,128)S(1)} %get-tuple-element.23), channel_id=1, source_target_pairs={{0,1},{1,2},{2,3},{3,0},{4,5},{5,6},{6,7},{7,4},{8,9},{9,10},{10,1... | collective-permute-start | bytes 61448 | tf_op jit(solution)/shard_map/ppermute | solution.py:21
  104.3 4.3 %collective-permute-start.15 = (f32[1,16,512]{2,1,0:T(8,128)S(1)}, f32[1,16,512]{2,1,0:T(8,128)S(1)}, u32[]{:S(2)}, u32[]{:S(2)}) collective-permute-start(f32[1,16,512]{2,1,0:T(8,128)S(1)} %get-tuple-element.62), channel_id=1, source_target_pairs={{0,4},{4,8},{8,12},{12,16},{16,20},{20,24},{24,28},{28,0},{1,5},{5... | collective-permute-start | bytes 98312 | tf_op jit(solution)/shard_map/ppermute | solution.py:21
  108.7 5.6 %collective-permute-start.17 = (f32[10,1,512]{2,1,0:T(1,128)S(1)}, f32[10,1,512]{2,1,0:T(1,128)S(1)}, u32[]{:S(2)}, u32[]{:S(2)}) collective-permute-start(f32[10,1,512]{2,1,0:T(1,128)S(1)} %get-tuple-element.21), channel_id=1, source_target_pairs={{0,1},{1,2},{2,3},{3,0},{4,5},{5,6},{6,7},{7,4},{8,9},{9,10},{10,1... | collective-permute-start | bytes 61448 | tf_op jit(solution)/shard_map/ppermute | solution.py:21
  114.9 4.3 %collective-permute-start.19 = (f32[1,16,512]{2,1,0:T(8,128)S(1)}, f32[1,16,512]{2,1,0:T(8,128)S(1)}, u32[]{:S(2)}, u32[]{:S(2)}) collective-permute-start(f32[1,16,512]{2,1,0:T(8,128)S(1)} %get-tuple-element.56), channel_id=1, source_target_pairs={{0,4},{4,8},{8,12},{12,16},{16,20},{20,24},{24,28},{28,0},{1,5},{5... | collective-permute-start | bytes 98312 | tf_op jit(solution)/shard_map/ppermute | solution.py:21
  119.3 5.6 %collective-permute-start.21 = (f32[10,1,512]{2,1,0:T(1,128)S(1)}, f32[10,1,512]{2,1,0:T(1,128)S(1)}, u32[]{:S(2)}, u32[]{:S(2)}) collective-permute-start(f32[10,1,512]{2,1,0:T(1,128)S(1)} %get-tuple-element.19), channel_id=1, source_target_pairs={{0,1},{1,2},{2,3},{3,0},{4,5},{5,6},{6,7},{7,4},{8,9},{9,10},{10,1... | collective-permute-start | bytes 61448 | tf_op jit(solution)/shard_map/ppermute | solution.py:21
  123.1 27.4 %collective-permute-start.27 = (f32[6,1,256]{2,1,0:T(1,128)S(1)}, f32[6,1,256]{2,1,0:T(1,128)S(1)}, u32[]{:S(2)}, u32[]{:S(2)}) collective-permute-start(f32[6,1,256]{2,1,0:T(1,128)S(1)} %get-tuple-element.96), channel_id=1, source_target_pairs={{0,1},{1,2},{2,3},{3,0},{4,5},{5,6},{6,7},{7,4},{8,9},{9,10},{10,1... | collective-permute-start | bytes 18440 | tf_op jit(solution)/shard_map/ppermute | solution.py:21
  156.7 5.4 %collective-permute-start.31 = (f32[6,1,256]{2,1,0:T(1,128)S(1)}, f32[6,1,256]{2,1,0:T(1,128)S(1)}, u32[]{:S(2)}, u32[]{:S(2)}) collective-permute-start(f32[6,1,256]{2,1,0:T(1,128)S(1)} %get-tuple-element.94), channel_id=1, source_target_pairs={{0,1},{1,2},{2,3},{3,0},{4,5},{5,6},{6,7},{7,4},{8,9},{9,10},{10,1... | collective-permute-start | bytes 18440 | tf_op jit(solution)/shard_map/ppermute | solution.py:21
  166.4 5.5 %collective-permute-start.35 = (f32[6,1,256]{2,1,0:T(1,128)S(1)}, f32[6,1,256]{2,1,0:T(1,128)S(1)}, u32[]{:S(2)}, u32[]{:S(2)}) collective-permute-start(f32[6,1,256]{2,1,0:T(1,128)S(1)} %get-tuple-element.92), channel_id=1, source_target_pairs={{0,1},{1,2},{2,3},{3,0},{4,5},{5,6},{6,7},{7,4},{8,9},{9,10},{10,1... | collective-permute-start | bytes 18440 | tf_op jit(solution)/shard_map/ppermute | solution.py:21
  176.2 5.5 %collective-permute-start.39 = (f32[6,1,256]{2,1,0:T(1,128)S(1)}, f32[6,1,256]{2,1,0:T(1,128)S(1)}, u32[]{:S(2)}, u32[]{:S(2)}) collective-permute-start(f32[6,1,256]{2,1,0:T(1,128)S(1)} %get-tuple-element.90), channel_id=1, source_target_pairs={{0,1},{1,2},{2,3},{3,0},{4,5},{5,6},{6,7},{7,4},{8,9},{9,10},{10,1... | collective-permute-start | bytes 18440 | tf_op jit(solution)/shard_map/ppermute | solution.py:21
  186.0 5.5 %collective-permute-start.43 = (f32[6,1,256]{2,1,0:T(1,128)S(1)}, f32[6,1,256]{2,1,0:T(1,128)S(1)}, u32[]{:S(2)}, u32[]{:S(2)}) collective-permute-start(f32[6,1,256]{2,1,0:T(1,128)S(1)} %get-tuple-element.88), channel_id=1, source_target_pairs={{0,1},{1,2},{2,3},{3,0},{4,5},{5,6},{6,7},{7,4},{8,9},{9,10},{10,1... | collective-permute-start | bytes 18440 | tf_op jit(solution)/shard_map/ppermute | solution.py:21
  228.3 5.4 %collective-permute-start.47 = (f32[6,1,256]{2,1,0:T(1,128)S(1)}, f32[6,1,256]{2,1,0:T(1,128)S(1)}, u32[]{:S(2)}, u32[]{:S(2)}) collective-permute-start(f32[6,1,256]{2,1,0:T(1,128)S(1)} %get-tuple-element.86), channel_id=1, source_target_pairs={{0,1},{1,2},{2,3},{3,0},{4,5},{5,6},{6,7},{7,4},{8,9},{9,10},{10,1... | collective-permute-start | bytes 18440 | tf_op jit(solution)/shard_map/ppermute | solution.py:21
  238.1 5.4 %collective-permute-start.51 = (f32[6,1,256]{2,1,0:T(1,128)S(1)}, f32[6,1,256]{2,1,0:T(1,128)S(1)}, u32[]{:S(2)}, u32[]{:S(2)}) collective-permute-start(f32[6,1,256]{2,1,0:T(1,128)S(1)} %get-tuple-element.84), channel_id=1, source_target_pairs={{0,1},{1,2},{2,3},{3,0},{4,5},{5,6},{6,7},{7,4},{8,9},{9,10},{10,1... | collective-permute-start | bytes 18440 | tf_op jit(solution)/shard_map/ppermute | solution.py:21
  247.8 5.5 %collective-permute-start.55 = (f32[6,1,256]{2,1,0:T(1,128)S(1)}, f32[6,1,256]{2,1,0:T(1,128)S(1)}, u32[]{:S(2)}, u32[]{:S(2)}) collective-permute-start(f32[6,1,256]{2,1,0:T(1,128)S(1)} %get-tuple-element.82), channel_id=1, source_target_pairs={{0,1},{1,2},{2,3},{3,0},{4,5},{5,6},{6,7},{7,4},{8,9},{9,10},{10,1... | collective-permute-start | bytes 18440 | tf_op jit(solution)/shard_map/ppermute | solution.py:21
  257.5 5.5 %collective-permute-start.59 = (f32[6,1,256]{2,1,0:T(1,128)S(1)}, f32[6,1,256]{2,1,0:T(1,128)S(1)}, u32[]{:S(2)}, u32[]{:S(2)}) collective-permute-start(f32[6,1,256]{2,1,0:T(1,128)S(1)} %get-tuple-element.80), channel_id=1, source_target_pairs={{0,1},{1,2},{2,3},{3,0},{4,5},{5,6},{6,7},{7,4},{8,9},{9,10},{10,1... | collective-permute-start | bytes 18440 | tf_op jit(solution)/shard_map/ppermute | solution.py:21
  271.8 5.6 %collective-permute-start.63 = (f32[10,1,512]{2,1,0:T(1,128)S(1)}, f32[10,1,512]{2,1,0:T(1,128)S(1)}, u32[]{:S(2)}, u32[]{:S(2)}) collective-permute-start(f32[10,1,512]{2,1,0:T(1,128)S(1)} %get-tuple-element.17), channel_id=1, source_target_pairs={{0,1},{1,2},{2,3},{3,0},{4,5},{5,6},{6,7},{7,4},{8,9},{9,10},{10,1... | collective-permute-start | bytes 61448 | tf_op jit(solution)/shard_map/ppermute | solution.py:21
  282.4 5.6 %collective-permute-start.67 = (f32[10,1,512]{2,1,0:T(1,128)S(1)}, f32[10,1,512]{2,1,0:T(1,128)S(1)}, u32[]{:S(2)}, u32[]{:S(2)}) collective-permute-start(f32[10,1,512]{2,1,0:T(1,128)S(1)} %get-tuple-element.15), channel_id=1, source_target_pairs={{0,1},{1,2},{2,3},{3,0},{4,5},{5,6},{6,7},{7,4},{8,9},{9,10},{10,1... | collective-permute-start | bytes 61448 | tf_op jit(solution)/shard_map/ppermute | solution.py:21
  293.0 5.6 %collective-permute-start.71 = (f32[10,1,512]{2,1,0:T(1,128)S(1)}, f32[10,1,512]{2,1,0:T(1,128)S(1)}, u32[]{:S(2)}, u32[]{:S(2)}) collective-permute-start(f32[10,1,512]{2,1,0:T(1,128)S(1)} %get-tuple-element.13), channel_id=1, source_target_pairs={{0,1},{1,2},{2,3},{3,0},{4,5},{5,6},{6,7},{7,4},{8,9},{9,10},{10,1... | collective-permute-start | bytes 61448 | tf_op jit(solution)/shard_map/ppermute | solution.py:21
  303.6 5.6 %collective-permute-start.75 = (f32[10,1,512]{2,1,0:T(1,128)S(1)}, f32[10,1,512]{2,1,0:T(1,128)S(1)}, u32[]{:S(2)}, u32[]{:S(2)}) collective-permute-start(f32[10,1,512]{2,1,0:T(1,128)S(1)} %get-tuple-element.11), channel_id=1, source_target_pairs={{0,1},{1,2},{2,3},{3,0},{4,5},{5,6},{6,7},{7,4},{8,9},{9,10},{10,1... | collective-permute-start | bytes 61448 | tf_op jit(solution)/shard_map/ppermute | solution.py:21
  (45 other events, 208.6 us)
where the time goes:
time: 311 us; the launch traced here: 310 us
  waiting for transfers between devices  116 us (37%)
  blocking collectives  62.6 us (20%)
  starting transfers between devices  60.7 us (20%)
  local copies, waits for them, and re-layouts  49.4 us (16%)
  other arithmetic  16.7 us (5%)
    ppermute x36, waiting for transfers between devices, with_halo(): lax.ppermute(lax.slice_in_dim(block, block.shape[dim] - width, None, axis...  75.2 us
    ppermute x36, waiting for transfers between devices, with_halo(): lax.ppermute(lax.slice_in_dim(block, 0, width, axis=dim), axis, backward)  40.6 us
    psum x1, blocking collectives, shards(): lax.psum(jnp.sum(coarsest, axis=(1, 2, 3)), ('gx', 'gy')) / cell_count  39.5 us
    ppermute x36, starting transfers between devices, with_halo(): lax.ppermute(lax.slice_in_dim(block, block.shape[dim] - width, None, axis...  36.8 us
    reshape x2, local copies, waits for them, and re-layouts, restrict(): residual.reshape(dims[0] // 2, 2, dims[1] // 2, 2, dims[2] // 2, 2)  21.5 us
    ppermute x36, starting transfers between devices, with_halo(): lax.ppermute(lax.slice_in_dim(block, 0, width, axis=dim), axis, backward)  20 us
    all_gather x1, blocking collectives, coarse_solve(): lax.all_gather(right_side, 'gy', axis=1, tiled=True)  13.1 us
    all_gather x1, blocking collectives, coarse_solve(): lax.all_gather(lax.all_gather(right_side, 'gy', axis=1, tiled=True), 'gx'...  10 us
  transfers between devices with their start and end apart: 76, of which 65 were waited for; matrix products, arithmetic and copies ran while one was open for 17% of the time, Pallas kernels for 0%

commit v1 on v0

v1 whole, which is shorter than its diff:
```python
import functools
import math

import jax
import jax.numpy as jnp
import ml_dtypes
import numpy as np
from jax import lax
from jax.experimental import pallas as pl
from jax.experimental.pallas import tpu as pltpu
from jax.sharding import PartitionSpec as P

LEVELS = 3
SWEEPS = 2
MASS = 0.002
BOTH = ("gx", "gy")
H = 2 * SWEEPS
F32 = jnp.float32
BF16 = jnp.bfloat16
VMEM = pl.BlockSpec(memory_space=pltpu.VMEM)

CORNER0 = (
    (0, 1, 1), (0, 1, 2), (0, 1, 3), (1, 2, 3), (3, 1, 1), (3, 1, 2), (3, 1, 3), (2, 2, 3),
    (1, 1, 1), (1, 1, 2), (1, 1, 3), (1, 1, 4), (2, 1, 1), (2, 1, 2), (2, 1, 3), (2, 1, 4),
    (0, 2, 1), (0, 2, 2), (0, 3, 1), (1, 4, 1), (3, 2, 1), (3, 2, 2), (3, 3, 1), (2, 4, 1),
    (1, 2, 1), (1, 2, 2), (1, 3, 1), (1, 3, 2), (2, 2, 1), (2, 2, 2), (2, 3, 1), (2, 3, 2),
)
CORNER1 = (
    (0, 1, 1), (0, 1, 2), (0, 1, 3), (0, 2, 1), (0, 2, 2), (0, 3, 1), (2, 1, 1), (2, 1, 2),
    (1, 1, 1), (1, 1, 2), (1, 1, 3), (1, 2, 1), (1, 2, 2), (1, 3, 1), (2, 2, 1), None,
)


def call(kernel, out, *args, scratch=()):
    return pl.pallas_call(
        kernel,
        out_shape=[jax.ShapeDtypeStruct(s, F32) for s in out],
        in_specs=[VMEM] * len(args),
        out_specs=[VMEM] * len(out),
        scratch_shapes=[pltpu.VMEM(s, F32) for s in scratch],
        compiler_params=pltpu.CompilerParams(vmem_limit_bytes=48 * 1024 * 1024),
    )(*args)


def moved(block, dx, dy):
    nx, ny = lax.axis_size("gx"), lax.axis_size("gy")
    if dy == 0:
        return lax.ppermute(block, "gx", [(i, (i + dx) % nx) for i in range(nx)])
    if dx == 0:
        return lax.ppermute(block, "gy", [(j, (j + dy) % ny) for j in range(ny)])
    route = []
    for i in range(nx):
        for j in range(ny):
            route.append((i * ny + j, ((i + dx) % nx) * ny + (j + dy) % ny))
    return lax.ppermute(block, BOTH, route)


def split3(x):
    high = x.astype(BF16)
    rest = x - high.astype(F32)
    middle = rest.astype(BF16)
    return high, middle, (rest - middle.astype(F32)).astype(BF16)


def dot(a, b):
    return jnp.dot(a, b, preferred_element_type=F32)


def dot_exact(x, table):
    high, middle, low = split3(x)
    return dot(high, table) + (dot(middle, table) + dot(low, table))


def dot_pair(a, b):
    a_high = a.astype(BF16)
    a_low = (a - a_high.astype(F32)).astype(BF16)
    b_high = b.astype(BF16)
    b_low = (b - b_high.astype(F32)).astype(BF16)
    return dot(a_high, b_high) + (dot(a_high, b_low) + dot(a_low, b_high))


def pair_table(depth):
    table = np.zeros((depth, depth // 2), ml_dtypes.bfloat16)
    table[np.arange(depth), np.arange(depth) // 2] = 1
    return table


def odd_table(depth):
    table = np.zeros((depth, depth // 2), ml_dtypes.bfloat16)
    table[np.arange(1, depth, 2), np.arange(depth // 2)] = 1
    return table


def put_tiles(tiles, x):
    for k in range(tiles.shape[0]):
        tiles[k] = x[:, 128 * k : 128 * k + 128]


def every_other(tiles, start, size):
    return jnp.concatenate(
        [tiles[k, pl.ds(start, size, stride=2), :] for k in range(tiles.shape[0])], axis=1
    )


def back(x, axis):
    return pltpu.roll(x, 1, axis)


def ahead(x, axis):
    return pltpu.roll(x, x.shape[axis] - 1, axis)


def parity2(shape):
    return (lax.broadcasted_iota(jnp.int32, shape, 0) + lax.broadcasted_iota(jnp.int32, shape, 1)) & 1


def row_sum(r, v, wx, wy, wz):
    centre = v[r]
    y, z = wy[r], wz[r]
    total = wx[r] * v[r + 1] + wx[r - 1] * v[r - 1]
    total = total + y * ahead(centre, 0) + back(y * centre, 0)
    return centre, total + z * ahead(centre, 1) + back(z * centre, 1)


def half_sweep(first, last, colour, parity, v, b, wx, wy, wz, rdiag):
    def body(r, carry):
        centre, total = row_sum(r, v, wx, wy, wz)
        mine = parity == ((r + colour) & 1)
        v[r] = jnp.where(mine, (b[r] + total) * rdiag[r], centre)
        return carry

    lax.fori_loop(first, last, body, 0)


def pack_kernel(src, face, pairs, odds, to_up, to_down, to_right, to_left, *rest):
    corners, w1 = rest[:4], rest[4]
    (tx,) = rest[5:]
    rows, cols, depth = src.shape
    half = depth // 2

    for i in range(rows // 2):
        put_tiles(tx, dot(face[0, 2 * i + 1], pairs[...]))
        w1[0, i] = 0.0625 * (every_other(tx, 0, cols // 2) + every_other(tx, 1, cols // 2))
        put_tiles(tx, dot(face[1, 2 * i], pairs[...]) + dot(face[1, 2 * i + 1], pairs[...]))
        w1[1, i] = 0.0625 * every_other(tx, 1, cols // 2)
        put_tiles(tx, dot(face[2, 2 * i], odds[...]) + dot(face[2, 2 * i + 1], odds[...]))
        w1[2, i] = 0.0625 * (every_other(tx, 0, cols // 2) + every_other(tx, 1, cols // 2))

    def plane(a, r):
        return src[r] if a == 0 else face[a - 1, r].astype(F32)

    for out, base in ((to_up, rows - H), (to_down, 0)):
        for a in range(4):
            for k in range(H):
                value = plane(a, base + k)
                if out is to_up and a == 3 and k == 0:
                    value = value + back(value, 1) + plane(1, base - 1)
                for t in range(cols // 8):
                    out[(a * H + k) * (cols // 8) + t] = value[8 * t : 8 * t + 8]
        base1 = 4 * H * (cols // 8)
        for d in range(3):
            for i in range(H // 2):
                out[base1 + d * (H // 2) + i] = jnp.concatenate((w1[d, 2 * i], w1[d, 2 * i + 1]), axis=1)

    for out, base, base1 in ((to_right, cols - H, cols // 2 - H), (to_left, 0, 0)):
        for r in range(rows):
            for t, pair in enumerate(((0, 3), (1, 2))):
                for s, a in enumerate(pair):
                    value = plane(a, r)
                    if out is to_right and a == 3:
                        value_all = value + back(value, 1) + back(plane(2, r), 0)
                        first = lax.broadcasted_iota(jnp.int32, value.shape, 0) == base
                        value = jnp.where(first, value_all, value)
                    out[2 * r + t, H * s : H * s + H] = value[base : base + H]
        for i in range(rows // 2):
            k, lane = 2 * rows + i // 2, half * (i % 2)
            out[k, 0:H, lane : lane + half] = w1[0, i, base1 : base1 + H]
            out[k, H : 2 * H, lane : lane + half] = w1[1, i, base1 : base1 + H]
            k = 2 * rows + rows // 4 + i // 4
            s = H * (i % 2)
            lane = half * ((i // 2) % 2)
            out[k, s : s + H, lane : lane + half] = w1[2, i, base1 : base1 + H]

    for out, (sx, sy) in zip(corners, ((1, 1), (1, -1), (-1, 1), (-1, -1))):
        def at(distance, size, sign):
            return size - distance if sign > 0 else distance - 1

        for n, (a, dx, dy) in enumerate(CORNER0):
            r, c = at(dx, rows, sx), at(dy, cols, sy)
            line = src[r, c : c + 1] if a == 0 else plane(a, r)[c : c + 1]
            out[n // 8, n % 8 : n % 8 + 1] = line
        for n, entry in enumerate(CORNER1):
            if entry is None:
                continue
            d, dx, dy = entry
            r, c = at(dx, rows // 2, sx), at(dy, cols // 2, sy)
            lane = half * (n // 8)
            out[len(CORNER0) // 8, n % 8 : n % 8 + 1, lane : lane + half] = w1[d, r, c : c + 1]


def pre_kernel(src, face, w1, up, down, right, left, c0, c1, c2, c3, pairs, *rest):
    (b, wx, wy, wz, rdiag, v_own, right1, to_up, to_down, w1e, rdiag1, diag1, merged_up, merged_down) = rest[:14]
    v, diag, t512, t256 = rest[14:]
    rows, cols, depth = src.shape
    half = depth // 2
    ext = (b, wx, wy, wz)
    er, ec = rows + 2 * H, cols + 2 * H
    rows1, cols1 = rows // 2, cols // 2

    for r in range(rows):
        b[H + r, H : H + cols] = src[r]
        for d in range(3):
            ext[1 + d][H + r, H : H + cols] = face[d, r].astype(F32)
    for d in range(3):
        for i in range(rows1):
            w1e[d, H + i, H : H + cols1] = w1[d, i]
    tiles = cols // 8
    for msg, base, base1 in ((up, 0, 0), (down, H + rows, H + rows1)):
        for a in range(4):
            for k in range(H):
                for t in range(tiles):
                    ext[a][base + k, H + 8 * t : H + 8 * t + 8] = msg[(a * H + k) * tiles + t]
        n = 4 * H * tiles
        for d in range(3):
            for i in range(H):
                lane = half * (i % 2)
                w1e[d, base1 + i, H : H + cols1] = msg[n + d * (H // 2) + i // 2, :, lane : lane + half]
    for msg, base, base1 in ((right, 0, 0), (left, H + cols, H + cols1)):
        for r in range(rows):
            for t, pair in enumerate(((0, 3), (1, 2))):
                for s, a in enumerate(pair):
                    ext[a][H + r, base : base + H] = msg[2 * r + t, H * s : H * s + H]
        for i in range(rows1):
            k, lane = 2 * rows + i // 2, half * (i % 2)
            w1e[0, H + i, base1 : base1 + H] = msg[k, 0:H, lane : lane + half]
            w1e[1, H + i, base1 : base1 + H] = msg[k, H : 2 * H, lane : lane + half]
            k = 2 * rows + rows // 4 + i // 4
            s = H * (i % 2)
            lane = half * ((i // 2) % 2)
            w1e[2, H + i, base1 : base1 + H] = msg[k, s : s + H, lane : lane + half]
    for msg, (sx, sy) in zip((c0, c1, c2, c3), ((1, 1), (1, -1), (-1, 1), (-1, -1))):
        def at(distance, size, sign):
            return H - distance if sign > 0 else H + size + distance - 1

        for n, (a, dx, dy) in enumerate(CORNER0):
            r, c = at(dx, rows, sx), at(dy, cols, sy)
            ext[a][r, c : c + 1] = msg[n // 8, n % 8 : n % 8 + 1]
        for n, entry in enumerate(CORNER1):
            if entry is None:
                continue
            d, dx, dy = entry
            r, c = at(dx, rows1, sx), at(dy, cols1, sy)
            lane = half * (n // 8)
            w1e[d, r, c : c + 1] = msg[len(CORNER0) // 8, n % 8 : n % 8 + 1, lane : lane + half]

    parity = parity2((ec, depth))
    low_col = lax.broadcasted_iota(jnp.int32, (ec, depth), 0) == 0

    def finish(r, total):
        diag[r] = total
        inverse = 1.0 / total
        rdiag[r] = inverse
        v[r] = jnp.where(parity == (r & 1), b[r] * inverse, 0.0)

    y = wy[0]
    finish(0, MASS + wx[0] + wz[0] + y + back(y, 0))

    def diag_body(r, carry):
        y, z = wy[r], wz[r]
        total = MASS + wx[r] + wx[r - 1] + y
        finish(r, total + jnp.where(low_col, z, z + back(z, 1) + back(y, 0)))
        return carry

    lax.fori_loop(1, er, diag_body, 0)
    half_sweep(1, er - 1, 1, parity, v, b, wx, wy, wz, rdiag)
    half_sweep(2, er - 2, 0, parity, v, b, wx, wy, wz, rdiag)
    half_sweep(3, er - 3, 1, parity, v, b, wx, wy, wz, rdiag)

    def residual_body(i, carry):
        total = 0.0
        for k in range(2):
            r = H + 2 * i + k
            centre, around = row_sum(r, v, wx, wy, wz)
            total = total + (b[r] - (diag[r] * centre - around))
        t512[i] = total
        return carry

    lax.fori_loop(0, rows1, residual_body, 0)
    put_tiles(t256, dot_exact(t512[...].reshape(rows1 * ec, depth), pairs[...]))
    for i in range(rows1):
        start = i * ec + H
        right1[i] = 0.125 * (every_other(t256, start, cols1) + every_other(t256, start + 1, cols1))

    for r in range(rows1 + 2 * H):
        y, z = w1e[1, r], w1e[2, r]
        total = MASS + w1e[0, r] + w1e[0, max(r - 1, 0)] + y + back(y, 0) + z + back(z, 1)
        diag1[r] = total
        rdiag1[r] = 1.0 / total
    for k in range(H):
        value = right1[rows1 - H + k]
        to_up[k] = value * rdiag1[rows1 + k, H : H + cols1] if k == 0 else value
        value = right1[k]
        to_down[k] = value * rdiag1[H + k, H : H + cols1] if k == H - 1 else value

    own_parity = parity2((cols, depth))
    for r in range(rows):
        v_own[r] = v[H + r, H : H + cols]
    for k in range(H // 2):
        for out, base in ((merged_up, rows - H), (merged_down, 0)):
            r = base + 2 * k
            out[k] = jnp.where(own_parity == ((r + 1) & 1), v_own[r], v_own[r + 1])


def pack1_kernel(own, up, down, rdiag1, to_right, to_left):
    rows, cols, depth = own.shape
    for out, base in ((to_right, cols - H), (to_left, 0)):
        for n in range(rows + 2 * H - 2):
            r = n + 1
            if r < H:
                value, distance = up[r], H - r
            elif r < H + rows:
                value, distance = own[r - H], 0
            else:
                value, distance = down[r - H - rows], r - H - rows + 1
            if out is to_right:
                c = cols - (H - distance)
            else:
                c = H - distance - 1
            edge = lax.broadcasted_iota(jnp.int32, value.shape, 0) == c
            value = jnp.where(edge, value * rdiag1[r, H : H + cols], value)
            s = H * (n % 2)
            out[n // 2, s : s + H] = value[base : base + H]


def fill1(ext, own, up, down, right, left):
    rows, cols, depth = own.shape
    for r in range(rows):
        ext[H + r, H : H + cols] = own[r]
    for k in range(H):
        ext[k, H : H + cols] = up[k]
        ext[H + rows + k, H : H + cols] = down[k]
    for n in range(rows + 2 * H - 2):
        s = H * (n % 2)
        ext[n + 1, 0:H] = right[n // 2, s : s + H]
        ext[n + 1, H + cols : 2 * H + cols] = left[n // 2, s : s + H]


def pre1_kernel(own, up, down, right, left, w1e, rdiag1, diag1, pairs, merged_up, merged_down, *rest):
    b1, v_own, chunk, to_up, to_down = rest[:5]
    v, t256, t128 = rest[5:]
    rows, cols, depth = own.shape
    er, ec = rows + 2 * H, cols + 2 * H
    half = depth // 2
    wx, wy, wz = w1e.at[0], w1e.at[1], w1e.at[2]
    fill1(b1, own, up, down, right, left)
    parity = parity2((ec, depth))
    col = lax.broadcasted_iota(jnp.int32, (ec, depth), 0)
    col_distance = jnp.maximum(jnp.maximum(H - col, col - (H + cols - 1)), 0)
    for r in range(er):
        distance = max(H - r, r - (H + rows - 1), 0)
        first = jnp.where(col_distance + distance >= H, b1[r], b1[r] * rdiag1[r])
        v[r] = jnp.where(parity == (r & 1), first, 0.0)
    half_sweep(1, er - 1, 1, parity, v, b1, wx, wy, wz, rdiag1)
    half_sweep(2, er - 2, 0, parity, v, b1, wx, wy, wz, rdiag1)
    half_sweep(3, er - 3, 1, parity, v, b1, wx, wy, wz, rdiag1)
    for i in range(rows // 2):
        total = 0.0
        for k in range(2):
            r = H + 2 * i + k
            centre, around = row_sum(r, v, wx, wy, wz)
            total = total + (b1[r] - (diag1[r] * centre - around))
        t256[i] = total
    n = rows // 2
    put_tiles(t128, dot_exact(t256[...].reshape(n * ec, depth), pairs[...]))
    for i in range(n):
        start = i * ec + H
        chunk[i * (cols // 2) : (i + 1) * (cols // 2)] = 0.125 * (
            every_other(t128, start, cols // 2) + every_other(t128, start + 1, cols // 2)
        )
    lane = lax.broadcasted_iota(jnp.int32, (1, half), 1)
    row_odd = lax.broadcasted_iota(jnp.int32, (cols, depth), 0) & 1
    depth_odd = lax.broadcasted_iota(jnp.int32, (cols, depth), 1) & 1
    parts = [0.0, 0.0, 0.0]
    for i in range(rows):
        if i % 2 == 1:
            parts[0] = parts[0] + w1e[0, H + i, H : H + cols]
        parts[1] = parts[1] + jnp.where(row_odd == 1, w1e[1, H + i, H : H + cols], 0.0)
        parts[2] = parts[2] + jnp.where(depth_odd == 1, w1e[2, H + i, H : H + cols], 0.0)
    line = jnp.zeros((1, half), F32)
    for d in range(3):
        line = jnp.where(lane == d, 0.0625 * jnp.sum(parts[d]), line)
    n = (rows // 2) * (cols // 2)
    chunk[n : n + 1] = line

    for r in range(rows):
        v_own[r] = v[H + r, H : H + cols]
    for out, base, merged in ((to_up, rows - H, merged_up), (to_down, 0, merged_down)):
        for k in range(H // 2):
            out[k] = jnp.concatenate((v_own[base + 2 * k], v_own[base + 2 * k + 1]), axis=1)
            for t in range(merged.shape[1] // 8):
                out[H // 2 + k * (merged.shape[1] // 8) + t] = merged[k, 8 * t : 8 * t + 8]


def pack_v_kernel(v1, up, down, v0, to_right, to_left):
    rows1, cols1, half = v1.shape
    rows, cols, depth = v0.shape
    tiles = cols // 8
    parity = parity2((cols, depth))
    for out, base1, base in ((to_right, cols1 - H, cols - H), (to_left, 0, 0)):
        for n in range(rows1 + 2 * H - 2):
            r = n + 1
            if r < H:
                line = up[r // 2, base1 : base1 + H, half * (r % 2) : half * (r % 2) + half]
            elif r < H + rows1:
                line = v1[r - H, base1 : base1 + H]
            else:
                k = r - H - rows1
                line = down[k // 2, base1 : base1 + H, half * (k % 2) : half * (k % 2) + half]
            s, lane = H * (n % 2), half * ((n // 2) % 2)
            out[n // 4, s : s + H, lane : lane + half] = line
        start = (rows1 + 2 * H - 2 + 3) // 4
        for r in range(rows):
            value = v0[r]
            value = jnp.where(parity == ((r + 1) & 1), value, ahead(value, 0))
            for p in range(H // 2):
                n = p * rows + r
                out[start + n // 8, n % 8 : n % 8 + 1] = value[base + 2 * p : base + 2 * p + 1]
        start += (rows * (H // 2)) // 8
        for m, msg in enumerate((up, down)):
            for k in range(H // 2):
                c = base // 8
                tile = msg[H // 2 + k * tiles + c]
                n = m * (H // 2) + k
                out[start + n // 2, H * (n % 2) : H * (n % 2) + H] = tile[base % 8 : base % 8 + H]


def solve_kernel(got, forward, back_x, back_y, depth_in, depth_out, eig_x, eig_y, eig_z, out, *, count):
    devices, lines, depth = got.shape
    own = lines - 1
    values = jnp.concatenate([got[d, 0:own] for d in range(devices)], axis=0)
    sums = got[0, own : own + 1]
    for d in range(1, devices):
        sums = sums + got[d, own : own + 1]
    sums = sums * (1.0 / count)
    lam = MASS + sums[0:1, 0:1] * eig_x[...] + sums[0:1, 1:2] * eig_y[...] + sums[0:1, 2:3] * eig_z[...]
    spec = dot_pair(forward[...], dot_pair(values, depth_in[...]))
    spec = spec / (lam * float(count))
    spec = dot_pair(spec, depth_out[...])
    rx, ry = back_x.shape[0], back_y.shape[0]
    table = jnp.concatenate([back_x[i : i + 1] * back_y[...] for i in range(rx)], axis=0)
    out[...] = dot_pair(table, spec).reshape(out.shape)


def post1_kernel(v1, up, down, right, left, correction, b1, w1e, rdiag1, out, v):
    rows, cols, depth = v1.shape
    er, ec = rows + 2 * H, cols + 2 * H
    for r in range(rows):
        v[H + r, H : H + cols] = v1[r]
    for k in range(H):
        lane = depth * (k % 2)
        v[k, H : H + cols] = up[k // 2, :, lane : lane + depth]
        v[H + rows + k, H : H + cols] = down[k // 2, :, lane : lane + depth]
    for n in range(rows + 2 * H - 2):
        s, lane = H * (n % 2), depth * ((n // 2) % 2)
        v[n + 1, 0:H] = right[n // 4, s : s + H, lane : lane + depth]
        v[n + 1, H + cols : 2 * H + cols] = left[n // 4, s : s + H, lane : lane + depth]
    for r in range(er):
        v[r] = v[r] + correction[r]
    parity = parity2((ec, depth))
    wx, wy, wz = w1e.at[0], w1e.at[1], w1e.at[2]
    half_sweep(1, er - 1, 0, parity, v, b1, wx, wy, wz, rdiag1)
    half_sweep(2, er - 2, 1, parity, v, b1, wx, wy, wz, rdiag1)
    half_sweep(3, er - 3, 0, parity, v, b1, wx, wy, wz, rdiag1)
    half_sweep(4, er - 4, 1, parity, v, b1, wx, wy, wz, rdiag1)
    for r in range(rows):
        out[r] = v[H + r, H : H + cols]


def pack2_kernel(own, up, down, to_right, to_left):
    rows, cols, depth = own.shape
    h = H // 2
    for out, base in ((to_right, cols - h), (to_left, 0)):
        for n in range(rows + 2 * h):
            if n < h:
                line = up[n, base : base + h]
            elif n < h + rows:
                line = own[n - h, base : base + h]
            else:
                line = down[n - h - rows, base : base + h]
            s = h * (n % 4)
            out[n // 4, s : s + h] = line


def post_kernel(v0, up, down, right, left, own1, up1, down1, right1, left1, b, wx, wy, wz, rdiag, spread, out, v, t256):
    rows, cols, depth = v0.shape
    rows1, cols1, half = own1.shape
    er, ec = rows + 2 * H, cols + 2 * H
    h = H // 2
    tiles = cols // 8
    for r in range(rows):
        v[H + r, H : H + cols] = v0[r]
    for msg, base in ((up, 0), (down, H + rows)):
        for k in range(H // 2):
            for t in range(tiles):
                tile = msg[H // 2 + k * tiles + t]
                v[base + 2 * k, H + 8 * t : H + 8 * t + 8] = tile
                v[base + 2 * k + 1, H + 8 * t : H + 8 * t + 8] = tile
    for msg, base in ((right, 0), (left, H + cols)):
        start = (rows1 + 2 * H - 2 + 3) // 4
        for r in range(rows):
            for p in range(H // 2):
                n = p * rows + r
                line = msg[start + n // 8, n % 8 : n % 8 + 1]
                v[H + r, base + 2 * p : base + 2 * p + 2] = jnp.broadcast_to(line, (2, depth))
        start += (rows * (H // 2)) // 8
        for m, row in enumerate((0, H + rows)):
            for k in range(H // 2):
                n = m * (H // 2) + k
                block = msg[start + n // 2, H * (n % 2) : H * (n % 2) + H]
                v[row + 2 * k, base : base + H] = block
                v[row + 2 * k + 1, base : base + H] = block
    ec1 = cols1 + 2 * h
    for n in range(rows1 + 2 * h):
        if n < h:
            line = up1[n]
        elif n < h + rows1:
            line = own1[n - h]
        else:
            line = down1[n - h - rows1]
        s = h * (n % 4)
        t256[n, h : h + cols1] = line
        t256[n, 0:h] = right1[n // 4, s : s + h]
        t256[n, h + cols1 : ec1] = left1[n // 4, s : s + h]
        t256[n, ec1:] = jnp.zeros((t256.shape[1] - ec1, half), F32)
    n1 = rows1 + 2 * h
    wide = dot_exact(t256[...].reshape(n1 * t256.shape[1], half), spread[...])
    wide = wide.reshape(n1, t256.shape[1], depth)
    for n in range(n1):
        line = wide[n, 0:ec1]
        line = jnp.broadcast_to(line[:, None, :], (ec1, 2, depth)).reshape(2 * ec1, depth)
        v[2 * n] = v[2 * n] + line
        v[2 * n + 1] = v[2 * n + 1] + line
    parity = parity2((ec, depth))
    half_sweep(1, er - 1, 0, parity, v, b, wx, wy, wz, rdiag)
    half_sweep(2, er - 2, 1, parity, v, b, wx, wy, wz, rdiag)
    half_sweep(3, er - 3, 0, parity, v, b, wx, wy, wz, rdiag)
    half_sweep(4, er - 4, 1, parity, v, b, wx, wy, wz, rdiag)
    for r in range(rows):
        out[r] = v[H + r, H : H + cols]


def hartley(rows, columns, length):
    angle = (np.outer(rows, columns) % length) * (2.0 * math.pi / length)
    return np.cos(angle) + np.sin(angle)


def waves(length):
    return 2.0 * (1.0 - np.cos(np.arange(length) * (2.0 * math.pi / length)))


def coarse_correction(chunk, rows, cols, depth):
    nx, ny = lax.axis_size("gx"), lax.axis_size("gy")
    total_rows, total_cols = rows * nx, cols * ny
    count = total_rows * total_cols * depth
    got = lax.all_to_all(jnp.broadcast_to(chunk[None], (nx * ny,) + chunk.shape), BOTH, 0, 0)
    out_rows, out_cols = 2 * rows + 2 * H, 2 * cols + 2 * H
    rows_ids = (np.arange(-H, 2 * total_rows + H) // 2) % total_rows
    cols_ids = (np.arange(-H, 2 * total_cols + H) // 2) % total_cols
    table_x = hartley(rows_ids, np.arange(total_rows), total_rows)
    table_y = hartley(cols_ids, np.arange(total_cols), total_cols)
    depth_in = hartley(np.arange(depth), np.arange(depth), depth)
    depth_out = np.repeat(depth_in, 2, axis=1)

    def own(table, axis, step, size):
        table = jnp.asarray(table, F32)
        return lax.dynamic_slice_in_dim(table, lax.axis_index(axis) * step, size, 0)

    if total_rows * total_cols <= 512:
        cells = total_rows * total_cols
        order = np.arange(cells).reshape(nx, rows, ny, cols).transpose(0, 2, 1, 3).reshape(-1)
        forward = np.einsum(
            "ax,by->abxy",
            hartley(np.arange(total_rows), np.arange(total_rows), total_rows),
            hartley(np.arange(total_cols), np.arange(total_cols), total_cols),
        ).reshape(cells, cells)[:, order]
        back_x = own(np.repeat(table_x, total_cols, axis=1), "gx", 2 * rows, out_rows)
        back_y = own(np.tile(table_y, (1, total_rows)), "gy", 2 * cols, out_cols)
        ones = np.ones((cells, depth))
        eig = (
            np.repeat(waves(total_rows), total_cols)[:, None] * ones,
            np.tile(waves(total_cols), total_rows)[:, None] * ones,
            waves(depth)[None, :] * ones,
        )
        constants = [jnp.asarray(x, F32) for x in (forward, depth_in, depth_out) + eig]
        return call(
            functools.partial(solve_kernel, count=count),
            [(out_rows, out_cols, 2 * depth)],
            got, constants[0], back_x, back_y, *constants[1:],
        )[0]

    hi = lax.Precision.HIGHEST
    averages = jnp.sum(got[:, rows * cols, :3], axis=0) / count
    full = got[:, : rows * cols].reshape(nx, ny, rows, cols, depth)
    full = full.transpose(0, 2, 1, 3, 4).reshape(total_rows, total_cols, depth)
    f32 = lambda x: jnp.asarray(x, F32)
    spec = jnp.einsum("abz,zk->abk", full, f32(depth_in), precision=hi)
    spec = jnp.einsum("ij,jbz->ibz", f32(hartley(np.arange(total_rows), np.arange(total_rows), total_rows)), spec, precision=hi)
    spec = jnp.einsum("ij,ajz->aiz", f32(hartley(np.arange(total_cols), np.arange(total_cols), total_cols)), spec, precision=hi)
    lam = (
        MASS
        + averages[0] * f32(waves(total_rows))[:, None, None]
        + averages[1] * f32(waves(total_cols))[None, :, None]
        + averages[2] * f32(waves(depth))[None, None, :]
    )
    spec = spec / (lam * float(count))
    out = jnp.einsum("ij,jbz->ibz", own(table_x, "gx", 2 * rows, out_rows), spec, precision=hi)
    out = jnp.einsum("ij,ajz->aiz", own(table_y, "gy", 2 * cols, out_cols), out, precision=hi)
    return jnp.einsum("abz,zk->abk", out, f32(depth_out), precision=hi)


def shards(source, face_coef):
    rows, cols, depth = source.shape
    rows1, cols1, depth1 = rows // 2, cols // 2, depth // 2
    er, ec, er1, ec1 = rows + 2 * H, cols + 2 * H, rows1 + 2 * H, cols1 + 2 * H
    pairs = jnp.asarray(pair_table(depth))
    odds = jnp.asarray(odd_table(depth))

    nx_tiles = 4 * H * (cols // 8) + 3 * (H // 2)
    ny_tiles = 2 * rows + rows // 4 + (rows // 2 + 3) // 4
    corner_tiles = len(CORNER0) // 8 + 1
    *sends, w1 = call(
        pack_kernel,
        [(nx_tiles, 8, depth)] * 2 + [(ny_tiles, 8, depth)] * 2 + [(corner_tiles, 8, depth)] * 4 + [(3, rows1, cols1, depth1)],
        source, face_coef, pairs, odds,
        scratch=[(depth1 // 128, cols, 128)],
    )
    right, left = moved(sends[2], 0, 1), moved(sends[3], 0, -1)
    corners = [moved(m, dx, dy) for m, (dx, dy) in zip(sends[4:], ((1, 1), (1, -1), (-1, 1), (-1, -1)))]
    up, down = moved(sends[0], 1, 0), moved(sends[1], -1, 0)

    b, wx, wy, wz, rdiag, v0, right1, to_up, to_down, w1e, rdiag1, diag1, merged_up, merged_down = call(
        pre_kernel,
        [(er, ec, depth)] * 5
        + [(rows, cols, depth), (rows1, cols1, depth1)]
        + [(H, cols1, depth1)] * 2
        + [(3, er1, ec1, depth1), (er1, ec1, depth1), (er1, ec1, depth1)]
        + [(H // 2, cols, depth)] * 2,
        source, face_coef, w1, up, down, right, left, *corners, pairs,
        scratch=[(er, ec, depth), (er, ec, depth), (rows1, ec, depth), (depth1 // 128, rows1 * ec, 128)],
    )

    up, down = moved(to_up, 1, 0), moved(to_down, -1, 0)
    beside = (er1 - 2 + 1) // 2
    to_right, to_left = call(pack1_kernel, [(beside, 8, depth1)] * 2, right1, up, down, rdiag1)
    right, left = moved(to_right, 0, 1), moved(to_left, 0, -1)
    x_tiles = H // 2 + (H // 2) * (cols // 8)
    b1, v1, chunk, to_up, to_down = call(
        pre1_kernel,
        [(er1, ec1, depth1), (rows1, cols1, depth1), (rows1 * cols1 // 4 + 1, depth1 // 2)]
        + [(x_tiles, 8, depth)] * 2,
        right1, up, down, right, left, w1e, rdiag1, diag1, jnp.asarray(pair_table(depth1)), merged_up, merged_down,
        scratch=[(er1, ec1, depth1), (rows1 // 2, ec1, depth1), (depth1 // 256, rows1 // 2 * ec1, 128)],
    )

    up, down = moved(to_up, 1, 0), moved(to_down, -1, 0)
    correction2 = coarse_correction(chunk, rows1 // 2, cols1 // 2, depth1 // 2)
    y_tiles = (er1 - 2 + 3) // 4 + (rows * (H // 2)) // 8 + H // 2
    to_right, to_left = call(pack_v_kernel, [(y_tiles, 8, depth)] * 2, v1, up, down, v0)
    right, left = moved(to_right, 0, 1), moved(to_left, 0, -1)
    (v1,) = call(
        post1_kernel,
        [(rows1, cols1, depth1)],
        v1, up, down, right, left, correction2, b1, w1e, rdiag1,
        scratch=[(er1, ec1, depth1)],
    )

    h = H // 2
    up1, down1 = moved(v1[rows1 - h :], 1, 0), moved(v1[:h], -1, 0)
    to_right, to_left = call(pack2_kernel, [((rows1 + 2 * h) // 4, 8, depth1)] * 2, v1, up1, down1)
    right1, left1 = moved(to_right, 0, 1), moved(to_left, 0, -1)
    (out,) = call(
        post_kernel,
        [(rows, cols, depth)],
        v0, up, down, right, left, v1, up1, down1, right1, left1, b, wx, wy, wz, rdiag,
        jnp.asarray(np.ascontiguousarray(pair_table(depth).T)),
        scratch=[(er, ec, depth), (rows1 + 2 * h, 16, depth1)],
    )
    return out


def solution(mesh):
    return jax.shard_map(
        shards,
        mesh=mesh,
        in_specs=(P("gx", "gy", None), P(None, "gx", "gy", None)),
        out_specs=P("gx", "gy", None),
        check_vma=False,
    )
```

time: 311 us -> 105 us (0.34)
  waiting for transfers between devices: 116 us -> 39.1 us
  blocking collectives: 62.6 us -> 0 us
  local copies, waits for them, and re-layouts: 49.4 us -> 10 us
  starting transfers between devices: 60.7 us -> 34.7 us
  Pallas kernels: 0 us -> 20.7 us
  other arithmetic: 16.7 us -> 0 us
    ppermute x76 -> x20, waiting for transfers between devices: 116 us -> 35.6 us  [the longest x4 28.8 us: moved(): return lax.ppermute(block, BOTH, route)]
    psum x1 -> x0, blocking collectives: 39.5 us -> none  [shards(): lax.psum(jnp.sum(coarsest, axis=(1, 2, 3)), ('gx', 'gy')) / cell_count]
    ppermute x76 -> x20, starting transfers between devices: 60.7 us -> 30.2 us  [the longest x8 15.4 us: moved(): return lax.ppermute(block, 'gy', [(j, (j + dy) % ny) for j in range(ny)])]
    reshape x7 -> x0, local copies, waits for them, and re-layouts: 24.4 us -> none  [the longest x2 21.5 us: restrict(): residual.reshape(dims[0] // 2, 2, dims[1] // 2, 2, dims[2] // 2, 2)]
    all_gather x2 -> x0, blocking collectives: 23.1 us -> none  [the longest x1 13.1 us: coarse_solve(): lax.all_gather(right_side, 'gy', axis=1, tiled=True)]
    slice x90 -> x1, local copies, waits for them, and re-layouts: 23.1 us -> 0.01 us  [shards(): up1, down1 = (moved(v1[rows1 - h:], 1, 0), moved(v1[:h], -1, 0))]
    pallas_call x0 -> x9, Pallas kernels: none -> 20.7 us  [call(): pl.pallas_call(kernel, out_shape=[jax.ShapeDtypeStruct(s, F32) for s in o...]
    reduce_sum x3 -> x0, other arithmetic: 8.9 us -> none  [the longest x2 8.79 us: restrict(): residual.reshape(dims[0] // 2, 2, dims[1] // 2, 2, dims[2] // 2, 2)]
  transfers between devices with their start and end apart: 76 -> 21, of which waited for: 65 -> 10; matrix products, arithmetic and copies ran while one was open for 17% -> 3% of each run, Pallas kernels for 0% -> 2%
where the time goes in v1:
time: 105 us
  waiting for transfers between devices  39.1 us (37%)
  starting transfers between devices  34.7 us (33%)
  Pallas kernels  20.7 us (20%)
  local copies, waits for them, and re-layouts  10 us (10%)
    ppermute x4, waiting for transfers between devices, moved(): return lax.ppermute(block, BOTH, route)  28.8 us
    pallas_call x9, Pallas kernels, call(): pl.pallas_call(kernel, out_shape=[jax.ShapeDtypeStruct(s, F32) for s in o...  20.7 us
    ppermute x8, starting transfers between devices, moved(): return lax.ppermute(block, 'gy', [(j, (j + dy) % ny) for j in range(ny)])  15.4 us
    ppermute x8, starting transfers between devices, moved(): return lax.ppermute(block, 'gx', [(i, (i + dx) % nx) for i in range(nx)])  13.8 us
    unnamed x34, local copies, waits for them, and re-layouts  7.24 us
    all_to_all x1, starting transfers between devices, coarse_correction(): lax.all_to_all(jnp.broadcast_to(chunk[None], (nx * ny,) + chunk.shape), B...  4.45 us
    ppermute x8, waiting for transfers between devices, moved(): return lax.ppermute(block, 'gy', [(j, (j + dy) % ny) for j in range(ny)])  3.74 us
    all_to_all x1, waiting for transfers between devices, coarse_correction(): lax.all_to_all(jnp.broadcast_to(chunk[None], (nx * ny,) + chunk.shape), B...  3.52 us
  transfers between devices with their start and end apart: 21, of which 10 were waited for; matrix products, arithmetic and copies ran while one was open for 3% of the time, Pallas kernels for 2%

profile of v1, /device:TPU:0, one launch (start us, length us, event | category | flops | bytes accessed | tf_op | source)
XLA Modules:
  0.0 104.7 jit_solution(16068136216335166440)
XLA Ops:
  0.0 1.0 copy-done
  1.0 0.9 copy-done.1
  1.9 0.9 copy-done.2
  2.9 0.9 copy-done.9
  5.2 2.9 %collective-permute-start.1 = (f32[38,8,512]{2,1,0:T(8,128)S(1)}, f32[38,8,512]{2,1,0:T(8,128)S(1)}, u32[]{:S(2)}, u32[]{:S(2)}) collective-permute-start(f32[38,8,512]{2,1,0:T(8,128)S(1)} %get-tuple-element.41), channel_id=1, source_target_pairs={{0,28},{4,0},{8,4},{12,8},{16,12},{20,16},{24,20},{28,24},{1,29},{... | collective-permute-start | bytes 1867784 | tf_op jit(solution)/shard_map/ppermute | solution.py:48
  9.0 1.6 %collective-permute-start.2 = (f32[19,8,512]{2,1,0:T(8,128)S(1)}, f32[19,8,512]{2,1,0:T(8,128)S(1)}, u32[]{:S(2)}, u32[]{:S(2)}) collective-permute-start(f32[19,8,512]{2,1,0:T(8,128)S(1)} %get-tuple-element.42), channel_id=1, source_target_pairs={{0,1},{1,2},{2,3},{3,0},{4,5},{5,6},{6,7},{7,4},{8,9},{9,10},{10,1... | collective-permute-start | bytes 933896 | tf_op jit(solution)/shard_map/ppermute | solution.py:50
  10.6 2.2 %collective-permute-start.3 = (f32[19,8,512]{2,1,0:T(8,128)S(1)}, f32[19,8,512]{2,1,0:T(8,128)S(1)}, u32[]{:S(2)}, u32[]{:S(2)}) collective-permute-start(f32[19,8,512]{2,1,0:T(8,128)S(1)} %get-tuple-element.43), channel_id=1, source_target_pairs={{0,3},{1,0},{2,1},{3,2},{4,7},{5,4},{6,5},{7,6},{8,11},{9,8},{10,9... | collective-permute-start | bytes 933896 | tf_op jit(solution)/shard_map/ppermute | solution.py:50
  12.8 3.5 %collective-permute-done.4.c0 = f32[5,8,512]{2,1,0:T(8,128)S(1)} collective-permute-done((f32[5,8,512]{2,1,0:T(8,128)S(1)}, f32[5,8,512]{2,1,0:T(8,128)S(1)}, u32[]{:S(2)}, u32[]{:S(2)}) %collective-permute-start.4) | collective-permute-done | bytes 81952 | tf_op jit(solution)/shard_map/ppermute | solution.py:55
  16.4 15.2 %collective-permute-done.5.c1 = f32[5,8,512]{2,1,0:T(8,128)S(1)} collective-permute-done((f32[5,8,512]{2,1,0:T(8,128)S(1)}, f32[5,8,512]{2,1,0:T(8,128)S(1)}, u32[]{:S(2)}, u32[]{:S(2)}) %collective-permute-start.5) | collective-permute-done | bytes 81952 | tf_op jit(solution)/shard_map/ppermute | solution.py:55
  31.8 6.2 %collective-permute-done.6.c2 = f32[5,8,512]{2,1,0:T(8,128)S(1)} collective-permute-done((f32[5,8,512]{2,1,0:T(8,128)S(1)}, f32[5,8,512]{2,1,0:T(8,128)S(1)}, u32[]{:S(2)}, u32[]{:S(2)}) %collective-permute-start.6) | collective-permute-done | bytes 81952 | tf_op jit(solution)/shard_map/ppermute | solution.py:55
  38.0 3.9 %collective-permute-done.7.c3 = f32[5,8,512]{2,1,0:T(8,128)S(1)} collective-permute-done((f32[5,8,512]{2,1,0:T(8,128)S(1)}, f32[5,8,512]{2,1,0:T(8,128)S(1)}, u32[]{:S(2)}, u32[]{:S(2)}) %collective-permute-start.7) | collective-permute-done | bytes 81952 | tf_op jit(solution)/shard_map/ppermute | solution.py:55
  41.8 7.8 %shard_map.137 = (f32[16,24,512]{2,1,0:T(8,128)S(1)}, f32[16,24,512]{2,1,0:T(8,128)}, f32[16,24,512]{2,1,0:T(8,128)}, f32[16,24,512]{2,1,0:T(8,128)}, f32[16,24,...) custom-call(f32[8,16,512]{2,1,0:T(8,128)S(1)} %copy-done.1, ...), custom_call_target="tpu_custom_call" | custom-call | tf_op jit(solution)/shard_map/pallas_call | solution.py:35
  50.4 3.0 %collective-permute-start.9 = (f32[4,8,256]{2,1,0:T(8,128)S(1)}, f32[4,8,256]{2,1,0:T(8,128)S(1)}, u32[]{:S(2)}, u32[]{:S(2)}) collective-permute-start(f32[4,8,256]{2,1,0:T(8,128)S(1)} %get-tuple-element.51), channel_id=1, source_target_pairs={{0,28},{4,0},{8,4},{12,8},{16,12},{20,16},{24,20},{28,24},{1,29},{... | collective-permute-start | bytes 98312 | tf_op jit(solution)/shard_map/ppermute | solution.py:48
  53.4 1.6 %collective-permute-done.8.up = f32[4,8,256]{2,1,0:T(8,128)S(1)} collective-permute-done((f32[4,8,256]{2,1,0:T(8,128)S(1)}, f32[4,8,256]{2,1,0:T(8,128)S(1)}, u32[]{:S(2)}, u32[]{:S(2)}) %collective-permute-start.8) | collective-permute-done | bytes 32800 | tf_op jit(solution)/shard_map/ppermute | solution.py:48
  55.8 3.1 %collective-permute-start.11 = (f32[5,8,256]{2,1,0:T(8,128)S(1)}, f32[5,8,256]{2,1,0:T(8,128)S(1)}, u32[]{:S(2)}, u32[]{:S(2)}) collective-permute-start(f32[5,8,256]{2,1,0:T(8,128)S(1)} %get-tuple-element.54), channel_id=1, source_target_pairs={{0,3},{1,0},{2,1},{3,2},{4,7},{5,4},{6,5},{7,6},{8,11},{9,8},{10,9... | collective-permute-start | bytes 122888 | tf_op jit(solution)/shard_map/ppermute | solution.py:50
  58.9 2.0 %collective-permute-done.10.right = f32[5,8,256]{2,1,0:T(8,128)S(1)} collective-permute-done((f32[5,8,256]{2,1,0:T(8,128)S(1)}, f32[5,8,256]{2,1,0:T(8,128)S(1)}, u32[]{:S(2)}, u32[]{:S(2)}) %collective-permute-start.10) | collective-permute-done | bytes 40992 | tf_op jit(solution)/shard_map/ppermute | solution.py:50
  60.9 2.3 %shard_map.139 = (f32[12,16,256]{2,1,0:T(8,128)S(1)}, f32[4,8,256]{2,1,0:T(8,128)S(1)}, f32[9,128]{1,0:T(8,128)S(1)}, f32[6,8,512]{2,1,0:T(8,128)S(1)}, f32[6,8,512]{2,1,0:T(8,128)S(1)}) custom-call(f32[4,8,256]{2,1,0:T(8,128)S(1)} %get-tuple-element.49.own, f32[4,8,256]{2,1,0:T(8,128)S(1)} %collective-permute-done.8.up, ...), custom_call_target="tpu_custom_call" | custom-call | tf_op jit(solution)/shard_map/pallas_call | solution.py:35
  63.3 2.6 %collective-permute-start.13 = (f32[6,8,512]{2,1,0:T(8,128)S(1)}, f32[6,8,512]{2,1,0:T(8,128)S(1)}, u32[]{:S(2)}, u32[]{:S(2)}) collective-permute-start(f32[6,8,512]{2,1,0:T(8,128)S(1)} %get-tuple-element.60), channel_id=1, source_target_pairs={{0,28},{4,0},{8,4},{12,8},{16,12},{20,16},{24,20},{28,24},{1,29},{... | collective-permute-start | bytes 294920 | tf_op jit(solution)/shard_map/ppermute | solution.py:48
  66.6 4.4 %all-to-all-start = ((f32[32,9,128]{2,1,0:T(8,128)}), f32[32,9,128]{2,1,0:T(8,128)S(1)}, u32[]{:S(2)}, u32[]{:S(2)}) async-start(f32[32,9,128]{2,1,0:T(8,128)} %broadcast_in_dim.2), calls=%async_computation | async-start | bytes 524288 | tf_op jit(solution)/shard_map/all_to_all | solution.py:565
  71.9 1.8 %collective-permute-start.14 = (f32[7,8,512]{2,1,0:T(8,128)}, f32[7,8,512]{2,1,0:T(8,128)S(1)}, u32[]{:S(2)}, u32[]{:S(2)}) collective-permute-start(f32[7,8,512]{2,1,0:T(8,128)} %get-tuple-element.62), channel_id=1, source_target_pairs={{0,1},{1,2},{2,3},{3,0},{4,5},{5,6},{6,7},{7,4},{8,9},{9,10},{10,1... | collective-permute-start | bytes 344072 | tf_op jit(solution)/shard_map/ppermute | solution.py:50
  73.7 2.1 %collective-permute-start.15 = (f32[7,8,512]{2,1,0:T(8,128)}, f32[7,8,512]{2,1,0:T(8,128)S(1)}, u32[]{:S(2)}, u32[]{:S(2)}) collective-permute-start(f32[7,8,512]{2,1,0:T(8,128)} %get-tuple-element.63), channel_id=1, source_target_pairs={{0,3},{1,0},{2,1},{3,2},{4,7},{5,4},{6,5},{7,6},{8,11},{9,8},{10,9... | collective-permute-start | bytes 344072 | tf_op jit(solution)/shard_map/ppermute | solution.py:50
  76.5 1.3 %constant_dynamic-slice_fusion.back_y = f32[16,256]{1,0:T(8,128)} fusion(f32[40,256]{1,0:T(8,128)} %constant.45.clone, s32[]{:T(128)S(6)} %select_n.7), kind=kLoop, calls=%fused_computation | loop fusion | bytes 32772 | tf_op jit(solution)/shard_map/dynamic_slice | solution.py:576
  77.8 3.5 %all-to-all-done.got = f32[32,9,128]{2,1,0:T(8,128)S(1)} async-done(((f32[32,9,128]{2,1,0:T(8,128)}), f32[32,9,128]{2,1,0:T(8,128)S(1)}, u32[]{:S(2)}, u32[]{:S(2)}) %all-to-all-start) | async-done | bytes 147488 | tf_op jit(solution)/shard_map/all_to_all | solution.py:565
  84.7 1.0 shard_map.141.correction
  85.8 2.4 %shard_map.142.own.own1 = f32[4,8,256]{2,1,0:T(8,128)S(1)} custom-call(f32[4,8,256]{2,1,0:T(8,128)S(1)} %get-tuple-element.61.v1, f32[6,8,512]{2,1,0:T(8,128)S(1)} %collective-permute-done.12.up, f32[6,8,512]{2,1,0:T(8,128)S(1)} %collective-permute-done.13.down, f32[7,8,512]{2,1,0:T(8,128)S(1)} %collective-permute-done.14.right, ...), custom_call_target="tpu_custom_call" | custom-call | tf_op jit(solution)/shard_map/pallas_call | solution.py:35
  88.1 2.7 %collective-permute-start.16 = (f32[2,8,256]{2,1,0:T(8,128)S(1)}, f32[2,8,256]{2,1,0:T(8,128)S(1)}, u32[]{:S(2)}, u32[]{:S(2)}) collective-permute-start(f32[2,8,256]{2,1,0:T(8,128)S(1)} %get-tuple-element.74), channel_id=1, source_target_pairs={{0,4},{4,8},{8,12},{12,16},{16,20},{20,24},{24,28},{28,0},{1,5},{5... | collective-permute-start | bytes 49160 | tf_op jit(solution)/shard_map/ppermute | solution.py:48
  90.9 1.1 %collective-permute-start.17 = (f32[2,8,256]{2,1,0:T(8,128)S(1)}, f32[2,8,256]{2,1,0:T(8,128)S(1)}, u32[]{:S(2)}, u32[]{:S(2)}) collective-permute-start(f32[2,8,256]{2,1,0:T(8,128)S(1)} %get-tuple-element.73), channel_id=1, source_target_pairs={{0,28},{4,0},{8,4},{12,8},{16,12},{20,16},{24,20},{28,24},{1,29},{... | collective-permute-start | bytes 49160 | tf_op jit(solution)/shard_map/ppermute | solution.py:48
  92.0 1.4 %collective-permute-done.16.up.up1 = f32[2,8,256]{2,1,0:T(8,128)S(1)} collective-permute-done((f32[2,8,256]{2,1,0:T(8,128)S(1)}, f32[2,8,256]{2,1,0:T(8,128)S(1)}, u32[]{:S(2)}, u32[]{:S(2)}) %collective-permute-start.16) | collective-permute-done | bytes 16416 | tf_op jit(solution)/shard_map/ppermute | solution.py:48
  93.5 1.5 %collective-permute-start.18 = (f32[2,8,256]{2,1,0:T(8,128)S(1)}, f32[2,8,256]{2,1,0:T(8,128)S(1)}, u32[]{:S(2)}, u32[]{:S(2)}) collective-permute-start(f32[2,8,256]{2,1,0:T(8,128)S(1)} %get-tuple-element.66), channel_id=1, source_target_pairs={{0,1},{1,2},{2,3},{3,0},{4,5},{5,6},{6,7},{7,4},{8,9},{9,10},{10,1... | collective-permute-start | bytes 49160 | tf_op jit(solution)/shard_map/ppermute | solution.py:50
  95.0 2.4 %collective-permute-start.19 = (f32[2,8,256]{2,1,0:T(8,128)S(1)}, f32[2,8,256]{2,1,0:T(8,128)S(1)}, u32[]{:S(2)}, u32[]{:S(2)}) collective-permute-start(f32[2,8,256]{2,1,0:T(8,128)S(1)} %get-tuple-element.67), channel_id=1, source_target_pairs={{0,3},{1,0},{2,1},{3,2},{4,7},{5,4},{6,5},{7,6},{8,11},{9,8},{10,9... | collective-permute-start | bytes 49160 | tf_op jit(solution)/shard_map/ppermute | solution.py:50
  97.3 1.7 %collective-permute-done.18.right1 = f32[2,8,256]{2,1,0:T(8,128)S(1)} collective-permute-done((f32[2,8,256]{2,1,0:T(8,128)S(1)}, f32[2,8,256]{2,1,0:T(8,128)S(1)}, u32[]{:S(2)}, u32[]{:S(2)}) %collective-permute-start.18) | collective-permute-done | bytes 16416 | tf_op jit(solution)/shard_map/ppermute | solution.py:50
  99.1 5.6 %shard_map.144 = f32[8,16,512]{2,1,0:T(8,128)} custom-call(f32[8,16,512]{2,1,0:T(8,128)S(1)} %get-tuple-element.48.v0, f32[6,8,512]{2,1,0:T(8,128)S(1)} %collective-permute-done.12.up, f32[6,8,512]{2,1,0:T(8,128)S(1)} %collective-permute-done.13.down, f32[7,8,512]{2,1,0:T(8,128)S(1)} %collective-permute-done.14.right, ...), custom_call_target="tpu_custom_call" | custom-call | tf_op jit(solution)/shard_map/pallas_call | solution.py:35
  (57 shorter events, 9.7 us)
Async XLA Ops:
  0.0 1.0 copy-start
  1.0 0.9 copy-start.1
  4.7 37.1 %collective-permute-start = (f32[38,8,512]{2,1,0:T(8,128)S(1)}, f32[38,8,512]{2,1,0:T(8,128)S(1)}, u32[]{:S(2)}, u32[]{:S(2)}) collective-permute-start(f32[38,8,512]{2,1,0:T(8,128)S(1)} %get-tuple-element.40), channel_id=1, source_target_pairs={{0,4},{4,8},{8,12},{12,16},{16,20},{20,24},{24,28},{28,0},{1,5},{5... | collective-permute-start | bytes 1867784 | tf_op jit(solution)/shard_map/ppermute | solution.py:48
  5.2 36.6 %collective-permute-start.1 = (f32[38,8,512]{2,1,0:T(8,128)S(1)}, f32[38,8,512]{2,1,0:T(8,128)S(1)}, u32[]{:S(2)}, u32[]{:S(2)}) collective-permute-start(f32[38,8,512]{2,1,0:T(8,128)S(1)} %get-tuple-element.41), channel_id=1, source_target_pairs={{0,28},{4,0},{8,4},{12,8},{16,12},{20,16},{24,20},{28,24},{1,29},{... | collective-permute-start | bytes 1867784 | tf_op jit(solution)/shard_map/ppermute | solution.py:48
  8.2 8.2 %collective-permute-start.4 = (f32[5,8,512]{2,1,0:T(8,128)S(1)}, f32[5,8,512]{2,1,0:T(8,128)S(1)}, u32[]{:S(2)}, u32[]{:S(2)}) collective-permute-start(f32[5,8,512]{2,1,0:T(8,128)S(1)} %get-tuple-element.44), channel_id=1, source_target_pairs={{0,5},{1,6},{2,7},{3,4},{4,9},{5,10},{6,11},{7,8},{8,13},{9,14},{1... | collective-permute-start | bytes 245768 | tf_op jit(solution)/shard_map/ppermute | solution.py:55
  9.0 32.8 %collective-permute-start.2 = (f32[19,8,512]{2,1,0:T(8,128)S(1)}, f32[19,8,512]{2,1,0:T(8,128)S(1)}, u32[]{:S(2)}, u32[]{:S(2)}) collective-permute-start(f32[19,8,512]{2,1,0:T(8,128)S(1)} %get-tuple-element.42), channel_id=1, source_target_pairs={{0,1},{1,2},{2,3},{3,0},{4,5},{5,6},{6,7},{7,4},{8,9},{9,10},{10,1... | collective-permute-start | bytes 933896 | tf_op jit(solution)/shard_map/ppermute | solution.py:50
  10.6 31.2 %collective-permute-start.3 = (f32[19,8,512]{2,1,0:T(8,128)S(1)}, f32[19,8,512]{2,1,0:T(8,128)S(1)}, u32[]{:S(2)}, u32[]{:S(2)}) collective-permute-start(f32[19,8,512]{2,1,0:T(8,128)S(1)} %get-tuple-element.43), channel_id=1, source_target_pairs={{0,3},{1,0},{2,1},{3,2},{4,7},{5,4},{6,5},{7,6},{8,11},{9,8},{10,9... | collective-permute-start | bytes 933896 | tf_op jit(solution)/shard_map/ppermute | solution.py:50
  16.4 15.2 %collective-permute-start.5 = (f32[5,8,512]{2,1,0:T(8,128)S(1)}, f32[5,8,512]{2,1,0:T(8,128)S(1)}, u32[]{:S(2)}, u32[]{:S(2)}) collective-permute-start(f32[5,8,512]{2,1,0:T(8,128)S(1)} %get-tuple-element.45), channel_id=1, source_target_pairs={{0,7},{1,4},{2,5},{3,6},{4,11},{5,8},{6,9},{7,10},{8,15},{9,12},{1... | collective-permute-start | bytes 245768 | tf_op jit(solution)/shard_map/ppermute | solution.py:55
  31.6 6.3 %collective-permute-start.6 = (f32[5,8,512]{2,1,0:T(8,128)S(1)}, f32[5,8,512]{2,1,0:T(8,128)S(1)}, u32[]{:S(2)}, u32[]{:S(2)}) collective-permute-start(f32[5,8,512]{2,1,0:T(8,128)S(1)} %get-tuple-element.46), channel_id=1, source_target_pairs={{0,29},{1,30},{2,31},{3,28},{4,1},{5,2},{6,3},{7,0},{8,5},{9,6},{1... | collective-permute-start | bytes 245768 | tf_op jit(solution)/shard_map/ppermute | solution.py:55
  38.0 3.9 %collective-permute-start.7 = (f32[5,8,512]{2,1,0:T(8,128)S(1)}, f32[5,8,512]{2,1,0:T(8,128)S(1)}, u32[]{:S(2)}, u32[]{:S(2)}) collective-permute-start(f32[5,8,512]{2,1,0:T(8,128)S(1)} %get-tuple-element.47), channel_id=1, source_target_pairs={{0,31},{1,28},{2,29},{3,30},{4,3},{5,0},{6,1},{7,2},{8,7},{9,4},{1... | collective-permute-start | bytes 245768 | tf_op jit(solution)/shard_map/ppermute | solution.py:55
  49.6 5.4 %collective-permute-start.8 = (f32[4,8,256]{2,1,0:T(8,128)S(1)}, f32[4,8,256]{2,1,0:T(8,128)S(1)}, u32[]{:S(2)}, u32[]{:S(2)}) collective-permute-start(f32[4,8,256]{2,1,0:T(8,128)S(1)} %get-tuple-element.50), channel_id=1, source_target_pairs={{0,4},{4,8},{8,12},{12,16},{16,20},{20,24},{24,28},{28,0},{1,5},{5... | collective-permute-start | bytes 98312 | tf_op jit(solution)/shard_map/ppermute | solution.py:48
  50.4 4.6 %collective-permute-start.9 = (f32[4,8,256]{2,1,0:T(8,128)S(1)}, f32[4,8,256]{2,1,0:T(8,128)S(1)}, u32[]{:S(2)}, u32[]{:S(2)}) collective-permute-start(f32[4,8,256]{2,1,0:T(8,128)S(1)} %get-tuple-element.51), channel_id=1, source_target_pairs={{0,28},{4,0},{8,4},{12,8},{16,12},{20,16},{24,20},{28,24},{1,29},{... | collective-permute-start | bytes 98312 | tf_op jit(solution)/shard_map/ppermute | solution.py:48
  55.0 5.9 %copy-start.16 = (bf16[256,128]{1,0:T(8,128)(2,1)S(1)}, bf16[256,128]{1,0:T(8,128)(2,1)}, u32[]{:S(2)}) copy-start(bf16[256,128]{1,0:T(8,128)(2,1)} %constant.43.clone.pairs) | copy-start | bytes 196612
  55.1 5.9 %collective-permute-start.10 = (f32[5,8,256]{2,1,0:T(8,128)S(1)}, f32[5,8,256]{2,1,0:T(8,128)S(1)}, u32[]{:S(2)}, u32[]{:S(2)}) collective-permute-start(f32[5,8,256]{2,1,0:T(8,128)S(1)} %get-tuple-element.53), channel_id=1, source_target_pairs={{0,1},{1,2},{2,3},{3,0},{4,5},{5,6},{6,7},{7,4},{8,9},{9,10},{10,1... | collective-permute-start | bytes 122888 | tf_op jit(solution)/shard_map/ppermute | solution.py:50
  55.8 5.1 %collective-permute-start.11 = (f32[5,8,256]{2,1,0:T(8,128)S(1)}, f32[5,8,256]{2,1,0:T(8,128)S(1)}, u32[]{:S(2)}, u32[]{:S(2)}) collective-permute-start(f32[5,8,256]{2,1,0:T(8,128)S(1)} %get-tuple-element.54), channel_id=1, source_target_pairs={{0,3},{1,0},{2,1},{3,2},{4,7},{5,4},{6,5},{7,6},{8,11},{9,8},{10,9... | collective-permute-start | bytes 122888 | tf_op jit(solution)/shard_map/ppermute | solution.py:50
  63.2 7.9 %collective-permute-start.12 = (f32[6,8,512]{2,1,0:T(8,128)S(1)}, f32[6,8,512]{2,1,0:T(8,128)S(1)}, u32[]{:S(2)}, u32[]{:S(2)}) collective-permute-start(f32[6,8,512]{2,1,0:T(8,128)S(1)} %get-tuple-element.59), channel_id=1, source_target_pairs={{0,4},{4,8},{8,12},{12,16},{16,20},{20,24},{24,28},{28,0},{1,5},{5... | collective-permute-start | bytes 294920 | tf_op jit(solution)/shard_map/ppermute | solution.py:48
  63.3 7.8 %collective-permute-start.13 = (f32[6,8,512]{2,1,0:T(8,128)S(1)}, f32[6,8,512]{2,1,0:T(8,128)S(1)}, u32[]{:S(2)}, u32[]{:S(2)}) collective-permute-start(f32[6,8,512]{2,1,0:T(8,128)S(1)} %get-tuple-element.60), channel_id=1, source_target_pairs={{0,28},{4,0},{8,4},{12,8},{16,12},{20,16},{24,20},{28,24},{1,29},{... | collective-permute-start | bytes 294920 | tf_op jit(solution)/shard_map/ppermute | solution.py:48
  66.6 14.7 %copy-start.10 = (f32[128,256]{1,0:T(8,128)S(1)}, f32[128,256]{1,0:T(8,128)}, u32[]{:S(2)}) copy-start(f32[128,256]{1,0:T(8,128)} %constant.48.clone.depth_out) | copy-start | bytes 393220
  66.6 14.7 %copy-start.11 = (f32[256,128]{1,0:T(8,128)S(1)}, f32[256,128]{1,0:T(8,128)}, u32[]{:S(2)}) copy-start(f32[256,128]{1,0:T(8,128)} %constant.49.clone.eig_x) | copy-start | bytes 393220
  66.6 14.7 %all-to-all-start = ((f32[32,9,128]{2,1,0:T(8,128)}), f32[32,9,128]{2,1,0:T(8,128)S(1)}, u32[]{:S(2)}, u32[]{:S(2)}) async-start(f32[32,9,128]{2,1,0:T(8,128)} %broadcast_in_dim.2), calls=%async_computation | async-start | bytes 524288 | tf_op jit(solution)/shard_map/all_to_all | solution.py:565
  71.1 10.2 %copy-start.8 = (f32[256,256]{1,0:T(8,128)S(1)}, f32[256,256]{1,0:T(8,128)}, u32[]{:S(2)}) copy-start(f32[256,256]{1,0:T(8,128)} %constant.46.clone.forward) | copy-start | bytes 786436
  71.1 28.0 %copy-start.7 = (bf16[256,512]{1,0:T(8,128)(2,1)S(1)}, bf16[256,512]{1,0:T(8,128)(2,1)}, u32[]{:S(2)}) copy-start(bf16[256,512]{1,0:T(8,128)(2,1)} %constant.52.clone.spread) | copy-start | bytes 786436
  71.9 13.8 %collective-permute-start.14 = (f32[7,8,512]{2,1,0:T(8,128)}, f32[7,8,512]{2,1,0:T(8,128)S(1)}, u32[]{:S(2)}, u32[]{:S(2)}) collective-permute-start(f32[7,8,512]{2,1,0:T(8,128)} %get-tuple-element.62), channel_id=1, source_target_pairs={{0,1},{1,2},{2,3},{3,0},{4,5},{5,6},{6,7},{7,4},{8,9},{9,10},{10,1... | collective-permute-start | bytes 344072 | tf_op jit(solution)/shard_map/ppermute | solution.py:50
  73.7 12.1 %collective-permute-start.15 = (f32[7,8,512]{2,1,0:T(8,128)}, f32[7,8,512]{2,1,0:T(8,128)S(1)}, u32[]{:S(2)}, u32[]{:S(2)}) collective-permute-start(f32[7,8,512]{2,1,0:T(8,128)} %get-tuple-element.63), channel_id=1, source_target_pairs={{0,3},{1,0},{2,1},{3,2},{4,7},{5,4},{6,5},{7,6},{8,11},{9,8},{10,9... | collective-permute-start | bytes 344072 | tf_op jit(solution)/shard_map/ppermute | solution.py:50
  84.7 14.4 %copy-start.5 = (f32[16,24,512]{2,1,0:T(8,128)S(1)}, f32[16,24,512]{2,1,0:T(8,128)}, u32[]{:S(2)}) copy-start(f32[16,24,512]{2,1,0:T(8,128)} %get-tuple-element.71.wz) | copy-start | bytes 2359300
  84.7 14.4 %copy-start.6 = (f32[16,24,512]{2,1,0:T(8,128)S(1)}, f32[16,24,512]{2,1,0:T(8,128)}, u32[]{:S(2)}) copy-start(f32[16,24,512]{2,1,0:T(8,128)} %get-tuple-element.72.rdiag) | copy-start | bytes 2359300
  85.7 13.4 %copy-start.3 = (f32[16,24,512]{2,1,0:T(8,128)S(1)}, f32[16,24,512]{2,1,0:T(8,128)}, u32[]{:S(2)}) copy-start(f32[16,24,512]{2,1,0:T(8,128)} %get-tuple-element.69.wx) | copy-start | bytes 2359300
  85.8 13.4 %copy-start.4 = (f32[16,24,512]{2,1,0:T(8,128)S(1)}, f32[16,24,512]{2,1,0:T(8,128)}, u32[]{:S(2)}) copy-start(f32[16,24,512]{2,1,0:T(8,128)} %get-tuple-element.70.wy) | copy-start | bytes 2359300
  88.1 5.2 %collective-permute-start.16 = (f32[2,8,256]{2,1,0:T(8,128)S(1)}, f32[2,8,256]{2,1,0:T(8,128)S(1)}, u32[]{:S(2)}, u32[]{:S(2)}) collective-permute-start(f32[2,8,256]{2,1,0:T(8,128)S(1)} %get-tuple-element.74), channel_id=1, source_target_pairs={{0,4},{4,8},{8,12},{12,16},{16,20},{20,24},{24,28},{28,0},{1,5},{5... | collective-permute-start | bytes 49160 | tf_op jit(solution)/shard_map/ppermute | solution.py:48
  90.9 2.6 %collective-permute-start.17 = (f32[2,8,256]{2,1,0:T(8,128)S(1)}, f32[2,8,256]{2,1,0:T(8,128)S(1)}, u32[]{:S(2)}, u32[]{:S(2)}) collective-permute-start(f32[2,8,256]{2,1,0:T(8,128)S(1)} %get-tuple-element.73), channel_id=1, source_target_pairs={{0,28},{4,0},{8,4},{12,8},{16,12},{20,16},{24,20},{28,24},{1,29},{... | collective-permute-start | bytes 49160 | tf_op jit(solution)/shard_map/ppermute | solution.py:48
  93.5 5.6 %collective-permute-start.18 = (f32[2,8,256]{2,1,0:T(8,128)S(1)}, f32[2,8,256]{2,1,0:T(8,128)S(1)}, u32[]{:S(2)}, u32[]{:S(2)}) collective-permute-start(f32[2,8,256]{2,1,0:T(8,128)S(1)} %get-tuple-element.66), channel_id=1, source_target_pairs={{0,1},{1,2},{2,3},{3,0},{4,5},{5,6},{6,7},{7,4},{8,9},{9,10},{10,1... | collective-permute-start | bytes 49160 | tf_op jit(solution)/shard_map/ppermute | solution.py:50
  95.0 4.1 %collective-permute-start.19 = (f32[2,8,256]{2,1,0:T(8,128)S(1)}, f32[2,8,256]{2,1,0:T(8,128)S(1)}, u32[]{:S(2)}, u32[]{:S(2)}) collective-permute-start(f32[2,8,256]{2,1,0:T(8,128)S(1)} %get-tuple-element.67), channel_id=1, source_target_pairs={{0,3},{1,0},{2,1},{3,2},{4,7},{5,4},{6,5},{7,6},{8,11},{9,8},{10,9... | collective-permute-start | bytes 49160 | tf_op jit(solution)/shard_map/ppermute | solution.py:50
  (6 other events, 5.3 us)

commit v2 on v1

v2 whole, which is shorter than its diff:
```python
import functools
import math

import jax
import jax.numpy as jnp
import ml_dtypes
import numpy as np
from jax import lax
from jax.experimental import pallas as pl
from jax.experimental.pallas import tpu as pltpu
from jax.sharding import PartitionSpec as P

LEVELS = 3
SWEEPS = 2
MASS = 0.002
BOTH = ("gx", "gy")
H = 2 * SWEEPS
F32 = jnp.float32
UNROLL = 4
VMEM_LIMIT = 12 * 1024 * 1024
K1LIMIT = 12 * 1024 * 1024
BF16 = jnp.bfloat16
VMEM = pl.BlockSpec(memory_space=pltpu.VMEM)
HBM = pl.BlockSpec(memory_space=pltpu.HBM)

CORNER0 = (
    (0, 1, 1), (0, 1, 2), (0, 1, 3), (1, 2, 3), (3, 1, 1), (3, 1, 2), (3, 1, 3), (2, 2, 3),
    (1, 1, 1), (1, 1, 2), (1, 1, 3), (1, 1, 4), (2, 1, 1), (2, 1, 2), (2, 1, 3), (2, 1, 4),
    (0, 2, 1), (0, 2, 2), (0, 3, 1), (1, 4, 1), (3, 2, 1), (3, 2, 2), (3, 3, 1), (2, 4, 1),
    (1, 2, 1), (1, 2, 2), (1, 3, 1), (1, 3, 2), (2, 2, 1), (2, 2, 2), (2, 3, 1), (2, 3, 2),
)
CORNER1 = (
    (0, 1, 1), (0, 1, 2), (0, 1, 3), (0, 2, 1), (0, 2, 2), (0, 3, 1), (2, 1, 1), (2, 1, 2),
    (1, 1, 1), (1, 1, 2), (1, 1, 3), (1, 2, 1), (1, 2, 2), (1, 3, 1), (2, 2, 1), None,
)


def call(kernel, out, *args, scratch=(), remote=(), limit=VMEM_LIMIT, near=()):
    count = len(args)
    args = (*args, *near)

    def body(*refs):
        kernel(*refs[:count], *refs[len(args) :])

    return pl.pallas_call(
        body,
        out_shape=[s if hasattr(s, "dtype") else jax.ShapeDtypeStruct(s, F32) for s in out],
        in_specs=[HBM if i in remote else VMEM for i in range(len(args))],
        out_specs=[VMEM] * len(out),
        scratch_shapes=[pltpu.VMEM(s, F32) if isinstance(s, tuple) else s for s in scratch],
        compiler_params=pltpu.CompilerParams(vmem_limit_bytes=limit),
    )(*args)


def moved(block, dx, dy):
    nx, ny = lax.axis_size("gx"), lax.axis_size("gy")
    if dy == 0:
        return lax.ppermute(block, "gx", [(i, (i + dx) % nx) for i in range(nx)])
    if dx == 0:
        return lax.ppermute(block, "gy", [(j, (j + dy) % ny) for j in range(ny)])
    route = []
    for i in range(nx):
        for j in range(ny):
            route.append((i * ny + j, ((i + dx) % nx) * ny + (j + dy) % ny))
    return lax.ppermute(block, BOTH, route)


def split3(x):
    high = x.astype(BF16)
    rest = x - high.astype(F32)
    middle = rest.astype(BF16)
    return high, middle, (rest - middle.astype(F32)).astype(BF16)


def dot(a, b):
    return jnp.dot(a, b, preferred_element_type=F32)


def dot_exact(x, table):
    high, middle, low = split3(x)
    return dot(high, table) + (dot(middle, table) + dot(low, table))


def pair_table(depth):
    table = np.zeros((depth, depth // 2), ml_dtypes.bfloat16)
    table[np.arange(depth), np.arange(depth) // 2] = 1
    return table


def put_tiles(tiles, x):
    for k in range(tiles.shape[0]):
        tiles[k] = x[:, 128 * k : 128 * k + 128]


def every_other(tiles, start, size):
    return jnp.concatenate(
        [tiles[k, pl.ds(start, size, stride=2), :] for k in range(tiles.shape[0])], axis=1
    )


def back(x, axis):
    return pltpu.roll(x, 1, axis)


def ahead(x, axis):
    return pltpu.roll(x, x.shape[axis] - 1, axis)


def parity2(shape):
    return (lax.broadcasted_iota(jnp.int32, shape, 0) + lax.broadcasted_iota(jnp.int32, shape, 1)) & 1


def row_sum(r, v, wx, wy, wz):
    centre = v[r]
    y, z = wy[r], wz[r]
    total = wx[r] * v[r + 1] + wx[r - 1] * v[r - 1]
    total = total + y * ahead(centre, 0) + back(y * centre, 0)
    return centre, total + z * ahead(centre, 1) + back(z * centre, 1)


def half_sweep(first, last, colour, parity, v, b, wx, wy, wz, rdiag):
    unroll = UNROLL if v.shape[-1] > 256 else last - first

    def body(r, carry):
        centre, total = row_sum(r, v, wx, wy, wz)
        mine = parity == ((r + colour) & 1)
        v[r] = jnp.where(mine, (b[r] + total) * rdiag[r], centre)
        return carry

    lax.fori_loop(first, last, body, 0, unroll=unroll)


def pack_kernel(src_in, face_in, to_right, to_left, to_up, to_down, w1, src, face, pairs, *scratch):
    odds, tx, sem = scratch
    rows, cols, depth = src.shape
    half = depth // 2
    copies = [pltpu.make_async_copy(src_in, src, sem.at[0]), pltpu.make_async_copy(face_in, face, sem.at[1])]
    for copy in copies:
        copy.start()
    fine = lax.broadcasted_iota(jnp.int32, pairs.shape, 0)
    coarse = 2 * lax.broadcasted_iota(jnp.int32, pairs.shape, 1)
    pairs[...] = jnp.where((fine & -2) == coarse, 1.0, 0.0).astype(BF16)
    odds[...] = jnp.where(fine == coarse + 1, 1.0, 0.0).astype(BF16)
    for copy in copies:
        copy.wait()

    for i in range(rows // 2):
        put_tiles(tx, dot(face[0, 2 * i + 1], pairs[...]))
        w1[0, i] = 0.0625 * (every_other(tx, 0, cols // 2) + every_other(tx, 1, cols // 2))
        put_tiles(tx, dot(face[1, 2 * i], pairs[...]) + dot(face[1, 2 * i + 1], pairs[...]))
        w1[1, i] = 0.0625 * every_other(tx, 1, cols // 2)
        put_tiles(tx, dot(face[2, 2 * i], odds[...]) + dot(face[2, 2 * i + 1], odds[...]))
        w1[2, i] = 0.0625 * (every_other(tx, 0, cols // 2) + every_other(tx, 1, cols // 2))

    def plane(a, r):
        return src[r] if a == 0 else face[a - 1, r].astype(F32)

    for out, base, base1 in ((to_right, cols - H, cols // 2 - H), (to_left, 0, 0)):
        for r in range(rows):
            for t, pair in enumerate(((0, 3), (1, 2))):
                for s, a in enumerate(pair):
                    value = plane(a, r)
                    if out is to_right and a == 3:
                        value_all = value + back(value, 1) + back(plane(2, r), 0)
                        first = lax.broadcasted_iota(jnp.int32, value.shape, 0) == base
                        value = jnp.where(first, value_all, value)
                    out[2 * r + t, H * s : H * s + H] = value[base : base + H]
        for i in range(rows // 2):
            k, lane = 2 * rows + i // 2, half * (i % 2)
            out[k, 0:H, lane : lane + half] = w1[0, i, base1 : base1 + H]
            out[k, H : 2 * H, lane : lane + half] = w1[1, i, base1 : base1 + H]
            k = 2 * rows + rows // 4 + i // 4
            s = H * (i % 2)
            lane = half * ((i // 2) % 2)
            out[k, s : s + H, lane : lane + half] = w1[2, i, base1 : base1 + H]

    for out, base in ((to_up, rows - H), (to_down, 0)):
        for a in range(4):
            for k in range(H):
                value = plane(a, base + k)
                if out is to_up and a == 3 and k == 0:
                    value = value + back(value, 1) + plane(1, base - 1)
                for t in range(cols // 8):
                    out[(a * H + k) * (cols // 8) + t] = value[8 * t : 8 * t + 8]
        base1 = 4 * H * (cols // 8)
        for d in range(3):
            for i in range(H // 2):
                out[base1 + d * (H // 2) + i] = jnp.concatenate((w1[d, 2 * i], w1[d, 2 * i + 1]), axis=1)


def forward_kernel(right, left, to_up, to_down, *, rows):
    half = right.shape[2] // 2
    tiles = to_up.shape[0] // 2
    place = {0: (0, 0), 3: (0, 1), 1: (1, 0), 2: (1, 1)}
    for msg, sy in ((right, 1), (left, -1)):
        start = 0 if sy > 0 else tiles
        for out, sx in ((to_up, 1), (to_down, -1)):
            for n, (a, dx, dy) in enumerate(CORNER0):
                r = rows - dx if sx > 0 else dx - 1
                t, s = place[a]
                s = H * s + (H - dy if sy > 0 else dy - 1)
                out[start + n // 8, n % 8 : n % 8 + 1] = msg[2 * r + t, s : s + 1]
            for n, entry in enumerate(CORNER1):
                if entry is None:
                    continue
                d, dx, dy = entry
                i = rows // 2 - dx if sx > 0 else dx - 1
                c = H - dy if sy > 0 else dy - 1
                if d == 2:
                    k, s, lane = 2 * rows + rows // 4 + i // 4, H * (i % 2) + c, half * ((i // 2) % 2)
                else:
                    k, s, lane = 2 * rows + i // 2, H * d + c, half * (i % 2)
                to = half * (n // 8)
                out[start + tiles - 1, n % 8 : n % 8 + 1, to : to + half] = msg[k, s : s + 1, lane : lane + half]


def diagonal_row(r, parity, low_col, b, wx, wy, wz, diag, rdiag, v):
    y, z = wy[r], wz[r]
    if isinstance(r, int) and r == 0:
        total = MASS + wx[r] + z + y + back(y, 0)
    else:
        total = MASS + wx[r] + wx[r - 1] + y
        total = total + jnp.where(low_col, z, z + back(z, 1) + back(y, 0))
    diag[r] = total
    inverse = 1.0 / total
    rdiag[r] = inverse
    v[r] = jnp.where(parity == (r & 1), b[r] * inverse, 0.0)


def assemble_kernel(src, face, w1, up, down, right, left, state, w1e):
    b, wx, wy, wz, rdiag, diag, v = (state.at[i] for i in range(7))
    rows, cols, depth = src.shape
    half = depth // 2
    ext = (b, wx, wy, wz)
    er, ec = rows + 2 * H, cols + 2 * H
    rows1, cols1 = rows // 2, cols // 2

    for r in range(rows):
        b[H + r, H : H + cols] = src[r]
        for d in range(3):
            ext[1 + d][H + r, H : H + cols] = face[d, r].astype(F32)
    for d in range(3):
        for i in range(rows1):
            w1e[d, H + i, H : H + cols1] = w1[d, i]
    tiles = cols // 8
    for msg, base, base1 in ((up, 0, 0), (down, H + rows, H + rows1)):
        for a in range(4):
            for k in range(H):
                for t in range(tiles):
                    ext[a][base + k, H + 8 * t : H + 8 * t + 8] = msg[(a * H + k) * tiles + t]
        n = 4 * H * tiles
        for d in range(3):
            for i in range(H):
                lane = half * (i % 2)
                w1e[d, base1 + i, H : H + cols1] = msg[n + d * (H // 2) + i // 2, :, lane : lane + half]
    for msg, base, base1 in ((right, 0, 0), (left, H + cols, H + cols1)):
        for r in range(rows):
            for t, pair in enumerate(((0, 3), (1, 2))):
                for s, a in enumerate(pair):
                    ext[a][H + r, base : base + H] = msg[2 * r + t, H * s : H * s + H]
        for i in range(rows1):
            k, lane = 2 * rows + i // 2, half * (i % 2)
            w1e[0, H + i, base1 : base1 + H] = msg[k, 0:H, lane : lane + half]
            w1e[1, H + i, base1 : base1 + H] = msg[k, H : 2 * H, lane : lane + half]
            k = 2 * rows + rows // 4 + i // 4
            s = H * (i % 2)
            lane = half * ((i // 2) % 2)
            w1e[2, H + i, base1 : base1 + H] = msg[k, s : s + H, lane : lane + half]
    parity = parity2((ec, depth))
    low_col = lax.broadcasted_iota(jnp.int32, (ec, depth), 0) == 0

    def body(r, carry):
        diagonal_row(r, parity, low_col, b, wx, wy, wz, diag, rdiag, v)
        return carry

    lax.fori_loop(H + 1, H + rows, body, 0)


def pre_kernel(up, down, pairs, *rest):
    state, w1_in, kept, w1e = rest[:4]
    (v_own, right1, to_right, to_left, rdiag1, diag1, merged_right, merged_left) = rest[4:12]
    t512, t256, diag, v = rest[12:]
    b, wx, wy, wz, rdiag = (kept.at[i] for i in range(5))
    kept[...] = state[0:5]
    diag[...] = state[5]
    v[...] = state[6]
    w1e[...] = w1_in[...]
    ext = (b, wx, wy, wz)
    rows, cols, depth = v_own.shape
    half = depth // 2
    er, ec = rows + 2 * H, cols + 2 * H
    rows1, cols1 = rows // 2, cols // 2
    tiles = len(CORNER0) // 8 + 1
    for msg, sx, sy in ((up, 1, 1), (up, 1, -1), (down, -1, 1), (down, -1, -1)):
        start = 0 if sy > 0 else tiles

        def at(distance, size, sign):
            return H - distance if sign > 0 else H + size + distance - 1

        for n, (a, dx, dy) in enumerate(CORNER0):
            r, c = at(dx, rows, sx), at(dy, cols, sy)
            ext[a][r, c : c + 1] = msg[start + n // 8, n % 8 : n % 8 + 1]
        for n, entry in enumerate(CORNER1):
            if entry is None:
                continue
            d, dx, dy = entry
            r, c = at(dx, rows1, sx), at(dy, cols1, sy)
            lane = half * (n // 8)
            w1e[d, r, c : c + 1] = msg[start + tiles - 1, n % 8 : n % 8 + 1, lane : lane + half]

    parity = parity2((ec, depth))
    low_col = lax.broadcasted_iota(jnp.int32, (ec, depth), 0) == 0
    for r in (*range(H + 1), *range(H + rows, er)):
        diagonal_row(r, parity, low_col, b, wx, wy, wz, diag, rdiag, v)
    half_sweep(1, er - 1, 1, parity, v, b, wx, wy, wz, rdiag)
    half_sweep(2, er - 2, 0, parity, v, b, wx, wy, wz, rdiag)
    half_sweep(3, er - 3, 1, parity, v, b, wx, wy, wz, rdiag)

    def residual_body(i, carry):
        total = 0.0
        for k in range(2):
            r = H + 2 * i + k
            centre, around = row_sum(r, v, wx, wy, wz)
            total = total + (b[r] - (diag[r] * centre - around))
        t512[i] = total
        return carry

    lax.fori_loop(0, rows1, residual_body, 0, unroll=UNROLL)
    put_tiles(t256, dot_exact(t512[...].reshape(rows1 * ec, depth), pairs[...]))
    for i in range(rows1):
        start = i * ec + H
        right1[i] = 0.125 * (every_other(t256, start, cols1) + every_other(t256, start + 1, cols1))

    for r in range(rows1 + 2 * H):
        y, z = w1e[1, r], w1e[2, r]
        total = MASS + w1e[0, r] + w1e[0, max(r - 1, 0)] + y + back(y, 0) + z + back(z, 1)
        diag1[r] = total
        rdiag1[r] = 1.0 / total
    for i in range(rows1):
        value, inverse = right1[i], rdiag1[H + i, H : H + cols1]
        col = lax.broadcasted_iota(jnp.int32, value.shape, 0)
        place = (i // 2, slice(H * (i % 2), H * (i % 2) + H))
        to_right[place] = jnp.where(col == cols1 - H, value * inverse, value)[cols1 - H :]
        to_left[place] = jnp.where(col == H - 1, value * inverse, value)[:H]

    own_parity = parity2((cols, depth))
    for r in range(rows):
        value = v[H + r, H : H + cols]
        v_own[r] = value
        value = jnp.where(own_parity == ((r + 1) & 1), value, ahead(value, 0))
        for p in range(H // 2):
            n = p * rows + r
            for out, base in ((merged_right, cols - H), (merged_left, 0)):
                out[n // 8, n % 8 : n % 8 + 1] = value[base + 2 * p : base + 2 * p + 1]


def pack1_kernel(own, right, left, rdiag1, rows_own, to_up, to_down):
    rows, cols, depth = own.shape
    for i in range(rows):
        rows_own[i, H : H + cols] = own[i]
        rows_own[i, 0:H] = right[i // 2, H * (i % 2) : H * (i % 2) + H]
        rows_own[i, H + cols : 2 * H + cols] = left[i // 2, H * (i % 2) : H * (i % 2) + H]
    shape = rows_own.shape[1:]
    col = lax.broadcasted_iota(jnp.int32, shape, 0)
    col_distance = jnp.maximum(jnp.maximum(H - col, col - (H + cols - 1)), 0)
    for k in range(H):
        for out, i, distance in ((to_up, rows - H + k, H - k), (to_down, k, k + 1)):
            edge = col_distance + distance == H
            value = rows_own[i]
            out[k] = jnp.where(edge, value * rdiag1[H + i], value)


def pre1_kernel(rows_own, up, down, w1e, rdiag1, diag1, pairs, merged_right, merged_left, *rest):
    kept, chunks, to_right, to_left = rest[:4]
    chunk = chunks.at[0]
    t256, t128 = rest[4:]
    b1, v = kept.at[4], kept.at[5]
    kept[0:3] = w1e[...]
    kept[3] = rdiag1[...]
    rows, _, depth = rows_own.shape
    cols = rows_own.shape[1] - 2 * H
    er, ec = rows + 2 * H, cols + 2 * H
    half = depth // 2
    wx, wy, wz = w1e.at[0], w1e.at[1], w1e.at[2]
    b1[0:H] = up[...]
    b1[H : H + rows] = rows_own[...]
    b1[H + rows :] = down[...]
    parity = parity2((ec, depth))
    col = lax.broadcasted_iota(jnp.int32, (ec, depth), 0)
    col_distance = jnp.maximum(jnp.maximum(H - col, col - (H + cols - 1)), 0)
    for r in range(er):
        distance = max(H - r, r - (H + rows - 1), 0)
        first = jnp.where(col_distance + distance >= H, b1[r], b1[r] * rdiag1[r])
        v[r] = jnp.where(parity == (r & 1), first, 0.0)
    half_sweep(1, er - 1, 1, parity, v, b1, wx, wy, wz, rdiag1)
    half_sweep(2, er - 2, 0, parity, v, b1, wx, wy, wz, rdiag1)
    half_sweep(3, er - 3, 1, parity, v, b1, wx, wy, wz, rdiag1)
    for i in range(rows // 2):
        total = 0.0
        for k in range(2):
            r = H + 2 * i + k
            centre, around = row_sum(r, v, wx, wy, wz)
            total = total + (b1[r] - (diag1[r] * centre - around))
        t256[i] = total
    n = rows // 2
    put_tiles(t128, dot_exact(t256[...].reshape(n * ec, depth), pairs[...]))
    for i in range(n):
        start = i * ec + H
        chunk[i * (cols // 2) : (i + 1) * (cols // 2)] = 0.125 * (
            every_other(t128, start, cols // 2) + every_other(t128, start + 1, cols // 2)
        )
    lane = lax.broadcasted_iota(jnp.int32, (1, half), 1)
    row_odd = lax.broadcasted_iota(jnp.int32, (cols, depth), 0) & 1
    depth_odd = lax.broadcasted_iota(jnp.int32, (cols, depth), 1) & 1
    parts = [0.0, 0.0, 0.0]
    for i in range(rows):
        if i % 2 == 1:
            parts[0] = parts[0] + w1e[0, H + i, H : H + cols]
        parts[1] = parts[1] + jnp.where(row_odd == 1, w1e[1, H + i, H : H + cols], 0.0)
        parts[2] = parts[2] + jnp.where(depth_odd == 1, w1e[2, H + i, H : H + cols], 0.0)
    line = jnp.zeros((1, half), F32)
    for d in range(3):
        line = jnp.where(lane == d, 0.0625 * jnp.sum(parts[d]), line)
    n = (rows // 2) * (cols // 2)
    chunk[n : n + 1] = line
    value = chunk[...]
    for i in range(1, chunks.shape[0]):
        chunks[i] = value

    for out, base, merged in ((to_right, cols - H, merged_right), (to_left, 0, merged_left)):
        n = merged.shape[0]
        out[0:n] = merged[...]
        for i in range(rows):
            s, lane = H * (i % 2), depth * ((i // 2) % 2)
            out[n + i // 4, s : s + H, lane : lane + depth] = v[H + i, H + base : 2 * H + base]


def pack_v_kernel(kept1, right, left, v0, rows_out, to_up, to_down, v1_rows):
    rows1, ec1, half = v1_rows.shape
    cols1 = ec1 - 2 * H
    rows, cols, depth = v0.shape
    v0_rows = rows_out.at[0:rows]
    n0 = rows * (H // 2) // 8
    for i in range(rows1):
        s, lane = H * (i % 2), half * ((i // 2) % 2)
        v1_rows[i] = kept1[5, H + i]
        v1_rows[i, 0:H] = right[n0 + i // 4, s : s + H, lane : lane + half]
        v1_rows[i, H + cols1 : 2 * H + cols1] = left[n0 + i // 4, s : s + H, lane : lane + half]
    for r in range(rows):
        v0_rows[r, H : H + cols] = v0[r]
        for msg, base in ((right, 0), (left, H + cols)):
            for p in range(H // 2):
                n = p * rows + r
                line = msg[n // 8, n % 8 : n % 8 + 1]
                v0_rows[r, base + 2 * p : base + 2 * p + 2] = jnp.broadcast_to(line, (2, depth))
    ec = v0_rows.shape[1]
    for i in range(rows1 // 2):
        rows_out[rows + i, 0:ec1] = jnp.concatenate((v1_rows[2 * i], v1_rows[2 * i + 1]), axis=1)
    parity = parity2((ec, depth))
    tiles, tiles1 = ec // 8, ec1 // 8
    for out, base, base1 in ((to_up, rows - H, rows1 - H), (to_down, 0, 0)):
        for k in range(H // 2):
            r = base + 2 * k
            value = jnp.where(parity == ((r + 1) & 1), v0_rows[r], v0_rows[r + 1])
            for t in range(tiles):
                out[k * tiles + t] = value[8 * t : 8 * t + 8]
            start = (H // 2) * tiles + k * tiles1
            value = jnp.concatenate((v1_rows[base1 + 2 * k], v1_rows[base1 + 2 * k + 1]), axis=1)
            for t in range(tiles1):
                out[start + t] = value[8 * t : 8 * t + 8]


def split2(x):
    high = x.astype(BF16)
    return high, (x - high.astype(F32)).astype(BF16)


def dot_split(a, b):
    return dot(a[0], b[0]) + (dot(a[0], b[1]) + dot(a[1], b[0]))


def solve_kernel(got, table, out, *, count, start):
    devices, lines, depth = got.shape
    own = lines - 1
    cells = devices * own
    rx, ry, _ = out.shape

    def part(name, size, lane=0, width=None):
        return table[start[name] : start[name] + size, lane : lane + (width or table.shape[1])]

    values = jnp.concatenate([got[d, 0:own] for d in range(devices)], axis=0)
    sums = got[0, own : own + 1]
    for d in range(1, devices):
        sums = sums + got[d, own : own + 1]
    sums = sums * (1.0 / count)
    lam = MASS + sums[0:1, 0:1] * part("eig", cells, 0, depth)
    lam = lam + sums[0:1, 1:2] * part("eig", cells, depth, depth)
    lam = lam + sums[0:1, 2:3] * part("depth", 1, depth, depth)
    spec = dot_split(split2(values), split2(part("depth_in", depth, 0, depth)))
    spec = dot_split(split2(part("forward", cells)), split2(spec))
    spec = spec / (lam * float(count))
    spec = dot_split(split2(spec), split2(part("depth_out", depth)))
    ix, iy = lax.axis_index("gx"), lax.axis_index("gy")
    x_step, y_step = -(-rx // 8) * 8, -(-ry // 8) * 8
    along_x = table[pl.ds(pl.multiple_of(start["x"] + ix * x_step, 8), x_step), :]
    along_y = table[pl.ds(pl.multiple_of(start["y"] + iy * y_step, 8), y_step), :][0:ry]
    back_table = jnp.concatenate([along_x[i : i + 1] * along_y for i in range(rx)], axis=0)
    out[...] = dot_split(split2(back_table), split2(spec)).reshape(out.shape)


def post1_kernel(v_rows, up, down, correction, kept1, out, to_right, to_left, v):
    rdiag1, b1 = kept1.at[3], kept1.at[4]
    rows, cols, depth = out.shape
    er, ec = rows + 2 * H, cols + 2 * H
    start = v_rows.shape[0] - rows // 2
    for i in range(rows // 2):
        value = v_rows[start + i, 0:ec]
        v[H + 2 * i] = value[:, :depth]
        v[H + 2 * i + 1] = value[:, depth:]
    tiles = ec // 8
    for msg, base in ((up, 0), (down, H + rows)):
        start = msg.shape[0] - (H // 2) * tiles
        for k in range(H // 2):
            for t in range(tiles):
                tile = msg[start + k * tiles + t]
                v[base + 2 * k, 8 * t : 8 * t + 8] = tile[:, :depth]
                v[base + 2 * k + 1, 8 * t : 8 * t + 8] = tile[:, depth:]
    for r in range(er):
        v[r] = v[r] + correction[r]
    parity = parity2((ec, depth))
    wx, wy, wz = kept1.at[0], kept1.at[1], kept1.at[2]
    half_sweep(1, er - 1, 0, parity, v, b1, wx, wy, wz, rdiag1)
    half_sweep(2, er - 2, 1, parity, v, b1, wx, wy, wz, rdiag1)
    half_sweep(3, er - 3, 0, parity, v, b1, wx, wy, wz, rdiag1)
    half_sweep(4, er - 4, 1, parity, v, b1, wx, wy, wz, rdiag1)
    for r in range(rows):
        out[r] = v[H + r, H : H + cols]
    h = H // 2
    for r in range(rows):
        s = h * (r % 4)
        to_right[r // 4, s : s + h] = out[r, cols - h : cols]
        to_left[r // 4, s : s + h] = out[r, 0:h]


def pack2_kernel(own, right, left, rows_own, to_up, to_down):
    rows, cols, depth = own.shape
    h = H // 2
    used = cols + 2 * h
    for r in range(rows):
        s = h * (r % 4)
        rows_own[r, h : h + cols] = own[r]
        rows_own[r, 0:h] = right[r // 4, s : s + h]
        rows_own[r, h + cols : used] = left[r // 4, s : s + h]
        if used < rows_own.shape[1]:
            rows_own[r, used:] = jnp.zeros((rows_own.shape[1] - used, depth), F32)
    to_up[...] = rows_own[rows - h :]
    to_down[...] = rows_own[0:h]


def spread_kernel(v0_rows, up, down, v):
    er, ec, _ = v.shape
    rows = er - 2 * H
    v[H : H + rows] = v0_rows[0:rows]
    tiles = ec // 8
    for msg, base in ((up, 0), (down, H + rows)):
        for k in range(H // 2):
            for t in range(tiles):
                tile = msg[k * tiles + t]
                v[base + 2 * k, 8 * t : 8 * t + 8] = tile
                v[base + 2 * k + 1, 8 * t : 8 * t + 8] = tile


def post_kernel(v_in, rows_own, up1, down1, kept, spread, out, v, t256):
    b, wx, wy, wz, rdiag = (kept.at[i] for i in range(5))
    rows, cols, depth = out.shape
    rows1, wide1, half = rows_own.shape
    er, ec = rows + 2 * H, cols + 2 * H
    h = H // 2
    ec1 = cols // 2 + 2 * h
    n1 = rows1 + 2 * h
    t256[0:h] = up1[...]
    t256[h : h + rows1] = rows_own[...]
    t256[h + rows1 :] = down1[...]
    wide = dot_exact(t256[...].reshape(n1 * t256.shape[1], half), spread[...])
    wide = wide.reshape(n1, t256.shape[1], depth)
    for n in range(n1):
        line = wide[n, 0:ec1]
        line = jnp.broadcast_to(line[:, None, :], (ec1, 2, depth)).reshape(2 * ec1, depth)
        v[2 * n] = v_in[2 * n] + line
        v[2 * n + 1] = v_in[2 * n + 1] + line
    parity = parity2((ec, depth))
    half_sweep(1, er - 1, 0, parity, v, b, wx, wy, wz, rdiag)
    half_sweep(2, er - 2, 1, parity, v, b, wx, wy, wz, rdiag)
    half_sweep(3, er - 3, 0, parity, v, b, wx, wy, wz, rdiag)
    half_sweep(4, er - 4, 1, parity, v, b, wx, wy, wz, rdiag)
    for r in range(rows):
        out[r] = v[H + r, H : H + cols]


def hartley(rows, columns, length):
    angle = (np.outer(rows, columns) % length) * (2.0 * math.pi / length)
    return np.cos(angle) + np.sin(angle)


def waves(length):
    return 2.0 * (1.0 - np.cos(np.arange(length) * (2.0 * math.pi / length)))


def windows(table, count, step, size):
    pad = -size % 8
    parts = [np.pad(table[i * step : i * step + size], ((0, pad), (0, 0))) for i in range(count)]
    return np.concatenate(parts)


def coarse_correction(chunks, rows, cols, depth):
    nx, ny = lax.axis_size("gx"), lax.axis_size("gy")
    total_rows, total_cols = rows * nx, cols * ny
    count = total_rows * total_cols * depth
    got = lax.all_to_all(chunks, BOTH, 0, 0)
    out_rows, out_cols = 2 * rows + 2 * H, 2 * cols + 2 * H
    rows_ids = (np.arange(-H, 2 * total_rows + H) // 2) % total_rows
    cols_ids = (np.arange(-H, 2 * total_cols + H) // 2) % total_cols
    table_x = hartley(rows_ids, np.arange(total_rows), total_rows)
    table_y = hartley(cols_ids, np.arange(total_cols), total_cols)
    depth_in = hartley(np.arange(depth), np.arange(depth), depth)
    depth_out = np.repeat(depth_in, 2, axis=1)

    def own(table, axis, step, size):
        table = jnp.asarray(table, F32)
        return lax.dynamic_slice_in_dim(table, lax.axis_index(axis) * step, size, 0)

    cells = total_rows * total_cols
    if cells <= 512 and cells == 2 * depth:
        order = np.arange(cells).reshape(nx, rows, ny, cols).transpose(0, 2, 1, 3).reshape(-1)
        forward = np.einsum(
            "ax,by->abxy",
            hartley(np.arange(total_rows), np.arange(total_rows), total_rows),
            hartley(np.arange(total_cols), np.arange(total_cols), total_cols),
        ).reshape(cells, cells)[:, order]
        ones = np.ones((1, depth))
        eig_x = np.repeat(waves(total_rows), total_cols)[:, None] * ones
        eig_y = np.tile(waves(total_cols), total_rows)[:, None] * ones
        eig_z = np.ones((depth, 1)) * waves(depth)[None, :]
        parts = {
            "forward": forward,
            "eig": np.concatenate((eig_x, eig_y), axis=1),
            "depth": np.concatenate((depth_in, eig_z), axis=1),
            "depth_out": depth_out,
            "x": windows(np.repeat(table_x, total_cols, axis=1), nx, 2 * rows, out_rows),
            "y": windows(np.tile(table_y, (1, total_rows)), ny, 2 * cols, out_cols),
        }
        start, size = {}, 0
        for name, part in parts.items():
            start[name] = size
            size += part.shape[0]
            assert size % 8 == 0
        start["depth_in"] = start["depth"]
        table = jnp.asarray(np.concatenate(list(parts.values())), F32)
        return call(
            functools.partial(solve_kernel, count=count, start=start),
            [(out_rows, out_cols, 2 * depth)],
            got, table,
        )[0]

    hi = lax.Precision.HIGHEST
    averages = jnp.sum(got[:, rows * cols, :3], axis=0) / count
    full = got[:, : rows * cols].reshape(nx, ny, rows, cols, depth)
    full = full.transpose(0, 2, 1, 3, 4).reshape(total_rows, total_cols, depth)
    f32 = lambda x: jnp.asarray(x, F32)
    spec = jnp.einsum("abz,zk->abk", full, f32(depth_in), precision=hi)
    spec = jnp.einsum("ij,jbz->ibz", f32(hartley(np.arange(total_rows), np.arange(total_rows), total_rows)), spec, precision=hi)
    spec = jnp.einsum("ij,ajz->aiz", f32(hartley(np.arange(total_cols), np.arange(total_cols), total_cols)), spec, precision=hi)
    lam = (
        MASS
        + averages[0] * f32(waves(total_rows))[:, None, None]
        + averages[1] * f32(waves(total_cols))[None, :, None]
        + averages[2] * f32(waves(depth))[None, None, :]
    )
    spec = spec / (lam * float(count))
    out = jnp.einsum("ij,jbz->ibz", own(table_x, "gx", 2 * rows, out_rows), spec, precision=hi)
    out = jnp.einsum("ij,ajz->aiz", own(table_y, "gy", 2 * cols, out_cols), out, precision=hi)
    return jnp.einsum("abz,zk->abk", out, f32(depth_out), precision=hi)


def shards(source, face_coef):
    rows, cols, depth = source.shape
    rows1, cols1, depth1 = rows // 2, cols // 2, depth // 2
    er, ec, er1, ec1 = rows + 2 * H, cols + 2 * H, rows1 + 2 * H, cols1 + 2 * H

    nx_tiles = 4 * H * (cols // 8) + 3 * (H // 2)
    ny_tiles = 2 * rows + rows // 4 + (rows // 2 + 3) // 4
    corner_tiles = len(CORNER0) // 8 + 1
    to_right, to_left, to_up, to_down, w1, source, face_coef, pairs = call(
        pack_kernel,
        [(ny_tiles, 8, depth)] * 2
        + [(nx_tiles, 8, depth)] * 2
        + [(3, rows1, cols1, depth1), (rows, cols, depth)]
        + [jax.ShapeDtypeStruct((3, rows, cols, depth), BF16), jax.ShapeDtypeStruct((depth, depth1), BF16)],
        source, face_coef,
        remote=(0, 1),
        limit=K1LIMIT,
        scratch=[
            pltpu.VMEM((depth, depth1), BF16),
            (depth1 // 128, cols, 128),
            pltpu.SemaphoreType.DMA((2,)),
        ],
    )
    right, left = moved(to_right, 0, 1), moved(to_left, 0, -1)
    up, down = moved(to_up, 1, 0), moved(to_down, -1, 0)
    to_up, to_down = call(
        functools.partial(forward_kernel, rows=rows), [(2 * corner_tiles, 8, depth)] * 2, right, left
    )
    corners = moved(to_up, 1, 0), moved(to_down, -1, 0)
    state = call(
        assemble_kernel,
        [(7, er, ec, depth), (3, er1, ec1, depth1)],
        source, face_coef, w1, up, down, right, left,
    )
    merged = [(rows * (H // 2) // 8, 8, depth)] * 2
    kept, w1e, v0, right1, to_right, to_left, rdiag1, diag1, merged_right, merged_left = call(
        pre_kernel,
        [(5, er, ec, depth), (3, er1, ec1, depth1), (rows, cols, depth), (rows1, cols1, depth1)]
        + [(rows1 // 2, 8, depth1)] * 2
        + [(er1, ec1, depth1), (er1, ec1, depth1)]
        + merged,
        *corners, pairs, *state,
        scratch=[(rows1, ec, depth), (depth1 // 128, rows1 * ec, 128)] + [(er, ec, depth)] * 2,
    )

    right, left = moved(to_right, 0, 1), moved(to_left, 0, -1)
    rows_own, to_up, to_down = call(
        pack1_kernel, [(rows1, ec1, depth1)] + [(H, ec1, depth1)] * 2, right1, right, left, rdiag1, near=(kept,)
    )
    up, down = moved(to_up, 1, 0), moved(to_down, -1, 0)
    y_tiles = merged[0][0] + (rows1 + 3) // 4
    kept1, chunks, to_right, to_left = call(
        pre1_kernel,
        [(6, er1, ec1, depth1), (lax.axis_size(BOTH), rows1 * cols1 // 4 + 1, depth1 // 2)]
        + [(y_tiles, 8, depth)] * 2,
        rows_own, up, down, w1e, rdiag1, diag1, jnp.asarray(pair_table(depth1)), merged_right, merged_left,
        near=(kept,),
        scratch=[(rows1 // 2, ec1, depth1), (depth1 // 256, rows1 // 2 * ec1, 128)],
    )

    right, left = moved(to_right, 0, 1), moved(to_left, 0, -1)
    correction2 = coarse_correction(chunks, rows1 // 2, cols1 // 2, depth1 // 2)
    x_tiles = (H // 2) * (ec // 8 + ec1 // 8)
    v_rows, to_up, to_down = call(
        pack_v_kernel,
        [(rows + rows1 // 2, ec, depth)] + [(x_tiles, 8, depth)] * 2,
        kept1, right, left, v0,
        scratch=[(rows1, ec1, depth1)],
    )
    up, down = moved(to_up, 1, 0), moved(to_down, -1, 0)
    h = H // 2
    v1, to_right, to_left = call(
        post1_kernel,
        [(rows1, cols1, depth1)] + [(rows1 // 4, 8, depth1)] * 2,
        v_rows, up, down, correction2, kept1,
        scratch=[(er1, ec1, depth1)],
    )

    (v0e,) = call(spread_kernel, [(er, ec, depth)], v_rows, up, down)
    right1, left1 = moved(to_right, 0, 1), moved(to_left, 0, -1)
    wide1 = -(-(cols1 + 2 * h) // 8) * 8
    rows_own, to_up, to_down = call(
        pack2_kernel, [(rows1, wide1, depth1)] + [(h, wide1, depth1)] * 2, v1, right1, left1
    )
    up1, down1 = moved(to_up, 1, 0), moved(to_down, -1, 0)
    (out,) = call(
        post_kernel,
        [(rows, cols, depth)],
        v0e, rows_own, up1, down1, kept,
        jnp.asarray(np.ascontiguousarray(pair_table(depth).T)),
        scratch=[(er, ec, depth), (rows1 + 2 * h, wide1, depth1)],
    )
    return out


def solution(mesh):
    return jax.shard_map(
        shards,
        mesh=mesh,
        in_specs=(P("gx", "gy", None), P(None, "gx", "gy", None)),
        out_specs=P("gx", "gy", None),
        check_vma=False,
    )
```

time: 105 us -> 84.7 us (0.81); the launches traced: 105 us -> 83 us
  Pallas kernels: 20.7 us -> 12.8 us
  waiting for transfers between devices: 39.1 us -> 31.6 us
  local copies, waits for them, and re-layouts: 10 us -> 2.58 us
  starting transfers between devices: 34.7 us -> 36 us
    ppermute x4 -> x0, waiting for transfers between devices: 28.8 us -> none  [moved(): return lax.ppermute(block, BOTH, route)]
    ppermute x8, waiting for transfers between devices: 3.74 us -> 22.7 us  [moved(): return lax.ppermute(block, 'gy', [(j, (j + dy) % ny) for j in range(ny)])]
    pallas_call x9 -> x12, Pallas kernels: 20.7 us -> 12.8 us  [call(): pl.pallas_call(body, out_shape=[s if hasattr(s, 'dtype') else jax.ShapeDt...]
    ppermute x8 -> x10, waiting for transfers between devices: 3.05 us -> 8.92 us  [moved(): return lax.ppermute(block, 'gx', [(i, (i + dx) % nx) for i in range(nx)])]
    unnamed x34 -> x16, local copies, waits for them, and re-layouts: 7.24 us -> 2.58 us
    all_to_all x1, waiting for transfers between devices: 3.52 us -> 0.01 us  [coarse_correction(): got = lax.all_to_all(chunks, BOTH, 0, 0)]
    dynamic_slice x2 -> x0, local copies, waits for them, and re-layouts: 2.06 us -> none  [own(): return lax.dynamic_slice_in_dim(table, lax.axis_index(axis) * step, size, 0)]
    all_to_all x1, starting transfers between devices: 4.45 us -> 5.85 us  [coarse_correction(): got = lax.all_to_all(chunks, BOTH, 0, 0)]
  transfers between devices with their start and end apart: 21 -> 19, of which waited for: 10 -> 9; matrix products, arithmetic and copies ran while one was open for 3% -> 0% of each run, Pallas kernels for 2% -> 4%
where the time goes in v2:
time: 84.7 us; the launch traced here: 83 us
  starting transfers between devices  36 us (43%)
  waiting for transfers between devices  31.6 us (37%)
  Pallas kernels  12.8 us (15%)
  local copies, waits for them, and re-layouts  2.58 us (3%)
    ppermute x8, waiting for transfers between devices, moved(): return lax.ppermute(block, 'gy', [(j, (j + dy) % ny) for j in range(ny)])  22.7 us
    ppermute x8, starting transfers between devices, moved(): return lax.ppermute(block, 'gy', [(j, (j + dy) % ny) for j in range(ny)])  15.9 us
    ppermute x10, starting transfers between devices, moved(): return lax.ppermute(block, 'gx', [(i, (i + dx) % nx) for i in range(nx)])  14.2 us
    pallas_call x12, Pallas kernels, call(): pl.pallas_call(body, out_shape=[s if hasattr(s, 'dtype') else jax.ShapeDt...  12.8 us
    ppermute x10, waiting for transfers between devices, moved(): return lax.ppermute(block, 'gx', [(i, (i + dx) % nx) for i in range(nx)])  8.92 us
    all_to_all x1, starting transfers between devices, coarse_correction(): got = lax.all_to_all(chunks, BOTH, 0, 0)  5.85 us
    unnamed x16, local copies, waits for them, and re-layouts  2.58 us
  transfers between devices with their start and end apart: 19, of which 9 were waited for; matrix products, arithmetic and copies ran while one was open for 0% of the time, Pallas kernels for 4%

profile of v2, /device:TPU:0, one launch (start us, length us, event | category | flops | bytes accessed | tf_op | source)
XLA Modules:
  0.0 83.0 jit_solution(14555518342851238725)
XLA Ops:
  0.0 1.0 %copy-done.3 = bf16[3,8,16,512]{3,2,1,0:T(8,128)(2,1)S(1)} copy-done((bf16[3,8,16,512]{3,2,1,0:T(8,128)(2,1)S(1)}, bf16[3,8,16,512]{3,2,1,0:T(8,128)(2,1)}, u32[]{:S(2)}) %copy-start.3) | copy-done | bytes 393240
  1.0 0.9 %copy-done.4 = f32[8,16,512]{2,1,0:T(8,128)S(1)} copy-done((f32[8,16,512]{2,1,0:T(8,128)S(1)}, f32[8,16,512]{2,1,0:T(8,128)}, u32[]{:S(2)}) %copy-start.4) | copy-done | bytes 262168
  1.9 1.3 %shard_map.55 = (f32[19,8,512]{2,1,0:T(8,128)S(1)}, f32[19,8,512]{2,1,0:T(8,128)S(1)}, f32[38,8,512]{2,1,0:T(8,128)S(1)}, f32[38,8,512]{2,1,0:T(8,128)S(1)}, f32...) custom-call(f32[8,16,512]{2,1,0:T(8,128)S(1)} %copy-done.4, ...), custom_call_target="tpu_custom_call" | custom-call | tf_op jit(solution)/shard_map/pallas_call | solution.py:45
  3.8 2.9 %collective-permute-start.5 = (f32[38,8,512]{2,1,0:T(8,128)S(1)}, f32[38,8,512]{2,1,0:T(8,128)S(1)}, u32[]{:S(2)}, u32[]{:S(2)}) collective-permute-start(f32[38,8,512]{2,1,0:T(8,128)S(1)} %get-tuple-element.52), channel_id=1, source_target_pairs={{0,28},{4,0},{8,4},{12,8},{16,12},{20,16},{24,20},{28,24},{1,29},{... | collective-permute-start | bytes 1867784 | tf_op jit(solution)/shard_map/ppermute | solution.py:58
  6.7 2.3 %collective-permute-start = (f32[19,8,512]{2,1,0:T(8,128)S(1)}, f32[19,8,512]{2,1,0:T(8,128)S(1)}, u32[]{:S(2)}, u32[]{:S(2)}) collective-permute-start(f32[19,8,512]{2,1,0:T(8,128)S(1)} %get-tuple-element.43), channel_id=1, source_target_pairs={{0,1},{1,2},{2,3},{3,0},{4,5},{5,6},{6,7},{7,4},{8,9},{9,10},{10,1... | collective-permute-start | bytes 933896 | tf_op jit(solution)/shard_map/ppermute | solution.py:60
  9.0 2.0 %collective-permute-start.1 = (f32[19,8,512]{2,1,0:T(8,128)S(1)}, f32[19,8,512]{2,1,0:T(8,128)S(1)}, u32[]{:S(2)}, u32[]{:S(2)}) collective-permute-start(f32[19,8,512]{2,1,0:T(8,128)S(1)} %get-tuple-element.44), channel_id=1, source_target_pairs={{0,3},{1,0},{2,1},{3,2},{4,7},{5,4},{6,5},{7,6},{8,11},{9,8},{10,9... | collective-permute-start | bytes 933896 | tf_op jit(solution)/shard_map/ppermute | solution.py:60
  11.0 8.3 %collective-permute-done.refs_0_.refs_5_ = f32[19,8,512]{2,1,0:T(8,128)S(1)} collective-permute-done((f32[19,8,512]{2,1,0:T(8,128)S(1)}, f32[19,8,512]{2,1,0:T(8,128)S(1)}, u32[]{:S(2)}, u32[]{:S(2)}) %collective-permute-start) | collective-permute-done | bytes 311328 | tf_op jit(solution)/shard_map/ppermute | solution.py:60
  19.3 4.3 %collective-permute-done.1.refs_1_.refs_6_ = f32[19,8,512]{2,1,0:T(8,128)S(1)} collective-permute-done((f32[19,8,512]{2,1,0:T(8,128)S(1)}, f32[19,8,512]{2,1,0:T(8,128)S(1)}, u32[]{:S(2)}, u32[]{:S(2)}) %collective-permute-start.1) | collective-permute-done | bytes 311328 | tf_op jit(solution)/shard_map/ppermute | solution.py:60
  23.8 2.6 %collective-permute-start.3 = (f32[10,8,512]{2,1,0:T(8,128)S(1)}, f32[10,8,512]{2,1,0:T(8,128)S(1)}, u32[]{:S(2)}, u32[]{:S(2)}) collective-permute-start(f32[10,8,512]{2,1,0:T(8,128)S(1)} %get-tuple-element.46), channel_id=1, source_target_pairs={{0,28},{4,0},{8,4},{12,8},{16,12},{20,16},{24,20},{28,24},{1,29},{... | collective-permute-start | bytes 491528 | tf_op jit(solution)/shard_map/ppermute | solution.py:58
  26.4 1.0 %shard_map.57 = (f32[7,16,24,512]{3,2,1,0:T(8,128)S(1)}, f32[3,12,16,256]{3,2,1,0:T(8,128)S(1)}) custom-call(f32[8,16,512]{2,1,0:T(8,128)S(1)} %get-tuple-element.48.refs_0_, bf16[3,8,16,512]{3,2,1,0:T(8,128)(2,1)S(1)} %get-tuple-element.49.refs_1_, f32[3,4,8,256]{3,2,1,0:T(8,128)S(1)} %get-tuple-element.50.refs_2_, ...), custom_call_target="tpu_custom_call" | custom-call | tf_op jit(solution)/shard_map/pallas_call | solution.py:45
  27.4 2.9 %collective-permute-done.2.refs_0_ = f32[10,8,512]{2,1,0:T(8,128)S(1)} collective-permute-done((f32[10,8,512]{2,1,0:T(8,128)S(1)}, f32[10,8,512]{2,1,0:T(8,128)S(1)}, u32[]{:S(2)}, u32[]{:S(2)}) %collective-permute-start.2) | collective-permute-done | bytes 163872 | tf_op jit(solution)/shard_map/ppermute | solution.py:58
  30.3 3.1 %shard_map.58 = (f32[5,16,24,512]{3,2,1,0:T(8,128)S(1)}, f32[3,12,16,256]{3,2,1,0:T(8,128)S(1)}, f32[8,16,512]{2,1,0:T(8,128)S(1)}, f32[4,8,256]{2,1,0:T(8,128)S...) custom-call(f32[10,8,512]{2,1,0:T(8,128)S(1)} %collective-permute-do, ...), custom_call_target="tpu_custom_call" | custom-call | tf_op jit(solution)/shard_map/pallas_call | solution.py:45
  33.5 1.2 %collective-permute-start.6 = (f32[2,8,256]{2,1,0:T(8,128)S(1)}, f32[2,8,256]{2,1,0:T(8,128)S(1)}, u32[]{:S(2)}, u32[]{:S(2)}) collective-permute-start(f32[2,8,256]{2,1,0:T(8,128)S(1)} %get-tuple-element.56), channel_id=1, source_target_pairs={{0,1},{1,2},{2,3},{3,0},{4,5},{5,6},{6,7},{7,4},{8,9},{9,10},{10,1... | collective-permute-start | bytes 49160 | tf_op jit(solution)/shard_map/ppermute | solution.py:60
  34.7 2.7 %collective-permute-start.7 = (f32[2,8,256]{2,1,0:T(8,128)S(1)}, f32[2,8,256]{2,1,0:T(8,128)S(1)}, u32[]{:S(2)}, u32[]{:S(2)}) collective-permute-start(f32[2,8,256]{2,1,0:T(8,128)S(1)} %get-tuple-element.57), channel_id=1, source_target_pairs={{0,3},{1,0},{2,1},{3,2},{4,7},{5,4},{6,5},{7,6},{8,11},{9,8},{10,9... | collective-permute-start | bytes 49160 | tf_op jit(solution)/shard_map/ppermute | solution.py:60
  37.4 1.9 %collective-permute-done.6.refs_1_ = f32[2,8,256]{2,1,0:T(8,128)S(1)} collective-permute-done((f32[2,8,256]{2,1,0:T(8,128)S(1)}, f32[2,8,256]{2,1,0:T(8,128)S(1)}, u32[]{:S(2)}, u32[]{:S(2)}) %collective-permute-start.6) | collective-permute-done | bytes 16416 | tf_op jit(solution)/shard_map/ppermute | solution.py:60
  39.3 2.6 %collective-permute-start.9 = (f32[4,16,256]{2,1,0:T(8,128)S(1)}, f32[4,16,256]{2,1,0:T(8,128)S(1)}, u32[]{:S(2)}, u32[]{:S(2)}) collective-permute-start(f32[4,16,256]{2,1,0:T(8,128)S(1)} %get-tuple-element.62), channel_id=1, source_target_pairs={{0,28},{4,0},{8,4},{12,8},{16,12},{20,16},{24,20},{28,24},{1,29},{... | collective-permute-start | bytes 196616 | tf_op jit(solution)/shard_map/ppermute | solution.py:58
  42.0 2.3 %collective-permute-done.8.refs_1_ = f32[4,16,256]{2,1,0:T(8,128)S(1)} collective-permute-done((f32[4,16,256]{2,1,0:T(8,128)S(1)}, f32[4,16,256]{2,1,0:T(8,128)S(1)}, u32[]{:S(2)}, u32[]{:S(2)}) %collective-permute-start.8) | collective-permute-done | bytes 65568 | tf_op jit(solution)/shard_map/ppermute | solution.py:58
  44.2 1.3 %shard_map.60 = (f32[6,12,16,256]{3,2,1,0:T(8,128)S(1)}, f32[32,9,128]{2,1,0:T(8,128)}, f32[3,8,512]{2,1,0:T(8,128)S(1)}, f32[3,8,512]{2,1,0:T(8,128)S(1)}) custom-call(f32[4,16,256]{2,1,0:T(8,128)S(1)} %get-tuple-element.60.refs_0_, f32[4,16,256]{2,1,0:T(8,128)S(1)} %collective-permute-done.8.refs_1_, f32[4,16,256]{2,1,0:T(8,128)S(1)} %collective-permute-done.9.refs_2_, ...), custom_call_target="tpu_custom_call" | custom-call | tf_op jit(solution)/shard_map/pallas_call | solution.py:45
  46.2 5.9 %all-to-all-start = ((f32[32,9,128]{2,1,0:T(8,128)}), f32[32,9,128]{2,1,0:T(8,128)S(1)}, u32[]{:S(2)}, u32[]{:S(2)}) async-start(f32[32,9,128]{2,1,0:T(8,128)} %get-tuple-element.74), calls=%async_computation | async-start | bytes 524288 | tf_op jit(solution)/shard_map/all_to_all | solution.py:619
  52.0 1.8 %collective-permute-start.10 = (f32[3,8,512]{2,1,0:T(8,128)}, f32[3,8,512]{2,1,0:T(8,128)S(1)}, u32[]{:S(2)}, u32[]{:S(2)}) collective-permute-start(f32[3,8,512]{2,1,0:T(8,128)} %copy-done.7), channel_id=1, source_target_pairs={{0,1},{1,2},{2,3},{3,0},{4,5},{5,6},{6,7},{7,4},{8,9},{9,10},{10,1... | collective-permute-start | bytes 147464 | tf_op jit(solution)/shard_map/ppermute | solution.py:60
  53.9 2.1 %collective-permute-start.11 = (f32[3,8,512]{2,1,0:T(8,128)S(1)}, f32[3,8,512]{2,1,0:T(8,128)S(1)}, u32[]{:S(2)}, u32[]{:S(2)}) collective-permute-start(f32[3,8,512]{2,1,0:T(8,128)S(1)} %get-tuple-element.69), channel_id=1, source_target_pairs={{0,3},{1,0},{2,1},{3,2},{4,7},{5,4},{6,5},{7,6},{8,11},{9,8},{10,9... | collective-permute-start | bytes 147464 | tf_op jit(solution)/shard_map/ppermute | solution.py:60
  55.9 6.6 %collective-permute-done.10.refs_1_ = f32[3,8,512]{2,1,0:T(8,128)S(1)} collective-permute-done((f32[3,8,512]{2,1,0:T(8,128)}, f32[3,8,512]{2,1,0:T(8,128)S(1)}, u32[]{:S(2)}, u32[]{:S(2)}) %collective-permute-start.10) | collective-permute-done | bytes 49184 | tf_op jit(solution)/shard_map/ppermute | solution.py:60
  62.5 0.9 %shard_map.61 = (f32[10,24,512]{2,1,0:T(8,128)S(1)}, f32[10,8,512]{2,1,0:T(8,128)}, f32[10,8,512]{2,1,0:T(8,128)}) custom-call(f32[6,12,16,256]{3,2,1,0:T(8,128)S(1)} %get-tuple-element.67.refs_0_.refs_4_, f32[3,8,512]{2,1,0:T(8,128)S(1)} %collective-permute-done.10.refs_1_, f32[3,8,512]{2,1,0:T(8,128)S(1)} %collective-permute-done.11.refs_2_, ...), custom_call_target="tpu_custom_call" | custom-call | tf_op jit(solution)/shard_map/pallas_call | solution.py:45
  63.3 2.6 %collective-permute-start.13 = (f32[10,8,512]{2,1,0:T(8,128)}, f32[10,8,512]{2,1,0:T(8,128)S(1)}, u32[]{:S(2)}, u32[]{:S(2)}) collective-permute-start(f32[10,8,512]{2,1,0:T(8,128)} %get-tuple-element.73), channel_id=1, source_target_pairs={{0,28},{4,0},{8,4},{12,8},{16,12},{20,16},{24,20},{28,24},{1,29},{... | collective-permute-start | bytes 491528 | tf_op jit(solution)/shard_map/ppermute | solution.py:58
  66.0 1.0 %shard_map.63.refs_3_ = f32[12,16,256]{2,1,0:T(8,128)S(1)} custom-call(f32[32,9,128]{2,1,0:T(8,128)S(1)} %all-to-all-done.refs_0_, f32[960,256]{1,0:T(8,128)S(1)} %copy-done.2), custom_call_target="tpu_custom_call" | custom-call | tf_op jit(solution)/shard_map/pallas_call | solution.py:45
  67.0 2.2 %collective-permute-done.12.refs_1_ = f32[10,8,512]{2,1,0:T(8,128)S(1)} collective-permute-done((f32[10,8,512]{2,1,0:T(8,128)}, f32[10,8,512]{2,1,0:T(8,128)S(1)}, u32[]{:S(2)}, u32[]{:S(2)}) %collective-permute-start.12) | collective-permute-done | bytes 163872 | tf_op jit(solution)/shard_map/ppermute | solution.py:58
  69.6 1.6 %collective-permute-start.14 = (f32[1,8,256]{2,1,0:T(8,128)S(1)}, f32[1,8,256]{2,1,0:T(8,128)S(1)}, u32[]{:S(2)}, u32[]{:S(2)}) collective-permute-start(f32[1,8,256]{2,1,0:T(8,128)S(1)} %get-tuple-element.76), channel_id=1, source_target_pairs={{0,1},{1,2},{2,3},{3,0},{4,5},{5,6},{6,7},{7,4},{8,9},{9,10},{10,1... | collective-permute-start | bytes 24584 | tf_op jit(solution)/shard_map/ppermute | solution.py:60
  71.3 2.2 %collective-permute-start.15 = (f32[1,8,256]{2,1,0:T(8,128)S(1)}, f32[1,8,256]{2,1,0:T(8,128)S(1)}, u32[]{:S(2)}, u32[]{:S(2)}) collective-permute-start(f32[1,8,256]{2,1,0:T(8,128)S(1)} %get-tuple-element.77), channel_id=1, source_target_pairs={{0,3},{1,0},{2,1},{3,2},{4,7},{5,4},{6,5},{7,6},{8,11},{9,8},{10,9... | collective-permute-start | bytes 24584 | tf_op jit(solution)/shard_map/ppermute | solution.py:60
  73.5 1.6 %collective-permute-done.14.refs_1_ = f32[1,8,256]{2,1,0:T(8,128)S(1)} collective-permute-done((f32[1,8,256]{2,1,0:T(8,128)S(1)}, f32[1,8,256]{2,1,0:T(8,128)S(1)}, u32[]{:S(2)}, u32[]{:S(2)}) %collective-permute-start.14) | collective-permute-done | bytes 8224 | tf_op jit(solution)/shard_map/ppermute | solution.py:60
  75.7 2.2 %collective-permute-start.17 = (f32[2,16,256]{2,1,0:T(8,128)S(1)}, f32[2,16,256]{2,1,0:T(8,128)S(1)}, u32[]{:S(2)}, u32[]{:S(2)}) collective-permute-start(f32[2,16,256]{2,1,0:T(8,128)S(1)} %get-tuple-element.80), channel_id=1, source_target_pairs={{0,28},{4,0},{8,4},{12,8},{16,12},{20,16},{24,20},{28,24},{1,29},{... | collective-permute-start | bytes 98312 | tf_op jit(solution)/shard_map/ppermute | solution.py:58
  77.9 1.5 %collective-permute-done.16.refs_2_ = f32[2,16,256]{2,1,0:T(8,128)S(1)} collective-permute-done((f32[2,16,256]{2,1,0:T(8,128)S(1)}, f32[2,16,256]{2,1,0:T(8,128)S(1)}, u32[]{:S(2)}, u32[]{:S(2)}) %collective-permute-start.16) | collective-permute-done | bytes 32800 | tf_op jit(solution)/shard_map/ppermute | solution.py:58
  79.5 3.5 %shard_map.66 = f32[8,16,512]{2,1,0:T(8,128)} custom-call(f32[16,24,512]{2,1,0:T(8,128)S(1)} %shard_map.62.refs_0_, f32[4,16,256]{2,1,0:T(8,128)S(1)} %get-tuple-element.78.refs_1_, f32[2,16,256]{2,1,0:T(8,128)S(1)} %collective-permute-done.16.refs_2_, f32[2,16,256]{2,1,0:T(8,128)S(1)} %collective-permute-done.17.refs_3_, f32[5,16,24,512]{3,2,1,0:T(8,128)S(1)} %copy-done.1, ...), custom_call_target="tpu_custom_call" | custom-call | tf_op jit(solution)/shard_map/pallas_call | solution.py:45
  (34 shorter events, 2.4 us)
Async XLA Ops:
  0.0 1.0 %copy-start.3 = (bf16[3,8,16,512]{3,2,1,0:T(8,128)(2,1)S(1)}, bf16[3,8,16,512]{3,2,1,0:T(8,128)(2,1)}, u32[]{:S(2)}) copy-start(bf16[3,8,16,512]{3,2,1,0:T(8,128)(2,1)} %refs_1_.2) | copy-start | bytes 1179652
  1.0 0.9 %copy-start.4 = (f32[8,16,512]{2,1,0:T(8,128)S(1)}, f32[8,16,512]{2,1,0:T(8,128)}, u32[]{:S(2)}) copy-start(f32[8,16,512]{2,1,0:T(8,128)} %refs_0_.1) | copy-start | bytes 786436
  3.3 23.1 %collective-permute-start.4 = (f32[38,8,512]{2,1,0:T(8,128)S(1)}, f32[38,8,512]{2,1,0:T(8,128)S(1)}, u32[]{:S(2)}, u32[]{:S(2)}) collective-permute-start(f32[38,8,512]{2,1,0:T(8,128)S(1)} %get-tuple-element.51), channel_id=1, source_target_pairs={{0,4},{4,8},{8,12},{12,16},{16,20},{20,24},{24,28},{28,0},{1,5},{5... | collective-permute-start | bytes 1867784 | tf_op jit(solution)/shard_map/ppermute | solution.py:58
  3.8 22.6 %collective-permute-start.5 = (f32[38,8,512]{2,1,0:T(8,128)S(1)}, f32[38,8,512]{2,1,0:T(8,128)S(1)}, u32[]{:S(2)}, u32[]{:S(2)}) collective-permute-start(f32[38,8,512]{2,1,0:T(8,128)S(1)} %get-tuple-element.52), channel_id=1, source_target_pairs={{0,28},{4,0},{8,4},{12,8},{16,12},{20,16},{24,20},{28,24},{1,29},{... | collective-permute-start | bytes 1867784 | tf_op jit(solution)/shard_map/ppermute | solution.py:58
  6.7 12.6 %collective-permute-start = (f32[19,8,512]{2,1,0:T(8,128)S(1)}, f32[19,8,512]{2,1,0:T(8,128)S(1)}, u32[]{:S(2)}, u32[]{:S(2)}) collective-permute-start(f32[19,8,512]{2,1,0:T(8,128)S(1)} %get-tuple-element.43), channel_id=1, source_target_pairs={{0,1},{1,2},{2,3},{3,0},{4,5},{5,6},{6,7},{7,4},{8,9},{9,10},{10,1... | collective-permute-start | bytes 933896 | tf_op jit(solution)/shard_map/ppermute | solution.py:60
  9.0 14.6 %collective-permute-start.1 = (f32[19,8,512]{2,1,0:T(8,128)S(1)}, f32[19,8,512]{2,1,0:T(8,128)S(1)}, u32[]{:S(2)}, u32[]{:S(2)}) collective-permute-start(f32[19,8,512]{2,1,0:T(8,128)S(1)} %get-tuple-element.44), channel_id=1, source_target_pairs={{0,3},{1,0},{2,1},{3,2},{4,7},{5,4},{6,5},{7,6},{8,11},{9,8},{10,9... | collective-permute-start | bytes 933896 | tf_op jit(solution)/shard_map/ppermute | solution.py:60
  23.7 6.6 %collective-permute-start.2 = (f32[10,8,512]{2,1,0:T(8,128)S(1)}, f32[10,8,512]{2,1,0:T(8,128)S(1)}, u32[]{:S(2)}, u32[]{:S(2)}) collective-permute-start(f32[10,8,512]{2,1,0:T(8,128)S(1)} %get-tuple-element.45), channel_id=1, source_target_pairs={{0,4},{4,8},{8,12},{12,16},{16,20},{20,24},{24,28},{28,0},{1,5},{5... | collective-permute-start | bytes 491528 | tf_op jit(solution)/shard_map/ppermute | solution.py:58
  23.8 6.6 %collective-permute-start.3 = (f32[10,8,512]{2,1,0:T(8,128)S(1)}, f32[10,8,512]{2,1,0:T(8,128)S(1)}, u32[]{:S(2)}, u32[]{:S(2)}) collective-permute-start(f32[10,8,512]{2,1,0:T(8,128)S(1)} %get-tuple-element.46), channel_id=1, source_target_pairs={{0,28},{4,0},{8,4},{12,8},{16,12},{20,16},{24,20},{28,24},{1,29},{... | collective-permute-start | bytes 491528 | tf_op jit(solution)/shard_map/ppermute | solution.py:58
  30.3 13.9 %copy-start.6 = (bf16[256,128]{1,0:T(8,128)(2,1)S(1)}, bf16[256,128]{1,0:T(8,128)(2,1)}, u32[]{:S(2)}) copy-start(bf16[256,128]{1,0:T(8,128)(2,1)} %constant.6.clone.refs_6_) | copy-start | bytes 196612
  33.5 12.1 %copy-start = (f32[5,16,24,512]{3,2,1,0:T(8,128)}, f32[5,16,24,512]{3,2,1,0:T(8,128)S(1)}, u32[]{:S(2)}) copy-start(f32[5,16,24,512]{3,2,1,0:T(8,128)S(1)} %get-tuple-element.59.refs_4_.refs_9_) | copy-start | bytes 11796484
  33.5 5.7 %collective-permute-start.6 = (f32[2,8,256]{2,1,0:T(8,128)S(1)}, f32[2,8,256]{2,1,0:T(8,128)S(1)}, u32[]{:S(2)}, u32[]{:S(2)}) collective-permute-start(f32[2,8,256]{2,1,0:T(8,128)S(1)} %get-tuple-element.56), channel_id=1, source_target_pairs={{0,1},{1,2},{2,3},{3,0},{4,5},{5,6},{6,7},{7,4},{8,9},{9,10},{10,1... | collective-permute-start | bytes 49160 | tf_op jit(solution)/shard_map/ppermute | solution.py:60
  34.7 4.6 %collective-permute-start.7 = (f32[2,8,256]{2,1,0:T(8,128)S(1)}, f32[2,8,256]{2,1,0:T(8,128)S(1)}, u32[]{:S(2)}, u32[]{:S(2)}) collective-permute-start(f32[2,8,256]{2,1,0:T(8,128)S(1)} %get-tuple-element.57), channel_id=1, source_target_pairs={{0,3},{1,0},{2,1},{3,2},{4,7},{5,4},{6,5},{7,6},{8,11},{9,8},{10,9... | collective-permute-start | bytes 49160 | tf_op jit(solution)/shard_map/ppermute | solution.py:60
  39.3 26.7 %copy-start.2 = (f32[960,256]{1,0:T(8,128)S(1)}, f32[960,256]{1,0:T(8,128)}, u32[]{:S(2)}) copy-start(f32[960,256]{1,0:T(8,128)} %constant.7.clone.refs_1_) | copy-start | bytes 2949124
  39.3 5.0 %collective-permute-start.8 = (f32[4,16,256]{2,1,0:T(8,128)S(1)}, f32[4,16,256]{2,1,0:T(8,128)S(1)}, u32[]{:S(2)}, u32[]{:S(2)}) collective-permute-start(f32[4,16,256]{2,1,0:T(8,128)S(1)} %get-tuple-element.61), channel_id=1, source_target_pairs={{0,4},{4,8},{8,12},{12,16},{16,20},{20,24},{24,28},{28,0},{1,5},{5... | collective-permute-start | bytes 196616 | tf_op jit(solution)/shard_map/ppermute | solution.py:58
  39.3 4.9 %collective-permute-start.9 = (f32[4,16,256]{2,1,0:T(8,128)S(1)}, f32[4,16,256]{2,1,0:T(8,128)S(1)}, u32[]{:S(2)}, u32[]{:S(2)}) collective-permute-start(f32[4,16,256]{2,1,0:T(8,128)S(1)} %get-tuple-element.62), channel_id=1, source_target_pairs={{0,28},{4,0},{8,4},{12,8},{16,12},{20,16},{24,20},{28,24},{1,29},{... | collective-permute-start | bytes 196616 | tf_op jit(solution)/shard_map/ppermute | solution.py:58
  45.5 0.6 copy-start.7
  46.2 33.3 %copy-start.5 = (bf16[256,512]{1,0:T(8,128)(2,1)S(1)}, bf16[256,512]{1,0:T(8,128)(2,1)}, u32[]{:S(2)}) copy-start(bf16[256,512]{1,0:T(8,128)(2,1)} %constant.8.clone.refs_5_) | copy-start | bytes 786436
  46.2 19.8 %all-to-all-start = ((f32[32,9,128]{2,1,0:T(8,128)}), f32[32,9,128]{2,1,0:T(8,128)S(1)}, u32[]{:S(2)}, u32[]{:S(2)}) async-start(f32[32,9,128]{2,1,0:T(8,128)} %get-tuple-element.74), calls=%async_computation | async-start | bytes 524288 | tf_op jit(solution)/shard_map/all_to_all | solution.py:619
  52.0 10.5 %collective-permute-start.10 = (f32[3,8,512]{2,1,0:T(8,128)}, f32[3,8,512]{2,1,0:T(8,128)S(1)}, u32[]{:S(2)}, u32[]{:S(2)}) collective-permute-start(f32[3,8,512]{2,1,0:T(8,128)} %copy-done.7), channel_id=1, source_target_pairs={{0,1},{1,2},{2,3},{3,0},{4,5},{5,6},{6,7},{7,4},{8,9},{9,10},{10,1... | collective-permute-start | bytes 147464 | tf_op jit(solution)/shard_map/ppermute | solution.py:60
  53.9 8.6 %collective-permute-start.11 = (f32[3,8,512]{2,1,0:T(8,128)S(1)}, f32[3,8,512]{2,1,0:T(8,128)S(1)}, u32[]{:S(2)}, u32[]{:S(2)}) collective-permute-start(f32[3,8,512]{2,1,0:T(8,128)S(1)} %get-tuple-element.69), channel_id=1, source_target_pairs={{0,3},{1,0},{2,1},{3,2},{4,7},{5,4},{6,5},{7,6},{8,11},{9,8},{10,9... | collective-permute-start | bytes 147464 | tf_op jit(solution)/shard_map/ppermute | solution.py:60
  63.3 5.9 %collective-permute-start.12 = (f32[10,8,512]{2,1,0:T(8,128)}, f32[10,8,512]{2,1,0:T(8,128)S(1)}, u32[]{:S(2)}, u32[]{:S(2)}) collective-permute-start(f32[10,8,512]{2,1,0:T(8,128)} %get-tuple-element.72), channel_id=1, source_target_pairs={{0,4},{4,8},{8,12},{12,16},{16,20},{20,24},{24,28},{28,0},{1,5},{5... | collective-permute-start | bytes 491528 | tf_op jit(solution)/shard_map/ppermute | solution.py:58
  63.3 5.9 %collective-permute-start.13 = (f32[10,8,512]{2,1,0:T(8,128)}, f32[10,8,512]{2,1,0:T(8,128)S(1)}, u32[]{:S(2)}, u32[]{:S(2)}) collective-permute-start(f32[10,8,512]{2,1,0:T(8,128)} %get-tuple-element.73), channel_id=1, source_target_pairs={{0,28},{4,0},{8,4},{12,8},{16,12},{20,16},{24,20},{28,24},{1,29},{... | collective-permute-start | bytes 491528 | tf_op jit(solution)/shard_map/ppermute | solution.py:58
  66.0 13.5 %copy-start.1 = (f32[5,16,24,512]{3,2,1,0:T(8,128)S(1)}, f32[5,16,24,512]{3,2,1,0:T(8,128)}, u32[]{:S(2)}) copy-start(f32[5,16,24,512]{3,2,1,0:T(8,128)} %copy-done) | copy-start | bytes 11796484
  69.6 5.5 %collective-permute-start.14 = (f32[1,8,256]{2,1,0:T(8,128)S(1)}, f32[1,8,256]{2,1,0:T(8,128)S(1)}, u32[]{:S(2)}, u32[]{:S(2)}) collective-permute-start(f32[1,8,256]{2,1,0:T(8,128)S(1)} %get-tuple-element.76), channel_id=1, source_target_pairs={{0,1},{1,2},{2,3},{3,0},{4,5},{5,6},{6,7},{7,4},{8,9},{9,10},{10,1... | collective-permute-start | bytes 24584 | tf_op jit(solution)/shard_map/ppermute | solution.py:60
  71.3 3.9 %collective-permute-start.15 = (f32[1,8,256]{2,1,0:T(8,128)S(1)}, f32[1,8,256]{2,1,0:T(8,128)S(1)}, u32[]{:S(2)}, u32[]{:S(2)}) collective-permute-start(f32[1,8,256]{2,1,0:T(8,128)S(1)} %get-tuple-element.77), channel_id=1, source_target_pairs={{0,3},{1,0},{2,1},{3,2},{4,7},{5,4},{6,5},{7,6},{8,11},{9,8},{10,9... | collective-permute-start | bytes 24584 | tf_op jit(solution)/shard_map/ppermute | solution.py:60
  75.2 4.3 %collective-permute-start.16 = (f32[2,16,256]{2,1,0:T(8,128)S(1)}, f32[2,16,256]{2,1,0:T(8,128)S(1)}, u32[]{:S(2)}, u32[]{:S(2)}) collective-permute-start(f32[2,16,256]{2,1,0:T(8,128)S(1)} %get-tuple-element.79), channel_id=1, source_target_pairs={{0,4},{4,8},{8,12},{12,16},{16,20},{20,24},{24,28},{28,0},{1,5},{5... | collective-permute-start | bytes 98312 | tf_op jit(solution)/shard_map/ppermute | solution.py:58
  75.7 3.8 %collective-permute-start.17 = (f32[2,16,256]{2,1,0:T(8,128)S(1)}, f32[2,16,256]{2,1,0:T(8,128)S(1)}, u32[]{:S(2)}, u32[]{:S(2)}) collective-permute-start(f32[2,16,256]{2,1,0:T(8,128)S(1)} %get-tuple-element.80), channel_id=1, source_target_pairs={{0,28},{4,0},{8,4},{12,8},{16,12},{20,16},{24,20},{28,24},{1,29},{... | collective-permute-start | bytes 98312 | tf_op jit(solution)/shard_map/ppermute | solution.py:58

commit v3 on v2

--- a/solution.py
+++ b/solution.py
@@ -370,10 +370,25 @@
             out[k] = jnp.where(edge, value * rdiag1[H + i], value)
 
 
-def pre1_kernel(rows_own, up, down, w1e, rdiag1, diag1, pairs, merged_right, merged_left, *rest):
-    kept, chunks, to_right, to_left = rest[:4]
-    chunk = chunks.at[0]
-    t256, t128 = rest[4:]
+def sums_kernel(w1, out):
+    _, rows, cols, depth = w1.shape
+    lane = lax.broadcasted_iota(jnp.int32, out.shape, 1)
+    row_odd = lax.broadcasted_iota(jnp.int32, (cols, depth), 0) & 1
+    depth_odd = lax.broadcasted_iota(jnp.int32, (cols, depth), 1) & 1
+    parts = [0.0, 0.0, 0.0]
+    for i in range(rows):
+        if i % 2 == 1:
+            parts[0] = parts[0] + w1[0, i]
+        parts[1] = parts[1] + jnp.where(row_odd == 1, w1[1, i], 0.0)
+        parts[2] = parts[2] + jnp.where(depth_odd == 1, w1[2, i], 0.0)
+    line = jnp.zeros(out.shape, F32)
+    for d in range(3):
+        line = jnp.where(lane == d, 0.0625 * jnp.sum(parts[d]), line)
+    out[...] = line
+
+
+def pre1_kernel(rows_own, up, down, w1e, rdiag1, merged_right, merged_left, *rest):
+    kept, to_right, to_left = rest
     b1, v = kept.at[4], kept.at[5]
     kept[0:3] = w1e[...]
     kept[3] = rdiag1[...]
@@ -395,6 +410,19 @@
     half_sweep(1, er - 1, 1, parity, v, b1, wx, wy, wz, rdiag1)
     half_sweep(2, er - 2, 0, parity, v, b1, wx, wy, wz, rdiag1)
     half_sweep(3, er - 3, 1, parity, v, b1, wx, wy, wz, rdiag1)
+    for out, base, merged in ((to_right, cols - H, merged_right), (to_left, 0, merged_left)):
+        n = merged.shape[0]
+        out[0:n] = merged[...]
+        for i in range(rows):
+            s, lane = H * (i % 2), depth * ((i // 2) % 2)
+            out[n + i // 4, s : s + H, lane : lane + depth] = v[H + i, H + base : 2 * H + base]
+
+
+def residual1_kernel(kept1, diag1, pairs, sums, chunks, t256, t128):
+    wx, wy, wz, _, b1, v = (kept1.at[i] for i in range(6))
+    chunk = chunks.at[0]
+    er, ec, depth = diag1.shape
+    rows, cols, half = er - 2 * H, ec - 2 * H, depth // 2
     for i in range(rows // 2):
         total = 0.0
         for k in range(2):
@@ -409,30 +437,9 @@
         chunk[i * (cols // 2) : (i + 1) * (cols // 2)] = 0.125 * (
             every_other(t128, start, cols // 2) + every_other(t128, start + 1, cols // 2)
         )
-    lane = lax.broadcasted_iota(jnp.int32, (1, half), 1)
-    row_odd = lax.broadcasted_iota(jnp.int32, (cols, depth), 0) & 1
-    depth_odd = lax.broadcasted_iota(jnp.int32, (cols, depth), 1) & 1
-    parts = [0.0, 0.0, 0.0]
-    for i in range(rows):
-        if i % 2 == 1:
-            parts[0] = parts[0] + w1e[0, H + i, H : H + cols]
-        parts[1] = parts[1] + jnp.where(row_odd == 1, w1e[1, H + i, H : H + cols], 0.0)
-        parts[2] = parts[2] + jnp.where(depth_odd == 1, w1e[2, H + i, H : H + cols], 0.0)
-    line = jnp.zeros((1, half), F32)
-    for d in range(3):
-        line = jnp.where(lane == d, 0.0625 * jnp.sum(parts[d]), line)
-    n = (rows // 2) * (cols // 2)
-    chunk[n : n + 1] = line
-    value = chunk[...]
+    chunk[chunk.shape[0] - 1 :] = sums[0:1]
     for i in range(1, chunks.shape[0]):
-        chunks[i] = value
-
-    for out, base, merged in ((to_right, cols - H, merged_right), (to_left, 0, merged_left)):
-        n = merged.shape[0]
-        out[0:n] = merged[...]
-        for i in range(rows):
-            s, lane = H * (i % 2), depth * ((i // 2) % 2)
-            out[n + i // 4, s : s + H, lane : lane + depth] = v[H + i, H + base : 2 * H + base]
+        chunks[i] = chunk[...]
 
 
 def pack_v_kernel(kept1, right, left, v0, rows_out, to_up, to_down, v1_rows):
@@ -711,6 +718,7 @@
         functools.partial(forward_kernel, rows=rows), [(2 * corner_tiles, 8, depth)] * 2, right, left
     )
     corners = moved(to_up, 1, 0), moved(to_down, -1, 0)
+    (sums,) = call(sums_kernel, [(8, depth1 // 2)], w1)
     state = call(
         assemble_kernel,
         [(7, er, ec, depth), (3, er1, ec1, depth1)],
@@ -733,16 +741,21 @@
     )
     up, down = moved(to_up, 1, 0), moved(to_down, -1, 0)
     y_tiles = merged[0][0] + (rows1 + 3) // 4
-    kept1, chunks, to_right, to_left = call(
+    kept1, to_right, to_left = call(
         pre1_kernel,
-        [(6, er1, ec1, depth1), (lax.axis_size(BOTH), rows1 * cols1 // 4 + 1, depth1 // 2)]
-        + [(y_tiles, 8, depth)] * 2,
-        rows_own, up, down, w1e, rdiag1, diag1, jnp.asarray(pair_table(depth1)), merged_right, merged_left,
+        [(6, er1, ec1, depth1)] + [(y_tiles, 8, depth)] * 2,
+        rows_own, up, down, w1e, rdiag1, merged_right, merged_left,
         near=(kept,),
+    )
+    right, left = moved(to_right, 0, 1), moved(to_left, 0, -1)
+    (chunks,) = call(
+        residual1_kernel,
+        [(lax.axis_size(BOTH), rows1 * cols1 // 4 + 1, depth1 // 2)],
+        kept1, diag1, jnp.asarray(pair_table(depth1)), sums,
+        near=(right, left),
         scratch=[(rows1 // 2, ec1, depth1), (depth1 // 256, rows1 // 2 * ec1, 128)],
     )
 
-    right, left = moved(to_right, 0, 1), moved(to_left, 0, -1)
     correction2 = coarse_correction(chunks, rows1 // 2, cols1 // 2, depth1 // 2)
     x_tiles = (H // 2) * (ec // 8 + ec1 // 8)
     v_rows, to_up, to_down = call(

time: 84.7 us -> 82.1 us (0.969); the launches traced: 83 us -> 81.8 us
    all_to_all x1, waiting for transfers between devices: 0.01 us -> 6.71 us  [coarse_correction(): got = lax.all_to_all(chunks, BOTH, 0, 0)]
    ppermute x8, waiting for transfers between devices: 22.7 us -> 18 us  [moved(): return lax.ppermute(block, 'gy', [(j, (j + dy) % ny) for j in range(ny)])]
    ppermute x10, waiting for transfers between devices: 8.92 us -> 6.76 us  [moved(): return lax.ppermute(block, 'gx', [(i, (i + dx) % nx) for i in range(nx)])]
    unnamed x16 -> x14, local copies, waits for them, and re-layouts: 2.58 us -> 1.96 us
    pallas_call x12 -> x14, Pallas kernels: 12.8 us -> 12.9 us  [call(): pl.pallas_call(body, out_shape=[s if hasattr(s, 'dtype') else jax.ShapeDt...]
where the time goes in v3:
time: 82.1 us; the launch traced here: 81.8 us
  starting transfers between devices  35.3 us (43%)
  waiting for transfers between devices  31.5 us (38%)
  Pallas kernels  12.9 us (16%)
  local copies, waits for them, and re-layouts  1.96 us (2%)
    ppermute x8, waiting for transfers between devices, moved(): return lax.ppermute(block, 'gy', [(j, (j + dy) % ny) for j in range(ny)])  18 us
    ppermute x8, starting transfers between devices, moved(): return lax.ppermute(block, 'gy', [(j, (j + dy) % ny) for j in range(ny)])  16 us
    ppermute x10, starting transfers between devices, moved(): return lax.ppermute(block, 'gx', [(i, (i + dx) % nx) for i in range(nx)])  14.2 us
    pallas_call x14, Pallas kernels, call(): pl.pallas_call(body, out_shape=[s if hasattr(s, 'dtype') else jax.ShapeDt...  12.9 us
    ppermute x10, waiting for transfers between devices, moved(): return lax.ppermute(block, 'gx', [(i, (i + dx) % nx) for i in range(nx)])  6.76 us
    all_to_all x1, waiting for transfers between devices, coarse_correction(): got = lax.all_to_all(chunks, BOTH, 0, 0)  6.71 us
    all_to_all x1, starting transfers between devices, coarse_correction(): got = lax.all_to_all(chunks, BOTH, 0, 0)  5.17 us
    unnamed x14, local copies, waits for them, and re-layouts  1.96 us
  transfers between devices with their start and end apart: 19, of which 9 were waited for; matrix products, arithmetic and copies ran while one was open for 0% of the time, Pallas kernels for 4%

profile of v3, /device:TPU:0, one launch (start us, length us, event | category | flops | bytes accessed | tf_op | source)
XLA Modules:
  0.0 81.8 jit_solution(14867464521453681449)
XLA Ops:
  0.0 1.0 %copy-done.3 = bf16[3,8,16,512]{3,2,1,0:T(8,128)(2,1)S(1)} copy-done((bf16[3,8,16,512]{3,2,1,0:T(8,128)(2,1)S(1)}, bf16[3,8,16,512]{3,2,1,0:T(8,128)(2,1)}, u32[]{:S(2)}) %copy-start.3) | copy-done | bytes 393240
  1.0 0.9 %copy-done.4 = f32[8,16,512]{2,1,0:T(8,128)S(1)} copy-done((f32[8,16,512]{2,1,0:T(8,128)S(1)}, f32[8,16,512]{2,1,0:T(8,128)}, u32[]{:S(2)}) %copy-start.4) | copy-done | bytes 262168
  1.9 1.3 %shard_map.55 = (f32[19,8,512]{2,1,0:T(8,128)S(1)}, f32[19,8,512]{2,1,0:T(8,128)S(1)}, f32[38,8,512]{2,1,0:T(8,128)S(1)}, f32[38,8,512]{2,1,0:T(8,128)S(1)}, f32...) custom-call(f32[8,16,512]{2,1,0:T(8,128)S(1)} %copy-done.4, ...), custom_call_target="tpu_custom_call" | custom-call | tf_op jit(solution)/shard_map/pallas_call | solution.py:45
  3.3 0.5 collective-permute-start.4
  3.8 2.9 %collective-permute-start.5 = (f32[38,8,512]{2,1,0:T(8,128)S(1)}, f32[38,8,512]{2,1,0:T(8,128)S(1)}, u32[]{:S(2)}, u32[]{:S(2)}) collective-permute-start(f32[38,8,512]{2,1,0:T(8,128)S(1)} %get-tuple-element.51), channel_id=1, source_target_pairs={{0,28},{4,0},{8,4},{12,8},{16,12},{20,16},{24,20},{28,24},{1,29},{... | collective-permute-start | bytes 1867784 | tf_op jit(solution)/shard_map/ppermute | solution.py:58
  6.7 2.3 %collective-permute-start = (f32[19,8,512]{2,1,0:T(8,128)S(1)}, f32[19,8,512]{2,1,0:T(8,128)S(1)}, u32[]{:S(2)}, u32[]{:S(2)}) collective-permute-start(f32[19,8,512]{2,1,0:T(8,128)S(1)} %get-tuple-element.42), channel_id=1, source_target_pairs={{0,1},{1,2},{2,3},{3,0},{4,5},{5,6},{6,7},{7,4},{8,9},{9,10},{10,1... | collective-permute-start | bytes 933896 | tf_op jit(solution)/shard_map/ppermute | solution.py:60
  9.0 2.0 %collective-permute-start.1 = (f32[19,8,512]{2,1,0:T(8,128)S(1)}, f32[19,8,512]{2,1,0:T(8,128)S(1)}, u32[]{:S(2)}, u32[]{:S(2)}) collective-permute-start(f32[19,8,512]{2,1,0:T(8,128)S(1)} %get-tuple-element.43), channel_id=1, source_target_pairs={{0,3},{1,0},{2,1},{3,2},{4,7},{5,4},{6,5},{7,6},{8,11},{9,8},{10,9... | collective-permute-start | bytes 933896 | tf_op jit(solution)/shard_map/ppermute | solution.py:60
  11.0 8.3 %collective-permute-done.refs_0_.refs_5_ = f32[19,8,512]{2,1,0:T(8,128)S(1)} collective-permute-done((f32[19,8,512]{2,1,0:T(8,128)S(1)}, f32[19,8,512]{2,1,0:T(8,128)S(1)}, u32[]{:S(2)}, u32[]{:S(2)}) %collective-permute-start) | collective-permute-done | bytes 311328 | tf_op jit(solution)/shard_map/ppermute | solution.py:60
  19.3 4.3 %collective-permute-done.1.refs_1_.refs_6_ = f32[19,8,512]{2,1,0:T(8,128)S(1)} collective-permute-done((f32[19,8,512]{2,1,0:T(8,128)S(1)}, f32[19,8,512]{2,1,0:T(8,128)S(1)}, u32[]{:S(2)}, u32[]{:S(2)}) %collective-permute-start.1) | collective-permute-done | bytes 311328 | tf_op jit(solution)/shard_map/ppermute | solution.py:60
  23.8 2.6 %collective-permute-start.3 = (f32[10,8,512]{2,1,0:T(8,128)S(1)}, f32[10,8,512]{2,1,0:T(8,128)S(1)}, u32[]{:S(2)}, u32[]{:S(2)}) collective-permute-start(f32[10,8,512]{2,1,0:T(8,128)S(1)} %get-tuple-element.45), channel_id=1, source_target_pairs={{0,28},{4,0},{8,4},{12,8},{16,12},{20,16},{24,20},{28,24},{1,29},{... | collective-permute-start | bytes 491528 | tf_op jit(solution)/shard_map/ppermute | solution.py:58
  26.4 1.0 %shard_map.57 = (f32[7,16,24,512]{3,2,1,0:T(8,128)S(1)}, f32[3,12,16,256]{3,2,1,0:T(8,128)S(1)}) custom-call(f32[8,16,512]{2,1,0:T(8,128)S(1)} %get-tuple-element.47.refs_0_, bf16[3,8,16,512]{3,2,1,0:T(8,128)(2,1)S(1)} %get-tuple-element.48.refs_1_, f32[3,4,8,256]{3,2,1,0:T(8,128)S(1)} %get-tuple-element.49.refs_2_.refs_0_, ...), custom_call_target="tpu_custom_call" | custom-call | tf_op jit(solution)/shard_map/pallas_call | solution.py:45
  27.4 2.9 %collective-permute-done.2.refs_0_ = f32[10,8,512]{2,1,0:T(8,128)S(1)} collective-permute-done((f32[10,8,512]{2,1,0:T(8,128)S(1)}, f32[10,8,512]{2,1,0:T(8,128)S(1)}, u32[]{:S(2)}, u32[]{:S(2)}) %collective-permute-start.2) | collective-permute-done | bytes 163872 | tf_op jit(solution)/shard_map/ppermute | solution.py:58
  30.3 3.1 %shard_map.58 = (f32[5,16,24,512]{3,2,1,0:T(8,128)S(1)}, f32[3,12,16,256]{3,2,1,0:T(8,128)S(1)}, f32[8,16,512]{2,1,0:T(8,128)S(1)}, f32[4,8,256]{2,1,0:T(8,128)S...) custom-call(f32[10,8,512]{2,1,0:T(8,128)S(1)} %collective-permute-do, ...), custom_call_target="tpu_custom_call" | custom-call | tf_op jit(solution)/shard_map/pallas_call | solution.py:45
  33.5 1.2 %collective-permute-start.6 = (f32[2,8,256]{2,1,0:T(8,128)S(1)}, f32[2,8,256]{2,1,0:T(8,128)S(1)}, u32[]{:S(2)}, u32[]{:S(2)}) collective-permute-start(f32[2,8,256]{2,1,0:T(8,128)S(1)} %get-tuple-element.55), channel_id=1, source_target_pairs={{0,1},{1,2},{2,3},{3,0},{4,5},{5,6},{6,7},{7,4},{8,9},{9,10},{10,1... | collective-permute-start | bytes 49160 | tf_op jit(solution)/shard_map/ppermute | solution.py:60
  34.7 2.7 %collective-permute-start.7 = (f32[2,8,256]{2,1,0:T(8,128)S(1)}, f32[2,8,256]{2,1,0:T(8,128)S(1)}, u32[]{:S(2)}, u32[]{:S(2)}) collective-permute-start(f32[2,8,256]{2,1,0:T(8,128)S(1)} %get-tuple-element.56), channel_id=1, source_target_pairs={{0,3},{1,0},{2,1},{3,2},{4,7},{5,4},{6,5},{7,6},{8,11},{9,8},{10,9... | collective-permute-start | bytes 49160 | tf_op jit(solution)/shard_map/ppermute | solution.py:60
  37.4 1.9 %collective-permute-done.6.refs_1_ = f32[2,8,256]{2,1,0:T(8,128)S(1)} collective-permute-done((f32[2,8,256]{2,1,0:T(8,128)S(1)}, f32[2,8,256]{2,1,0:T(8,128)S(1)}, u32[]{:S(2)}, u32[]{:S(2)}) %collective-permute-start.6) | collective-permute-done | bytes 16416 | tf_op jit(solution)/shard_map/ppermute | solution.py:60
  39.3 2.6 %collective-permute-start.9 = (f32[4,16,256]{2,1,0:T(8,128)S(1)}, f32[4,16,256]{2,1,0:T(8,128)S(1)}, u32[]{:S(2)}, u32[]{:S(2)}) collective-permute-start(f32[4,16,256]{2,1,0:T(8,128)S(1)} %get-tuple-element.61), channel_id=1, source_target_pairs={{0,28},{4,0},{8,4},{12,8},{16,12},{20,16},{24,20},{28,24},{1,29},{... | collective-permute-start | bytes 196616 | tf_op jit(solution)/shard_map/ppermute | solution.py:58
  41.9 2.3 %collective-permute-done.8.refs_1_ = f32[4,16,256]{2,1,0:T(8,128)S(1)} collective-permute-done((f32[4,16,256]{2,1,0:T(8,128)S(1)}, f32[4,16,256]{2,1,0:T(8,128)S(1)}, u32[]{:S(2)}, u32[]{:S(2)}) %collective-permute-start.8) | collective-permute-done | bytes 65568 | tf_op jit(solution)/shard_map/ppermute | solution.py:58
  44.7 3.8 %collective-permute-start.11 = (f32[3,8,512]{2,1,0:T(8,128)S(1)}, f32[3,8,512]{2,1,0:T(8,128)S(1)}, u32[]{:S(2)}, u32[]{:S(2)}) collective-permute-start(f32[3,8,512]{2,1,0:T(8,128)S(1)} %get-tuple-element.67), channel_id=1, source_target_pairs={{0,3},{1,0},{2,1},{3,2},{4,7},{5,4},{6,5},{7,6},{8,11},{9,8},{10,9... | collective-permute-start | bytes 147464 | tf_op jit(solution)/shard_map/ppermute | solution.py:60
  48.7 1.9 %collective-permute-done.10.refs_1_.refs_4_ = f32[3,8,512]{2,1,0:T(8,128)S(1)} collective-permute-done((f32[3,8,512]{2,1,0:T(8,128)S(1)}, f32[3,8,512]{2,1,0:T(8,128)S(1)}, u32[]{:S(2)}, u32[]{:S(2)}) %collective-permute-start.10) | collective-permute-done | bytes 49184 | tf_op jit(solution)/shard_map/ppermute | solution.py:60
  50.6 1.0 %shard_map.64 = f32[32,9,128]{2,1,0:T(8,128)} custom-call(f32[6,12,16,256]{3,2,1,0:T(8,128)S(1)} %get-tuple-element.65.refs_0_.refs_4_, f32[12,16,256]{2,1,0:T(8,128)S(1)} %get-tuple-element.72.refs_1_, bf16[256,128]{1,0:T(8,128)(2,1)S(1)} %copy-done.6, f32[8,128]{1,0:T(8,128)S(1)} %shard_map.63.refs_3_, ...), custom_call_target="tpu_custom_call" | custom-call | tf_op jit(solution)/shard_map/pallas_call | solution.py:45
  51.6 5.2 %all-to-all-start = ((f32[32,9,128]{2,1,0:T(8,128)}), f32[32,9,128]{2,1,0:T(8,128)S(1)}, u32[]{:S(2)}, u32[]{:S(2)}) async-start(f32[32,9,128]{2,1,0:T(8,128)} %shard_map.64), calls=%async_computation | async-start | bytes 524288 | tf_op jit(solution)/shard_map/all_to_all | solution.py:626
  56.8 0.8 %shard_map.61 = (f32[10,24,512]{2,1,0:T(8,128)S(1)}, f32[10,8,512]{2,1,0:T(8,128)}, f32[10,8,512]{2,1,0:T(8,128)}) custom-call(f32[6,12,16,256]{3,2,1,0:T(8,128)S(1)} %get-tuple-element.65.refs_0_.refs_4_, f32[3,8,512]{2,1,0:T(8,128)S(1)} %collective-permute-done.10.refs_1_.refs_4_, f32[3,8,512]{2,1,0:T(8,128)S(1)} %collective-permute-done.11.refs_2_.refs_5_, ...), custom_call_target="tpu_custom_call" | custom-call | tf_op jit(solution)/shard_map/pallas_call | solution.py:45
  57.9 2.4 %collective-permute-start.13 = (f32[10,8,512]{2,1,0:T(8,128)}, f32[10,8,512]{2,1,0:T(8,128)S(1)}, u32[]{:S(2)}, u32[]{:S(2)}) collective-permute-start(f32[10,8,512]{2,1,0:T(8,128)} %get-tuple-element.71), channel_id=1, source_target_pairs={{0,28},{4,0},{8,4},{12,8},{16,12},{20,16},{24,20},{28,24},{1,29},{... | collective-permute-start | bytes 491528 | tf_op jit(solution)/shard_map/ppermute | solution.py:58
  60.2 6.7 %all-to-all-done.refs_0_ = f32[32,9,128]{2,1,0:T(8,128)S(1)} async-done(((f32[32,9,128]{2,1,0:T(8,128)}), f32[32,9,128]{2,1,0:T(8,128)S(1)}, u32[]{:S(2)}, u32[]{:S(2)}) %all-to-all-start) | async-done | bytes 147488 | tf_op jit(solution)/shard_map/all_to_all | solution.py:626
  67.0 1.0 %shard_map.65.refs_3_ = f32[12,16,256]{2,1,0:T(8,128)S(1)} custom-call(f32[32,9,128]{2,1,0:T(8,128)S(1)} %all-to-all-done.refs_0_, f32[960,256]{1,0:T(8,128)S(1)} %copy-done.2), custom_call_target="tpu_custom_call" | custom-call | tf_op jit(solution)/shard_map/pallas_call | solution.py:45
  68.5 1.2 %collective-permute-start.14 = (f32[1,8,256]{2,1,0:T(8,128)S(1)}, f32[1,8,256]{2,1,0:T(8,128)S(1)}, u32[]{:S(2)}, u32[]{:S(2)}) collective-permute-start(f32[1,8,256]{2,1,0:T(8,128)S(1)} %get-tuple-element.74), channel_id=1, source_target_pairs={{0,1},{1,2},{2,3},{3,0},{4,5},{5,6},{6,7},{7,4},{8,9},{9,10},{10,1... | collective-permute-start | bytes 24584 | tf_op jit(solution)/shard_map/ppermute | solution.py:60
  69.6 2.8 %collective-permute-start.15 = (f32[1,8,256]{2,1,0:T(8,128)S(1)}, f32[1,8,256]{2,1,0:T(8,128)S(1)}, u32[]{:S(2)}, u32[]{:S(2)}) collective-permute-start(f32[1,8,256]{2,1,0:T(8,128)S(1)} %get-tuple-element.75), channel_id=1, source_target_pairs={{0,3},{1,0},{2,1},{3,2},{4,7},{5,4},{6,5},{7,6},{8,11},{9,8},{10,9... | collective-permute-start | bytes 24584 | tf_op jit(solution)/shard_map/ppermute | solution.py:60
  72.4 1.6 %collective-permute-done.14.refs_1_ = f32[1,8,256]{2,1,0:T(8,128)S(1)} collective-permute-done((f32[1,8,256]{2,1,0:T(8,128)S(1)}, f32[1,8,256]{2,1,0:T(8,128)S(1)}, u32[]{:S(2)}, u32[]{:S(2)}) %collective-permute-start.14) | collective-permute-done | bytes 8224 | tf_op jit(solution)/shard_map/ppermute | solution.py:60
  74.1 2.6 %collective-permute-start.17 = (f32[2,16,256]{2,1,0:T(8,128)S(1)}, f32[2,16,256]{2,1,0:T(8,128)S(1)}, u32[]{:S(2)}, u32[]{:S(2)}) collective-permute-start(f32[2,16,256]{2,1,0:T(8,128)S(1)} %get-tuple-element.78), channel_id=1, source_target_pairs={{0,28},{4,0},{8,4},{12,8},{16,12},{20,16},{24,20},{28,24},{1,29},{... | collective-permute-start | bytes 98312 | tf_op jit(solution)/shard_map/ppermute | solution.py:58
  76.8 1.5 %collective-permute-done.16.refs_2_ = f32[2,16,256]{2,1,0:T(8,128)S(1)} collective-permute-done((f32[2,16,256]{2,1,0:T(8,128)S(1)}, f32[2,16,256]{2,1,0:T(8,128)S(1)}, u32[]{:S(2)}, u32[]{:S(2)}) %collective-permute-start.16) | collective-permute-done | bytes 32800 | tf_op jit(solution)/shard_map/ppermute | solution.py:58
  78.3 3.5 %shard_map.68 = f32[8,16,512]{2,1,0:T(8,128)} custom-call(f32[16,24,512]{2,1,0:T(8,128)S(1)} %shard_map.62.refs_0_, f32[4,16,256]{2,1,0:T(8,128)S(1)} %get-tuple-element.76.refs_1_, f32[2,16,256]{2,1,0:T(8,128)S(1)} %collective-permute-done.16.refs_2_, f32[2,16,256]{2,1,0:T(8,128)S(1)} %collective-permute-done.17.refs_3_, f32[5,16,24,512]{3,2,1,0:T(8,128)S(1)} %copy-done.1, ...), custom_call_target="tpu_custom_call" | custom-call | tf_op jit(solution)/shard_map/pallas_call | solution.py:45
  (34 shorter events, 1.7 us)
Async XLA Ops:
  0.0 1.0 %copy-start.3 = (bf16[3,8,16,512]{3,2,1,0:T(8,128)(2,1)S(1)}, bf16[3,8,16,512]{3,2,1,0:T(8,128)(2,1)}, u32[]{:S(2)}) copy-start(bf16[3,8,16,512]{3,2,1,0:T(8,128)(2,1)} %refs_1_.2) | copy-start | bytes 1179652
  1.0 0.9 %copy-start.4 = (f32[8,16,512]{2,1,0:T(8,128)S(1)}, f32[8,16,512]{2,1,0:T(8,128)}, u32[]{:S(2)}) copy-start(f32[8,16,512]{2,1,0:T(8,128)} %refs_0_.1) | copy-start | bytes 786436
  3.3 23.1 %collective-permute-start.4 = (f32[38,8,512]{2,1,0:T(8,128)S(1)}, f32[38,8,512]{2,1,0:T(8,128)S(1)}, u32[]{:S(2)}, u32[]{:S(2)}) collective-permute-start(f32[38,8,512]{2,1,0:T(8,128)S(1)} %get-tuple-element.50), channel_id=1, source_target_pairs={{0,4},{4,8},{8,12},{12,16},{16,20},{20,24},{24,28},{28,0},{1,5},{5... | collective-permute-start | bytes 1867784 | tf_op jit(solution)/shard_map/ppermute | solution.py:58
  3.8 22.6 %collective-permute-start.5 = (f32[38,8,512]{2,1,0:T(8,128)S(1)}, f32[38,8,512]{2,1,0:T(8,128)S(1)}, u32[]{:S(2)}, u32[]{:S(2)}) collective-permute-start(f32[38,8,512]{2,1,0:T(8,128)S(1)} %get-tuple-element.51), channel_id=1, source_target_pairs={{0,28},{4,0},{8,4},{12,8},{16,12},{20,16},{24,20},{28,24},{1,29},{... | collective-permute-start | bytes 1867784 | tf_op jit(solution)/shard_map/ppermute | solution.py:58
  6.7 12.6 %collective-permute-start = (f32[19,8,512]{2,1,0:T(8,128)S(1)}, f32[19,8,512]{2,1,0:T(8,128)S(1)}, u32[]{:S(2)}, u32[]{:S(2)}) collective-permute-start(f32[19,8,512]{2,1,0:T(8,128)S(1)} %get-tuple-element.42), channel_id=1, source_target_pairs={{0,1},{1,2},{2,3},{3,0},{4,5},{5,6},{6,7},{7,4},{8,9},{9,10},{10,1... | collective-permute-start | bytes 933896 | tf_op jit(solution)/shard_map/ppermute | solution.py:60
  9.0 14.6 %collective-permute-start.1 = (f32[19,8,512]{2,1,0:T(8,128)S(1)}, f32[19,8,512]{2,1,0:T(8,128)S(1)}, u32[]{:S(2)}, u32[]{:S(2)}) collective-permute-start(f32[19,8,512]{2,1,0:T(8,128)S(1)} %get-tuple-element.43), channel_id=1, source_target_pairs={{0,3},{1,0},{2,1},{3,2},{4,7},{5,4},{6,5},{7,6},{8,11},{9,8},{10,9... | collective-permute-start | bytes 933896 | tf_op jit(solution)/shard_map/ppermute | solution.py:60
  23.7 6.6 %collective-permute-start.2 = (f32[10,8,512]{2,1,0:T(8,128)S(1)}, f32[10,8,512]{2,1,0:T(8,128)S(1)}, u32[]{:S(2)}, u32[]{:S(2)}) collective-permute-start(f32[10,8,512]{2,1,0:T(8,128)S(1)} %get-tuple-element.44), channel_id=1, source_target_pairs={{0,4},{4,8},{8,12},{12,16},{16,20},{20,24},{24,28},{28,0},{1,5},{5... | collective-permute-start | bytes 491528 | tf_op jit(solution)/shard_map/ppermute | solution.py:58
  23.8 6.6 %collective-permute-start.3 = (f32[10,8,512]{2,1,0:T(8,128)S(1)}, f32[10,8,512]{2,1,0:T(8,128)S(1)}, u32[]{:S(2)}, u32[]{:S(2)}) collective-permute-start(f32[10,8,512]{2,1,0:T(8,128)S(1)} %get-tuple-element.45), channel_id=1, source_target_pairs={{0,28},{4,0},{8,4},{12,8},{16,12},{20,16},{24,20},{28,24},{1,29},{... | collective-permute-start | bytes 491528 | tf_op jit(solution)/shard_map/ppermute | solution.py:58
  33.5 11.1 %copy-start = (f32[5,16,24,512]{3,2,1,0:T(8,128)}, f32[5,16,24,512]{3,2,1,0:T(8,128)S(1)}, u32[]{:S(2)}) copy-start(f32[5,16,24,512]{3,2,1,0:T(8,128)S(1)} %get-tuple-element.58.refs_4_.refs_7_) | copy-start | bytes 11796484
  33.5 5.7 %collective-permute-start.6 = (f32[2,8,256]{2,1,0:T(8,128)S(1)}, f32[2,8,256]{2,1,0:T(8,128)S(1)}, u32[]{:S(2)}, u32[]{:S(2)}) collective-permute-start(f32[2,8,256]{2,1,0:T(8,128)S(1)} %get-tuple-element.55), channel_id=1, source_target_pairs={{0,1},{1,2},{2,3},{3,0},{4,5},{5,6},{6,7},{7,4},{8,9},{9,10},{10,1... | collective-permute-start | bytes 49160 | tf_op jit(solution)/shard_map/ppermute | solution.py:60
  34.7 4.6 %collective-permute-start.7 = (f32[2,8,256]{2,1,0:T(8,128)S(1)}, f32[2,8,256]{2,1,0:T(8,128)S(1)}, u32[]{:S(2)}, u32[]{:S(2)}) collective-permute-start(f32[2,8,256]{2,1,0:T(8,128)S(1)} %get-tuple-element.56), channel_id=1, source_target_pairs={{0,3},{1,0},{2,1},{3,2},{4,7},{5,4},{6,5},{7,6},{8,11},{9,8},{10,9... | collective-permute-start | bytes 49160 | tf_op jit(solution)/shard_map/ppermute | solution.py:60
  39.2 11.4 %copy-start.6 = (bf16[256,128]{1,0:T(8,128)(2,1)S(1)}, bf16[256,128]{1,0:T(8,128)(2,1)}, u32[]{:S(2)}) copy-start(bf16[256,128]{1,0:T(8,128)(2,1)} %constant.6.clone.refs_2_) | copy-start | bytes 196612
  39.3 5.0 %collective-permute-start.8 = (f32[4,16,256]{2,1,0:T(8,128)S(1)}, f32[4,16,256]{2,1,0:T(8,128)S(1)}, u32[]{:S(2)}, u32[]{:S(2)}) collective-permute-start(f32[4,16,256]{2,1,0:T(8,128)S(1)} %get-tuple-element.60), channel_id=1, source_target_pairs={{0,4},{4,8},{8,12},{12,16},{16,20},{20,24},{24,28},{28,0},{1,5},{5... | collective-permute-start | bytes 196616 | tf_op jit(solution)/shard_map/ppermute | solution.py:58
  39.3 4.9 %collective-permute-start.9 = (f32[4,16,256]{2,1,0:T(8,128)S(1)}, f32[4,16,256]{2,1,0:T(8,128)S(1)}, u32[]{:S(2)}, u32[]{:S(2)}) collective-permute-start(f32[4,16,256]{2,1,0:T(8,128)S(1)} %get-tuple-element.61), channel_id=1, source_target_pairs={{0,28},{4,0},{8,4},{12,8},{16,12},{20,16},{24,20},{28,24},{1,29},{... | collective-permute-start | bytes 196616 | tf_op jit(solution)/shard_map/ppermute | solution.py:58
  44.2 22.7 %copy-start.2 = (f32[960,256]{1,0:T(8,128)S(1)}, f32[960,256]{1,0:T(8,128)}, u32[]{:S(2)}) copy-start(f32[960,256]{1,0:T(8,128)} %constant.7.clone.refs_1_) | copy-start | bytes 2949124
  44.6 6.0 %collective-permute-start.10 = (f32[3,8,512]{2,1,0:T(8,128)S(1)}, f32[3,8,512]{2,1,0:T(8,128)S(1)}, u32[]{:S(2)}, u32[]{:S(2)}) collective-permute-start(f32[3,8,512]{2,1,0:T(8,128)S(1)} %get-tuple-element.66), channel_id=1, source_target_pairs={{0,1},{1,2},{2,3},{3,0},{4,5},{5,6},{6,7},{7,4},{8,9},{9,10},{10,1... | collective-permute-start | bytes 147464 | tf_op jit(solution)/shard_map/ppermute | solution.py:60
  44.7 5.9 %collective-permute-start.11 = (f32[3,8,512]{2,1,0:T(8,128)S(1)}, f32[3,8,512]{2,1,0:T(8,128)S(1)}, u32[]{:S(2)}, u32[]{:S(2)}) collective-permute-start(f32[3,8,512]{2,1,0:T(8,128)S(1)} %get-tuple-element.67), channel_id=1, source_target_pairs={{0,3},{1,0},{2,1},{3,2},{4,7},{5,4},{6,5},{7,6},{8,11},{9,8},{10,9... | collective-permute-start | bytes 147464 | tf_op jit(solution)/shard_map/ppermute | solution.py:60
  51.6 26.7 %copy-start.5 = (bf16[256,512]{1,0:T(8,128)(2,1)S(1)}, bf16[256,512]{1,0:T(8,128)(2,1)}, u32[]{:S(2)}) copy-start(bf16[256,512]{1,0:T(8,128)(2,1)} %constant.8.clone.refs_5_) | copy-start | bytes 786436
  51.6 15.4 %all-to-all-start = ((f32[32,9,128]{2,1,0:T(8,128)}), f32[32,9,128]{2,1,0:T(8,128)S(1)}, u32[]{:S(2)}, u32[]{:S(2)}) async-start(f32[32,9,128]{2,1,0:T(8,128)} %shard_map.64), calls=%async_computation | async-start | bytes 524288 | tf_op jit(solution)/shard_map/all_to_all | solution.py:626
  57.6 10.4 %collective-permute-start.12 = (f32[10,8,512]{2,1,0:T(8,128)}, f32[10,8,512]{2,1,0:T(8,128)S(1)}, u32[]{:S(2)}, u32[]{:S(2)}) collective-permute-start(f32[10,8,512]{2,1,0:T(8,128)} %get-tuple-element.70), channel_id=1, source_target_pairs={{0,4},{4,8},{8,12},{12,16},{16,20},{20,24},{24,28},{28,0},{1,5},{5... | collective-permute-start | bytes 491528 | tf_op jit(solution)/shard_map/ppermute | solution.py:58
  57.9 10.2 %collective-permute-start.13 = (f32[10,8,512]{2,1,0:T(8,128)}, f32[10,8,512]{2,1,0:T(8,128)S(1)}, u32[]{:S(2)}, u32[]{:S(2)}) collective-permute-start(f32[10,8,512]{2,1,0:T(8,128)} %get-tuple-element.71), channel_id=1, source_target_pairs={{0,28},{4,0},{8,4},{12,8},{16,12},{20,16},{24,20},{28,24},{1,29},{... | collective-permute-start | bytes 491528 | tf_op jit(solution)/shard_map/ppermute | solution.py:58
  67.0 11.4 %copy-start.1 = (f32[5,16,24,512]{3,2,1,0:T(8,128)S(1)}, f32[5,16,24,512]{3,2,1,0:T(8,128)}, u32[]{:S(2)}) copy-start(f32[5,16,24,512]{3,2,1,0:T(8,128)} %copy-done) | copy-start | bytes 11796484
  68.5 5.5 %collective-permute-start.14 = (f32[1,8,256]{2,1,0:T(8,128)S(1)}, f32[1,8,256]{2,1,0:T(8,128)S(1)}, u32[]{:S(2)}, u32[]{:S(2)}) collective-permute-start(f32[1,8,256]{2,1,0:T(8,128)S(1)} %get-tuple-element.74), channel_id=1, source_target_pairs={{0,1},{1,2},{2,3},{3,0},{4,5},{5,6},{6,7},{7,4},{8,9},{9,10},{10,1... | collective-permute-start | bytes 24584 | tf_op jit(solution)/shard_map/ppermute | solution.py:60
  69.6 4.4 %collective-permute-start.15 = (f32[1,8,256]{2,1,0:T(8,128)S(1)}, f32[1,8,256]{2,1,0:T(8,128)S(1)}, u32[]{:S(2)}, u32[]{:S(2)}) collective-permute-start(f32[1,8,256]{2,1,0:T(8,128)S(1)} %get-tuple-element.75), channel_id=1, source_target_pairs={{0,3},{1,0},{2,1},{3,2},{4,7},{5,4},{6,5},{7,6},{8,11},{9,8},{10,9... | collective-permute-start | bytes 24584 | tf_op jit(solution)/shard_map/ppermute | solution.py:60
  74.0 4.3 %collective-permute-start.16 = (f32[2,16,256]{2,1,0:T(8,128)S(1)}, f32[2,16,256]{2,1,0:T(8,128)S(1)}, u32[]{:S(2)}, u32[]{:S(2)}) collective-permute-start(f32[2,16,256]{2,1,0:T(8,128)S(1)} %get-tuple-element.77), channel_id=1, source_target_pairs={{0,4},{4,8},{8,12},{12,16},{16,20},{20,24},{24,28},{28,0},{1,5},{5... | collective-permute-start | bytes 98312 | tf_op jit(solution)/shard_map/ppermute | solution.py:58
  74.1 4.2 %collective-permute-start.17 = (f32[2,16,256]{2,1,0:T(8,128)S(1)}, f32[2,16,256]{2,1,0:T(8,128)S(1)}, u32[]{:S(2)}, u32[]{:S(2)}) collective-permute-start(f32[2,16,256]{2,1,0:T(8,128)S(1)} %get-tuple-element.78), channel_id=1, source_target_pairs={{0,28},{4,0},{8,4},{12,8},{16,12},{20,16},{24,20},{28,24},{1,29},{... | collective-permute-start | bytes 98312 | tf_op jit(solution)/shard_map/ppermute | solution.py:58

commit v4 on v2

v4 whole, which is shorter than its diff:
```python
import functools
import math

import jax
import jax.numpy as jnp
import ml_dtypes
import numpy as np
from jax import lax
from jax.experimental import pallas as pl
from jax.experimental.pallas import tpu as pltpu
from jax.sharding import PartitionSpec as P

LEVELS = 3
SWEEPS = 2
MASS = 0.002
BOTH = ("gx", "gy")
H = 2 * SWEEPS
F32 = jnp.float32
UNROLL = 4
VMEM_LIMIT = 12 * 1024 * 1024
BF16 = jnp.bfloat16
VMEM = pl.BlockSpec(memory_space=pltpu.VMEM)
HBM = pl.BlockSpec(memory_space=pltpu.HBM)

CORNER0 = (
    (0, 1, 1), (0, 1, 2), (0, 1, 3), (1, 2, 3), (3, 1, 1), (3, 1, 2), (3, 1, 3), (2, 2, 3),
    (1, 1, 1), (1, 1, 2), (1, 1, 3), (1, 1, 4), (2, 1, 1), (2, 1, 2), (2, 1, 3), (2, 1, 4),
    (0, 2, 1), (0, 2, 2), (0, 3, 1), (1, 4, 1), (3, 2, 1), (3, 2, 2), (3, 3, 1), (2, 4, 1),
    (1, 2, 1), (1, 2, 2), (1, 3, 1), (1, 3, 2), (2, 2, 1), (2, 2, 2), (2, 3, 1), (2, 3, 2),
)

def call(kernel, out, *args, scratch=(), remote=(), limit=VMEM_LIMIT, near=()):
    count = len(args)
    args = (*args, *near)

    def body(*refs):
        kernel(*refs[:count], *refs[len(args) :])

    return pl.pallas_call(
        body,
        out_shape=[s if hasattr(s, "dtype") else jax.ShapeDtypeStruct(s, F32) for s in out],
        in_specs=[HBM if i in remote else VMEM for i in range(len(args))],
        out_specs=[VMEM] * len(out),
        scratch_shapes=[pltpu.VMEM(s, F32) if isinstance(s, tuple) else s for s in scratch],
        compiler_params=pltpu.CompilerParams(vmem_limit_bytes=limit),
    )(*args)


def moved(block, dx, dy):
    nx, ny = lax.axis_size("gx"), lax.axis_size("gy")
    if dy == 0:
        return lax.ppermute(block, "gx", [(i, (i + dx) % nx) for i in range(nx)])
    if dx == 0:
        return lax.ppermute(block, "gy", [(j, (j + dy) % ny) for j in range(ny)])
    route = []
    for i in range(nx):
        for j in range(ny):
            route.append((i * ny + j, ((i + dx) % nx) * ny + (j + dy) % ny))
    return lax.ppermute(block, BOTH, route)


def split3(x):
    high = x.astype(BF16)
    rest = x - high.astype(F32)
    middle = rest.astype(BF16)
    return high, middle, (rest - middle.astype(F32)).astype(BF16)


def dot(a, b):
    return jnp.dot(a, b, preferred_element_type=F32)


def dot_exact(x, table):
    high, middle, low = split3(x)
    return dot(high, table) + (dot(middle, table) + dot(low, table))


def pair_table(depth):
    table = np.zeros((depth, depth // 2), ml_dtypes.bfloat16)
    table[np.arange(depth), np.arange(depth) // 2] = 1
    return table


def put_tiles(tiles, x):
    for k in range(tiles.shape[0]):
        tiles[k] = x[:, 128 * k : 128 * k + 128]


def every_other(tiles, start, size):
    return jnp.concatenate(
        [tiles[k, pl.ds(start, size, stride=2), :] for k in range(tiles.shape[0])], axis=1
    )


def back(x, axis):
    return pltpu.roll(x, 1, axis)


def ahead(x, axis):
    return pltpu.roll(x, x.shape[axis] - 1, axis)


def parity2(shape):
    return (lax.broadcasted_iota(jnp.int32, shape, 0) + lax.broadcasted_iota(jnp.int32, shape, 1)) & 1


def row_sum(r, v, wx, wy, wz):
    centre = v[r]
    y, z = wy[r], wz[r]
    total = wx[r] * v[r + 1] + wx[r - 1] * v[r - 1]
    total = total + y * ahead(centre, 0) + back(y * centre, 0)
    return centre, total + z * ahead(centre, 1) + back(z * centre, 1)


def half_sweep(first, last, colour, parity, v, b, wx, wy, wz, rdiag):
    unroll = UNROLL if v.shape[-1] > 256 else last - first

    def body(r, carry):
        centre, total = row_sum(r, v, wx, wy, wz)
        mine = parity == ((r + colour) & 1)
        v[r] = jnp.where(mine, (b[r] + total) * rdiag[r], centre)
        return carry

    lax.fori_loop(first, last, body, 0, unroll=unroll)


def pack_kernel(src_in, face_in, to_right, to_left, to_up, to_down, w1, src, face, pairs, *scratch):
    odds, tx, sem = scratch
    rows, cols, depth = src.shape
    copies = [pltpu.make_async_copy(src_in, src, sem.at[0]), pltpu.make_async_copy(face_in, face, sem.at[1])]
    for copy in copies:
        copy.start()
    fine = lax.broadcasted_iota(jnp.int32, pairs.shape, 0)
    coarse = 2 * lax.broadcasted_iota(jnp.int32, pairs.shape, 1)
    pairs[...] = jnp.where((fine & -2) == coarse, 1.0, 0.0).astype(BF16)
    odds[...] = jnp.where(fine == coarse + 1, 1.0, 0.0).astype(BF16)
    for copy in copies:
        copy.wait()

    for i in range(rows // 2):
        put_tiles(tx, dot(face[0, 2 * i + 1], pairs[...]))
        w1[0, i] = 0.0625 * (every_other(tx, 0, cols // 2) + every_other(tx, 1, cols // 2))
        put_tiles(tx, dot(face[1, 2 * i], pairs[...]) + dot(face[1, 2 * i + 1], pairs[...]))
        w1[1, i] = 0.0625 * every_other(tx, 1, cols // 2)
        put_tiles(tx, dot(face[2, 2 * i], odds[...]) + dot(face[2, 2 * i + 1], odds[...]))
        w1[2, i] = 0.0625 * (every_other(tx, 0, cols // 2) + every_other(tx, 1, cols // 2))

    def plane(a, r):
        return src[r] if a == 0 else face[a - 1, r].astype(F32)

    for out, base in ((to_right, cols - H), (to_left, 0)):
        for r in range(rows):
            for t, pair in enumerate(((0, 3), (1, 2))):
                for s, a in enumerate(pair):
                    value = plane(a, r)
                    if out is to_right and a == 3:
                        value_all = value + back(value, 1) + back(plane(2, r), 0)
                        first = lax.broadcasted_iota(jnp.int32, value.shape, 0) == base
                        value = jnp.where(first, value_all, value)
                    out[2 * r + t, H * s : H * s + H] = value[base : base + H]

    tiles = cols // 8
    for out, base in ((to_up, rows - H), (to_down, 0)):
        for a in range(4):
            for k in range(H):
                value = plane(a, base + k)
                if out is to_up and a == 3 and k == 0:
                    value = value + back(value, 1) + plane(1, base - 1)
                for t in range(tiles):
                    out[(a * H + k) * tiles + t] = value[8 * t : 8 * t + 8]
    last = w1[0, rows // 2 - 1]
    to_up[4 * H * tiles] = jnp.concatenate((last, last), axis=1)


def forward_kernel(right, left, to_up, to_down, *, rows):
    tiles = to_up.shape[0] // 2
    place = {0: (0, 0), 3: (0, 1), 1: (1, 0), 2: (1, 1)}
    for msg, sy in ((right, 1), (left, -1)):
        start = 0 if sy > 0 else tiles
        for out, sx in ((to_up, 1), (to_down, -1)):
            for n, (a, dx, dy) in enumerate(CORNER0):
                r = rows - dx if sx > 0 else dx - 1
                t, s = place[a]
                s = H * s + (H - dy if sy > 0 else dy - 1)
                out[start + n // 8, n % 8 : n % 8 + 1] = msg[2 * r + t, s : s + 1]


def diagonal_row(r, parity, low_col, b, wx, wy, wz, diag, rdiag, v):
    y, z = wy[r], wz[r]
    if isinstance(r, int) and r == 0:
        total = MASS + wx[r] + z + y + back(y, 0)
    else:
        total = MASS + wx[r] + wx[r - 1] + y
        total = total + jnp.where(low_col, z, z + back(z, 1) + back(y, 0))
    diag[r] = total
    inverse = 1.0 / total
    rdiag[r] = inverse
    v[r] = jnp.where(parity == (r & 1), b[r] * inverse, 0.0)


def assemble_kernel(src, face, up, down, right, left, state):
    b, wx, wy, wz, rdiag, diag, v = (state.at[i] for i in range(7))
    rows, cols, depth = src.shape
    ext = (b, wx, wy, wz)
    ec = cols + 2 * H
    for r in range(rows):
        b[H + r, H : H + cols] = src[r]
        for d in range(3):
            ext[1 + d][H + r, H : H + cols] = face[d, r].astype(F32)
    tiles = cols // 8
    for msg, base in ((up, 0), (down, H + rows)):
        for a in range(4):
            for k in range(H):
                for t in range(tiles):
                    ext[a][base + k, H + 8 * t : H + 8 * t + 8] = msg[(a * H + k) * tiles + t]
    for msg, base in ((right, 0), (left, H + cols)):
        for r in range(rows):
            for t, pair in enumerate(((0, 3), (1, 2))):
                for s, a in enumerate(pair):
                    ext[a][H + r, base : base + H] = msg[2 * r + t, H * s : H * s + H]
    parity = parity2((ec, depth))
    low_col = lax.broadcasted_iota(jnp.int32, (ec, depth), 0) == 0

    def body(r, carry):
        diagonal_row(r, parity, low_col, b, wx, wy, wz, diag, rdiag, v)
        return carry

    lax.fori_loop(H + 1, H + rows, body, 0)


def pre_kernel(up, down, pairs, state, kept, v_own, right1, to_right, to_left, *scratch):
    t512, t256, diag, v = scratch
    b, wx, wy, wz, rdiag = (kept.at[i] for i in range(5))
    kept[...] = state[0:5]
    diag[...] = state[5]
    v[...] = state[6]
    ext = (b, wx, wy, wz)
    rows, cols, depth = v_own.shape
    er, ec = rows + 2 * H, cols + 2 * H
    rows1, cols1 = rows // 2, cols // 2
    tiles = len(CORNER0) // 8
    for msg, sx, sy in ((up, 1, 1), (up, 1, -1), (down, -1, 1), (down, -1, -1)):
        start = 0 if sy > 0 else tiles

        def at(distance, size, sign):
            return H - distance if sign > 0 else H + size + distance - 1

        for n, (a, dx, dy) in enumerate(CORNER0):
            r, c = at(dx, rows, sx), at(dy, cols, sy)
            ext[a][r, c : c + 1] = msg[start + n // 8, n % 8 : n % 8 + 1]
    parity = parity2((ec, depth))
    low_col = lax.broadcasted_iota(jnp.int32, (ec, depth), 0) == 0
    for r in (*range(H + 1), *range(H + rows, er)):
        diagonal_row(r, parity, low_col, b, wx, wy, wz, diag, rdiag, v)
    half_sweep(1, er - 1, 1, parity, v, b, wx, wy, wz, rdiag)
    half_sweep(2, er - 2, 0, parity, v, b, wx, wy, wz, rdiag)
    half_sweep(3, er - 3, 1, parity, v, b, wx, wy, wz, rdiag)

    def residual_body(i, carry):
        total = 0.0
        for k in range(2):
            r = H + 2 * i + k
            centre, around = row_sum(r, v, wx, wy, wz)
            total = total + (b[r] - (diag[r] * centre - around))
        t512[i] = total
        return carry

    lax.fori_loop(0, rows1, residual_body, 0, unroll=UNROLL)
    put_tiles(t256, dot_exact(t512[...].reshape(rows1 * ec, depth), pairs[...]))
    for i in range(rows1):
        start = i * ec + H
        right1[i] = 0.125 * (every_other(t256, start, cols1) + every_other(t256, start + 1, cols1))

    start = to_right.shape[0] - rows1 // 2
    for i in range(rows1 // 2):
        to_right[start + i] = jnp.concatenate((right1[2 * i], right1[2 * i + 1]), axis=1)
        to_left[start + i] = to_right[start + i]

    own_parity = parity2((cols, depth))
    for r in range(rows):
        value = v[H + r, H : H + cols]
        v_own[r] = value
        value = jnp.where(own_parity == ((r + 1) & 1), value, ahead(value, 0))
        for p in range(H // 2):
            n = p * rows + r
            for out, base in ((to_right, cols - H), (to_left, 0)):
                out[n // 8, n % 8 : n % 8 + 1] = value[base + 2 * p : base + 2 * p + 1]


def pack_v_kernel(v0, right, left, v0_rows, to_up, to_down):
    rows, cols, depth = v0.shape
    for r in range(rows):
        v0_rows[r, H : H + cols] = v0[r]
        for msg, base in ((right, 0), (left, H + cols)):
            for p in range(H // 2):
                n = p * rows + r
                line = msg[n // 8, n % 8 : n % 8 + 1]
                v0_rows[r, base + 2 * p : base + 2 * p + 2] = jnp.broadcast_to(line, (2, depth))
    ec = v0_rows.shape[1]
    parity = parity2((ec, depth))
    for out, base in ((to_up, rows - H), (to_down, 0)):
        for k in range(H // 2):
            r = base + 2 * k
            out[k] = jnp.where(parity == ((r + 1) & 1), v0_rows[r], v0_rows[r + 1])


def gather1_kernel(w1, up, out):
    rows, cols, depth = w1.shape[1:]
    for d in range(3):
        for i in range(rows):
            out[d * rows + i] = w1[d, i]
    out[3 * rows] = up[up.shape[0] - 1, :, :depth]


def couplings1_kernel(*refs):
    *blocks, w, rdiag, to_up, to_down, sums = refs
    planes, cols, depth = blocks[0].shape
    rows = planes // 3
    wide = cols * len(blocks)

    def plane(n):
        return jnp.concatenate([block[n] for block in blocks], axis=0)

    before = plane(3 * rows)
    for i in range(rows):
        x, y, z = plane(i), plane(rows + i), plane(2 * rows + i)
        w[0, i], w[1, i], w[2, i] = x, y, z
        rdiag[i] = 1.0 / (MASS + x + before + y + back(y, 0) + z + back(z, 1))
        before = x
    for d in range(3):
        for k in range(H - 1):
            to_up[d * (H - 1) + k] = w[d, rows - H + 1 + k]
            to_down[d * (H - 1) + k] = w[d, k]
    to_up[3 * (H - 1)] = w[0, rows - H]
    lane = lax.broadcasted_iota(jnp.int32, sums.shape, 1)
    row_odd = lax.broadcasted_iota(jnp.int32, (wide, depth), 0) & 1
    depth_odd = lax.broadcasted_iota(jnp.int32, (wide, depth), 1) & 1
    parts = [0.0, 0.0, 0.0]
    for i in range(rows):
        if i % 2 == 1:
            parts[0] = parts[0] + w[0, i]
        parts[1] = parts[1] + jnp.where(row_odd == 1, w[1, i], 0.0)
        parts[2] = parts[2] + jnp.where(depth_odd == 1, w[2, i], 0.0)
    line = jnp.zeros(sums.shape, F32)
    for d in range(3):
        line = jnp.where(lane == d, 0.0625 * jnp.sum(parts[d]), line)
    sums[...] = line


def pack1_kernel(right, left, own1, *refs):
    *between, rdiag, own, to_up, to_down = refs
    rows, cols, depth = own1.shape
    start = right.shape[0] - rows // 2
    for i in range(rows):
        lane = depth * (i % 2)
        parts = [own1[i], left[start + i // 2, :, lane : lane + depth]]
        parts += [block[i] for block in between]
        own[i] = jnp.concatenate(parts + [right[start + i // 2, :, lane : lane + depth]], axis=0)
    for k in range(H):
        value = own[rows - H + k]
        to_up[k] = value * rdiag[rows - H] if k == 0 else value
        value = own[k]
        to_down[k] = value * rdiag[k] if k == H - 1 else value


def pre1_kernel(own, up, down, w, w_up, w_down, v0_up, v0_down, kept, to_up, to_down):
    rows, wide, depth = own.shape
    er = rows + 2 * H
    wx, wy, wz, rdiag, b, v, diag = (kept.at[i] for i in range(7))
    b[0:H] = up[...]
    b[H : H + rows] = own[...]
    b[H + rows :] = down[...]
    for d in range(3):
        kept[d, H : H + rows] = w[d]
        kept[d, 1:H] = w_up[d * (H - 1) : (d + 1) * (H - 1)]
        kept[d, H + rows : er - 1] = w_down[d * (H - 1) : (d + 1) * (H - 1)]
    wx[0] = w_up[3 * (H - 1)]
    parity = parity2((wide, depth))
    for r in range(er):
        if 0 < r < er - 1:
            y, z = wy[r], wz[r]
            total = MASS + wx[r] + wx[r - 1] + y + back(y, 0) + z + back(z, 1)
            diag[r] = total
            inverse = 1.0 / total
            rdiag[r] = inverse
            first = b[r] * inverse
        else:
            first = b[r]
        v[r] = jnp.where(parity == (r & 1), first, 0.0)
    half_sweep(1, er - 1, 1, parity, v, b, wx, wy, wz, rdiag)
    half_sweep(2, er - 2, 0, parity, v, b, wx, wy, wz, rdiag)
    half_sweep(3, er - 3, 1, parity, v, b, wx, wy, wz, rdiag)
    for out, base, v0 in ((to_up, rows, v0_up), (to_down, H, v0_down)):
        n = 0
        for k in range(H // 2):
            value = jnp.concatenate((v[base + 2 * k], v[base + 2 * k + 1]), axis=1)
            for t in range(wide // 8):
                out[n] = value[8 * t : 8 * t + 8]
                n += 1
        for k in range(H // 2):
            for t in range(v0.shape[1] // 8):
                out[n] = v0[k, 8 * t : 8 * t + 8]
                n += 1


def residual1_kernel(kept1, pairs, sums, chunks, t256, t128):
    wx, wy, wz, _, b, v, diag = (kept1.at[i] for i in range(7))
    _, er, wide, depth = kept1.shape
    rows = er - 2 * H
    chunk = chunks.at[0]
    for i in range(rows // 2):
        total = 0.0
        for k in range(2):
            r = H + 2 * i + k
            centre, around = row_sum(r, v, wx, wy, wz)
            total = total + (b[r] - (diag[r] * centre - around))
        t256[i] = total
    n = rows // 2
    put_tiles(t128, dot_exact(t256[...].reshape(n * wide, depth), pairs[...]))
    half = wide // 2
    for i in range(n):
        start = i * wide
        chunk[i * half : (i + 1) * half] = 0.125 * (every_other(t128, start, half) + every_other(t128, start + 1, half))
    chunk[n * half : n * half + 1] = sums[0:1]
    for i in range(1, chunks.shape[0]):
        chunks[i] = chunk[...]


def split2(x):
    high = x.astype(BF16)
    return high, (x - high.astype(F32)).astype(BF16)


def dot_split(a, b):
    return dot(a[0], b[0]) + (dot(a[0], b[1]) + dot(a[1], b[0]))


def solve_kernel(got, table, out, *, count, start):
    devices, lines, depth = got.shape
    own = lines - 1
    cells = devices * own
    rx, ry, _ = out.shape

    def part(name, size, lane=0, width=None):
        return table[start[name] : start[name] + size, lane : lane + (width or table.shape[1])]

    values = jnp.concatenate([got[d, 0:own] for d in range(devices)], axis=0)
    sums = got[0, own : own + 1]
    for d in range(1, devices):
        sums = sums + got[d, own : own + 1]
    sums = sums * (1.0 / count)
    lam = MASS + sums[0:1, 0:1] * part("eig", cells, 0, depth)
    lam = lam + sums[0:1, 1:2] * part("eig", cells, depth, depth)
    lam = lam + sums[0:1, 2:3] * part("depth", 1, depth, depth)
    spec = dot_split(split2(values), split2(part("depth", depth, 0, depth)))
    spec = dot_split(split2(part("forward", cells)), split2(spec))
    spec = spec / (lam * float(count))
    spec = dot_split(split2(spec), split2(part("depth_out", depth)))
    step = -(-rx // 8) * 8
    along_x = table[pl.ds(pl.multiple_of(start["x"] + lax.axis_index("gx") * step, 8), step), :]
    along_y = part("y", ry)
    back_table = jnp.concatenate([along_x[i : i + 1] * along_y for i in range(rx)], axis=0)
    out[...] = dot_split(split2(back_table), split2(spec)).reshape(out.shape)


def post1_kernel(kept1, up, down, correction, own, to_up, to_down, v, *, cols):
    wx, wy, wz, rdiag, b, before, _ = (kept1.at[i] for i in range(7))
    er, wide, depth = before.shape
    rows = er - 2 * H
    for r in range(rows):
        v[H + r] = before[H + r] + correction[H + r]
    for msg, base in ((up, 0), (down, H + rows)):
        for k in range(H // 2):
            n = k * (wide // 8)
            value = jnp.concatenate([msg[n + t] for t in range(wide // 8)], axis=0)
            v[base + 2 * k] = value[:, :depth] + correction[base + 2 * k]
            v[base + 2 * k + 1] = value[:, depth:] + correction[base + 2 * k + 1]
    parity = parity2((wide, depth))
    half_sweep(1, er - 1, 0, parity, v, b, wx, wy, wz, rdiag)
    half_sweep(2, er - 2, 1, parity, v, b, wx, wy, wz, rdiag)
    half_sweep(3, er - 3, 0, parity, v, b, wx, wy, wz, rdiag)
    half_sweep(4, er - 4, 1, parity, v, b, wx, wy, wz, rdiag)
    h = H // 2
    used = cols + 2 * h
    for r in range(rows):
        value = v[H + r]
        own[r, 0:h] = value[wide - h :]
        own[r, h:used] = value[0 : cols + h]
        if used < own.shape[1]:
            own[r, used:] = jnp.zeros((own.shape[1] - used, depth), F32)
    to_up[...] = own[rows - h :]
    to_down[...] = own[0:h]


def spread_kernel(v0_rows, up, down, v):
    er, ec, _ = v.shape
    rows = er - 2 * H
    v[H : H + rows] = v0_rows[...]
    tiles = ec // 8
    for msg, base in ((up, 0), (down, H + rows)):
        start = msg.shape[0] - (H // 2) * tiles
        for k in range(H // 2):
            for t in range(tiles):
                tile = msg[start + k * tiles + t]
                v[base + 2 * k, 8 * t : 8 * t + 8] = tile
                v[base + 2 * k + 1, 8 * t : 8 * t + 8] = tile


def post_kernel(v_in, rows_own, up1, down1, kept, spread, out, v, t256):
    b, wx, wy, wz, rdiag = (kept.at[i] for i in range(5))
    rows, cols, depth = out.shape
    rows1, wide1, half = rows_own.shape
    er, ec = rows + 2 * H, cols + 2 * H
    h = H // 2
    ec1 = cols // 2 + 2 * h
    n1 = rows1 + 2 * h
    t256[0:h] = up1[...]
    t256[h : h + rows1] = rows_own[...]
    t256[h + rows1 :] = down1[...]
    wide = dot_exact(t256[...].reshape(n1 * t256.shape[1], half), spread[...])
    wide = wide.reshape(n1, t256.shape[1], depth)
    for n in range(n1):
        line = wide[n, 0:ec1]
        line = jnp.broadcast_to(line[:, None, :], (ec1, 2, depth)).reshape(2 * ec1, depth)
        v[2 * n] = v_in[2 * n] + line
        v[2 * n + 1] = v_in[2 * n + 1] + line
    parity = parity2((ec, depth))
    half_sweep(1, er - 1, 0, parity, v, b, wx, wy, wz, rdiag)
    half_sweep(2, er - 2, 1, parity, v, b, wx, wy, wz, rdiag)
    half_sweep(3, er - 3, 0, parity, v, b, wx, wy, wz, rdiag)
    half_sweep(4, er - 4, 1, parity, v, b, wx, wy, wz, rdiag)
    for r in range(rows):
        out[r] = v[H + r, H : H + cols]


def hartley(rows, columns, length):
    angle = (np.outer(rows, columns) % length) * (2.0 * math.pi / length)
    return np.cos(angle) + np.sin(angle)


def waves(length):
    return 2.0 * (1.0 - np.cos(np.arange(length) * (2.0 * math.pi / length)))


def windows(table, count, step, size):
    pad = -size % 8
    parts = [np.pad(table[i * step : i * step + size], ((0, pad), (0, 0))) for i in range(count)]
    return np.concatenate(parts)


def coarse_correction(chunks, rows, cols, depth):
    nx = lax.axis_size("gx")
    total_rows = rows * nx
    count = total_rows * cols * depth
    got = lax.all_to_all(chunks, "gx", 0, 0)
    out_rows = 2 * rows + 2 * H
    rows_ids = (np.arange(-H, 2 * total_rows + H) // 2) % total_rows
    table_x = hartley(rows_ids, np.arange(total_rows), total_rows)
    table_y = hartley(np.arange(2 * cols) // 2, np.arange(cols), cols)
    forward_x = hartley(np.arange(total_rows), np.arange(total_rows), total_rows)
    forward_y = hartley(np.arange(cols), np.arange(cols), cols)
    depth_in = hartley(np.arange(depth), np.arange(depth), depth)
    depth_out = np.repeat(depth_in, 2, axis=1)
    cells = total_rows * cols
    if cells <= 512 and cells == 2 * depth:
        ones = np.ones((1, depth))
        eig_x = np.repeat(waves(total_rows), cols)[:, None] * ones
        eig_y = np.tile(waves(cols), total_rows)[:, None] * ones
        eig_z = np.ones((depth, 1)) * waves(depth)[None, :]
        parts = {
            "forward": np.kron(forward_x, forward_y),
            "eig": np.concatenate((eig_x, eig_y), axis=1),
            "depth": np.concatenate((depth_in, eig_z), axis=1),
            "depth_out": depth_out,
            "x": windows(np.repeat(table_x, cols, axis=1), nx, 2 * rows, out_rows),
            "y": np.tile(table_y, (1, total_rows)),
        }
        start, size = {}, 0
        for name, part in parts.items():
            start[name] = size
            size += part.shape[0]
            assert size % 8 == 0
        table = jnp.asarray(np.concatenate(list(parts.values())), F32)
        return call(
            functools.partial(solve_kernel, count=count, start=start),
            [(out_rows, 2 * cols, 2 * depth)],
            got, table,
        )[0]

    hi = lax.Precision.HIGHEST
    f32 = lambda x: jnp.asarray(x, F32)
    averages = jnp.sum(got[:, rows * cols, :3], axis=0) / count
    full = got[:, : rows * cols].reshape(total_rows, cols, depth)
    spec = jnp.einsum("abz,zk->abk", full, f32(depth_in), precision=hi)
    spec = jnp.einsum("ij,jbz->ibz", f32(forward_x), spec, precision=hi)
    spec = jnp.einsum("ij,ajz->aiz", f32(forward_y), spec, precision=hi)
    lam = (
        MASS
        + averages[0] * f32(waves(total_rows))[:, None, None]
        + averages[1] * f32(waves(cols))[None, :, None]
        + averages[2] * f32(waves(depth))[None, None, :]
    )
    spec = spec / (lam * float(count))
    own_x = lax.dynamic_slice_in_dim(f32(table_x), lax.axis_index("gx") * 2 * rows, out_rows, 0)
    out = jnp.einsum("ij,jbz->ibz", own_x, spec, precision=hi)
    out = jnp.einsum("ij,ajz->aiz", f32(table_y), out, precision=hi)
    return jnp.einsum("abz,zk->abk", out, f32(depth_out), precision=hi)


def gathered(block):
    return [block] + [moved(block, 0, -k) for k in range(1, lax.axis_size("gy"))]


def shards(source, face_coef):
    rows, cols, depth = source.shape
    rows1, cols1, depth1 = rows // 2, cols // 2, depth // 2
    er, ec, er1 = rows + 2 * H, cols + 2 * H, rows1 + 2 * H
    wide = cols1 * lax.axis_size("gy")
    h = H // 2
    limit = VMEM_LIMIT if wide * depth1 <= 8192 else 5 * VMEM_LIMIT

    x_tiles = 4 * H * (cols // 8) + 1
    corner_tiles = len(CORNER0) // 8
    to_right, to_left, to_up, to_down, w1, source, face_coef, pairs = call(
        pack_kernel,
        [(2 * rows, 8, depth)] * 2
        + [(x_tiles, 8, depth)] * 2
        + [(3, rows1, cols1, depth1), (rows, cols, depth)]
        + [jax.ShapeDtypeStruct((3, rows, cols, depth), BF16), jax.ShapeDtypeStruct((depth, depth1), BF16)],
        source, face_coef,
        remote=(0, 1),
        scratch=[
            pltpu.VMEM((depth, depth1), BF16),
            (depth1 // 128, cols, 128),
            pltpu.SemaphoreType.DMA((2,)),
        ],
    )
    right, left = moved(to_right, 0, 1), moved(to_left, 0, -1)
    up, down = moved(to_up, 1, 0), moved(to_down, -1, 0)
    to_up, to_down = call(
        functools.partial(forward_kernel, rows=rows), [(2 * corner_tiles, 8, depth)] * 2, right, left
    )
    corners = moved(to_up, 1, 0), moved(to_down, -1, 0)
    (block,) = call(gather1_kernel, [(3 * rows1 + 1, cols1, depth1)], w1, up, near=(to_up,))
    blocks = gathered(block)
    (state,) = call(assemble_kernel, [(7, er, ec, depth)], source, face_coef, up, down, right, left)
    kept, v0, right1, to_right, to_left = call(
        pre_kernel,
        [(5, er, ec, depth), (rows, cols, depth), (rows1, cols1, depth1)]
        + [(rows * h // 8 + rows1 // 2, 8, depth)] * 2,
        *corners, pairs, state,
        scratch=[(rows1, ec, depth), (depth1 // 128, rows1 * ec, 128)] + [(er, ec, depth)] * 2,
    )

    count = lax.axis_size("gy")
    left = moved(to_left, 0, -1)
    between = [moved(right1, 0, -k) for k in range(2, count - 1)]
    right = moved(to_right, 0, 1)
    w_own, rdiag_own, to_up, to_down, sums = call(
        couplings1_kernel,
        [(3, rows1, wide, depth1), (rows1, wide, depth1), (3 * H - 2, wide, depth1), (3 * H - 3, wide, depth1)]
        + [(8, depth1 // 2)],
        *blocks,
        near=(right1,), limit=limit,
    )
    w_up, w_down = moved(to_up, 1, 0), moved(to_down, -1, 0)
    own, to_up, to_down = call(
        pack1_kernel,
        [(rows1, wide, depth1)] + [(H, wide, depth1)] * 2,
        right, left, right1, *between, rdiag_own,
        near=(kept,), limit=limit,
    )
    up, down = moved(to_up, 1, 0), moved(to_down, -1, 0)
    v0_rows, v0_up, v0_down = call(pack_v_kernel, [(rows, ec, depth)] + [(h, ec, depth)] * 2, v0, right, left)
    tiles = h * (wide // 8 + ec // 8)
    kept1, to_up, to_down = call(
        pre1_kernel,
        [(7, er1, wide, depth1)] + [(tiles, 8, depth)] * 2,
        own, up, down, w_own, w_up, w_down, v0_up, v0_down,
        near=(kept,), limit=limit,
    )
    up, down = moved(to_up, 1, 0), moved(to_down, -1, 0)
    (chunks,) = call(
        residual1_kernel,
        [(lax.axis_size("gx"), rows1 * wide // 4 + 1, depth1 // 2)],
        kept1, jnp.asarray(pair_table(depth1)), sums,
        scratch=[(rows1 // 2, wide, depth1), (depth1 // 256, rows1 // 2 * wide, 128)],
        limit=limit,
    )
    correction2 = coarse_correction(chunks, rows1 // 2, wide // 2, depth1 // 2)
    used = -(-(cols1 + 2 * h) // 8) * 8
    own, to_up, to_down = call(
        functools.partial(post1_kernel, cols=cols1),
        [(rows1, used, depth1)] + [(h, used, depth1)] * 2,
        kept1, up, down, correction2,
        scratch=[(er1, wide, depth1)],
        limit=limit,
    )

    (v0e,) = call(spread_kernel, [(er, ec, depth)], v0_rows, up, down)
    up1, down1 = moved(to_up, 1, 0), moved(to_down, -1, 0)
    (out,) = call(
        post_kernel,
        [(rows, cols, depth)],
        v0e, own, up1, down1, kept,
        jnp.asarray(np.ascontiguousarray(pair_table(depth).T)),
        scratch=[(er, ec, depth), (rows1 + 2 * h, used, depth1)],
    )
    return out


def solution(mesh):
    return jax.shard_map(
        shards,
        mesh=mesh,
        in_specs=(P("gx", "gy", None), P(None, "gx", "gy", None)),
        out_specs=P("gx", "gy", None),
        check_vma=False,
    )
```

time: 84.7 us -> 75.3 us (0.89); the launches traced: 83 us -> 75 us
  blocking collectives: 0 us -> 8.41 us
  starting transfers between devices: 36 us -> 27.6 us
  waiting for transfers between devices: 31.6 us -> 24.6 us
    all_to_all x0 -> x1, blocking collectives: none -> 8.41 us  [coarse_correction(): got = lax.all_to_all(chunks, 'gx', 0, 0)]
    all_to_all x1 -> x0, starting transfers between devices: 5.85 us -> none  [coarse_correction(): got = lax.all_to_all(chunks, BOTH, 0, 0)]
    ppermute x8, waiting for transfers between devices: 22.7 us -> 18.4 us  [moved(): return lax.ppermute(block, 'gy', [(j, (j + dy) % ny) for j in range(ny)])]
    ppermute x8, starting transfers between devices: 15.9 us -> 12.8 us  [moved(): return lax.ppermute(block, 'gy', [(j, (j + dy) % ny) for j in range(ny)])]
    ppermute x10 -> x12, waiting for transfers between devices: 8.92 us -> 6.18 us  [moved(): return lax.ppermute(block, 'gx', [(i, (i + dx) % nx) for i in range(nx)])]
    unnamed x16 -> x10, local copies, waits for them, and re-layouts: 2.58 us -> 1.97 us
    ppermute x10 -> x12, starting transfers between devices: 14.2 us -> 14.8 us  [moved(): return lax.ppermute(block, 'gx', [(i, (i + dx) % nx) for i in range(nx)])]
    pallas_call x12 -> x14, Pallas kernels: 12.8 us -> 12.3 us  [call(): pl.pallas_call(body, out_shape=[s if hasattr(s, 'dtype') else jax.ShapeDt...]
  transfers between devices with their start and end apart: 19 -> 20, of which waited for: 9 -> 7; matrix products, arithmetic and copies ran while one was open for 0% -> 0% of each run, Pallas kernels for 4% -> 8%
where the time goes in v4:
time: 75.3 us; the launch traced here: 75 us
  starting transfers between devices  27.6 us (37%)
  waiting for transfers between devices  24.6 us (33%)
  Pallas kernels  12.3 us (16%)
  blocking collectives  8.41 us (11%)
  local copies, waits for them, and re-layouts  1.97 us (3%)
    ppermute x8, waiting for transfers between devices, moved(): return lax.ppermute(block, 'gy', [(j, (j + dy) % ny) for j in range(ny)])  18.4 us
    ppermute x12, starting transfers between devices, moved(): return lax.ppermute(block, 'gx', [(i, (i + dx) % nx) for i in range(nx)])  14.8 us
    ppermute x8, starting transfers between devices, moved(): return lax.ppermute(block, 'gy', [(j, (j + dy) % ny) for j in range(ny)])  12.8 us
    pallas_call x14, Pallas kernels, call(): pl.pallas_call(body, out_shape=[s if hasattr(s, 'dtype') else jax.ShapeDt...  12.3 us
    all_to_all x1, blocking collectives, coarse_correction(): got = lax.all_to_all(chunks, 'gx', 0, 0)  8.41 us
    ppermute x12, waiting for transfers between devices, moved(): return lax.ppermute(block, 'gx', [(i, (i + dx) % nx) for i in range(nx)])  6.18 us
    unnamed x10, local copies, waits for them, and re-layouts  1.97 us
  transfers between devices with their start and end apart: 20, of which 7 were waited for; matrix products, arithmetic and copies ran while one was open for 0% of the time, Pallas kernels for 8%

profile of v4, /device:TPU:0, one launch (start us, length us, event | category | flops | bytes accessed | tf_op | source)
XLA Modules:
  0.0 75.0 jit_solution(16513524941913702511)
XLA Ops:
  0.0 1.0 %copy-done.1 = bf16[3,8,16,512]{3,2,1,0:T(8,128)(2,1)S(1)} copy-done((bf16[3,8,16,512]{3,2,1,0:T(8,128)(2,1)S(1)}, bf16[3,8,16,512]{3,2,1,0:T(8,128)(2,1)}, u32[]{:S(2)}) %copy-start.1) | copy-done | bytes 393240
  1.0 0.9 %copy-done.2 = f32[8,16,512]{2,1,0:T(8,128)S(1)} copy-done((f32[8,16,512]{2,1,0:T(8,128)S(1)}, f32[8,16,512]{2,1,0:T(8,128)}, u32[]{:S(2)}) %copy-start.2) | copy-done | bytes 262168
  1.9 1.3 %shard_map.55 = (f32[16,8,512]{2,1,0:T(8,128)S(1)}, f32[16,8,512]{2,1,0:T(8,128)S(1)}, f32[33,8,512]{2,1,0:T(8,128)S(1)}, f32[33,8,512]{2,1,0:T(8,128)S(1)}, f32...) custom-call(f32[8,16,512]{2,1,0:T(8,128)S(1)} %copy-done.2, ...), custom_call_target="tpu_custom_call" | custom-call | tf_op jit(solution)/shard_map/pallas_call | solution.py:39
  3.2 0.5 collective-permute-start.4
  3.7 2.9 %collective-permute-start.5 = (f32[33,8,512]{2,1,0:T(8,128)S(1)}, f32[33,8,512]{2,1,0:T(8,128)S(1)}, u32[]{:S(2)}, u32[]{:S(2)}) collective-permute-start(f32[33,8,512]{2,1,0:T(8,128)S(1)} %get-tuple-element.45), channel_id=1, source_target_pairs={{0,28},{4,0},{8,4},{12,8},{16,12},{20,16},{24,20},{28,24},{1,29},{... | collective-permute-start | bytes 1622024 | tf_op jit(solution)/shard_map/ppermute | solution.py:52
  6.7 2.3 %collective-permute-start = (f32[16,8,512]{2,1,0:T(8,128)S(1)}, f32[16,8,512]{2,1,0:T(8,128)S(1)}, u32[]{:S(2)}, u32[]{:S(2)}) collective-permute-start(f32[16,8,512]{2,1,0:T(8,128)S(1)} %get-tuple-element.37), channel_id=1, source_target_pairs={{0,1},{1,2},{2,3},{3,0},{4,5},{5,6},{6,7},{7,4},{8,9},{9,10},{10,1... | collective-permute-start | bytes 786440 | tf_op jit(solution)/shard_map/ppermute | solution.py:54
  9.0 2.0 %collective-permute-start.1 = (f32[16,8,512]{2,1,0:T(8,128)S(1)}, f32[16,8,512]{2,1,0:T(8,128)S(1)}, u32[]{:S(2)}, u32[]{:S(2)}) collective-permute-start(f32[16,8,512]{2,1,0:T(8,128)S(1)} %get-tuple-element.38), channel_id=1, source_target_pairs={{0,3},{1,0},{2,1},{3,2},{4,7},{5,4},{6,5},{7,6},{8,11},{9,8},{10,9... | collective-permute-start | bytes 786440 | tf_op jit(solution)/shard_map/ppermute | solution.py:54
  11.0 7.3 %collective-permute-done.refs_0_.refs_4_ = f32[16,8,512]{2,1,0:T(8,128)S(1)} collective-permute-done((f32[16,8,512]{2,1,0:T(8,128)S(1)}, f32[16,8,512]{2,1,0:T(8,128)S(1)}, u32[]{:S(2)}, u32[]{:S(2)}) %collective-permute-start) | collective-permute-done | bytes 262176 | tf_op jit(solution)/shard_map/ppermute | solution.py:54
  18.2 3.2 %collective-permute-done.1.refs_1_.refs_5_ = f32[16,8,512]{2,1,0:T(8,128)S(1)} collective-permute-done((f32[16,8,512]{2,1,0:T(8,128)S(1)}, f32[16,8,512]{2,1,0:T(8,128)S(1)}, u32[]{:S(2)}, u32[]{:S(2)}) %collective-permute-start.1) | collective-permute-done | bytes 262176 | tf_op jit(solution)/shard_map/ppermute | solution.py:54
  21.5 0.4 collective-permute-start.3
  22.1 1.7 %collective-permute-start.11 = (f32[13,8,256]{2,1,0:T(8,128)S(1)}, f32[13,8,256]{2,1,0:T(8,128)S(1)}, u32[]{:S(2)}, u32[]{:S(2)}) collective-permute-start(f32[13,8,256]{2,1,0:T(8,128)S(1)} %shard_map.60.refs_0_), channel_id=1, source_target_pairs={{0,1},{1,2},{2,3},{3,0},{4,5},{5,6},{6,7},{7,4},{8,9},{9,10},{10,1... | collective-permute-start | bytes 319496 | tf_op jit(solution)/shard_map/ppermute | solution.py:54
  23.8 1.2 %collective-permute-start.10 = (f32[13,8,256]{2,1,0:T(8,128)S(1)}, f32[13,8,256]{2,1,0:T(8,128)S(1)}, u32[]{:S(2)}, u32[]{:S(2)}) collective-permute-start(f32[13,8,256]{2,1,0:T(8,128)S(1)} %shard_map.60.refs_0_), channel_id=1, source_target_pairs={{0,2},{1,3},{2,0},{3,1},{4,6},{5,7},{6,4},{7,5},{8,10},{9,11},{10,... | collective-permute-start | bytes 319496 | tf_op jit(solution)/shard_map/ppermute | solution.py:54
  25.0 1.3 %collective-permute-start.9 = (f32[13,8,256]{2,1,0:T(8,128)S(1)}, f32[13,8,256]{2,1,0:T(8,128)S(1)}, u32[]{:S(2)}, u32[]{:S(2)}) collective-permute-start(f32[13,8,256]{2,1,0:T(8,128)S(1)} %shard_map.60.refs_0_), channel_id=1, source_target_pairs={{0,3},{1,0},{2,1},{3,2},{4,7},{5,4},{6,5},{7,6},{8,11},{9,8},{10,9... | collective-permute-start | bytes 319496 | tf_op jit(solution)/shard_map/ppermute | solution.py:54
  26.4 0.9 %shard_map.57.refs_3_ = f32[7,16,24,512]{3,2,1,0:T(8,128)S(1)} custom-call(f32[8,16,512]{2,1,0:T(8,128)S(1)} %get-tuple-element.42.refs_0_, bf16[3,8,16,512]{3,2,1,0:T(8,128)(2,1)S(1)} %get-tuple-element.43.refs_1_, f32[33,8,512]{2,1,0:T(8,128)S(1)} %collective-permute-done.4.refs_2_.refs_1_, f32[33,8,512]{2,1,0:T(8,128)S(1)} %collective-permute-done.5.refs_3_, ...), custom_call_target="tpu_custom_call" | custom-call | tf_op jit(solution)/shard_map/pallas_call | solution.py:39
  27.4 0.5 collective-permute-done.2.refs_0_
  27.9 3.0 %shard_map.58 = (f32[5,16,24,512]{3,2,1,0:T(8,128)S(1)}, f32[8,16,512]{2,1,0:T(8,128)S(1)}, f32[4,8,256]{2,1,0:T(8,128)S(1)}, f32[4,8,512]{2,1,0:T(8,128)S(1)}, f32[4,8,512]{2,1,0:T(8,128)S(1)}) custom-call(f32[8,8,512]{2,1,0:T(8,128)S(1)} %collective-permute-done.2.refs_0_, f32[8,8,512]{2,1,0:T(8,128)S(1)} %collective-permute-done.3.refs_1_, ...), custom_call_target="tpu_custom_call" | custom-call | tf_op jit(solution)/shard_map/pallas_call | solution.py:39
  30.9 3.5 %collective-permute-done.10.refs_2_ = f32[13,8,256]{2,1,0:T(8,128)S(1)} collective-permute-done((f32[13,8,256]{2,1,0:T(8,128)S(1)}, f32[13,8,256]{2,1,0:T(8,128)S(1)}, u32[]{:S(2)}, u32[]{:S(2)}) %collective-permute-start.10) | collective-permute-done | bytes 106528 | tf_op jit(solution)/shard_map/ppermute | solution.py:54
  34.7 2.6 %collective-permute-start.15 = (f32[9,32,256]{2,1,0:T(8,128)S(1)}, f32[9,32,256]{2,1,0:T(8,128)S(1)}, u32[]{:S(2)}, u32[]{:S(2)}) collective-permute-start(f32[9,32,256]{2,1,0:T(8,128)S(1)} %get-tuple-element.59), channel_id=1, source_target_pairs={{0,28},{4,0},{8,4},{12,8},{16,12},{20,16},{24,20},{28,24},{1,29},{... | collective-permute-start | bytes 884744 | tf_op jit(solution)/shard_map/ppermute | solution.py:52
  37.3 2.8 %collective-permute-start.6 = (f32[4,8,512]{2,1,0:T(8,128)S(1)}, f32[4,8,512]{2,1,0:T(8,128)S(1)}, u32[]{:S(2)}, u32[]{:S(2)}) collective-permute-start(f32[4,8,512]{2,1,0:T(8,128)S(1)} %get-tuple-element.47), channel_id=1, source_target_pairs={{0,1},{1,2},{2,3},{3,0},{4,5},{5,6},{6,7},{7,4},{8,9},{9,10},{10,1... | collective-permute-start | bytes 196616 | tf_op jit(solution)/shard_map/ppermute | solution.py:54
  40.1 1.0 %collective-permute-start.7 = (f32[4,8,512]{2,1,0:T(8,128)S(1)}, f32[4,8,512]{2,1,0:T(8,128)S(1)}, u32[]{:S(2)}, u32[]{:S(2)}) collective-permute-start(f32[4,8,512]{2,1,0:T(8,128)S(1)} %get-tuple-element.48), channel_id=1, source_target_pairs={{0,3},{1,0},{2,1},{3,2},{4,7},{5,4},{6,5},{7,6},{8,11},{9,8},{10,9... | collective-permute-start | bytes 196616 | tf_op jit(solution)/shard_map/ppermute | solution.py:54
  41.1 0.4 collective-permute-start.8
  41.6 4.4 %collective-permute-done.8.refs_3_ = f32[4,8,256]{2,1,0:T(8,128)S(1)} collective-permute-done((f32[4,8,256]{2,1,0:T(8,128)S(1)}, f32[4,8,256]{2,1,0:T(8,128)S(1)}, u32[]{:S(2)}, u32[]{:S(2)}) %collective-permute-start.8) | collective-permute-done | bytes 32800 | tf_op jit(solution)/shard_map/ppermute | solution.py:54
  46.1 2.6 %collective-permute-start.13 = (f32[4,32,256]{2,1,0:T(8,128)S(1)}, f32[4,32,256]{2,1,0:T(8,128)S(1)}, u32[]{:S(2)}, u32[]{:S(2)}) collective-permute-start(f32[4,32,256]{2,1,0:T(8,128)S(1)} %get-tuple-element.56), channel_id=1, source_target_pairs={{0,28},{4,0},{8,4},{12,8},{16,12},{20,16},{24,20},{28,24},{1,29},{... | collective-permute-start | bytes 393224 | tf_op jit(solution)/shard_map/ppermute | solution.py:52
  48.8 3.8 %collective-permute-done.12.refs_1_ = f32[4,32,256]{2,1,0:T(8,128)S(1)} collective-permute-done((f32[4,32,256]{2,1,0:T(8,128)S(1)}, f32[4,32,256]{2,1,0:T(8,128)S(1)}, u32[]{:S(2)}, u32[]{:S(2)}) %collective-permute-start.12) | collective-permute-done | bytes 131104 | tf_op jit(solution)/shard_map/ppermute | solution.py:52
  52.6 0.9 %shard_map.63 = (f32[7,12,32,256]{3,2,1,0:T(8,128)S(1)}, f32[14,8,512]{2,1,0:T(8,128)S(1)}, f32[14,8,512]{2,1,0:T(8,128)S(1)}) custom-call(f32[4,32,256]{2,1,0:T(8,128)S(1)} %get-tuple-element.54.refs_0_, f32[4,32,256]{2,1,0:T(8,128)S(1)} %collective-permute-done.12.refs_1_, f32[4,32,256]{2,1,0:T(8,128)S(1)} %collective-permute-done.13.refs_2_, ...), custom_call_target="tpu_custom_call" | custom-call | tf_op jit(solution)/shard_map/pallas_call | solution.py:39
  53.6 2.6 %collective-permute-start.17 = (f32[14,8,512]{2,1,0:T(8,128)S(1)}, f32[14,8,512]{2,1,0:T(8,128)S(1)}, u32[]{:S(2)}, u32[]{:S(2)}) collective-permute-start(f32[14,8,512]{2,1,0:T(8,128)S(1)} %get-tuple-element.63), channel_id=1, source_target_pairs={{0,28},{4,0},{8,4},{12,8},{16,12},{20,16},{24,20},{28,24},{1,29},{... | collective-permute-start | bytes 688136 | tf_op jit(solution)/shard_map/ppermute | solution.py:52
  56.5 8.4 %all_to_all.5.refs_0_ = f32[8,33,128]{2,1,0:T(8,128)S(1)} all-to-all(f32[8,33,128]{2,1,0:T(8,128)S(1)} %shard_map.65), channel_id=1, replica_groups=mesh['gx'=8,'gy'=4] {'gx'}, dimensions={0} | all-to-all | bytes 270336 | tf_op jit(solution)/shard_map/all_to_all | solution.py:555
  64.9 1.2 %shard_map.66.refs_3_ = f32[12,32,256]{2,1,0:T(8,128)S(1)} custom-call(f32[8,33,128]{2,1,0:T(8,128)S(1)} %all_to_all.5.refs_0_, f32[928,256]{1,0:T(8,128)S(1)} %copy-done), custom_call_target="tpu_custom_call" | custom-call | tf_op jit(solution)/shard_map/pallas_call | solution.py:39
  66.2 0.7 shard_map.67
  67.0 2.6 %collective-permute-start.19 = (f32[2,16,256]{2,1,0:T(8,128)S(1)}, f32[2,16,256]{2,1,0:T(8,128)S(1)}, u32[]{:S(2)}, u32[]{:S(2)}) collective-permute-start(f32[2,16,256]{2,1,0:T(8,128)S(1)} %get-tuple-element.68), channel_id=1, source_target_pairs={{0,28},{4,0},{8,4},{12,8},{16,12},{20,16},{24,20},{28,24},{1,29},{... | collective-permute-start | bytes 98312 | tf_op jit(solution)/shard_map/ppermute | solution.py:52
  69.7 1.8 %collective-permute-done.18.refs_2_ = f32[2,16,256]{2,1,0:T(8,128)S(1)} collective-permute-done((f32[2,16,256]{2,1,0:T(8,128)S(1)}, f32[2,16,256]{2,1,0:T(8,128)S(1)}, u32[]{:S(2)}, u32[]{:S(2)}) %collective-permute-start.18) | collective-permute-done | bytes 32800 | tf_op jit(solution)/shard_map/ppermute | solution.py:52
  71.5 3.5 %shard_map.68 = f32[8,16,512]{2,1,0:T(8,128)} custom-call(f32[16,24,512]{2,1,0:T(8,128)S(1)} %shard_map.64.refs_0_, f32[4,16,256]{2,1,0:T(8,128)S(1)} %get-tuple-element.66.refs_1_, f32[2,16,256]{2,1,0:T(8,128)S(1)} %collective-permute-done.18.refs_2_, f32[2,16,256]{2,1,0:T(8,128)S(1)} %collective-permute-done.19.refs_3_, ...), custom_call_target="tpu_custom_call" | custom-call | tf_op jit(solution)/shard_map/pallas_call | solution.py:39
  (33 shorter events, 1.2 us)
Async XLA Ops:
  0.0 1.0 %copy-start.1 = (bf16[3,8,16,512]{3,2,1,0:T(8,128)(2,1)S(1)}, bf16[3,8,16,512]{3,2,1,0:T(8,128)(2,1)}, u32[]{:S(2)}) copy-start(bf16[3,8,16,512]{3,2,1,0:T(8,128)(2,1)} %refs_1_.3) | copy-start | bytes 1179652
  1.0 0.9 %copy-start.2 = (f32[8,16,512]{2,1,0:T(8,128)S(1)}, f32[8,16,512]{2,1,0:T(8,128)}, u32[]{:S(2)}) copy-start(f32[8,16,512]{2,1,0:T(8,128)} %refs_0_.1) | copy-start | bytes 786436
  3.2 18.9 %collective-permute-start.4 = (f32[33,8,512]{2,1,0:T(8,128)S(1)}, f32[33,8,512]{2,1,0:T(8,128)S(1)}, u32[]{:S(2)}, u32[]{:S(2)}) collective-permute-start(f32[33,8,512]{2,1,0:T(8,128)S(1)} %get-tuple-element.44), channel_id=1, source_target_pairs={{0,4},{4,8},{8,12},{12,16},{16,20},{20,24},{24,28},{28,0},{1,5},{5... | collective-permute-start | bytes 1622024 | tf_op jit(solution)/shard_map/ppermute | solution.py:52
  3.7 21.3 %collective-permute-start.5 = (f32[33,8,512]{2,1,0:T(8,128)S(1)}, f32[33,8,512]{2,1,0:T(8,128)S(1)}, u32[]{:S(2)}, u32[]{:S(2)}) collective-permute-start(f32[33,8,512]{2,1,0:T(8,128)S(1)} %get-tuple-element.45), channel_id=1, source_target_pairs={{0,28},{4,0},{8,4},{12,8},{16,12},{20,16},{24,20},{28,24},{1,29},{... | collective-permute-start | bytes 1622024 | tf_op jit(solution)/shard_map/ppermute | solution.py:52
  6.7 11.6 %collective-permute-start = (f32[16,8,512]{2,1,0:T(8,128)S(1)}, f32[16,8,512]{2,1,0:T(8,128)S(1)}, u32[]{:S(2)}, u32[]{:S(2)}) collective-permute-start(f32[16,8,512]{2,1,0:T(8,128)S(1)} %get-tuple-element.37), channel_id=1, source_target_pairs={{0,1},{1,2},{2,3},{3,0},{4,5},{5,6},{6,7},{7,4},{8,9},{9,10},{10,1... | collective-permute-start | bytes 786440 | tf_op jit(solution)/shard_map/ppermute | solution.py:54
  9.0 12.5 %collective-permute-start.1 = (f32[16,8,512]{2,1,0:T(8,128)S(1)}, f32[16,8,512]{2,1,0:T(8,128)S(1)}, u32[]{:S(2)}, u32[]{:S(2)}) collective-permute-start(f32[16,8,512]{2,1,0:T(8,128)S(1)} %get-tuple-element.38), channel_id=1, source_target_pairs={{0,3},{1,0},{2,1},{3,2},{4,7},{5,4},{6,5},{7,6},{8,11},{9,8},{10,9... | collective-permute-start | bytes 786440 | tf_op jit(solution)/shard_map/ppermute | solution.py:54
  21.5 5.8 %collective-permute-start.3 = (f32[8,8,512]{2,1,0:T(8,128)S(1)}, f32[8,8,512]{2,1,0:T(8,128)S(1)}, u32[]{:S(2)}, u32[]{:S(2)}) collective-permute-start(f32[8,8,512]{2,1,0:T(8,128)S(1)} %get-tuple-element.40), channel_id=1, source_target_pairs={{0,28},{4,0},{8,4},{12,8},{16,12},{20,16},{24,20},{28,24},{1,29},{... | collective-permute-start | bytes 393224 | tf_op jit(solution)/shard_map/ppermute | solution.py:52
  22.0 5.9 %collective-permute-start.2 = (f32[8,8,512]{2,1,0:T(8,128)S(1)}, f32[8,8,512]{2,1,0:T(8,128)S(1)}, u32[]{:S(2)}, u32[]{:S(2)}) collective-permute-start(f32[8,8,512]{2,1,0:T(8,128)S(1)} %get-tuple-element.39.refs_2_), channel_id=1, source_target_pairs={{0,4},{4,8},{8,12},{12,16},{16,20},{20,24},{24,28},{28,0},{1,5},{5... | collective-permute-start | bytes 393224 | tf_op jit(solution)/shard_map/ppermute | solution.py:52
  22.1 8.8 %collective-permute-start.11 = (f32[13,8,256]{2,1,0:T(8,128)S(1)}, f32[13,8,256]{2,1,0:T(8,128)S(1)}, u32[]{:S(2)}, u32[]{:S(2)}) collective-permute-start(f32[13,8,256]{2,1,0:T(8,128)S(1)} %shard_map.60.refs_0_), channel_id=1, source_target_pairs={{0,1},{1,2},{2,3},{3,0},{4,5},{5,6},{6,7},{7,4},{8,9},{9,10},{10,1... | collective-permute-start | bytes 319496 | tf_op jit(solution)/shard_map/ppermute | solution.py:54
  23.8 10.6 %collective-permute-start.10 = (f32[13,8,256]{2,1,0:T(8,128)S(1)}, f32[13,8,256]{2,1,0:T(8,128)S(1)}, u32[]{:S(2)}, u32[]{:S(2)}) collective-permute-start(f32[13,8,256]{2,1,0:T(8,128)S(1)} %shard_map.60.refs_0_), channel_id=1, source_target_pairs={{0,2},{1,3},{2,0},{3,1},{4,6},{5,7},{6,4},{7,5},{8,10},{9,11},{10,... | collective-permute-start | bytes 319496 | tf_op jit(solution)/shard_map/ppermute | solution.py:54
  25.0 9.4 %collective-permute-start.9 = (f32[13,8,256]{2,1,0:T(8,128)S(1)}, f32[13,8,256]{2,1,0:T(8,128)S(1)}, u32[]{:S(2)}, u32[]{:S(2)}) collective-permute-start(f32[13,8,256]{2,1,0:T(8,128)S(1)} %shard_map.60.refs_0_), channel_id=1, source_target_pairs={{0,3},{1,0},{2,1},{3,2},{4,7},{5,4},{6,5},{7,6},{8,11},{9,8},{10,9... | collective-permute-start | bytes 319496 | tf_op jit(solution)/shard_map/ppermute | solution.py:54
  34.6 18.0 %collective-permute-start.14 = (f32[10,32,256]{2,1,0:T(8,128)S(1)}, f32[10,32,256]{2,1,0:T(8,128)S(1)}, u32[]{:S(2)}, u32[]{:S(2)}) collective-permute-start(f32[10,32,256]{2,1,0:T(8,128)S(1)} %get-tuple-element.58), channel_id=1, source_target_pairs={{0,4},{4,8},{8,12},{12,16},{16,20},{20,24},{24,28},{28,0},{1,5},{5... | collective-permute-start | bytes 983048 | tf_op jit(solution)/shard_map/ppermute | solution.py:52
  34.7 17.9 %collective-permute-start.15 = (f32[9,32,256]{2,1,0:T(8,128)S(1)}, f32[9,32,256]{2,1,0:T(8,128)S(1)}, u32[]{:S(2)}, u32[]{:S(2)}) collective-permute-start(f32[9,32,256]{2,1,0:T(8,128)S(1)} %get-tuple-element.59), channel_id=1, source_target_pairs={{0,28},{4,0},{8,4},{12,8},{16,12},{20,16},{24,20},{28,24},{1,29},{... | collective-permute-start | bytes 884744 | tf_op jit(solution)/shard_map/ppermute | solution.py:52
  37.3 8.6 %collective-permute-start.6 = (f32[4,8,512]{2,1,0:T(8,128)S(1)}, f32[4,8,512]{2,1,0:T(8,128)S(1)}, u32[]{:S(2)}, u32[]{:S(2)}) collective-permute-start(f32[4,8,512]{2,1,0:T(8,128)S(1)} %get-tuple-element.47), channel_id=1, source_target_pairs={{0,1},{1,2},{2,3},{3,0},{4,5},{5,6},{6,7},{7,4},{8,9},{9,10},{10,1... | collective-permute-start | bytes 196616 | tf_op jit(solution)/shard_map/ppermute | solution.py:54
  40.1 5.8 %collective-permute-start.7 = (f32[4,8,512]{2,1,0:T(8,128)S(1)}, f32[4,8,512]{2,1,0:T(8,128)S(1)}, u32[]{:S(2)}, u32[]{:S(2)}) collective-permute-start(f32[4,8,512]{2,1,0:T(8,128)S(1)} %get-tuple-element.48), channel_id=1, source_target_pairs={{0,3},{1,0},{2,1},{3,2},{4,7},{5,4},{6,5},{7,6},{8,11},{9,8},{10,9... | collective-permute-start | bytes 196616 | tf_op jit(solution)/shard_map/ppermute | solution.py:54
  41.1 4.8 %collective-permute-start.8 = (f32[4,8,256]{2,1,0:T(8,128)S(1)}, f32[4,8,256]{2,1,0:T(8,128)S(1)}, u32[]{:S(2)}, u32[]{:S(2)}) collective-permute-start(f32[4,8,256]{2,1,0:T(8,128)S(1)} %get-tuple-element.50.refs_4_.refs_2_), channel_id=1, source_target_pairs={{0,2},{1,3},{2,0},{3,1},{4,6},{5,7},{6,4},{7,5},{8,10},{9,11},{10,... | collective-permute-start | bytes 98312 | tf_op jit(solution)/shard_map/ppermute | solution.py:54
  46.0 10.2 %copy-start.4 = (bf16[256,128]{1,0:T(8,128)(2,1)S(1)}, bf16[256,128]{1,0:T(8,128)(2,1)}, u32[]{:S(2)}) copy-start(bf16[256,128]{1,0:T(8,128)(2,1)} %constant.6.clone.refs_1_) | copy-start | bytes 196612
  46.0 6.6 %collective-permute-start.12 = (f32[4,32,256]{2,1,0:T(8,128)S(1)}, f32[4,32,256]{2,1,0:T(8,128)S(1)}, u32[]{:S(2)}, u32[]{:S(2)}) collective-permute-start(f32[4,32,256]{2,1,0:T(8,128)S(1)} %get-tuple-element.55), channel_id=1, source_target_pairs={{0,4},{4,8},{8,12},{12,16},{16,20},{20,24},{24,28},{28,0},{1,5},{5... | collective-permute-start | bytes 393224 | tf_op jit(solution)/shard_map/ppermute | solution.py:52
  46.1 6.6 %collective-permute-start.13 = (f32[4,32,256]{2,1,0:T(8,128)S(1)}, f32[4,32,256]{2,1,0:T(8,128)S(1)}, u32[]{:S(2)}, u32[]{:S(2)}) collective-permute-start(f32[4,32,256]{2,1,0:T(8,128)S(1)} %get-tuple-element.56), channel_id=1, source_target_pairs={{0,28},{4,0},{8,4},{12,8},{16,12},{20,16},{24,20},{28,24},{1,29},{... | collective-permute-start | bytes 393224 | tf_op jit(solution)/shard_map/ppermute | solution.py:52
  52.6 12.3 %copy-start = (f32[928,256]{1,0:T(8,128)S(1)}, f32[928,256]{1,0:T(8,128)}, u32[]{:S(2)}) copy-start(f32[928,256]{1,0:T(8,128)} %constant.7.clone.refs_1_) | copy-start | bytes 2850820
  53.5 12.7 %collective-permute-start.16 = (f32[14,8,512]{2,1,0:T(8,128)S(1)}, f32[14,8,512]{2,1,0:T(8,128)S(1)}, u32[]{:S(2)}, u32[]{:S(2)}) collective-permute-start(f32[14,8,512]{2,1,0:T(8,128)S(1)} %get-tuple-element.62), channel_id=1, source_target_pairs={{0,4},{4,8},{8,12},{12,16},{16,20},{20,24},{24,28},{28,0},{1,5},{5... | collective-permute-start | bytes 688136 | tf_op jit(solution)/shard_map/ppermute | solution.py:52
  53.6 12.6 %collective-permute-start.17 = (f32[14,8,512]{2,1,0:T(8,128)S(1)}, f32[14,8,512]{2,1,0:T(8,128)S(1)}, u32[]{:S(2)}, u32[]{:S(2)}) collective-permute-start(f32[14,8,512]{2,1,0:T(8,128)S(1)} %get-tuple-element.63), channel_id=1, source_target_pairs={{0,28},{4,0},{8,4},{12,8},{16,12},{20,16},{24,20},{28,24},{1,29},{... | collective-permute-start | bytes 688136 | tf_op jit(solution)/shard_map/ppermute | solution.py:52
  56.5 15.0 %copy-start.3 = (bf16[256,512]{1,0:T(8,128)(2,1)S(1)}, bf16[256,512]{1,0:T(8,128)(2,1)}, u32[]{:S(2)}) copy-start(bf16[256,512]{1,0:T(8,128)(2,1)} %constant.8.clone.refs_5_) | copy-start | bytes 786436
  66.9 4.6 %collective-permute-start.18 = (f32[2,16,256]{2,1,0:T(8,128)S(1)}, f32[2,16,256]{2,1,0:T(8,128)S(1)}, u32[]{:S(2)}, u32[]{:S(2)}) collective-permute-start(f32[2,16,256]{2,1,0:T(8,128)S(1)} %get-tuple-element.67), channel_id=1, source_target_pairs={{0,4},{4,8},{8,12},{12,16},{16,20},{20,24},{24,28},{28,0},{1,5},{5... | collective-permute-start | bytes 98312 | tf_op jit(solution)/shard_map/ppermute | solution.py:52
  67.0 4.5 %collective-permute-start.19 = (f32[2,16,256]{2,1,0:T(8,128)S(1)}, f32[2,16,256]{2,1,0:T(8,128)S(1)}, u32[]{:S(2)}, u32[]{:S(2)}) collective-permute-start(f32[2,16,256]{2,1,0:T(8,128)S(1)} %get-tuple-element.68), channel_id=1, source_target_pairs={{0,28},{4,0},{8,4},{12,8},{16,12},{20,16},{24,20},{28,24},{1,29},{... | collective-permute-start | bytes 98312 | tf_op jit(solution)/shard_map/ppermute | solution.py:52

commit v5 on v4

--- a/solution.py
+++ b/solution.py
@@ -29,34 +29,103 @@
     (1, 2, 1), (1, 2, 2), (1, 3, 1), (1, 3, 2), (2, 2, 1), (2, 2, 2), (2, 3, 1), (2, 3, 2),
 )
 
+def moved(block, axis, distance):
+    count = lax.axis_size(axis)
+    return lax.ppermute(block, axis, [(i, (i + distance) % count) for i in range(count)])
+
+
+class Beside:
+    def __init__(self, axis, shape, outer=None, inner=None):
+        self.axis, self.shape, self.outer, self.inner = axis, shape, outer, inner
+
+    def exchanged(self):
+        count = lax.axis_size(self.axis)
+        assert count % 2 == 0
+        got = []
+        for block, first in ((self.outer, 1), (self.inner, 0)):
+            route = []
+            for i in range(first, count + first, 2):
+                a, b = i % count, (i + 1) % count
+                route += [(a, b), (b, a)]
+            got.append(lax.ppermute(block, self.axis, route))
+        return Beside(self.axis, self.shape, *got)
+
+
 def call(kernel, out, *args, scratch=(), remote=(), limit=VMEM_LIMIT, near=()):
-    count = len(args)
-    args = (*args, *near)
+    flat, pairs_in, pairs_out, shapes = [], [], [], []
+    for i, arg in enumerate(args):
+        if isinstance(arg, Beside):
+            pairs_in.append((len(flat), arg))
+            flat += [arg.outer, arg.inner]
+        else:
+            flat.append(arg)
+    for item in out:
+        if isinstance(item, Beside):
+            pairs_out.append((len(shapes), item))
+            shapes += [item.shape] * 2
+        else:
+            shapes.append(item)
+    count = len(flat)
+    for item in near:
+        flat += [item.outer, item.inner] if isinstance(item, Beside) else [item]
+    total = len(flat)
+    own = [pltpu.VMEM(p.shape, F32) for _, p in pairs_in + pairs_out for _ in range(2)]
 
     def body(*refs):
-        kernel(*refs[:count], *refs[len(args) :])
-
-    return pl.pallas_call(
+        refs_in, refs_out = list(refs[:count]), list(refs[total : total + len(shapes)])
+        rest = list(refs[total + len(shapes) :])
+        held, rest = rest[: len(own)], rest[len(own) :]
+        sends = []
+        for n, (i, pair) in enumerate(pairs_in + pairs_out):
+            forward, backward = held[2 * n], held[2 * n + 1]
+            is_in = n < len(pairs_in)
+            refs_here = refs_in if is_in else refs_out
+            outer, inner = refs_here[i], refs_here[i + 1]
+            refs_here[i], refs_here[i + 1] = forward, backward
+            if is_in:
+                odd = lax.axis_index(pair.axis) & 1
+
+                @pl.when(odd == 0)
+                def _():
+                    forward[...] = outer[...]
+                    backward[...] = inner[...]
+
+                @pl.when(odd == 1)
+                def _():
+                    forward[...] = inner[...]
+                    backward[...] = outer[...]
+
+            else:
+                sends.append((pair.axis, outer, inner, forward, backward))
+        kernel(*refs_in, *refs_out, *rest)
+        for axis, outer, inner, forward, backward in sends:
+            odd = lax.axis_index(axis) & 1
+
+            @pl.when(odd == 0)
+            def _():
+                outer[...] = backward[...]
+                inner[...] = forward[...]
+
+            @pl.when(odd == 1)
+            def _():
+                outer[...] = forward[...]
+                inner[...] = backward[...]
+
+    results = pl.pallas_call(
         body,
-        out_shape=[s if hasattr(s, "dtype") else jax.ShapeDtypeStruct(s, F32) for s in out],
-        in_specs=[HBM if i in remote else VMEM for i in range(len(args))],
-        out_specs=[VMEM] * len(out),
-        scratch_shapes=[pltpu.VMEM(s, F32) if isinstance(s, tuple) else s for s in scratch],
+        out_shape=[s if hasattr(s, "dtype") else jax.ShapeDtypeStruct(s, F32) for s in shapes],
+        in_specs=[HBM if i in remote else VMEM for i in range(total)],
+        out_specs=[VMEM] * len(shapes),
+        scratch_shapes=own + [pltpu.VMEM(s, F32) if isinstance(s, tuple) else s for s in scratch],
         compiler_params=pltpu.CompilerParams(vmem_limit_bytes=limit),
-    )(*args)
-
-
-def moved(block, dx, dy):
-    nx, ny = lax.axis_size("gx"), lax.axis_size("gy")
-    if dy == 0:
-        return lax.ppermute(block, "gx", [(i, (i + dx) % nx) for i in range(nx)])
-    if dx == 0:
-        return lax.ppermute(block, "gy", [(j, (j + dy) % ny) for j in range(ny)])
-    route = []
-    for i in range(nx):
-        for j in range(ny):
-            route.append((i * ny + j, ((i + dx) % nx) * ny + (j + dy) % ny))
-    return lax.ppermute(block, BOTH, route)
+    )(*flat)
+    results, joined = list(results), []
+    for item in out:
+        if isinstance(item, Beside):
+            joined.append(Beside(item.axis, item.shape, results.pop(0), results.pop(0)))
+        else:
+            joined.append(results.pop(0))
+    return joined
 
 
 def split3(x):
@@ -124,52 +193,59 @@
     lax.fori_loop(first, last, body, 0, unroll=unroll)
 
 
-def pack_kernel(src_in, face_in, to_right, to_left, to_up, to_down, w1, src, face, pairs, *scratch):
-    odds, tx, sem = scratch
+def plane(src, face, a, r):
+    return src[r] if a == 0 else face[a - 1, r].astype(F32)
+
+
+def pack_y_kernel(src_in, face_in, to_right, to_left, src, face, sem):
     rows, cols, depth = src.shape
     copies = [pltpu.make_async_copy(src_in, src, sem.at[0]), pltpu.make_async_copy(face_in, face, sem.at[1])]
     for copy in copies:
         copy.start()
+    for copy in copies:
+        copy.wait()
+    for out, base in ((to_right, cols - H), (to_left, 0)):
+        for r in range(rows):
+            for t, pair in enumerate(((0, 3), (1, 2))):
+                for s, a in enumerate(pair):
+                    value = plane(src, face, a, r)
+                    if out is to_right and a == 3:
+                        value_all = value + back(value, 1) + back(plane(src, face, 2, r), 0)
+                        first = lax.broadcasted_iota(jnp.int32, value.shape, 0) == base
+                        value = jnp.where(first, value_all, value)
+                    out[2 * r + t, H * s : H * s + H] = value[base : base + H]
+
+
+def pack_x_kernel(src, face, to_up, to_down):
+    rows, cols, depth = src.shape
+    tiles = cols // 8
+    for out, base in ((to_up, rows - H), (to_down, 0)):
+        for a in range(4):
+            for k in range(H):
+                value = plane(src, face, a, base + k)
+                if out is to_up and a == 3 and k == 0:
+                    value = value + back(value, 1) + plane(src, face, 1, base - 1)
+                for t in range(tiles):
+                    out[(a * H + k) * tiles + t] = value[8 * t : 8 * t + 8]
+
+
+def coarsen_kernel(face, out, pairs, odds, tx):
+    _, rows, cols, depth = face.shape
     fine = lax.broadcasted_iota(jnp.int32, pairs.shape, 0)
     coarse = 2 * lax.broadcasted_iota(jnp.int32, pairs.shape, 1)
     pairs[...] = jnp.where((fine & -2) == coarse, 1.0, 0.0).astype(BF16)
     odds[...] = jnp.where(fine == coarse + 1, 1.0, 0.0).astype(BF16)
-    for copy in copies:
-        copy.wait()
-
-    for i in range(rows // 2):
-        put_tiles(tx, dot(face[0, 2 * i + 1], pairs[...]))
-        w1[0, i] = 0.0625 * (every_other(tx, 0, cols // 2) + every_other(tx, 1, cols // 2))
+    half, n = cols // 2, rows // 2
+
+    def both(x):
+        put_tiles(tx, x)
+        return 0.0625 * (every_other(tx, 0, half) + every_other(tx, 1, half))
+
+    for i in range(n):
+        out[i] = both(dot(face[0, 2 * i + 1], pairs[...]))
         put_tiles(tx, dot(face[1, 2 * i], pairs[...]) + dot(face[1, 2 * i + 1], pairs[...]))
-        w1[1, i] = 0.0625 * every_other(tx, 1, cols // 2)
-        put_tiles(tx, dot(face[2, 2 * i], odds[...]) + dot(face[2, 2 * i + 1], odds[...]))
-        w1[2, i] = 0.0625 * (every_other(tx, 0, cols // 2) + every_other(tx, 1, cols // 2))
-
-    def plane(a, r):
-        return src[r] if a == 0 else face[a - 1, r].astype(F32)
-
-    for out, base in ((to_right, cols - H), (to_left, 0)):
-        for r in range(rows):
-            for t, pair in enumerate(((0, 3), (1, 2))):
-                for s, a in enumerate(pair):
-                    value = plane(a, r)
-                    if out is to_right and a == 3:
-                        value_all = value + back(value, 1) + back(plane(2, r), 0)
-                        first = lax.broadcasted_iota(jnp.int32, value.shape, 0) == base
-                        value = jnp.where(first, value_all, value)
-                    out[2 * r + t, H * s : H * s + H] = value[base : base + H]
-
-    tiles = cols // 8
-    for out, base in ((to_up, rows - H), (to_down, 0)):
-        for a in range(4):
-            for k in range(H):
-                value = plane(a, base + k)
-                if out is to_up and a == 3 and k == 0:
-                    value = value + back(value, 1) + plane(1, base - 1)
-                for t in range(tiles):
-                    out[(a * H + k) * tiles + t] = value[8 * t : 8 * t + 8]
-    last = w1[0, rows // 2 - 1]
-    to_up[4 * H * tiles] = jnp.concatenate((last, last), axis=1)
+        out[n + i] = 0.0625 * every_other(tx, 1, half)
+        out[2 * n + i] = both(dot(face[2, 2 * i], odds[...]) + dot(face[2, 2 * i + 1], odds[...]))
 
 
 def forward_kernel(right, left, to_up, to_down, *, rows):
@@ -304,16 +380,19 @@
             out[k] = jnp.where(parity == ((r + 1) & 1), v0_rows[r], v0_rows[r + 1])
 
 
-def gather1_kernel(w1, up, out):
-    rows, cols, depth = w1.shape[1:]
-    for d in range(3):
-        for i in range(rows):
-            out[d * rows + i] = w1[d, i]
-    out[3 * rows] = up[up.shape[0] - 1, :, :depth]
-
-
-def couplings1_kernel(*refs):
-    *blocks, w, rdiag, to_up, to_down, sums = refs
+def before_kernel(x, up, down, pairs, out, tx):
+    n, half, _ = x.shape
+    tiles = 2 * half // 8
+    start = (2 * H - 1) * tiles
+    before = jnp.concatenate([up[start + t] for t in range(tiles)], axis=0)
+    put_tiles(tx, dot(before.astype(BF16), pairs[...]))
+    out[n] = 0.0625 * (every_other(tx, 0, half) + every_other(tx, 1, half))
+    out[0:n] = x[...]
+
+
+def couplings1_kernel(own, before_block, after_block, *refs):
+    *between, w, rdiag, to_up, to_down, sums = refs
+    blocks = [own, after_block, *between, before_block]
     planes, cols, depth = blocks[0].shape
     rows = planes // 3
     wide = cols * len(blocks)
@@ -619,67 +698,74 @@
     h = H // 2
     limit = VMEM_LIMIT if wide * depth1 <= 8192 else 5 * VMEM_LIMIT
 
-    x_tiles = 4 * H * (cols // 8) + 1
+    count = lax.axis_size("gy")
     corner_tiles = len(CORNER0) // 8
-    to_right, to_left, to_up, to_down, w1, source, face_coef, pairs = call(
-        pack_kernel,
-        [(2 * rows, 8, depth)] * 2
-        + [(x_tiles, 8, depth)] * 2
-        + [(3, rows1, cols1, depth1), (rows, cols, depth)]
-        + [jax.ShapeDtypeStruct((3, rows, cols, depth), BF16), jax.ShapeDtypeStruct((depth, depth1), BF16)],
+    y_first, source, face_coef = call(
+        pack_y_kernel,
+        [Beside("gy", (2 * rows, 8, depth)), (rows, cols, depth), jax.ShapeDtypeStruct((3, rows, cols, depth), BF16)],
         source, face_coef,
         remote=(0, 1),
-        scratch=[
-            pltpu.VMEM((depth, depth1), BF16),
-            (depth1 // 128, cols, 128),
-            pltpu.SemaphoreType.DMA((2,)),
-        ],
-    )
-    right, left = moved(to_right, 0, 1), moved(to_left, 0, -1)
-    up, down = moved(to_up, 1, 0), moved(to_down, -1, 0)
-    to_up, to_down = call(
-        functools.partial(forward_kernel, rows=rows), [(2 * corner_tiles, 8, depth)] * 2, right, left
-    )
-    corners = moved(to_up, 1, 0), moved(to_down, -1, 0)
-    (block,) = call(gather1_kernel, [(3 * rows1 + 1, cols1, depth1)], w1, up, near=(to_up,))
-    blocks = gathered(block)
-    (state,) = call(assemble_kernel, [(7, er, ec, depth)], source, face_coef, up, down, right, left)
-    kept, v0, right1, to_right, to_left = call(
+        scratch=[pltpu.SemaphoreType.DMA((2,))],
+    )
+    y_first = y_first.exchanged()
+    block, pairs = call(
+        coarsen_kernel,
+        [(3 * rows1, cols1, depth1), jax.ShapeDtypeStruct((depth, depth1), BF16)],
+        face_coef,
+        scratch=[pltpu.VMEM((depth, depth1), BF16), (depth1 // 128, cols, 128)],
+    )
+    (x_first,) = call(pack_x_kernel, [Beside("gx", (4 * H * (cols // 8), 8, depth))], source, face_coef, near=(block,))
+    x_first = x_first.exchanged()
+    (corners,) = call(
+        functools.partial(forward_kernel, rows=rows),
+        [Beside("gx", (2 * corner_tiles, 8, depth))],
+        y_first,
+    )
+    (block,) = call(
+        before_kernel,
+        [(3 * rows1 + 1, cols1, depth1)],
+        block, x_first, pairs,
+        near=(corners,),
+        scratch=[(depth1 // 128, cols, 128)],
+    )
+    corners = corners.exchanged()
+    blocks = Beside("gy", block.shape, block, block).exchanged()
+    blocks_between = [moved(block, "gy", -k) for k in range(2, count - 1)]
+    (state,) = call(assemble_kernel, [(7, er, ec, depth)], source, face_coef, x_first, y_first)
+    kept, v0, right1, y_second = call(
         pre_kernel,
         [(5, er, ec, depth), (rows, cols, depth), (rows1, cols1, depth1)]
-        + [(rows * h // 8 + rows1 // 2, 8, depth)] * 2,
-        *corners, pairs, state,
+        + [Beside("gy", (rows * h // 8 + rows1 // 2, 8, depth))],
+        corners, pairs, state,
         scratch=[(rows1, ec, depth), (depth1 // 128, rows1 * ec, 128)] + [(er, ec, depth)] * 2,
     )
 
-    count = lax.axis_size("gy")
-    left = moved(to_left, 0, -1)
-    between = [moved(right1, 0, -k) for k in range(2, count - 1)]
-    right = moved(to_right, 0, 1)
-    w_own, rdiag_own, to_up, to_down, sums = call(
+    y_second = y_second.exchanged()
+    between = [moved(right1, "gy", -k) for k in range(2, count - 1)]
+    w_own, rdiag_own, w_x, sums = call(
         couplings1_kernel,
-        [(3, rows1, wide, depth1), (rows1, wide, depth1), (3 * H - 2, wide, depth1), (3 * H - 3, wide, depth1)]
+        [(3, rows1, wide, depth1), (rows1, wide, depth1), Beside("gx", (3 * H - 2, wide, depth1))]
         + [(8, depth1 // 2)],
-        *blocks,
+        block, blocks, *blocks_between,
         near=(right1,), limit=limit,
     )
-    w_up, w_down = moved(to_up, 1, 0), moved(to_down, -1, 0)
-    own, to_up, to_down = call(
+    w_x = w_x.exchanged()
+    own, x_second = call(
         pack1_kernel,
-        [(rows1, wide, depth1)] + [(H, wide, depth1)] * 2,
-        right, left, right1, *between, rdiag_own,
+        [(rows1, wide, depth1), Beside("gx", (H, wide, depth1))],
+        y_second, right1, *between, rdiag_own,
         near=(kept,), limit=limit,
     )
-    up, down = moved(to_up, 1, 0), moved(to_down, -1, 0)
-    v0_rows, v0_up, v0_down = call(pack_v_kernel, [(rows, ec, depth)] + [(h, ec, depth)] * 2, v0, right, left)
+    x_second = x_second.exchanged()
+    v0_rows, v0_up, v0_down = call(pack_v_kernel, [(rows, ec, depth)] + [(h, ec, depth)] * 2, v0, y_second)
     tiles = h * (wide // 8 + ec // 8)
-    kept1, to_up, to_down = call(
+    kept1, x_third = call(
         pre1_kernel,
-        [(7, er1, wide, depth1)] + [(tiles, 8, depth)] * 2,
-        own, up, down, w_own, w_up, w_down, v0_up, v0_down,
+        [(7, er1, wide, depth1), Beside("gx", (tiles, 8, depth))],
+        own, x_second, w_own, w_x, v0_up, v0_down,
         near=(kept,), limit=limit,
     )
-    up, down = moved(to_up, 1, 0), moved(to_down, -1, 0)
+    x_third = x_third.exchanged()
     (chunks,) = call(
         residual1_kernel,
         [(lax.axis_size("gx"), rows1 * wide // 4 + 1, depth1 // 2)],
@@ -689,20 +775,19 @@
     )
     correction2 = coarse_correction(chunks, rows1 // 2, wide // 2, depth1 // 2)
     used = -(-(cols1 + 2 * h) // 8) * 8
-    own, to_up, to_down = call(
+    own, x_fourth = call(
         functools.partial(post1_kernel, cols=cols1),
-        [(rows1, used, depth1)] + [(h, used, depth1)] * 2,
-        kept1, up, down, correction2,
+        [(rows1, used, depth1), Beside("gx", (h, used, depth1))],
+        kept1, x_third, correction2,
         scratch=[(er1, wide, depth1)],
         limit=limit,
     )
-
-    (v0e,) = call(spread_kernel, [(er, ec, depth)], v0_rows, up, down)
-    up1, down1 = moved(to_up, 1, 0), moved(to_down, -1, 0)
+    x_fourth = x_fourth.exchanged()
+    (v0e,) = call(spread_kernel, [(er, ec, depth)], v0_rows, x_third)
     (out,) = call(
         post_kernel,
         [(rows, cols, depth)],
-        v0e, own, up1, down1, kept,
+        v0e, own, x_fourth, kept,
         jnp.asarray(np.ascontiguousarray(pair_table(depth).T)),
         scratch=[(er, ec, depth), (rows1 + 2 * h, used, depth1)],
     )

time: 75.3 us -> 73.5 us (0.976)
  starting transfers between devices: 27.6 us -> 21.4 us
  waiting for transfers between devices: 24.6 us -> 26.9 us
  blocking collectives: 8.41 us -> 9.7 us
  Pallas kernels: 12.3 us -> 13.1 us
    ppermute x20, starting transfers between devices: 27.6 us -> 21.4 us  [the longest x18 18.9 us: exchanged(): got.append(lax.ppermute(block, self.axis, route))]
    ppermute x20, waiting for transfers between devices: 24.6 us -> 26.9 us  [the longest x18 22.5 us: exchanged(): got.append(lax.ppermute(block, self.axis, route))]
    all_to_all x1, blocking collectives: 8.41 us -> 9.7 us  [coarse_correction(): got = lax.all_to_all(chunks, 'gx', 0, 0)]
    pallas_call x14 -> x16, Pallas kernels: 12.3 us -> 13.1 us  [call(): pl.pallas_call(body, out_shape=[s if hasattr(s, 'dtype') else jax.ShapeDt...]
where the time goes in v5:
time: 73.5 us; the launch traced here: 73.3 us
  waiting for transfers between devices  26.9 us (37%)
  starting transfers between devices  21.4 us (29%)
  Pallas kernels  13.1 us (18%)
  blocking collectives  9.7 us (13%)
  local copies, waits for them, and re-layouts  1.97 us (3%)
    ppermute x18, waiting for transfers between devices, exchanged(): got.append(lax.ppermute(block, self.axis, route))  22.5 us
    ppermute x18, starting transfers between devices, exchanged(): got.append(lax.ppermute(block, self.axis, route))  18.9 us
    pallas_call x16, Pallas kernels, call(): pl.pallas_call(body, out_shape=[s if hasattr(s, 'dtype') else jax.ShapeDt...  13.1 us
    all_to_all x1, blocking collectives, coarse_correction(): got = lax.all_to_all(chunks, 'gx', 0, 0)  9.7 us
    ppermute x2, waiting for transfers between devices, moved(): lax.ppermute(block, axis, [(i, (i + distance) % count) for i in range(cou...  4.44 us
    ppermute x2, starting transfers between devices, moved(): lax.ppermute(block, axis, [(i, (i + distance) % count) for i in range(cou...  2.47 us
    unnamed x10, local copies, waits for them, and re-layouts  1.97 us
  transfers between devices with their start and end apart: 20, of which 7 were waited for; matrix products, arithmetic and copies ran while one was open for 0% of the time, Pallas kernels for 8%

profile of v5, /device:TPU:0, one launch (start us, length us, event | category | flops | bytes accessed | tf_op | source)
XLA Modules:
  0.0 73.3 jit_solution(1524770815760438408)
XLA Ops:
  0.0 1.0 %copy-done.1 = bf16[3,8,16,512]{3,2,1,0:T(8,128)(2,1)S(1)} copy-done((bf16[3,8,16,512]{3,2,1,0:T(8,128)(2,1)S(1)}, bf16[3,8,16,512]{3,2,1,0:T(8,128)(2,1)}, u32[]{:S(2)}) %copy-start.1) | copy-done | bytes 393240
  1.0 0.9 %copy-done.2 = f32[8,16,512]{2,1,0:T(8,128)S(1)} copy-done((f32[8,16,512]{2,1,0:T(8,128)S(1)}, f32[8,16,512]{2,1,0:T(8,128)}, u32[]{:S(2)}) %copy-start.2) | copy-done | bytes 262168
  1.9 0.4 shard_map.55
  2.4 0.9 %shard_map.57 = (f32[12,8,256]{2,1,0:T(8,128)S(1)}, bf16[512,256]{1,0:T(8,128)(2,1)S(1)}) custom-call(bf16[3,8,16,512]{3,2,1,0:T(8,128)(2,1)S(1)} %get-tuple-element.41.refs_0_.refs_1_), custom_call_target="tpu_custom_call" | custom-call | tf_op jit(solution)/shard_map/pallas_call | solution.py:114
  3.4 3.4 %collective-permute-start.4 = (f32[32,8,512]{2,1,0:T(8,128)S(1)}, f32[32,8,512]{2,1,0:T(8,128)S(1)}, u32[]{:S(2)}, u32[]{:S(2)}) collective-permute-start(f32[32,8,512]{2,1,0:T(8,128)S(1)} %get-tuple-element.45), channel_id=1, source_target_pairs={{4,8},{8,4},{12,16},{16,12},{20,24},{24,20},{28,0},{0,28},{5,9},{9... | collective-permute-start | bytes 1572872 | tf_op jit(solution)/shard_map/ppermute | solution.py:50
  6.8 3.6 %collective-permute-start = (f32[16,8,512]{2,1,0:T(8,128)S(1)}, f32[16,8,512]{2,1,0:T(8,128)S(1)}, u32[]{:S(2)}, u32[]{:S(2)}) collective-permute-start(f32[16,8,512]{2,1,0:T(8,128)S(1)} %get-tuple-element.37), channel_id=1, source_target_pairs={{1,2},{2,1},{3,0},{0,3},{5,6},{6,5},{7,4},{4,7},{9,10},{10,9},{11,... | collective-permute-start | bytes 786440 | tf_op jit(solution)/shard_map/ppermute | solution.py:50
  10.4 7.4 %collective-permute-done.refs_0_.refs_4_ = f32[16,8,512]{2,1,0:T(8,128)S(1)} collective-permute-done((f32[16,8,512]{2,1,0:T(8,128)S(1)}, f32[16,8,512]{2,1,0:T(8,128)S(1)}, u32[]{:S(2)}, u32[]{:S(2)}) %collective-permute-start) | collective-permute-done | bytes 262176 | tf_op jit(solution)/shard_map/ppermute | solution.py:50
  17.8 5.3 %collective-permute-done.1.refs_1_.refs_5_ = f32[16,8,512]{2,1,0:T(8,128)S(1)} collective-permute-done((f32[16,8,512]{2,1,0:T(8,128)S(1)}, f32[16,8,512]{2,1,0:T(8,128)S(1)}, u32[]{:S(2)}, u32[]{:S(2)}) %collective-permute-start.1) | collective-permute-done | bytes 262176 | tf_op jit(solution)/shard_map/ppermute | solution.py:50
  23.6 0.6 collective-permute-start.3
  24.3 0.6 collective-permute-start.11
  24.9 1.6 %collective-permute-start.10 = (f32[13,8,256]{2,1,0:T(8,128)S(1)}, f32[13,8,256]{2,1,0:T(8,128)S(1)}, u32[]{:S(2)}, u32[]{:S(2)}) collective-permute-start(f32[13,8,256]{2,1,0:T(8,128)S(1)} %shard_map.62.refs_0_), channel_id=1, source_target_pairs={{0,1},{1,0},{2,3},{3,2},{4,5},{5,4},{6,7},{7,6},{8,9},{9,8},{10,11... | collective-permute-start | bytes 319496 | tf_op jit(solution)/shard_map/ppermute | solution.py:50
  26.5 2.2 %collective-permute-start.9 = (f32[13,8,256]{2,1,0:T(8,128)S(1)}, f32[13,8,256]{2,1,0:T(8,128)S(1)}, u32[]{:S(2)}, u32[]{:S(2)}) collective-permute-start(f32[13,8,256]{2,1,0:T(8,128)S(1)} %shard_map.62.refs_0_), channel_id=1, source_target_pairs={{1,2},{2,1},{3,0},{0,3},{5,6},{6,5},{7,4},{4,7},{9,10},{10,9},{11,... | collective-permute-start | bytes 319496 | tf_op jit(solution)/shard_map/ppermute | solution.py:50
  28.7 1.1 %shard_map.59.refs_3_ = f32[7,16,24,512]{3,2,1,0:T(8,128)S(1)} custom-call(f32[8,16,512]{2,1,0:T(8,128)S(1)} %get-tuple-element.43.refs_0_, bf16[3,8,16,512]{3,2,1,0:T(8,128)(2,1)S(1)} %get-tuple-element.41.refs_0_.refs_1_, f32[32,8,512]{2,1,0:T(8,128)S(1)} %collective-permute-done.4.refs_2_.refs_1_, ...), custom_call_target="tpu_custom_call" | custom-call | tf_op jit(solution)/shard_map/pallas_call | solution.py:114
  29.8 3.1 %shard_map.60 = (f32[5,16,24,512]{3,2,1,0:T(8,128)S(1)}, f32[8,16,512]{2,1,0:T(8,128)S(1)}, f32[4,8,256]{2,1,0:T(8,128)S(1)}, f32[4,8,512]{2,1,0:T(8,128)S(1)}, f32[4,8,512]{2,1,0:T(8,128)S(1)}) custom-call(f32[8,8,512]{2,1,0:T(8,128)S(1)} %collective-permute-done.2.refs_0_, f32[8,8,512]{2,1,0:T(8,128)S(1)} %collective-permute-done.3.refs_1_, ...), custom_call_target="tpu_custom_call" | custom-call | tf_op jit(solution)/shard_map/pallas_call | solution.py:114
  32.9 1.2 %collective-permute-done.11.refs_3_ = f32[13,8,256]{2,1,0:T(8,128)S(1)} collective-permute-done((f32[13,8,256]{2,1,0:T(8,128)S(1)}, f32[13,8,256]{2,1,0:T(8,128)S(1)}, u32[]{:S(2)}, u32[]{:S(2)}) %collective-permute-start.11) | collective-permute-done | bytes 106528 | tf_op jit(solution)/shard_map/ppermute | solution.py:34
  34.1 1.8 %collective-permute-done.9.refs_1_ = f32[13,8,256]{2,1,0:T(8,128)S(1)} collective-permute-done((f32[13,8,256]{2,1,0:T(8,128)S(1)}, f32[13,8,256]{2,1,0:T(8,128)S(1)}, u32[]{:S(2)}, u32[]{:S(2)}) %collective-permute-start.9) | collective-permute-done | bytes 106528 | tf_op jit(solution)/shard_map/ppermute | solution.py:50
  36.1 1.0 %collective-permute-start.14 = (f32[10,32,256]{2,1,0:T(8,128)S(1)}, f32[10,32,256]{2,1,0:T(8,128)S(1)}, u32[]{:S(2)}, u32[]{:S(2)}) collective-permute-start(f32[10,32,256]{2,1,0:T(8,128)S(1)} %get-tuple-element.58), channel_id=1, source_target_pairs={{4,8},{8,4},{12,16},{16,12},{20,24},{24,20},{28,0},{0,28},{5,9},{9... | collective-permute-start | bytes 983048 | tf_op jit(solution)/shard_map/ppermute | solution.py:50
  37.1 0.6 collective-permute-start.15
  37.8 1.6 %collective-permute-start.6 = (f32[4,8,512]{2,1,0:T(8,128)S(1)}, f32[4,8,512]{2,1,0:T(8,128)S(1)}, u32[]{:S(2)}, u32[]{:S(2)}) collective-permute-start(f32[4,8,512]{2,1,0:T(8,128)S(1)} %get-tuple-element.48), channel_id=1, source_target_pairs={{1,2},{2,1},{3,0},{0,3},{5,6},{6,5},{7,4},{4,7},{9,10},{10,9},{11,... | collective-permute-start | bytes 196616 | tf_op jit(solution)/shard_map/ppermute | solution.py:50
  39.3 1.0 %collective-permute-start.7 = (f32[4,8,512]{2,1,0:T(8,128)S(1)}, f32[4,8,512]{2,1,0:T(8,128)S(1)}, u32[]{:S(2)}, u32[]{:S(2)}) collective-permute-start(f32[4,8,512]{2,1,0:T(8,128)S(1)} %get-tuple-element.49), channel_id=1, source_target_pairs={{0,1},{1,0},{2,3},{3,2},{4,5},{5,4},{6,7},{7,6},{8,9},{9,8},{10,11... | collective-permute-start | bytes 196616 | tf_op jit(solution)/shard_map/ppermute | solution.py:50
  40.3 1.8 %collective-permute-start.8 = (f32[4,8,256]{2,1,0:T(8,128)S(1)}, f32[4,8,256]{2,1,0:T(8,128)S(1)}, u32[]{:S(2)}, u32[]{:S(2)}) collective-permute-start(f32[4,8,256]{2,1,0:T(8,128)S(1)} %get-tuple-element.51.refs_4_.refs_2_), channel_id=1, source_target_pairs={{0,2},{1,3},{2,0},{3,1},{4,6},{5,7},{6,4},{7,5},{8,10},{9,11},{10,... | collective-permute-start | bytes 98312 | tf_op jit(solution)/shard_map/ppermute | solution.py:34
  42.2 3.2 %collective-permute-done.8.refs_3_ = f32[4,8,256]{2,1,0:T(8,128)S(1)} collective-permute-done((f32[4,8,256]{2,1,0:T(8,128)S(1)}, f32[4,8,256]{2,1,0:T(8,128)S(1)}, u32[]{:S(2)}, u32[]{:S(2)}) %collective-permute-start.8) | collective-permute-done | bytes 32800 | tf_op jit(solution)/shard_map/ppermute | solution.py:34
  45.8 1.4 %collective-permute-start.13 = (f32[4,32,256]{2,1,0:T(8,128)S(1)}, f32[4,32,256]{2,1,0:T(8,128)S(1)}, u32[]{:S(2)}, u32[]{:S(2)}) collective-permute-start(f32[4,32,256]{2,1,0:T(8,128)S(1)} %get-tuple-element.56), channel_id=1, source_target_pairs={{0,4},{4,0},{8,12},{12,8},{16,20},{20,16},{24,28},{28,24},{1,5},{5... | collective-permute-start | bytes 393224 | tf_op jit(solution)/shard_map/ppermute | solution.py:50
  47.4 4.5 %collective-permute-done.12.refs_1_ = f32[4,32,256]{2,1,0:T(8,128)S(1)} collective-permute-done((f32[4,32,256]{2,1,0:T(8,128)S(1)}, f32[4,32,256]{2,1,0:T(8,128)S(1)}, u32[]{:S(2)}, u32[]{:S(2)}) %collective-permute-start.12) | collective-permute-done | bytes 131104 | tf_op jit(solution)/shard_map/ppermute | solution.py:50
  51.9 1.0 %shard_map.65 = (f32[7,12,32,256]{3,2,1,0:T(8,128)S(1)}, f32[14,8,512]{2,1,0:T(8,128)S(1)}, f32[14,8,512]{2,1,0:T(8,128)S(1)}) custom-call(f32[4,32,256]{2,1,0:T(8,128)S(1)} %get-tuple-element.54.refs_0_, f32[4,32,256]{2,1,0:T(8,128)S(1)} %collective-permute-done.12.refs_1_, f32[4,32,256]{2,1,0:T(8,128)S(1)} %collective-permute-done.13.refs_2_, ...), custom_call_target="tpu_custom_call" | custom-call | tf_op jit(solution)/shard_map/pallas_call | solution.py:114
  53.0 0.4 collective-permute-start.17
  53.7 9.7 %all_to_all.5.refs_0_ = f32[8,33,128]{2,1,0:T(8,128)S(1)} all-to-all(f32[8,33,128]{2,1,0:T(8,128)S(1)} %shard_map.67), channel_id=1, replica_groups=mesh['gx'=8,'gy'=4] {'gx'}, dimensions={0} | all-to-all | bytes 270336 | tf_op jit(solution)/shard_map/all_to_all | solution.py:634
  63.4 1.2 %shard_map.68.refs_3_ = f32[12,32,256]{2,1,0:T(8,128)S(1)} custom-call(f32[8,33,128]{2,1,0:T(8,128)S(1)} %all_to_all.5.refs_0_, f32[928,256]{1,0:T(8,128)S(1)} %copy-done), custom_call_target="tpu_custom_call" | custom-call | tf_op jit(solution)/shard_map/pallas_call | solution.py:114
  64.7 0.8 %shard_map.69 = (f32[4,16,256]{2,1,0:T(8,128)S(1)}, f32[2,16,256]{2,1,0:T(8,128)S(1)}, f32[2,16,256]{2,1,0:T(8,128)S(1)}) custom-call(f32[7,12,32,256]{3,2,1,0:T(8,128)S(1)} %get-tuple-element.64.refs_0_, f32[14,8,512]{2,1,0:T(8,128)S(1)} %collective-permute-done.16.refs_1_, f32[14,8,512]{2,1,0:T(8,128)S(1)} %collective-permute-done.17.refs_2_, ...), custom_call_target="tpu_custom_call" | custom-call | tf_op jit(solution)/shard_map/pallas_call | solution.py:114
  65.5 0.7 collective-permute-start.19
  66.3 3.5 %collective-permute-done.18.refs_2_ = f32[2,16,256]{2,1,0:T(8,128)S(1)} collective-permute-done((f32[2,16,256]{2,1,0:T(8,128)S(1)}, f32[2,16,256]{2,1,0:T(8,128)S(1)}, u32[]{:S(2)}, u32[]{:S(2)}) %collective-permute-start.18) | collective-permute-done | bytes 32800 | tf_op jit(solution)/shard_map/ppermute | solution.py:50
  69.8 3.5 %shard_map.70 = f32[8,16,512]{2,1,0:T(8,128)} custom-call(f32[16,24,512]{2,1,0:T(8,128)S(1)} %shard_map.66.refs_0_, f32[4,16,256]{2,1,0:T(8,128)S(1)} %get-tuple-element.66.refs_1_, f32[2,16,256]{2,1,0:T(8,128)S(1)} %collective-permute-done.18.refs_2_, f32[2,16,256]{2,1,0:T(8,128)S(1)} %collective-permute-done.19.refs_3_, ...), custom_call_target="tpu_custom_call" | custom-call | tf_op jit(solution)/shard_map/pallas_call | solution.py:114
  (35 shorter events, 2.1 us)
Async XLA Ops:
  0.0 1.0 %copy-start.1 = (bf16[3,8,16,512]{3,2,1,0:T(8,128)(2,1)S(1)}, bf16[3,8,16,512]{3,2,1,0:T(8,128)(2,1)}, u32[]{:S(2)}) copy-start(bf16[3,8,16,512]{3,2,1,0:T(8,128)(2,1)} %refs_1_.3) | copy-start | bytes 1179652
  1.0 0.9 %copy-start.2 = (f32[8,16,512]{2,1,0:T(8,128)S(1)}, f32[8,16,512]{2,1,0:T(8,128)}, u32[]{:S(2)}) copy-start(f32[8,16,512]{2,1,0:T(8,128)} %refs_0_.1) | copy-start | bytes 786436
  3.4 20.7 %collective-permute-start.4 = (f32[32,8,512]{2,1,0:T(8,128)S(1)}, f32[32,8,512]{2,1,0:T(8,128)S(1)}, u32[]{:S(2)}, u32[]{:S(2)}) collective-permute-start(f32[32,8,512]{2,1,0:T(8,128)S(1)} %get-tuple-element.45), channel_id=1, source_target_pairs={{4,8},{8,4},{12,16},{16,12},{20,24},{24,20},{28,0},{0,28},{5,9},{9... | collective-permute-start | bytes 1572872 | tf_op jit(solution)/shard_map/ppermute | solution.py:50
  6.8 17.3 %collective-permute-start.5 = (f32[32,8,512]{2,1,0:T(8,128)S(1)}, f32[32,8,512]{2,1,0:T(8,128)S(1)}, u32[]{:S(2)}, u32[]{:S(2)}) collective-permute-start(f32[32,8,512]{2,1,0:T(8,128)S(1)} %get-tuple-element.46), channel_id=1, source_target_pairs={{0,4},{4,0},{8,12},{12,8},{16,20},{20,16},{24,28},{28,24},{1,5},{5... | collective-permute-start | bytes 1572872 | tf_op jit(solution)/shard_map/ppermute | solution.py:50
  6.8 11.0 %collective-permute-start = (f32[16,8,512]{2,1,0:T(8,128)S(1)}, f32[16,8,512]{2,1,0:T(8,128)S(1)}, u32[]{:S(2)}, u32[]{:S(2)}) collective-permute-start(f32[16,8,512]{2,1,0:T(8,128)S(1)} %get-tuple-element.37), channel_id=1, source_target_pairs={{1,2},{2,1},{3,0},{0,3},{5,6},{6,5},{7,4},{4,7},{9,10},{10,9},{11,... | collective-permute-start | bytes 786440 | tf_op jit(solution)/shard_map/ppermute | solution.py:50
  10.4 12.7 %collective-permute-start.1 = (f32[16,8,512]{2,1,0:T(8,128)S(1)}, f32[16,8,512]{2,1,0:T(8,128)S(1)}, u32[]{:S(2)}, u32[]{:S(2)}) collective-permute-start(f32[16,8,512]{2,1,0:T(8,128)S(1)} %get-tuple-element.38), channel_id=1, source_target_pairs={{0,1},{1,0},{2,3},{3,2},{4,5},{5,4},{6,7},{7,6},{8,9},{9,8},{10,11... | collective-permute-start | bytes 786440 | tf_op jit(solution)/shard_map/ppermute | solution.py:50
  23.2 6.5 %collective-permute-start.2 = (f32[8,8,512]{2,1,0:T(8,128)S(1)}, f32[8,8,512]{2,1,0:T(8,128)S(1)}, u32[]{:S(2)}, u32[]{:S(2)}) collective-permute-start(f32[8,8,512]{2,1,0:T(8,128)S(1)} %get-tuple-element.39.refs_4_), channel_id=1, source_target_pairs={{4,8},{8,4},{12,16},{16,12},{20,24},{24,20},{28,0},{0,28},{5,9},{9... | collective-permute-start | bytes 393224 | tf_op jit(solution)/shard_map/ppermute | solution.py:50
  23.6 6.2 %collective-permute-start.3 = (f32[8,8,512]{2,1,0:T(8,128)S(1)}, f32[8,8,512]{2,1,0:T(8,128)S(1)}, u32[]{:S(2)}, u32[]{:S(2)}) collective-permute-start(f32[8,8,512]{2,1,0:T(8,128)S(1)} %get-tuple-element.40.refs_5_), channel_id=1, source_target_pairs={{0,4},{4,0},{8,12},{12,8},{16,20},{20,16},{24,28},{28,24},{1,5},{5... | collective-permute-start | bytes 393224 | tf_op jit(solution)/shard_map/ppermute | solution.py:50
  24.3 9.8 %collective-permute-start.11 = (f32[13,8,256]{2,1,0:T(8,128)S(1)}, f32[13,8,256]{2,1,0:T(8,128)S(1)}, u32[]{:S(2)}, u32[]{:S(2)}) collective-permute-start(f32[13,8,256]{2,1,0:T(8,128)S(1)} %shard_map.62.refs_0_), channel_id=1, source_target_pairs={{0,2},{1,3},{2,0},{3,1},{4,6},{5,7},{6,4},{7,5},{8,10},{9,11},{10,... | collective-permute-start | bytes 319496 | tf_op jit(solution)/shard_map/ppermute | solution.py:34
  24.9 9.2 %collective-permute-start.10 = (f32[13,8,256]{2,1,0:T(8,128)S(1)}, f32[13,8,256]{2,1,0:T(8,128)S(1)}, u32[]{:S(2)}, u32[]{:S(2)}) collective-permute-start(f32[13,8,256]{2,1,0:T(8,128)S(1)} %shard_map.62.refs_0_), channel_id=1, source_target_pairs={{0,1},{1,0},{2,3},{3,2},{4,5},{5,4},{6,7},{7,6},{8,9},{9,8},{10,11... | collective-permute-start | bytes 319496 | tf_op jit(solution)/shard_map/ppermute | solution.py:50
  26.5 9.4 %collective-permute-start.9 = (f32[13,8,256]{2,1,0:T(8,128)S(1)}, f32[13,8,256]{2,1,0:T(8,128)S(1)}, u32[]{:S(2)}, u32[]{:S(2)}) collective-permute-start(f32[13,8,256]{2,1,0:T(8,128)S(1)} %shard_map.62.refs_0_), channel_id=1, source_target_pairs={{1,2},{2,1},{3,0},{0,3},{5,6},{6,5},{7,4},{4,7},{9,10},{10,9},{11,... | collective-permute-start | bytes 319496 | tf_op jit(solution)/shard_map/ppermute | solution.py:50
  36.1 15.8 %collective-permute-start.14 = (f32[10,32,256]{2,1,0:T(8,128)S(1)}, f32[10,32,256]{2,1,0:T(8,128)S(1)}, u32[]{:S(2)}, u32[]{:S(2)}) collective-permute-start(f32[10,32,256]{2,1,0:T(8,128)S(1)} %get-tuple-element.58), channel_id=1, source_target_pairs={{4,8},{8,4},{12,16},{16,12},{20,24},{24,20},{28,0},{0,28},{5,9},{9... | collective-permute-start | bytes 983048 | tf_op jit(solution)/shard_map/ppermute | solution.py:50
  37.1 14.8 %collective-permute-start.15 = (f32[10,32,256]{2,1,0:T(8,128)S(1)}, f32[10,32,256]{2,1,0:T(8,128)S(1)}, u32[]{:S(2)}, u32[]{:S(2)}) collective-permute-start(f32[10,32,256]{2,1,0:T(8,128)S(1)} %get-tuple-element.59), channel_id=1, source_target_pairs={{0,4},{4,0},{8,12},{12,8},{16,20},{20,16},{24,28},{28,24},{1,5},{5... | collective-permute-start | bytes 983048 | tf_op jit(solution)/shard_map/ppermute | solution.py:50
  37.8 7.6 %collective-permute-start.6 = (f32[4,8,512]{2,1,0:T(8,128)S(1)}, f32[4,8,512]{2,1,0:T(8,128)S(1)}, u32[]{:S(2)}, u32[]{:S(2)}) collective-permute-start(f32[4,8,512]{2,1,0:T(8,128)S(1)} %get-tuple-element.48), channel_id=1, source_target_pairs={{1,2},{2,1},{3,0},{0,3},{5,6},{6,5},{7,4},{4,7},{9,10},{10,9},{11,... | collective-permute-start | bytes 196616 | tf_op jit(solution)/shard_map/ppermute | solution.py:50
  39.3 6.0 %collective-permute-start.7 = (f32[4,8,512]{2,1,0:T(8,128)S(1)}, f32[4,8,512]{2,1,0:T(8,128)S(1)}, u32[]{:S(2)}, u32[]{:S(2)}) collective-permute-start(f32[4,8,512]{2,1,0:T(8,128)S(1)} %get-tuple-element.49), channel_id=1, source_target_pairs={{0,1},{1,0},{2,3},{3,2},{4,5},{5,4},{6,7},{7,6},{8,9},{9,8},{10,11... | collective-permute-start | bytes 196616 | tf_op jit(solution)/shard_map/ppermute | solution.py:50
  40.3 5.0 %collective-permute-start.8 = (f32[4,8,256]{2,1,0:T(8,128)S(1)}, f32[4,8,256]{2,1,0:T(8,128)S(1)}, u32[]{:S(2)}, u32[]{:S(2)}) collective-permute-start(f32[4,8,256]{2,1,0:T(8,128)S(1)} %get-tuple-element.51.refs_4_.refs_2_), channel_id=1, source_target_pairs={{0,2},{1,3},{2,0},{3,1},{4,6},{5,7},{6,4},{7,5},{8,10},{9,11},{10,... | collective-permute-start | bytes 98312 | tf_op jit(solution)/shard_map/ppermute | solution.py:34
  45.4 8.0 %copy-start.4 = (bf16[256,128]{1,0:T(8,128)(2,1)S(1)}, bf16[256,128]{1,0:T(8,128)(2,1)}, u32[]{:S(2)}) copy-start(bf16[256,128]{1,0:T(8,128)(2,1)} %constant.6.clone.refs_1_) | copy-start | bytes 196612
  45.5 6.4 %collective-permute-start.12 = (f32[4,32,256]{2,1,0:T(8,128)S(1)}, f32[4,32,256]{2,1,0:T(8,128)S(1)}, u32[]{:S(2)}, u32[]{:S(2)}) collective-permute-start(f32[4,32,256]{2,1,0:T(8,128)S(1)} %get-tuple-element.55), channel_id=1, source_target_pairs={{4,8},{8,4},{12,16},{16,12},{20,24},{24,20},{28,0},{0,28},{5,9},{9... | collective-permute-start | bytes 393224 | tf_op jit(solution)/shard_map/ppermute | solution.py:50
  45.8 6.1 %collective-permute-start.13 = (f32[4,32,256]{2,1,0:T(8,128)S(1)}, f32[4,32,256]{2,1,0:T(8,128)S(1)}, u32[]{:S(2)}, u32[]{:S(2)}) collective-permute-start(f32[4,32,256]{2,1,0:T(8,128)S(1)} %get-tuple-element.56), channel_id=1, source_target_pairs={{0,4},{4,0},{8,12},{12,8},{16,20},{20,16},{24,28},{28,24},{1,5},{5... | collective-permute-start | bytes 393224 | tf_op jit(solution)/shard_map/ppermute | solution.py:50
  51.9 11.5 %copy-start = (f32[928,256]{1,0:T(8,128)S(1)}, f32[928,256]{1,0:T(8,128)}, u32[]{:S(2)}) copy-start(f32[928,256]{1,0:T(8,128)} %constant.7.clone.refs_1_) | copy-start | bytes 2850820
  52.9 11.8 %collective-permute-start.16 = (f32[14,8,512]{2,1,0:T(8,128)S(1)}, f32[14,8,512]{2,1,0:T(8,128)S(1)}, u32[]{:S(2)}, u32[]{:S(2)}) collective-permute-start(f32[14,8,512]{2,1,0:T(8,128)S(1)} %get-tuple-element.62), channel_id=1, source_target_pairs={{4,8},{8,4},{12,16},{16,12},{20,24},{24,20},{28,0},{0,28},{5,9},{9... | collective-permute-start | bytes 688136 | tf_op jit(solution)/shard_map/ppermute | solution.py:50
  53.0 11.7 %collective-permute-start.17 = (f32[14,8,512]{2,1,0:T(8,128)S(1)}, f32[14,8,512]{2,1,0:T(8,128)S(1)}, u32[]{:S(2)}, u32[]{:S(2)}) collective-permute-start(f32[14,8,512]{2,1,0:T(8,128)S(1)} %get-tuple-element.63), channel_id=1, source_target_pairs={{0,4},{4,0},{8,12},{12,8},{16,20},{20,16},{24,28},{28,24},{1,5},{5... | collective-permute-start | bytes 688136 | tf_op jit(solution)/shard_map/ppermute | solution.py:50
  53.7 16.1 %copy-start.3 = (bf16[256,512]{1,0:T(8,128)(2,1)S(1)}, bf16[256,512]{1,0:T(8,128)(2,1)}, u32[]{:S(2)}) copy-start(bf16[256,512]{1,0:T(8,128)(2,1)} %constant.8.clone.refs_5_) | copy-start | bytes 786436
  65.4 4.3 %collective-permute-start.18 = (f32[2,16,256]{2,1,0:T(8,128)S(1)}, f32[2,16,256]{2,1,0:T(8,128)S(1)}, u32[]{:S(2)}, u32[]{:S(2)}) collective-permute-start(f32[2,16,256]{2,1,0:T(8,128)S(1)} %get-tuple-element.67), channel_id=1, source_target_pairs={{4,8},{8,4},{12,16},{16,12},{20,24},{24,20},{28,0},{0,28},{5,9},{9... | collective-permute-start | bytes 98312 | tf_op jit(solution)/shard_map/ppermute | solution.py:50
  65.5 4.2 %collective-permute-start.19 = (f32[2,16,256]{2,1,0:T(8,128)S(1)}, f32[2,16,256]{2,1,0:T(8,128)S(1)}, u32[]{:S(2)}, u32[]{:S(2)}) collective-permute-start(f32[2,16,256]{2,1,0:T(8,128)S(1)} %get-tuple-element.68), channel_id=1, source_target_pairs={{0,4},{4,0},{8,12},{12,8},{16,20},{20,16},{24,28},{28,24},{1,5},{5... | collective-permute-start | bytes 98312 | tf_op jit(solution)/shard_map/ppermute | solution.py:50

commit v6 on v5

--- a/solution.py
+++ b/solution.py
@@ -274,13 +274,11 @@
     v[r] = jnp.where(parity == (r & 1), b[r] * inverse, 0.0)
 
 
-def assemble_kernel(src, face, up, down, right, left, state):
-    b, wx, wy, wz, rdiag, diag, v = (state.at[i] for i in range(7))
+def assemble_kernel(src, face, up, down, state):
+    ext = [state.at[i] for i in range(4)]
     rows, cols, depth = src.shape
-    ext = (b, wx, wy, wz)
-    ec = cols + 2 * H
     for r in range(rows):
-        b[H + r, H : H + cols] = src[r]
+        ext[0][H + r, H : H + cols] = src[r]
         for d in range(3):
             ext[1 + d][H + r, H : H + cols] = face[d, r].astype(F32)
     tiles = cols // 8
@@ -289,31 +287,21 @@
             for k in range(H):
                 for t in range(tiles):
                     ext[a][base + k, H + 8 * t : H + 8 * t + 8] = msg[(a * H + k) * tiles + t]
+
+
+def pre_kernel(up, down, right, left, pairs, state, kept, v_own, right1, to_right, to_left, *scratch):
+    t512, t256, diag, v = scratch
+    b, wx, wy, wz, rdiag = (kept.at[i] for i in range(5))
+    kept[0:4] = state[...]
+    ext = (b, wx, wy, wz)
+    rows, cols, depth = v_own.shape
+    er, ec = rows + 2 * H, cols + 2 * H
+    rows1, cols1 = rows // 2, cols // 2
     for msg, base in ((right, 0), (left, H + cols)):
         for r in range(rows):
             for t, pair in enumerate(((0, 3), (1, 2))):
                 for s, a in enumerate(pair):
                     ext[a][H + r, base : base + H] = msg[2 * r + t, H * s : H * s + H]
-    parity = parity2((ec, depth))
-    low_col = lax.broadcasted_iota(jnp.int32, (ec, depth), 0) == 0
-
-    def body(r, carry):
-        diagonal_row(r, parity, low_col, b, wx, wy, wz, diag, rdiag, v)
-        return carry
-
-    lax.fori_loop(H + 1, H + rows, body, 0)
-
-
-def pre_kernel(up, down, pairs, state, kept, v_own, right1, to_right, to_left, *scratch):
-    t512, t256, diag, v = scratch
-    b, wx, wy, wz, rdiag = (kept.at[i] for i in range(5))
-    kept[...] = state[0:5]
-    diag[...] = state[5]
-    v[...] = state[6]
-    ext = (b, wx, wy, wz)
-    rows, cols, depth = v_own.shape
-    er, ec = rows + 2 * H, cols + 2 * H
-    rows1, cols1 = rows // 2, cols // 2
     tiles = len(CORNER0) // 8
     for msg, sx, sy in ((up, 1, 1), (up, 1, -1), (down, -1, 1), (down, -1, -1)):
         start = 0 if sy > 0 else tiles
@@ -326,8 +314,13 @@
             ext[a][r, c : c + 1] = msg[start + n // 8, n % 8 : n % 8 + 1]
     parity = parity2((ec, depth))
     low_col = lax.broadcasted_iota(jnp.int32, (ec, depth), 0) == 0
-    for r in (*range(H + 1), *range(H + rows, er)):
+    diagonal_row(0, parity, low_col, b, wx, wy, wz, diag, rdiag, v)
+
+    def diagonal_body(r, carry):
         diagonal_row(r, parity, low_col, b, wx, wy, wz, diag, rdiag, v)
+        return carry
+
+    lax.fori_loop(1, er, diagonal_body, 0, unroll=UNROLL)
     half_sweep(1, er - 1, 1, parity, v, b, wx, wy, wz, rdiag)
     half_sweep(2, er - 2, 0, parity, v, b, wx, wy, wz, rdiag)
     half_sweep(3, er - 3, 1, parity, v, b, wx, wy, wz, rdiag)
@@ -571,10 +564,27 @@
     to_down[...] = own[0:h]
 
 
-def spread_kernel(v0_rows, up, down, v):
-    er, ec, _ = v.shape
+def spread_rows(lines, spread, used):
+    rows, padded, _ = lines.shape
+    wide = dot_exact(lines.reshape(rows * padded, lines.shape[2]), spread)
+    depth = wide.shape[1]
+    wide = wide.reshape(rows, padded, depth)
+    out = []
+    for n in range(rows):
+        line = jnp.broadcast_to(wide[n, 0:used][:, None, :], (used, 2, depth))
+        out.append(line.reshape(2 * used, depth))
+    return out
+
+
+def post_sweep(n, rows, v, kept, parity):
+    b, wx, wy, wz, rdiag = (kept.at[i] for i in range(5))
+    for first, last in rows:
+        half_sweep(first, last, n % 2, parity, v, b, wx, wy, wz, rdiag)
+
+
+def inner_kernel(v0_rows, up, down, own, kept, spread, v):
+    er, ec, depth = v.shape
     rows = er - 2 * H
-    v[H : H + rows] = v0_rows[...]
     tiles = ec // 8
     for msg, base in ((up, 0), (down, H + rows)):
         start = msg.shape[0] - (H // 2) * tiles
@@ -583,31 +593,30 @@
                 tile = msg[start + k * tiles + t]
                 v[base + 2 * k, 8 * t : 8 * t + 8] = tile
                 v[base + 2 * k + 1, 8 * t : 8 * t + 8] = tile
-
-
-def post_kernel(v_in, rows_own, up1, down1, kept, spread, out, v, t256):
-    b, wx, wy, wz, rdiag = (kept.at[i] for i in range(5))
+    for n, line in enumerate(spread_rows(own[...], spread[...], ec // 2)):
+        v[H + 2 * n] = v0_rows[2 * n] + line
+        v[H + 2 * n + 1] = v0_rows[2 * n + 1] + line
+    parity = parity2((ec, depth))
+    for n in range(H - 1):
+        if H + 1 + n < er - H - 1 - n:
+            post_sweep(n, ((H + 1 + n, er - H - 1 - n),), v, kept, parity)
+
+
+def post_kernel(v_in, up1, down1, kept, spread, out, v):
     rows, cols, depth = out.shape
-    rows1, wide1, half = rows_own.shape
     er, ec = rows + 2 * H, cols + 2 * H
-    h = H // 2
-    ec1 = cols // 2 + 2 * h
-    n1 = rows1 + 2 * h
-    t256[0:h] = up1[...]
-    t256[h : h + rows1] = rows_own[...]
-    t256[h + rows1 :] = down1[...]
-    wide = dot_exact(t256[...].reshape(n1 * t256.shape[1], half), spread[...])
-    wide = wide.reshape(n1, t256.shape[1], depth)
-    for n in range(n1):
-        line = wide[n, 0:ec1]
-        line = jnp.broadcast_to(line[:, None, :], (ec1, 2, depth)).reshape(2 * ec1, depth)
-        v[2 * n] = v_in[2 * n] + line
-        v[2 * n + 1] = v_in[2 * n + 1] + line
+    v[H : H + rows] = v_in[H : H + rows]
+    for msg, base in ((up1, 0), (down1, H + rows)):
+        for n, line in enumerate(spread_rows(msg[...], spread[...], ec // 2)):
+            v[base + 2 * n] = v_in[base + 2 * n] + line
+            v[base + 2 * n + 1] = v_in[base + 2 * n + 1] + line
     parity = parity2((ec, depth))
-    half_sweep(1, er - 1, 0, parity, v, b, wx, wy, wz, rdiag)
-    half_sweep(2, er - 2, 1, parity, v, b, wx, wy, wz, rdiag)
-    half_sweep(3, er - 3, 0, parity, v, b, wx, wy, wz, rdiag)
-    half_sweep(4, er - 4, 1, parity, v, b, wx, wy, wz, rdiag)
+    for n in range(H):
+        low, high = H + 1 + n, er - H - 1 - n
+        if n < H - 1 and low < high:
+            post_sweep(n, ((1 + n, low), (high, er - 1 - n)), v, kept, parity)
+        else:
+            post_sweep(n, ((1 + n, er - 1 - n),), v, kept, parity)
     for r in range(rows):
         out[r] = v[H + r, H : H + cols]
 
@@ -708,35 +717,36 @@
         scratch=[pltpu.SemaphoreType.DMA((2,))],
     )
     y_first = y_first.exchanged()
+    (x_first,) = call(pack_x_kernel, [Beside("gx", (4 * H * (cols // 8), 8, depth))], source, face_coef)
+    x_first = x_first.exchanged()
     block, pairs = call(
         coarsen_kernel,
         [(3 * rows1, cols1, depth1), jax.ShapeDtypeStruct((depth, depth1), BF16)],
         face_coef,
+        near=(x_first,),
         scratch=[pltpu.VMEM((depth, depth1), BF16), (depth1 // 128, cols, 128)],
     )
-    (x_first,) = call(pack_x_kernel, [Beside("gx", (4 * H * (cols // 8), 8, depth))], source, face_coef, near=(block,))
-    x_first = x_first.exchanged()
+    (block,) = call(
+        before_kernel,
+        [(3 * rows1 + 1, cols1, depth1)],
+        block, x_first, pairs,
+        scratch=[(depth1 // 128, cols, 128)],
+    )
     (corners,) = call(
         functools.partial(forward_kernel, rows=rows),
         [Beside("gx", (2 * corner_tiles, 8, depth))],
         y_first,
-    )
-    (block,) = call(
-        before_kernel,
-        [(3 * rows1 + 1, cols1, depth1)],
-        block, x_first, pairs,
-        near=(corners,),
-        scratch=[(depth1 // 128, cols, 128)],
+        near=(block,),
     )
     corners = corners.exchanged()
     blocks = Beside("gy", block.shape, block, block).exchanged()
     blocks_between = [moved(block, "gy", -k) for k in range(2, count - 1)]
-    (state,) = call(assemble_kernel, [(7, er, ec, depth)], source, face_coef, x_first, y_first)
+    (state,) = call(assemble_kernel, [(4, er, ec, depth)], source, face_coef, x_first)
     kept, v0, right1, y_second = call(
         pre_kernel,
         [(5, er, ec, depth), (rows, cols, depth), (rows1, cols1, depth1)]
         + [Beside("gy", (rows * h // 8 + rows1 // 2, 8, depth))],
-        corners, pairs, state,
+        corners, y_first, pairs, state,
         scratch=[(rows1, ec, depth), (depth1 // 128, rows1 * ec, 128)] + [(er, ec, depth)] * 2,
     )
 
@@ -783,14 +793,9 @@
         limit=limit,
     )
     x_fourth = x_fourth.exchanged()
-    (v0e,) = call(spread_kernel, [(er, ec, depth)], v0_rows, x_third)
-    (out,) = call(
-        post_kernel,
-        [(rows, cols, depth)],
-        v0e, own, x_fourth, kept,
-        jnp.asarray(np.ascontiguousarray(pair_table(depth).T)),
-        scratch=[(er, ec, depth), (rows1 + 2 * h, used, depth1)],
-    )
+    spread = jnp.asarray(np.ascontiguousarray(pair_table(depth).T))
+    (v,) = call(inner_kernel, [(er, ec, depth)], v0_rows, x_third, own, kept, spread)
+    (out,) = call(post_kernel, [(rows, cols, depth)], v, x_fourth, kept, spread, scratch=[(er, ec, depth)])
     return out
 
 

time: 73.5 us -> 71.3 us (0.970)
  waiting for transfers between devices: 26.9 us -> 24.9 us
    ppermute x18, waiting for transfers between devices: 22.5 us -> 21.1 us  [exchanged(): got.append(lax.ppermute(block, self.axis, route))]
  transfers between devices with their start and end apart: 20 -> 20, of which waited for: 7 -> 8; matrix products, arithmetic and copies ran while one was open for 0% -> 0% of each run, Pallas kernels for 8% -> 11%
where the time goes in v6:
time: 71.3 us; the launch traced here: 71.1 us
  waiting for transfers between devices  24.9 us (35%)
  starting transfers between devices  21.6 us (30%)
  Pallas kernels  13 us (18%)
  blocking collectives  9.55 us (13%)
  local copies, waits for them, and re-layouts  1.97 us (3%)
    ppermute x18, waiting for transfers between devices, exchanged(): got.append(lax.ppermute(block, self.axis, route))  21.1 us
    ppermute x18, starting transfers between devices, exchanged(): got.append(lax.ppermute(block, self.axis, route))  19 us
    pallas_call x16, Pallas kernels, call(): pl.pallas_call(body, out_shape=[s if hasattr(s, 'dtype') else jax.ShapeDt...  13 us
    all_to_all x1, blocking collectives, coarse_correction(): got = lax.all_to_all(chunks, 'gx', 0, 0)  9.55 us
    ppermute x2, waiting for transfers between devices, moved(): lax.ppermute(block, axis, [(i, (i + distance) % count) for i in range(cou...  3.82 us
    ppermute x2, starting transfers between devices, moved(): lax.ppermute(block, axis, [(i, (i + distance) % count) for i in range(cou...  2.52 us
    unnamed x10, local copies, waits for them, and re-layouts  1.97 us
  transfers between devices with their start and end apart: 20, of which 8 were waited for; matrix products, arithmetic and copies ran while one was open for 0% of the time, Pallas kernels for 11%

profile of v6, /device:TPU:0, one launch (start us, length us, event | category | flops | bytes accessed | tf_op | source)
XLA Modules:
  0.0 71.1 jit_solution(16969719005593781611)
XLA Ops:
  0.0 1.0 %copy-done.2 = bf16[3,8,16,512]{3,2,1,0:T(8,128)(2,1)S(1)} copy-done((bf16[3,8,16,512]{3,2,1,0:T(8,128)(2,1)S(1)}, bf16[3,8,16,512]{3,2,1,0:T(8,128)(2,1)}, u32[]{:S(2)}) %copy-start.2) | copy-done | bytes 393240
  1.0 0.9 %copy-done.3 = f32[8,16,512]{2,1,0:T(8,128)S(1)} copy-done((f32[8,16,512]{2,1,0:T(8,128)S(1)}, f32[8,16,512]{2,1,0:T(8,128)}, u32[]{:S(2)}) %copy-start.3) | copy-done | bytes 262168
  2.5 3.4 %collective-permute-start.2 = (f32[32,8,512]{2,1,0:T(8,128)S(1)}, f32[32,8,512]{2,1,0:T(8,128)S(1)}, u32[]{:S(2)}, u32[]{:S(2)}) collective-permute-start(f32[32,8,512]{2,1,0:T(8,128)S(1)} %get-tuple-element.41), channel_id=1, source_target_pairs={{4,8},{8,4},{12,16},{16,12},{20,24},{24,20},{28,0},{0,28},{5,9},{9... | collective-permute-start | bytes 1572872 | tf_op jit(solution)/shard_map/ppermute | solution.py:50
  5.9 3.6 %collective-permute-start = (f32[16,8,512]{2,1,0:T(8,128)S(1)}, f32[16,8,512]{2,1,0:T(8,128)S(1)}, u32[]{:S(2)}, u32[]{:S(2)}) collective-permute-start(f32[16,8,512]{2,1,0:T(8,128)S(1)} %get-tuple-element.37), channel_id=1, source_target_pairs={{1,2},{2,1},{3,0},{0,3},{5,6},{6,5},{7,4},{4,7},{9,10},{10,9},{11,... | collective-permute-start | bytes 786440 | tf_op jit(solution)/shard_map/ppermute | solution.py:50
  9.5 8.0 %collective-permute-done.2.refs_1_.refs_2_ = f32[32,8,512]{2,1,0:T(8,128)S(1)} collective-permute-done((f32[32,8,512]{2,1,0:T(8,128)S(1)}, f32[32,8,512]{2,1,0:T(8,128)S(1)}, u32[]{:S(2)}, u32[]{:S(2)}) %collective-permute-start.2) | collective-permute-done | bytes 524320 | tf_op jit(solution)/shard_map/ppermute | solution.py:50
  17.6 0.9 %shard_map.57 = (f32[12,8,256]{2,1,0:T(8,128)S(1)}, bf16[512,256]{1,0:T(8,128)(2,1)S(1)}) custom-call(bf16[3,8,16,512]{3,2,1,0:T(8,128)(2,1)S(1)} %get-tuple-element.39.refs_1_.refs_0_, f32[32,8,512]{2,1,0:T(8,128)S(1)} %collective-permute-done.2.refs_1_.refs_2_, f32[32,8,512]{2,1,0:T(8,128)S(1)} %collective-permute-done.3.refs_2_.refs_3_), custom_call_target="tpu_custom_call" | custom-call | tf_op jit(solution)/shard_map/pallas_call | solution.py:114
  18.6 3.6 %collective-permute-done.1.refs_1_.refs_3_ = f32[16,8,512]{2,1,0:T(8,128)S(1)} collective-permute-done((f32[16,8,512]{2,1,0:T(8,128)S(1)}, f32[16,8,512]{2,1,0:T(8,128)S(1)}, u32[]{:S(2)}, u32[]{:S(2)}) %collective-permute-start.1) | collective-permute-done | bytes 262176 | tf_op jit(solution)/shard_map/ppermute | solution.py:50
  22.7 0.6 collective-permute-start.5
  23.2 0.7 collective-permute-start.11
  23.9 1.6 %collective-permute-start.10 = (f32[13,8,256]{2,1,0:T(8,128)S(1)}, f32[13,8,256]{2,1,0:T(8,128)S(1)}, u32[]{:S(2)}, u32[]{:S(2)}) collective-permute-start(f32[13,8,256]{2,1,0:T(8,128)S(1)} %shard_map.58.refs_2_.refs_0_), channel_id=1, source_target_pairs={{0,1},{1,0},{2,3},{3,2},{4,5},{5,4},{6,7},{7,6},{8,9},{9,8},{10,11... | collective-permute-start | bytes 319496 | tf_op jit(solution)/shard_map/ppermute | solution.py:50
  25.5 2.1 %collective-permute-start.9 = (f32[13,8,256]{2,1,0:T(8,128)S(1)}, f32[13,8,256]{2,1,0:T(8,128)S(1)}, u32[]{:S(2)}, u32[]{:S(2)}) collective-permute-start(f32[13,8,256]{2,1,0:T(8,128)S(1)} %shard_map.58.refs_2_.refs_0_), channel_id=1, source_target_pairs={{1,2},{2,1},{3,0},{0,3},{5,6},{6,5},{7,4},{4,7},{9,10},{10,9},{11,... | collective-permute-start | bytes 319496 | tf_op jit(solution)/shard_map/ppermute | solution.py:50
  27.9 0.7 collective-permute-done.4.refs_0_
  28.6 3.8 %shard_map.61 = (f32[5,16,24,512]{3,2,1,0:T(8,128)S(1)}, f32[8,16,512]{2,1,0:T(8,128)S(1)}, f32[4,8,256]{2,1,0:T(8,128)S(1)}, f32[4,8,512]{2,1,0:T(8,128)S(1)}, f32[4,8,512]{2,1,0:T(8,128)S(1)}) custom-call(f32[8,8,512]{2,1,0:T(8,128)S(1)} %collective-permute-done.4.refs_0_, f32[8,8,512]{2,1,0:T(8,128)S(1)} %collective-permute-done.5.refs_1_, ...), custom_call_target="tpu_custom_call" | custom-call | tf_op jit(solution)/shard_map/pallas_call | solution.py:114
  32.4 0.6 collective-permute-done.11.refs_3_
  33.0 1.8 %collective-permute-done.9.refs_1_ = f32[13,8,256]{2,1,0:T(8,128)S(1)} collective-permute-done((f32[13,8,256]{2,1,0:T(8,128)S(1)}, f32[13,8,256]{2,1,0:T(8,128)S(1)}, u32[]{:S(2)}, u32[]{:S(2)}) %collective-permute-start.9) | collective-permute-done | bytes 106528 | tf_op jit(solution)/shard_map/ppermute | solution.py:50
  35.1 1.0 %collective-permute-start.14 = (f32[10,32,256]{2,1,0:T(8,128)S(1)}, f32[10,32,256]{2,1,0:T(8,128)S(1)}, u32[]{:S(2)}, u32[]{:S(2)}) collective-permute-start(f32[10,32,256]{2,1,0:T(8,128)S(1)} %get-tuple-element.58), channel_id=1, source_target_pairs={{4,8},{8,4},{12,16},{16,12},{20,24},{24,20},{28,0},{0,28},{5,9},{9... | collective-permute-start | bytes 983048 | tf_op jit(solution)/shard_map/ppermute | solution.py:50
  36.1 0.7 collective-permute-start.15
  36.7 1.6 %collective-permute-start.6 = (f32[4,8,512]{2,1,0:T(8,128)S(1)}, f32[4,8,512]{2,1,0:T(8,128)S(1)}, u32[]{:S(2)}, u32[]{:S(2)}) collective-permute-start(f32[4,8,512]{2,1,0:T(8,128)S(1)} %get-tuple-element.48), channel_id=1, source_target_pairs={{1,2},{2,1},{3,0},{0,3},{5,6},{6,5},{7,4},{4,7},{9,10},{10,9},{11,... | collective-permute-start | bytes 196616 | tf_op jit(solution)/shard_map/ppermute | solution.py:50
  38.3 1.0 %collective-permute-start.7 = (f32[4,8,512]{2,1,0:T(8,128)S(1)}, f32[4,8,512]{2,1,0:T(8,128)S(1)}, u32[]{:S(2)}, u32[]{:S(2)}) collective-permute-start(f32[4,8,512]{2,1,0:T(8,128)S(1)} %get-tuple-element.49), channel_id=1, source_target_pairs={{0,1},{1,0},{2,3},{3,2},{4,5},{5,4},{6,7},{7,6},{8,9},{9,8},{10,11... | collective-permute-start | bytes 196616 | tf_op jit(solution)/shard_map/ppermute | solution.py:50
  39.3 1.8 %collective-permute-start.8 = (f32[4,8,256]{2,1,0:T(8,128)S(1)}, f32[4,8,256]{2,1,0:T(8,128)S(1)}, u32[]{:S(2)}, u32[]{:S(2)}) collective-permute-start(f32[4,8,256]{2,1,0:T(8,128)S(1)} %get-tuple-element.51.refs_4_.refs_2_), channel_id=1, source_target_pairs={{0,2},{1,3},{2,0},{3,1},{4,6},{5,7},{6,4},{7,5},{8,10},{9,11},{10,... | collective-permute-start | bytes 98312 | tf_op jit(solution)/shard_map/ppermute | solution.py:34
  41.1 3.2 %collective-permute-done.8.refs_3_ = f32[4,8,256]{2,1,0:T(8,128)S(1)} collective-permute-done((f32[4,8,256]{2,1,0:T(8,128)S(1)}, f32[4,8,256]{2,1,0:T(8,128)S(1)}, u32[]{:S(2)}, u32[]{:S(2)}) %collective-permute-start.8) | collective-permute-done | bytes 32800 | tf_op jit(solution)/shard_map/ppermute | solution.py:34
  44.4 0.5 collective-permute-start.12
  44.9 1.3 %collective-permute-start.13 = (f32[4,32,256]{2,1,0:T(8,128)S(1)}, f32[4,32,256]{2,1,0:T(8,128)S(1)}, u32[]{:S(2)}, u32[]{:S(2)}) collective-permute-start(f32[4,32,256]{2,1,0:T(8,128)S(1)} %get-tuple-element.56), channel_id=1, source_target_pairs={{0,4},{4,0},{8,12},{12,8},{16,20},{20,16},{24,28},{28,24},{1,5},{5... | collective-permute-start | bytes 393224 | tf_op jit(solution)/shard_map/ppermute | solution.py:50
  46.3 4.5 %collective-permute-done.12.refs_1_ = f32[4,32,256]{2,1,0:T(8,128)S(1)} collective-permute-done((f32[4,32,256]{2,1,0:T(8,128)S(1)}, f32[4,32,256]{2,1,0:T(8,128)S(1)}, u32[]{:S(2)}, u32[]{:S(2)}) %collective-permute-start.12) | collective-permute-done | bytes 131104 | tf_op jit(solution)/shard_map/ppermute | solution.py:50
  50.9 1.0 %shard_map.65 = (f32[7,12,32,256]{3,2,1,0:T(8,128)S(1)}, f32[14,8,512]{2,1,0:T(8,128)S(1)}, f32[14,8,512]{2,1,0:T(8,128)S(1)}) custom-call(f32[4,32,256]{2,1,0:T(8,128)S(1)} %get-tuple-element.54.refs_0_, f32[4,32,256]{2,1,0:T(8,128)S(1)} %collective-permute-done.12.refs_1_, f32[4,32,256]{2,1,0:T(8,128)S(1)} %collective-permute-done.13.refs_2_, ...), custom_call_target="tpu_custom_call" | custom-call | tf_op jit(solution)/shard_map/pallas_call | solution.py:114
  52.8 9.5 %all_to_all.5.refs_0_ = f32[8,33,128]{2,1,0:T(8,128)S(1)} all-to-all(f32[8,33,128]{2,1,0:T(8,128)S(1)} %shard_map.66), channel_id=1, replica_groups=mesh['gx'=8,'gy'=4] {'gx'}, dimensions={0} | all-to-all | bytes 270336 | tf_op jit(solution)/shard_map/all_to_all | solution.py:643
  62.3 1.2 %shard_map.67.refs_3_ = f32[12,32,256]{2,1,0:T(8,128)S(1)} custom-call(f32[8,33,128]{2,1,0:T(8,128)S(1)} %all_to_all.5.refs_0_, f32[928,256]{1,0:T(8,128)S(1)} %copy-done.1), custom_call_target="tpu_custom_call" | custom-call | tf_op jit(solution)/shard_map/pallas_call | solution.py:114
  63.6 0.8 %shard_map.68 = (f32[4,16,256]{2,1,0:T(8,128)S(1)}, f32[2,16,256]{2,1,0:T(8,128)S(1)}, f32[2,16,256]{2,1,0:T(8,128)S(1)}) custom-call(f32[7,12,32,256]{3,2,1,0:T(8,128)S(1)} %get-tuple-element.64.refs_0_, f32[14,8,512]{2,1,0:T(8,128)S(1)} %collective-permute-done.16.refs_1_, f32[14,8,512]{2,1,0:T(8,128)S(1)} %collective-permute-done.17.refs_2_, ...), custom_call_target="tpu_custom_call" | custom-call | tf_op jit(solution)/shard_map/pallas_call | solution.py:114
  64.6 0.5 collective-permute-start.19
  65.1 1.1 %shard_map.69.refs_0_ = f32[16,24,512]{2,1,0:T(8,128)S(1)} custom-call(f32[8,24,512]{2,1,0:T(8,128)S(1)} %get-tuple-element.50.refs_0_, f32[14,8,512]{2,1,0:T(8,128)S(1)} %collective-permute-done.16.refs_1_, f32[14,8,512]{2,1,0:T(8,128)S(1)} %collective-permute-done.17.refs_2_, f32[4,16,256]{2,1,0:T(8,128)S(1)} %get-tuple-element.66.refs_3_, ...), custom_call_target="tpu_custom_call" | custom-call | tf_op jit(solution)/shard_map/pallas_call | solution.py:114
  66.3 2.4 %collective-permute-done.18.refs_1_ = f32[2,16,256]{2,1,0:T(8,128)S(1)} collective-permute-done((f32[2,16,256]{2,1,0:T(8,128)S(1)}, f32[2,16,256]{2,1,0:T(8,128)S(1)}, u32[]{:S(2)}, u32[]{:S(2)}) %collective-permute-start.18) | collective-permute-done | bytes 32800 | tf_op jit(solution)/shard_map/ppermute | solution.py:50
  68.7 2.4 %shard_map.70 = f32[8,16,512]{2,1,0:T(8,128)} custom-call(f32[16,24,512]{2,1,0:T(8,128)S(1)} %shard_map.69.refs_0_, f32[2,16,256]{2,1,0:T(8,128)S(1)} %collective-permute-done.18.refs_1_, f32[2,16,256]{2,1,0:T(8,128)S(1)} %collective-permute-done.19.refs_2_, f32[5,16,24,512]{3,2,1,0:T(8,128)S(1)} %get-tuple-element.53.refs_5_.refs_8_.refs_4_.refs_3_, ...), custom_call_target="tpu_custom_call" | custom-call | tf_op jit(solution)/shard_map/pallas_call | solution.py:114
  (35 shorter events, 3.1 us)
Async XLA Ops:
  0.0 1.0 %copy-start.2 = (bf16[3,8,16,512]{3,2,1,0:T(8,128)(2,1)S(1)}, bf16[3,8,16,512]{3,2,1,0:T(8,128)(2,1)}, u32[]{:S(2)}) copy-start(bf16[3,8,16,512]{3,2,1,0:T(8,128)(2,1)} %refs_1_.3) | copy-start | bytes 1179652
  1.0 0.9 %copy-start.3 = (f32[8,16,512]{2,1,0:T(8,128)S(1)}, f32[8,16,512]{2,1,0:T(8,128)}, u32[]{:S(2)}) copy-start(f32[8,16,512]{2,1,0:T(8,128)} %refs_0_.1) | copy-start | bytes 786436
  2.5 15.1 %collective-permute-start.2 = (f32[32,8,512]{2,1,0:T(8,128)S(1)}, f32[32,8,512]{2,1,0:T(8,128)S(1)}, u32[]{:S(2)}, u32[]{:S(2)}) collective-permute-start(f32[32,8,512]{2,1,0:T(8,128)S(1)} %get-tuple-element.41), channel_id=1, source_target_pairs={{4,8},{8,4},{12,16},{16,12},{20,24},{24,20},{28,0},{0,28},{5,9},{9... | collective-permute-start | bytes 1572872 | tf_op jit(solution)/shard_map/ppermute | solution.py:50
  5.9 11.7 %collective-permute-start.3 = (f32[32,8,512]{2,1,0:T(8,128)S(1)}, f32[32,8,512]{2,1,0:T(8,128)S(1)}, u32[]{:S(2)}, u32[]{:S(2)}) collective-permute-start(f32[32,8,512]{2,1,0:T(8,128)S(1)} %get-tuple-element.42), channel_id=1, source_target_pairs={{0,4},{4,0},{8,12},{12,8},{16,20},{20,16},{24,28},{28,24},{1,5},{5... | collective-permute-start | bytes 1572872 | tf_op jit(solution)/shard_map/ppermute | solution.py:50
  5.9 12.7 %collective-permute-start = (f32[16,8,512]{2,1,0:T(8,128)S(1)}, f32[16,8,512]{2,1,0:T(8,128)S(1)}, u32[]{:S(2)}, u32[]{:S(2)}) collective-permute-start(f32[16,8,512]{2,1,0:T(8,128)S(1)} %get-tuple-element.37), channel_id=1, source_target_pairs={{1,2},{2,1},{3,0},{0,3},{5,6},{6,5},{7,4},{4,7},{9,10},{10,9},{11,... | collective-permute-start | bytes 786440 | tf_op jit(solution)/shard_map/ppermute | solution.py:50
  9.5 12.7 %collective-permute-start.1 = (f32[16,8,512]{2,1,0:T(8,128)S(1)}, f32[16,8,512]{2,1,0:T(8,128)S(1)}, u32[]{:S(2)}, u32[]{:S(2)}) collective-permute-start(f32[16,8,512]{2,1,0:T(8,128)S(1)} %get-tuple-element.38), channel_id=1, source_target_pairs={{0,1},{1,0},{2,3},{3,2},{4,5},{5,4},{6,7},{7,6},{8,9},{9,8},{10,11... | collective-permute-start | bytes 786440 | tf_op jit(solution)/shard_map/ppermute | solution.py:50
  22.4 6.2 %collective-permute-start.4 = (f32[8,8,512]{2,1,0:T(8,128)S(1)}, f32[8,8,512]{2,1,0:T(8,128)S(1)}, u32[]{:S(2)}, u32[]{:S(2)}) collective-permute-start(f32[8,8,512]{2,1,0:T(8,128)S(1)} %get-tuple-element.45), channel_id=1, source_target_pairs={{4,8},{8,4},{12,16},{16,12},{20,24},{24,20},{28,0},{0,28},{5,9},{9... | collective-permute-start | bytes 393224 | tf_op jit(solution)/shard_map/ppermute | solution.py:50
  22.7 5.9 %collective-permute-start.5 = (f32[8,8,512]{2,1,0:T(8,128)S(1)}, f32[8,8,512]{2,1,0:T(8,128)S(1)}, u32[]{:S(2)}, u32[]{:S(2)}) collective-permute-start(f32[8,8,512]{2,1,0:T(8,128)S(1)} %get-tuple-element.46), channel_id=1, source_target_pairs={{0,4},{4,0},{8,12},{12,8},{16,20},{20,16},{24,28},{28,24},{1,5},{5... | collective-permute-start | bytes 393224 | tf_op jit(solution)/shard_map/ppermute | solution.py:50
  23.2 9.8 %collective-permute-start.11 = (f32[13,8,256]{2,1,0:T(8,128)S(1)}, f32[13,8,256]{2,1,0:T(8,128)S(1)}, u32[]{:S(2)}, u32[]{:S(2)}) collective-permute-start(f32[13,8,256]{2,1,0:T(8,128)S(1)} %shard_map.58.refs_2_.refs_0_), channel_id=1, source_target_pairs={{0,2},{1,3},{2,0},{3,1},{4,6},{5,7},{6,4},{7,5},{8,10},{9,11},{10,... | collective-permute-start | bytes 319496 | tf_op jit(solution)/shard_map/ppermute | solution.py:34
  23.9 9.1 %collective-permute-start.10 = (f32[13,8,256]{2,1,0:T(8,128)S(1)}, f32[13,8,256]{2,1,0:T(8,128)S(1)}, u32[]{:S(2)}, u32[]{:S(2)}) collective-permute-start(f32[13,8,256]{2,1,0:T(8,128)S(1)} %shard_map.58.refs_2_.refs_0_), channel_id=1, source_target_pairs={{0,1},{1,0},{2,3},{3,2},{4,5},{5,4},{6,7},{7,6},{8,9},{9,8},{10,11... | collective-permute-start | bytes 319496 | tf_op jit(solution)/shard_map/ppermute | solution.py:50
  25.5 9.3 %collective-permute-start.9 = (f32[13,8,256]{2,1,0:T(8,128)S(1)}, f32[13,8,256]{2,1,0:T(8,128)S(1)}, u32[]{:S(2)}, u32[]{:S(2)}) collective-permute-start(f32[13,8,256]{2,1,0:T(8,128)S(1)} %shard_map.58.refs_2_.refs_0_), channel_id=1, source_target_pairs={{1,2},{2,1},{3,0},{0,3},{5,6},{6,5},{7,4},{4,7},{9,10},{10,9},{11,... | collective-permute-start | bytes 319496 | tf_op jit(solution)/shard_map/ppermute | solution.py:50
  35.1 15.8 %collective-permute-start.14 = (f32[10,32,256]{2,1,0:T(8,128)S(1)}, f32[10,32,256]{2,1,0:T(8,128)S(1)}, u32[]{:S(2)}, u32[]{:S(2)}) collective-permute-start(f32[10,32,256]{2,1,0:T(8,128)S(1)} %get-tuple-element.58), channel_id=1, source_target_pairs={{4,8},{8,4},{12,16},{16,12},{20,24},{24,20},{28,0},{0,28},{5,9},{9... | collective-permute-start | bytes 983048 | tf_op jit(solution)/shard_map/ppermute | solution.py:50
  36.1 14.8 %collective-permute-start.15 = (f32[10,32,256]{2,1,0:T(8,128)S(1)}, f32[10,32,256]{2,1,0:T(8,128)S(1)}, u32[]{:S(2)}, u32[]{:S(2)}) collective-permute-start(f32[10,32,256]{2,1,0:T(8,128)S(1)} %get-tuple-element.59), channel_id=1, source_target_pairs={{0,4},{4,0},{8,12},{12,8},{16,20},{20,16},{24,28},{28,24},{1,5},{5... | collective-permute-start | bytes 983048 | tf_op jit(solution)/shard_map/ppermute | solution.py:50
  36.7 7.6 %collective-permute-start.6 = (f32[4,8,512]{2,1,0:T(8,128)S(1)}, f32[4,8,512]{2,1,0:T(8,128)S(1)}, u32[]{:S(2)}, u32[]{:S(2)}) collective-permute-start(f32[4,8,512]{2,1,0:T(8,128)S(1)} %get-tuple-element.48), channel_id=1, source_target_pairs={{1,2},{2,1},{3,0},{0,3},{5,6},{6,5},{7,4},{4,7},{9,10},{10,9},{11,... | collective-permute-start | bytes 196616 | tf_op jit(solution)/shard_map/ppermute | solution.py:50
  38.3 6.0 %collective-permute-start.7 = (f32[4,8,512]{2,1,0:T(8,128)S(1)}, f32[4,8,512]{2,1,0:T(8,128)S(1)}, u32[]{:S(2)}, u32[]{:S(2)}) collective-permute-start(f32[4,8,512]{2,1,0:T(8,128)S(1)} %get-tuple-element.49), channel_id=1, source_target_pairs={{0,1},{1,0},{2,3},{3,2},{4,5},{5,4},{6,7},{7,6},{8,9},{9,8},{10,11... | collective-permute-start | bytes 196616 | tf_op jit(solution)/shard_map/ppermute | solution.py:50
  39.3 5.0 %collective-permute-start.8 = (f32[4,8,256]{2,1,0:T(8,128)S(1)}, f32[4,8,256]{2,1,0:T(8,128)S(1)}, u32[]{:S(2)}, u32[]{:S(2)}) collective-permute-start(f32[4,8,256]{2,1,0:T(8,128)S(1)} %get-tuple-element.51.refs_4_.refs_2_), channel_id=1, source_target_pairs={{0,2},{1,3},{2,0},{3,1},{4,6},{5,7},{6,4},{7,5},{8,10},{9,11},{10,... | collective-permute-start | bytes 98312 | tf_op jit(solution)/shard_map/ppermute | solution.py:34
  44.4 8.1 %copy-start.4 = (bf16[256,128]{1,0:T(8,128)(2,1)S(1)}, bf16[256,128]{1,0:T(8,128)(2,1)}, u32[]{:S(2)}) copy-start(bf16[256,128]{1,0:T(8,128)(2,1)} %constant.6.clone.refs_1_) | copy-start | bytes 196612
  44.4 6.4 %collective-permute-start.12 = (f32[4,32,256]{2,1,0:T(8,128)S(1)}, f32[4,32,256]{2,1,0:T(8,128)S(1)}, u32[]{:S(2)}, u32[]{:S(2)}) collective-permute-start(f32[4,32,256]{2,1,0:T(8,128)S(1)} %get-tuple-element.55), channel_id=1, source_target_pairs={{4,8},{8,4},{12,16},{16,12},{20,24},{24,20},{28,0},{0,28},{5,9},{9... | collective-permute-start | bytes 393224 | tf_op jit(solution)/shard_map/ppermute | solution.py:50
  44.9 5.9 %collective-permute-start.13 = (f32[4,32,256]{2,1,0:T(8,128)S(1)}, f32[4,32,256]{2,1,0:T(8,128)S(1)}, u32[]{:S(2)}, u32[]{:S(2)}) collective-permute-start(f32[4,32,256]{2,1,0:T(8,128)S(1)} %get-tuple-element.56), channel_id=1, source_target_pairs={{0,4},{4,0},{8,12},{12,8},{16,20},{20,16},{24,28},{28,24},{1,5},{5... | collective-permute-start | bytes 393224 | tf_op jit(solution)/shard_map/ppermute | solution.py:50
  50.9 11.5 %copy-start.1 = (f32[928,256]{1,0:T(8,128)S(1)}, f32[928,256]{1,0:T(8,128)}, u32[]{:S(2)}) copy-start(f32[928,256]{1,0:T(8,128)} %constant.7.clone.refs_1_) | copy-start | bytes 2850820
  51.8 11.8 %collective-permute-start.16 = (f32[14,8,512]{2,1,0:T(8,128)S(1)}, f32[14,8,512]{2,1,0:T(8,128)S(1)}, u32[]{:S(2)}, u32[]{:S(2)}) collective-permute-start(f32[14,8,512]{2,1,0:T(8,128)S(1)} %get-tuple-element.62), channel_id=1, source_target_pairs={{4,8},{8,4},{12,16},{16,12},{20,24},{24,20},{28,0},{0,28},{5,9},{9... | collective-permute-start | bytes 688136 | tf_op jit(solution)/shard_map/ppermute | solution.py:50
  52.1 11.5 %collective-permute-start.17 = (f32[14,8,512]{2,1,0:T(8,128)S(1)}, f32[14,8,512]{2,1,0:T(8,128)S(1)}, u32[]{:S(2)}, u32[]{:S(2)}) collective-permute-start(f32[14,8,512]{2,1,0:T(8,128)S(1)} %get-tuple-element.63), channel_id=1, source_target_pairs={{0,4},{4,0},{8,12},{12,8},{16,20},{20,16},{24,28},{28,24},{1,5},{5... | collective-permute-start | bytes 688136 | tf_op jit(solution)/shard_map/ppermute | solution.py:50
  52.8 12.3 %copy-start = (bf16[256,512]{1,0:T(8,128)(2,1)S(1)}, bf16[256,512]{1,0:T(8,128)(2,1)}, u32[]{:S(2)}) copy-start(bf16[256,512]{1,0:T(8,128)(2,1)} %constant.8.clone.refs_5_.refs_4_) | copy-start | bytes 786436
  64.4 4.3 %collective-permute-start.18 = (f32[2,16,256]{2,1,0:T(8,128)S(1)}, f32[2,16,256]{2,1,0:T(8,128)S(1)}, u32[]{:S(2)}, u32[]{:S(2)}) collective-permute-start(f32[2,16,256]{2,1,0:T(8,128)S(1)} %get-tuple-element.67), channel_id=1, source_target_pairs={{4,8},{8,4},{12,16},{16,12},{20,24},{24,20},{28,0},{0,28},{5,9},{9... | collective-permute-start | bytes 98312 | tf_op jit(solution)/shard_map/ppermute | solution.py:50
  64.6 4.1 %collective-permute-start.19 = (f32[2,16,256]{2,1,0:T(8,128)S(1)}, f32[2,16,256]{2,1,0:T(8,128)S(1)}, u32[]{:S(2)}, u32[]{:S(2)}) collective-permute-start(f32[2,16,256]{2,1,0:T(8,128)S(1)} %get-tuple-element.68), channel_id=1, source_target_pairs={{0,4},{4,0},{8,12},{12,8},{16,20},{20,16},{24,28},{28,24},{1,5},{5... | collective-permute-start | bytes 98312 | tf_op jit(solution)/shard_map/ppermute | solution.py:50

commit v7 on v6

--- a/solution.py
+++ b/solution.py
@@ -152,7 +152,7 @@
 
 def put_tiles(tiles, x):
     for k in range(tiles.shape[0]):
-        tiles[k] = x[:, 128 * k : 128 * k + 128]
+        tiles[k, 0 : x.shape[0]] = x[:, 128 * k : 128 * k + 128]
 
 
 def every_other(tiles, start, size):
@@ -528,11 +528,15 @@
     spec = dot_split(split2(part("forward", cells)), split2(spec))
     spec = spec / (lam * float(count))
     spec = dot_split(split2(spec), split2(part("depth_out", depth)))
-    step = -(-rx // 8) * 8
+    step = -(-rx // 16) * 8
     along_x = table[pl.ds(pl.multiple_of(start["x"] + lax.axis_index("gx") * step, 8), step), :]
-    along_y = part("y", ry)
-    back_table = jnp.concatenate([along_x[i : i + 1] * along_y for i in range(rx)], axis=0)
-    out[...] = dot_split(split2(back_table), split2(spec)).reshape(out.shape)
+    along_y = part("y", ry // 2)
+    back_table = jnp.concatenate([along_x[i : i + 1] * along_y for i in range(rx // 2)], axis=0)
+    rows = dot_split(split2(back_table), split2(spec)).reshape(rx // 2, ry // 2, out.shape[2])
+    for i in range(rx // 2):
+        line = jnp.broadcast_to(rows[i][:, None, :], (ry // 2, 2, out.shape[2])).reshape(out.shape[1:])
+        out[2 * i] = line
+        out[2 * i + 1] = line
 
 
 def post1_kernel(kept1, up, down, correction, own, to_up, to_down, v, *, cols):
@@ -660,8 +664,8 @@
             "eig": np.concatenate((eig_x, eig_y), axis=1),
             "depth": np.concatenate((depth_in, eig_z), axis=1),
             "depth_out": depth_out,
-            "x": windows(np.repeat(table_x, cols, axis=1), nx, 2 * rows, out_rows),
-            "y": np.tile(table_y, (1, total_rows)),
+            "x": windows(np.repeat(table_x[::2], cols, axis=1), nx, rows, out_rows // 2),
+            "y": np.tile(forward_y, (1, total_rows)),
         }
         start, size = {}, 0
         for name, part in parts.items():
@@ -724,30 +728,30 @@
         [(3 * rows1, cols1, depth1), jax.ShapeDtypeStruct((depth, depth1), BF16)],
         face_coef,
         near=(x_first,),
-        scratch=[pltpu.VMEM((depth, depth1), BF16), (depth1 // 128, cols, 128)],
+        scratch=[pltpu.VMEM((depth, depth1), BF16), (depth1 // 128, cols + 8, 128)],
     )
     (block,) = call(
         before_kernel,
         [(3 * rows1 + 1, cols1, depth1)],
         block, x_first, pairs,
-        scratch=[(depth1 // 128, cols, 128)],
-    )
+        scratch=[(depth1 // 128, cols + 8, 128)],
+    )
+    (state,) = call(assemble_kernel, [(4, er, ec, depth)], source, face_coef, x_first)
     (corners,) = call(
         functools.partial(forward_kernel, rows=rows),
         [Beside("gx", (2 * corner_tiles, 8, depth))],
         y_first,
-        near=(block,),
+        near=(block, state),
     )
     corners = corners.exchanged()
     blocks = Beside("gy", block.shape, block, block).exchanged()
     blocks_between = [moved(block, "gy", -k) for k in range(2, count - 1)]
-    (state,) = call(assemble_kernel, [(4, er, ec, depth)], source, face_coef, x_first)
     kept, v0, right1, y_second = call(
         pre_kernel,
         [(5, er, ec, depth), (rows, cols, depth), (rows1, cols1, depth1)]
         + [Beside("gy", (rows * h // 8 + rows1 // 2, 8, depth))],
         corners, y_first, pairs, state,
-        scratch=[(rows1, ec, depth), (depth1 // 128, rows1 * ec, 128)] + [(er, ec, depth)] * 2,
+        scratch=[(rows1, ec, depth), (depth1 // 128, rows1 * ec + 8, 128)] + [(er, ec, depth)] * 2,
     )
 
     y_second = y_second.exchanged()
@@ -780,7 +784,7 @@
         residual1_kernel,
         [(lax.axis_size("gx"), rows1 * wide // 4 + 1, depth1 // 2)],
         kept1, jnp.asarray(pair_table(depth1)), sums,
-        scratch=[(rows1 // 2, wide, depth1), (depth1 // 256, rows1 // 2 * wide, 128)],
+        scratch=[(rows1 // 2, wide, depth1), (depth1 // 256, rows1 // 2 * wide + 8, 128)],
         limit=limit,
     )
     correction2 = coarse_correction(chunks, rows1 // 2, wide // 2, depth1 // 2)

time: 71.3 us -> 71.2 us (level)
  no operation moved by 1% of the time
where the time goes in v7:
time: 71.2 us; the launch traced here: 71 us
  waiting for transfers between devices  24.6 us (35%)
  starting transfers between devices  21.6 us (30%)
  Pallas kernels  13 us (18%)
  blocking collectives  9.66 us (14%)
  local copies, waits for them, and re-layouts  1.97 us (3%)
    ppermute x18, waiting for transfers between devices, exchanged(): got.append(lax.ppermute(block, self.axis, route))  21 us
    ppermute x18, starting transfers between devices, exchanged(): got.append(lax.ppermute(block, self.axis, route))  18.9 us
    pallas_call x16, Pallas kernels, call(): pl.pallas_call(body, out_shape=[s if hasattr(s, 'dtype') else jax.ShapeDt...  13 us
    all_to_all x1, blocking collectives, coarse_correction(): got = lax.all_to_all(chunks, 'gx', 0, 0)  9.66 us
    ppermute x2, waiting for transfers between devices, moved(): lax.ppermute(block, axis, [(i, (i + distance) % count) for i in range(cou...  3.59 us
    ppermute x2, starting transfers between devices, moved(): lax.ppermute(block, axis, [(i, (i + distance) % count) for i in range(cou...  2.66 us
    unnamed x10, local copies, waits for them, and re-layouts  1.97 us
  transfers between devices with their start and end apart: 20, of which 8 were waited for; matrix products, arithmetic and copies ran while one was open for 0% of the time, Pallas kernels for 11%

profile of v7, /device:TPU:0, one launch (start us, length us, event | category | flops | bytes accessed | tf_op | source)
XLA Modules:
  0.0 71.0 jit_solution(17791667812680187903)
XLA Ops:
  0.0 1.0 %copy-done.2 = bf16[3,8,16,512]{3,2,1,0:T(8,128)(2,1)S(1)} copy-done((bf16[3,8,16,512]{3,2,1,0:T(8,128)(2,1)S(1)}, bf16[3,8,16,512]{3,2,1,0:T(8,128)(2,1)}, u32[]{:S(2)}) %copy-start.2) | copy-done | bytes 393240
  1.0 0.9 %copy-done.3 = f32[8,16,512]{2,1,0:T(8,128)S(1)} copy-done((f32[8,16,512]{2,1,0:T(8,128)S(1)}, f32[8,16,512]{2,1,0:T(8,128)}, u32[]{:S(2)}) %copy-start.3) | copy-done | bytes 262168
  2.5 3.4 %collective-permute-start.2 = (f32[32,8,512]{2,1,0:T(8,128)S(1)}, f32[32,8,512]{2,1,0:T(8,128)S(1)}, u32[]{:S(2)}, u32[]{:S(2)}) collective-permute-start(f32[32,8,512]{2,1,0:T(8,128)S(1)} %get-tuple-element.41), channel_id=1, source_target_pairs={{4,8},{8,4},{12,16},{16,12},{20,24},{24,20},{28,0},{0,28},{5,9},{9... | collective-permute-start | bytes 1572872 | tf_op jit(solution)/shard_map/ppermute | solution.py:50
  5.9 3.6 %collective-permute-start = (f32[16,8,512]{2,1,0:T(8,128)S(1)}, f32[16,8,512]{2,1,0:T(8,128)S(1)}, u32[]{:S(2)}, u32[]{:S(2)}) collective-permute-start(f32[16,8,512]{2,1,0:T(8,128)S(1)} %get-tuple-element.37), channel_id=1, source_target_pairs={{1,2},{2,1},{3,0},{0,3},{5,6},{6,5},{7,4},{4,7},{9,10},{10,9},{11,... | collective-permute-start | bytes 786440 | tf_op jit(solution)/shard_map/ppermute | solution.py:50
  9.5 8.0 %collective-permute-done.2.refs_1_.refs_2_ = f32[32,8,512]{2,1,0:T(8,128)S(1)} collective-permute-done((f32[32,8,512]{2,1,0:T(8,128)S(1)}, f32[32,8,512]{2,1,0:T(8,128)S(1)}, u32[]{:S(2)}, u32[]{:S(2)}) %collective-permute-start.2) | collective-permute-done | bytes 524320 | tf_op jit(solution)/shard_map/ppermute | solution.py:50
  17.6 0.9 %shard_map.57 = (f32[12,8,256]{2,1,0:T(8,128)S(1)}, bf16[512,256]{1,0:T(8,128)(2,1)S(1)}) custom-call(bf16[3,8,16,512]{3,2,1,0:T(8,128)(2,1)S(1)} %get-tuple-element.39.refs_1_.refs_0_, f32[32,8,512]{2,1,0:T(8,128)S(1)} %collective-permute-done.2.refs_1_.refs_2_, f32[32,8,512]{2,1,0:T(8,128)S(1)} %collective-permute-done.3.refs_2_.refs_3_), custom_call_target="tpu_custom_call" | custom-call | tf_op jit(solution)/shard_map/pallas_call | solution.py:114
  18.9 3.3 %collective-permute-done.1.refs_1_.refs_3_ = f32[16,8,512]{2,1,0:T(8,128)S(1)} collective-permute-done((f32[16,8,512]{2,1,0:T(8,128)S(1)}, f32[16,8,512]{2,1,0:T(8,128)S(1)}, u32[]{:S(2)}, u32[]{:S(2)}) %collective-permute-start.1) | collective-permute-done | bytes 262176 | tf_op jit(solution)/shard_map/ppermute | solution.py:50
  22.7 0.6 collective-permute-start.5
  23.2 1.0 %collective-permute-start.11 = (f32[13,8,256]{2,1,0:T(8,128)S(1)}, f32[13,8,256]{2,1,0:T(8,128)S(1)}, u32[]{:S(2)}, u32[]{:S(2)}) collective-permute-start(f32[13,8,256]{2,1,0:T(8,128)S(1)} %shard_map.58.refs_2_.refs_0_), channel_id=1, source_target_pairs={{0,2},{1,3},{2,0},{3,1},{4,6},{5,7},{6,4},{7,5},{8,10},{9,11},{10,... | collective-permute-start | bytes 319496 | tf_op jit(solution)/shard_map/ppermute | solution.py:34
  24.2 1.6 %collective-permute-start.10 = (f32[13,8,256]{2,1,0:T(8,128)S(1)}, f32[13,8,256]{2,1,0:T(8,128)S(1)}, u32[]{:S(2)}, u32[]{:S(2)}) collective-permute-start(f32[13,8,256]{2,1,0:T(8,128)S(1)} %shard_map.58.refs_2_.refs_0_), channel_id=1, source_target_pairs={{0,1},{1,0},{2,3},{3,2},{4,5},{5,4},{6,7},{7,6},{8,9},{9,8},{10,11... | collective-permute-start | bytes 319496 | tf_op jit(solution)/shard_map/ppermute | solution.py:50
  25.8 1.8 %collective-permute-start.9 = (f32[13,8,256]{2,1,0:T(8,128)S(1)}, f32[13,8,256]{2,1,0:T(8,128)S(1)}, u32[]{:S(2)}, u32[]{:S(2)}) collective-permute-start(f32[13,8,256]{2,1,0:T(8,128)S(1)} %shard_map.58.refs_2_.refs_0_), channel_id=1, source_target_pairs={{1,2},{2,1},{3,0},{0,3},{5,6},{6,5},{7,4},{4,7},{9,10},{10,9},{11,... | collective-permute-start | bytes 319496 | tf_op jit(solution)/shard_map/ppermute | solution.py:50
  27.6 1.0 %collective-permute-done.4.refs_0_ = f32[8,8,512]{2,1,0:T(8,128)S(1)} collective-permute-done((f32[8,8,512]{2,1,0:T(8,128)S(1)}, f32[8,8,512]{2,1,0:T(8,128)S(1)}, u32[]{:S(2)}, u32[]{:S(2)}) %collective-permute-start.4) | collective-permute-done | bytes 131104 | tf_op jit(solution)/shard_map/ppermute | solution.py:50
  28.6 4.0 %shard_map.61 = (f32[5,16,24,512]{3,2,1,0:T(8,128)S(1)}, f32[8,16,512]{2,1,0:T(8,128)S(1)}, f32[4,8,256]{2,1,0:T(8,128)S(1)}, f32[4,8,512]{2,1,0:T(8,128)S(1)}, f32[4,8,512]{2,1,0:T(8,128)S(1)}) custom-call(f32[8,8,512]{2,1,0:T(8,128)S(1)} %collective-permute-done.4.refs_0_, f32[8,8,512]{2,1,0:T(8,128)S(1)} %collective-permute-done.5.refs_1_, ...), custom_call_target="tpu_custom_call" | custom-call | tf_op jit(solution)/shard_map/pallas_call | solution.py:114
  33.0 1.8 %collective-permute-done.9.refs_1_ = f32[13,8,256]{2,1,0:T(8,128)S(1)} collective-permute-done((f32[13,8,256]{2,1,0:T(8,128)S(1)}, f32[13,8,256]{2,1,0:T(8,128)S(1)}, u32[]{:S(2)}, u32[]{:S(2)}) %collective-permute-start.9) | collective-permute-done | bytes 106528 | tf_op jit(solution)/shard_map/ppermute | solution.py:50
  35.1 1.0 %collective-permute-start.14 = (f32[10,32,256]{2,1,0:T(8,128)S(1)}, f32[10,32,256]{2,1,0:T(8,128)S(1)}, u32[]{:S(2)}, u32[]{:S(2)}) collective-permute-start(f32[10,32,256]{2,1,0:T(8,128)S(1)} %get-tuple-element.58), channel_id=1, source_target_pairs={{4,8},{8,4},{12,16},{16,12},{20,24},{24,20},{28,0},{0,28},{5,9},{9... | collective-permute-start | bytes 983048 | tf_op jit(solution)/shard_map/ppermute | solution.py:50
  36.1 0.7 collective-permute-start.15
  36.7 1.6 %collective-permute-start.6 = (f32[4,8,512]{2,1,0:T(8,128)S(1)}, f32[4,8,512]{2,1,0:T(8,128)S(1)}, u32[]{:S(2)}, u32[]{:S(2)}) collective-permute-start(f32[4,8,512]{2,1,0:T(8,128)S(1)} %get-tuple-element.48), channel_id=1, source_target_pairs={{1,2},{2,1},{3,0},{0,3},{5,6},{6,5},{7,4},{4,7},{9,10},{10,9},{11,... | collective-permute-start | bytes 196616 | tf_op jit(solution)/shard_map/ppermute | solution.py:50
  38.3 1.2 %collective-permute-start.7 = (f32[4,8,512]{2,1,0:T(8,128)S(1)}, f32[4,8,512]{2,1,0:T(8,128)S(1)}, u32[]{:S(2)}, u32[]{:S(2)}) collective-permute-start(f32[4,8,512]{2,1,0:T(8,128)S(1)} %get-tuple-element.49), channel_id=1, source_target_pairs={{0,1},{1,0},{2,3},{3,2},{4,5},{5,4},{6,7},{7,6},{8,9},{9,8},{10,11... | collective-permute-start | bytes 196616 | tf_op jit(solution)/shard_map/ppermute | solution.py:50
  39.4 1.7 %collective-permute-start.8 = (f32[4,8,256]{2,1,0:T(8,128)S(1)}, f32[4,8,256]{2,1,0:T(8,128)S(1)}, u32[]{:S(2)}, u32[]{:S(2)}) collective-permute-start(f32[4,8,256]{2,1,0:T(8,128)S(1)} %get-tuple-element.51.refs_4_.refs_2_), channel_id=1, source_target_pairs={{0,2},{1,3},{2,0},{3,1},{4,6},{5,7},{6,4},{7,5},{8,10},{9,11},{10,... | collective-permute-start | bytes 98312 | tf_op jit(solution)/shard_map/ppermute | solution.py:34
  41.1 3.2 %collective-permute-done.8.refs_3_ = f32[4,8,256]{2,1,0:T(8,128)S(1)} collective-permute-done((f32[4,8,256]{2,1,0:T(8,128)S(1)}, f32[4,8,256]{2,1,0:T(8,128)S(1)}, u32[]{:S(2)}, u32[]{:S(2)}) %collective-permute-start.8) | collective-permute-done | bytes 32800 | tf_op jit(solution)/shard_map/ppermute | solution.py:34
  44.4 0.5 collective-permute-start.12
  44.9 1.4 %collective-permute-start.13 = (f32[4,32,256]{2,1,0:T(8,128)S(1)}, f32[4,32,256]{2,1,0:T(8,128)S(1)}, u32[]{:S(2)}, u32[]{:S(2)}) collective-permute-start(f32[4,32,256]{2,1,0:T(8,128)S(1)} %get-tuple-element.56), channel_id=1, source_target_pairs={{0,4},{4,0},{8,12},{12,8},{16,20},{20,16},{24,28},{28,24},{1,5},{5... | collective-permute-start | bytes 393224 | tf_op jit(solution)/shard_map/ppermute | solution.py:50
  46.4 4.5 %collective-permute-done.12.refs_1_ = f32[4,32,256]{2,1,0:T(8,128)S(1)} collective-permute-done((f32[4,32,256]{2,1,0:T(8,128)S(1)}, f32[4,32,256]{2,1,0:T(8,128)S(1)}, u32[]{:S(2)}, u32[]{:S(2)}) %collective-permute-start.12) | collective-permute-done | bytes 131104 | tf_op jit(solution)/shard_map/ppermute | solution.py:50
  51.0 1.0 %shard_map.65 = (f32[7,12,32,256]{3,2,1,0:T(8,128)S(1)}, f32[14,8,512]{2,1,0:T(8,128)S(1)}, f32[14,8,512]{2,1,0:T(8,128)S(1)}) custom-call(f32[4,32,256]{2,1,0:T(8,128)S(1)} %get-tuple-element.54.refs_0_, f32[4,32,256]{2,1,0:T(8,128)S(1)} %collective-permute-done.12.refs_1_, f32[4,32,256]{2,1,0:T(8,128)S(1)} %collective-permute-done.13.refs_2_, ...), custom_call_target="tpu_custom_call" | custom-call | tf_op jit(solution)/shard_map/pallas_call | solution.py:114
  52.0 0.5 collective-permute-start.17
  52.8 9.7 %all_to_all.5.refs_0_ = f32[8,33,128]{2,1,0:T(8,128)S(1)} all-to-all(f32[8,33,128]{2,1,0:T(8,128)S(1)} %shard_map.66), channel_id=1, replica_groups=mesh['gx'=8,'gy'=4] {'gx'}, dimensions={0} | all-to-all | bytes 270336 | tf_op jit(solution)/shard_map/all_to_all | solution.py:647
  62.5 1.0 %shard_map.67.refs_3_ = f32[12,32,256]{2,1,0:T(8,128)S(1)} custom-call(f32[8,33,128]{2,1,0:T(8,128)S(1)} %all_to_all.5.refs_0_, f32[848,256]{1,0:T(8,128)S(1)} %copy-done.1), custom_call_target="tpu_custom_call" | custom-call | tf_op jit(solution)/shard_map/pallas_call | solution.py:114
  63.5 0.8 %shard_map.68 = (f32[4,16,256]{2,1,0:T(8,128)S(1)}, f32[2,16,256]{2,1,0:T(8,128)S(1)}, f32[2,16,256]{2,1,0:T(8,128)S(1)}) custom-call(f32[7,12,32,256]{3,2,1,0:T(8,128)S(1)} %get-tuple-element.64.refs_0_, f32[14,8,512]{2,1,0:T(8,128)S(1)} %collective-permute-done.16.refs_1_, f32[14,8,512]{2,1,0:T(8,128)S(1)} %collective-permute-done.17.refs_2_, ...), custom_call_target="tpu_custom_call" | custom-call | tf_op jit(solution)/shard_map/pallas_call | solution.py:114
  64.4 0.7 collective-permute-start.19
  65.0 1.1 %shard_map.69.refs_0_ = f32[16,24,512]{2,1,0:T(8,128)S(1)} custom-call(f32[8,24,512]{2,1,0:T(8,128)S(1)} %get-tuple-element.50.refs_0_, f32[14,8,512]{2,1,0:T(8,128)S(1)} %collective-permute-done.16.refs_1_, f32[14,8,512]{2,1,0:T(8,128)S(1)} %collective-permute-done.17.refs_2_, f32[4,16,256]{2,1,0:T(8,128)S(1)} %get-tuple-element.66.refs_3_, ...), custom_call_target="tpu_custom_call" | custom-call | tf_op jit(solution)/shard_map/pallas_call | solution.py:114
  66.2 2.4 %collective-permute-done.18.refs_1_ = f32[2,16,256]{2,1,0:T(8,128)S(1)} collective-permute-done((f32[2,16,256]{2,1,0:T(8,128)S(1)}, f32[2,16,256]{2,1,0:T(8,128)S(1)}, u32[]{:S(2)}, u32[]{:S(2)}) %collective-permute-start.18) | collective-permute-done | bytes 32800 | tf_op jit(solution)/shard_map/ppermute | solution.py:50
  68.6 2.4 %shard_map.70 = f32[8,16,512]{2,1,0:T(8,128)} custom-call(f32[16,24,512]{2,1,0:T(8,128)S(1)} %shard_map.69.refs_0_, f32[2,16,256]{2,1,0:T(8,128)S(1)} %collective-permute-done.18.refs_1_, f32[2,16,256]{2,1,0:T(8,128)S(1)} %collective-permute-done.19.refs_2_, f32[5,16,24,512]{3,2,1,0:T(8,128)S(1)} %get-tuple-element.53.refs_5_.refs_8_.refs_4_.refs_3_, ...), custom_call_target="tpu_custom_call" | custom-call | tf_op jit(solution)/shard_map/pallas_call | solution.py:114
  (35 shorter events, 2.8 us)
Async XLA Ops:
  0.0 1.0 %copy-start.2 = (bf16[3,8,16,512]{3,2,1,0:T(8,128)(2,1)S(1)}, bf16[3,8,16,512]{3,2,1,0:T(8,128)(2,1)}, u32[]{:S(2)}) copy-start(bf16[3,8,16,512]{3,2,1,0:T(8,128)(2,1)} %refs_1_.3) | copy-start | bytes 1179652
  1.0 0.9 %copy-start.3 = (f32[8,16,512]{2,1,0:T(8,128)S(1)}, f32[8,16,512]{2,1,0:T(8,128)}, u32[]{:S(2)}) copy-start(f32[8,16,512]{2,1,0:T(8,128)} %refs_0_.1) | copy-start | bytes 786436
  2.5 15.1 %collective-permute-start.2 = (f32[32,8,512]{2,1,0:T(8,128)S(1)}, f32[32,8,512]{2,1,0:T(8,128)S(1)}, u32[]{:S(2)}, u32[]{:S(2)}) collective-permute-start(f32[32,8,512]{2,1,0:T(8,128)S(1)} %get-tuple-element.41), channel_id=1, source_target_pairs={{4,8},{8,4},{12,16},{16,12},{20,24},{24,20},{28,0},{0,28},{5,9},{9... | collective-permute-start | bytes 1572872 | tf_op jit(solution)/shard_map/ppermute | solution.py:50
  5.9 11.7 %collective-permute-start.3 = (f32[32,8,512]{2,1,0:T(8,128)S(1)}, f32[32,8,512]{2,1,0:T(8,128)S(1)}, u32[]{:S(2)}, u32[]{:S(2)}) collective-permute-start(f32[32,8,512]{2,1,0:T(8,128)S(1)} %get-tuple-element.42), channel_id=1, source_target_pairs={{0,4},{4,0},{8,12},{12,8},{16,20},{20,16},{24,28},{28,24},{1,5},{5... | collective-permute-start | bytes 1572872 | tf_op jit(solution)/shard_map/ppermute | solution.py:50
  5.9 13.0 %collective-permute-start = (f32[16,8,512]{2,1,0:T(8,128)S(1)}, f32[16,8,512]{2,1,0:T(8,128)S(1)}, u32[]{:S(2)}, u32[]{:S(2)}) collective-permute-start(f32[16,8,512]{2,1,0:T(8,128)S(1)} %get-tuple-element.37), channel_id=1, source_target_pairs={{1,2},{2,1},{3,0},{0,3},{5,6},{6,5},{7,4},{4,7},{9,10},{10,9},{11,... | collective-permute-start | bytes 786440 | tf_op jit(solution)/shard_map/ppermute | solution.py:50
  9.5 12.7 %collective-permute-start.1 = (f32[16,8,512]{2,1,0:T(8,128)S(1)}, f32[16,8,512]{2,1,0:T(8,128)S(1)}, u32[]{:S(2)}, u32[]{:S(2)}) collective-permute-start(f32[16,8,512]{2,1,0:T(8,128)S(1)} %get-tuple-element.38), channel_id=1, source_target_pairs={{0,1},{1,0},{2,3},{3,2},{4,5},{5,4},{6,7},{7,6},{8,9},{9,8},{10,11... | collective-permute-start | bytes 786440 | tf_op jit(solution)/shard_map/ppermute | solution.py:50
  22.4 6.2 %collective-permute-start.4 = (f32[8,8,512]{2,1,0:T(8,128)S(1)}, f32[8,8,512]{2,1,0:T(8,128)S(1)}, u32[]{:S(2)}, u32[]{:S(2)}) collective-permute-start(f32[8,8,512]{2,1,0:T(8,128)S(1)} %get-tuple-element.45), channel_id=1, source_target_pairs={{4,8},{8,4},{12,16},{16,12},{20,24},{24,20},{28,0},{0,28},{5,9},{9... | collective-permute-start | bytes 393224 | tf_op jit(solution)/shard_map/ppermute | solution.py:50
  22.7 5.9 %collective-permute-start.5 = (f32[8,8,512]{2,1,0:T(8,128)S(1)}, f32[8,8,512]{2,1,0:T(8,128)S(1)}, u32[]{:S(2)}, u32[]{:S(2)}) collective-permute-start(f32[8,8,512]{2,1,0:T(8,128)S(1)} %get-tuple-element.46), channel_id=1, source_target_pairs={{0,4},{4,0},{8,12},{12,8},{16,20},{20,16},{24,28},{28,24},{1,5},{5... | collective-permute-start | bytes 393224 | tf_op jit(solution)/shard_map/ppermute | solution.py:50
  23.2 9.8 %collective-permute-start.11 = (f32[13,8,256]{2,1,0:T(8,128)S(1)}, f32[13,8,256]{2,1,0:T(8,128)S(1)}, u32[]{:S(2)}, u32[]{:S(2)}) collective-permute-start(f32[13,8,256]{2,1,0:T(8,128)S(1)} %shard_map.58.refs_2_.refs_0_), channel_id=1, source_target_pairs={{0,2},{1,3},{2,0},{3,1},{4,6},{5,7},{6,4},{7,5},{8,10},{9,11},{10,... | collective-permute-start | bytes 319496 | tf_op jit(solution)/shard_map/ppermute | solution.py:34
  24.2 8.8 %collective-permute-start.10 = (f32[13,8,256]{2,1,0:T(8,128)S(1)}, f32[13,8,256]{2,1,0:T(8,128)S(1)}, u32[]{:S(2)}, u32[]{:S(2)}) collective-permute-start(f32[13,8,256]{2,1,0:T(8,128)S(1)} %shard_map.58.refs_2_.refs_0_), channel_id=1, source_target_pairs={{0,1},{1,0},{2,3},{3,2},{4,5},{5,4},{6,7},{7,6},{8,9},{9,8},{10,11... | collective-permute-start | bytes 319496 | tf_op jit(solution)/shard_map/ppermute | solution.py:50
  25.8 9.0 %collective-permute-start.9 = (f32[13,8,256]{2,1,0:T(8,128)S(1)}, f32[13,8,256]{2,1,0:T(8,128)S(1)}, u32[]{:S(2)}, u32[]{:S(2)}) collective-permute-start(f32[13,8,256]{2,1,0:T(8,128)S(1)} %shard_map.58.refs_2_.refs_0_), channel_id=1, source_target_pairs={{1,2},{2,1},{3,0},{0,3},{5,6},{6,5},{7,4},{4,7},{9,10},{10,9},{11,... | collective-permute-start | bytes 319496 | tf_op jit(solution)/shard_map/ppermute | solution.py:50
  35.1 15.9 %collective-permute-start.14 = (f32[10,32,256]{2,1,0:T(8,128)S(1)}, f32[10,32,256]{2,1,0:T(8,128)S(1)}, u32[]{:S(2)}, u32[]{:S(2)}) collective-permute-start(f32[10,32,256]{2,1,0:T(8,128)S(1)} %get-tuple-element.58), channel_id=1, source_target_pairs={{4,8},{8,4},{12,16},{16,12},{20,24},{24,20},{28,0},{0,28},{5,9},{9... | collective-permute-start | bytes 983048 | tf_op jit(solution)/shard_map/ppermute | solution.py:50
  36.1 14.9 %collective-permute-start.15 = (f32[10,32,256]{2,1,0:T(8,128)S(1)}, f32[10,32,256]{2,1,0:T(8,128)S(1)}, u32[]{:S(2)}, u32[]{:S(2)}) collective-permute-start(f32[10,32,256]{2,1,0:T(8,128)S(1)} %get-tuple-element.59), channel_id=1, source_target_pairs={{0,4},{4,0},{8,12},{12,8},{16,20},{20,16},{24,28},{28,24},{1,5},{5... | collective-permute-start | bytes 983048 | tf_op jit(solution)/shard_map/ppermute | solution.py:50
  36.7 7.6 %collective-permute-start.6 = (f32[4,8,512]{2,1,0:T(8,128)S(1)}, f32[4,8,512]{2,1,0:T(8,128)S(1)}, u32[]{:S(2)}, u32[]{:S(2)}) collective-permute-start(f32[4,8,512]{2,1,0:T(8,128)S(1)} %get-tuple-element.48), channel_id=1, source_target_pairs={{1,2},{2,1},{3,0},{0,3},{5,6},{6,5},{7,4},{4,7},{9,10},{10,9},{11,... | collective-permute-start | bytes 196616 | tf_op jit(solution)/shard_map/ppermute | solution.py:50
  38.3 6.0 %collective-permute-start.7 = (f32[4,8,512]{2,1,0:T(8,128)S(1)}, f32[4,8,512]{2,1,0:T(8,128)S(1)}, u32[]{:S(2)}, u32[]{:S(2)}) collective-permute-start(f32[4,8,512]{2,1,0:T(8,128)S(1)} %get-tuple-element.49), channel_id=1, source_target_pairs={{0,1},{1,0},{2,3},{3,2},{4,5},{5,4},{6,7},{7,6},{8,9},{9,8},{10,11... | collective-permute-start | bytes 196616 | tf_op jit(solution)/shard_map/ppermute | solution.py:50
  39.4 4.9 %collective-permute-start.8 = (f32[4,8,256]{2,1,0:T(8,128)S(1)}, f32[4,8,256]{2,1,0:T(8,128)S(1)}, u32[]{:S(2)}, u32[]{:S(2)}) collective-permute-start(f32[4,8,256]{2,1,0:T(8,128)S(1)} %get-tuple-element.51.refs_4_.refs_2_), channel_id=1, source_target_pairs={{0,2},{1,3},{2,0},{3,1},{4,6},{5,7},{6,4},{7,5},{8,10},{9,11},{10,... | collective-permute-start | bytes 98312 | tf_op jit(solution)/shard_map/ppermute | solution.py:34
  44.4 8.1 %copy-start.4 = (bf16[256,128]{1,0:T(8,128)(2,1)S(1)}, bf16[256,128]{1,0:T(8,128)(2,1)}, u32[]{:S(2)}) copy-start(bf16[256,128]{1,0:T(8,128)(2,1)} %constant.6.clone.refs_1_) | copy-start | bytes 196612
  44.4 6.6 %collective-permute-start.12 = (f32[4,32,256]{2,1,0:T(8,128)S(1)}, f32[4,32,256]{2,1,0:T(8,128)S(1)}, u32[]{:S(2)}, u32[]{:S(2)}) collective-permute-start(f32[4,32,256]{2,1,0:T(8,128)S(1)} %get-tuple-element.55), channel_id=1, source_target_pairs={{4,8},{8,4},{12,16},{16,12},{20,24},{24,20},{28,0},{0,28},{5,9},{9... | collective-permute-start | bytes 393224 | tf_op jit(solution)/shard_map/ppermute | solution.py:50
  44.9 6.0 %collective-permute-start.13 = (f32[4,32,256]{2,1,0:T(8,128)S(1)}, f32[4,32,256]{2,1,0:T(8,128)S(1)}, u32[]{:S(2)}, u32[]{:S(2)}) collective-permute-start(f32[4,32,256]{2,1,0:T(8,128)S(1)} %get-tuple-element.56), channel_id=1, source_target_pairs={{0,4},{4,0},{8,12},{12,8},{16,20},{20,16},{24,28},{28,24},{1,5},{5... | collective-permute-start | bytes 393224 | tf_op jit(solution)/shard_map/ppermute | solution.py:50
  51.0 11.5 %copy-start.1 = (f32[848,256]{1,0:T(8,128)S(1)}, f32[848,256]{1,0:T(8,128)}, u32[]{:S(2)}) copy-start(f32[848,256]{1,0:T(8,128)} %constant.7.clone.refs_1_) | copy-start | bytes 2605060
  51.9 11.5 %collective-permute-start.16 = (f32[14,8,512]{2,1,0:T(8,128)S(1)}, f32[14,8,512]{2,1,0:T(8,128)S(1)}, u32[]{:S(2)}, u32[]{:S(2)}) collective-permute-start(f32[14,8,512]{2,1,0:T(8,128)S(1)} %get-tuple-element.62), channel_id=1, source_target_pairs={{4,8},{8,4},{12,16},{16,12},{20,24},{24,20},{28,0},{0,28},{5,9},{9... | collective-permute-start | bytes 688136 | tf_op jit(solution)/shard_map/ppermute | solution.py:50
  52.0 11.5 %collective-permute-start.17 = (f32[14,8,512]{2,1,0:T(8,128)S(1)}, f32[14,8,512]{2,1,0:T(8,128)S(1)}, u32[]{:S(2)}, u32[]{:S(2)}) collective-permute-start(f32[14,8,512]{2,1,0:T(8,128)S(1)} %get-tuple-element.63), channel_id=1, source_target_pairs={{0,4},{4,0},{8,12},{12,8},{16,20},{20,16},{24,28},{28,24},{1,5},{5... | collective-permute-start | bytes 688136 | tf_op jit(solution)/shard_map/ppermute | solution.py:50
  52.8 12.2 %copy-start = (bf16[256,512]{1,0:T(8,128)(2,1)S(1)}, bf16[256,512]{1,0:T(8,128)(2,1)}, u32[]{:S(2)}) copy-start(bf16[256,512]{1,0:T(8,128)(2,1)} %constant.8.clone.refs_5_.refs_4_) | copy-start | bytes 786436
  64.3 4.3 %collective-permute-start.18 = (f32[2,16,256]{2,1,0:T(8,128)S(1)}, f32[2,16,256]{2,1,0:T(8,128)S(1)}, u32[]{:S(2)}, u32[]{:S(2)}) collective-permute-start(f32[2,16,256]{2,1,0:T(8,128)S(1)} %get-tuple-element.67), channel_id=1, source_target_pairs={{4,8},{8,4},{12,16},{16,12},{20,24},{24,20},{28,0},{0,28},{5,9},{9... | collective-permute-start | bytes 98312 | tf_op jit(solution)/shard_map/ppermute | solution.py:50
  64.4 4.2 %collective-permute-start.19 = (f32[2,16,256]{2,1,0:T(8,128)S(1)}, f32[2,16,256]{2,1,0:T(8,128)S(1)}, u32[]{:S(2)}, u32[]{:S(2)}) collective-permute-start(f32[2,16,256]{2,1,0:T(8,128)S(1)} %get-tuple-element.68), channel_id=1, source_target_pairs={{0,4},{4,0},{8,12},{12,8},{16,20},{20,16},{24,28},{28,24},{1,5},{5... | collective-permute-start | bytes 98312 | tf_op jit(solution)/shard_map/ppermute | solution.py:50

commit v8 on v7

--- a/solution.py
+++ b/solution.py
@@ -568,6 +568,11 @@
     to_down[...] = own[0:h]
 
 
+def solve_post1_kernel(kept1, up, down, got, table, own, to_up, to_down, v, correction, *, cols, count, start):
+    solve_kernel(got, table, correction, count=count, start=start)
+    post1_kernel(kept1, up, down, correction, own, to_up, to_down, v, cols=cols)
+
+
 def spread_rows(lines, spread, used):
     rows, padded, _ = lines.shape
     wide = dot_exact(lines.reshape(rows * padded, lines.shape[2]), spread)
@@ -673,11 +678,8 @@
             size += part.shape[0]
             assert size % 8 == 0
         table = jnp.asarray(np.concatenate(list(parts.values())), F32)
-        return call(
-            functools.partial(solve_kernel, count=count, start=start),
-            [(out_rows, 2 * cols, 2 * depth)],
-            got, table,
-        )[0]
+        kernel = functools.partial(solve_post1_kernel, count=count, start=start)
+        return kernel, (got, table), [(out_rows, 2 * cols, 2 * depth)]
 
     hi = lax.Precision.HIGHEST
     f32 = lambda x: jnp.asarray(x, F32)
@@ -696,7 +698,7 @@
     own_x = lax.dynamic_slice_in_dim(f32(table_x), lax.axis_index("gx") * 2 * rows, out_rows, 0)
     out = jnp.einsum("ij,jbz->ibz", own_x, spec, precision=hi)
     out = jnp.einsum("ij,ajz->aiz", f32(table_y), out, precision=hi)
-    return jnp.einsum("abz,zk->abk", out, f32(depth_out), precision=hi)
+    return post1_kernel, (jnp.einsum("abz,zk->abk", out, f32(depth_out), precision=hi),), []
 
 
 def gathered(block):
@@ -787,13 +789,13 @@
         scratch=[(rows1 // 2, wide, depth1), (depth1 // 256, rows1 // 2 * wide + 8, 128)],
         limit=limit,
     )
-    correction2 = coarse_correction(chunks, rows1 // 2, wide // 2, depth1 // 2)
+    kernel, operands, held = coarse_correction(chunks, rows1 // 2, wide // 2, depth1 // 2)
     used = -(-(cols1 + 2 * h) // 8) * 8
     own, x_fourth = call(
-        functools.partial(post1_kernel, cols=cols1),
+        functools.partial(kernel, cols=cols1),
         [(rows1, used, depth1), Beside("gx", (h, used, depth1))],
-        kept1, x_third, correction2,
-        scratch=[(er1, wide, depth1)],
+        kept1, x_third, *operands,
+        scratch=[(er1, wide, depth1)] + held,
         limit=limit,
     )
     x_fourth = x_fourth.exchanged()

time: 71.2 us -> 71.1 us (level)
    pallas_call x16 -> x15, Pallas kernels: 13 us -> 13 us  [call(): pl.pallas_call(body, out_shape=[s if hasattr(s, 'dtype') else jax.ShapeDt...]
  transfers between devices with their start and end apart: 20 -> 20, of which waited for: 8 -> 8; matrix products, arithmetic and copies ran while one was open for 0% -> 0% of each run, Pallas kernels for 11% -> 10%
where the time goes in v8:
time: 71.1 us; the launch traced here: 70.8 us
  waiting for transfers between devices  24.6 us (35%)
  starting transfers between devices  21.6 us (30%)
  Pallas kernels  13 us (18%)
  blocking collectives  9.52 us (13%)
  local copies, waits for them, and re-layouts  1.96 us (3%)
    ppermute x18, waiting for transfers between devices, exchanged(): got.append(lax.ppermute(block, self.axis, route))  21 us
    ppermute x18, starting transfers between devices, exchanged(): got.append(lax.ppermute(block, self.axis, route))  18.9 us
    pallas_call x15, Pallas kernels, call(): pl.pallas_call(body, out_shape=[s if hasattr(s, 'dtype') else jax.ShapeDt...  13 us
    all_to_all x1, blocking collectives, coarse_correction(): got = lax.all_to_all(chunks, 'gx', 0, 0)  9.52 us
    ppermute x2, waiting for transfers between devices, moved(): lax.ppermute(block, axis, [(i, (i + distance) % count) for i in range(cou...  3.59 us
    ppermute x2, starting transfers between devices, moved(): lax.ppermute(block, axis, [(i, (i + distance) % count) for i in range(cou...  2.66 us
    unnamed x10, local copies, waits for them, and re-layouts  1.96 us
  transfers between devices with their start and end apart: 20, of which 8 were waited for; matrix products, arithmetic and copies ran while one was open for 0% of the time, Pallas kernels for 10%

profile of v8, /device:TPU:0, one launch (start us, length us, event | category | flops | bytes accessed | tf_op | source)
XLA Modules:
  0.0 70.8 jit_solution(10541183584060156127)
XLA Ops:
  0.0 1.0 %copy-done.2 = bf16[3,8,16,512]{3,2,1,0:T(8,128)(2,1)S(1)} copy-done((bf16[3,8,16,512]{3,2,1,0:T(8,128)(2,1)S(1)}, bf16[3,8,16,512]{3,2,1,0:T(8,128)(2,1)}, u32[]{:S(2)}) %copy-start.2) | copy-done | bytes 393240
  1.0 0.9 %copy-done.3 = f32[8,16,512]{2,1,0:T(8,128)S(1)} copy-done((f32[8,16,512]{2,1,0:T(8,128)S(1)}, f32[8,16,512]{2,1,0:T(8,128)}, u32[]{:S(2)}) %copy-start.3) | copy-done | bytes 262168
  1.9 0.4 shard_map.55
  2.5 3.4 %collective-permute-start.2 = (f32[32,8,512]{2,1,0:T(8,128)S(1)}, f32[32,8,512]{2,1,0:T(8,128)S(1)}, u32[]{:S(2)}, u32[]{:S(2)}) collective-permute-start(f32[32,8,512]{2,1,0:T(8,128)S(1)} %get-tuple-element.41), channel_id=1, source_target_pairs={{4,8},{8,4},{12,16},{16,12},{20,24},{24,20},{28,0},{0,28},{5,9},{9... | collective-permute-start | bytes 1572872 | tf_op jit(solution)/shard_map/ppermute | solution.py:50
  5.9 3.6 %collective-permute-start = (f32[16,8,512]{2,1,0:T(8,128)S(1)}, f32[16,8,512]{2,1,0:T(8,128)S(1)}, u32[]{:S(2)}, u32[]{:S(2)}) collective-permute-start(f32[16,8,512]{2,1,0:T(8,128)S(1)} %get-tuple-element.37), channel_id=1, source_target_pairs={{1,2},{2,1},{3,0},{0,3},{5,6},{6,5},{7,4},{4,7},{9,10},{10,9},{11,... | collective-permute-start | bytes 786440 | tf_op jit(solution)/shard_map/ppermute | solution.py:50
  9.5 8.0 %collective-permute-done.2.refs_1_.refs_2_ = f32[32,8,512]{2,1,0:T(8,128)S(1)} collective-permute-done((f32[32,8,512]{2,1,0:T(8,128)S(1)}, f32[32,8,512]{2,1,0:T(8,128)S(1)}, u32[]{:S(2)}, u32[]{:S(2)}) %collective-permute-start.2) | collective-permute-done | bytes 524320 | tf_op jit(solution)/shard_map/ppermute | solution.py:50
  17.6 0.9 %shard_map.57 = (f32[12,8,256]{2,1,0:T(8,128)S(1)}, bf16[512,256]{1,0:T(8,128)(2,1)S(1)}) custom-call(bf16[3,8,16,512]{3,2,1,0:T(8,128)(2,1)S(1)} %get-tuple-element.39.refs_1_.refs_0_, f32[32,8,512]{2,1,0:T(8,128)S(1)} %collective-permute-done.2.refs_1_.refs_2_, f32[32,8,512]{2,1,0:T(8,128)S(1)} %collective-permute-done.3.refs_2_.refs_3_), custom_call_target="tpu_custom_call" | custom-call | tf_op jit(solution)/shard_map/pallas_call | solution.py:114
  18.9 3.3 %collective-permute-done.1.refs_1_.refs_3_ = f32[16,8,512]{2,1,0:T(8,128)S(1)} collective-permute-done((f32[16,8,512]{2,1,0:T(8,128)S(1)}, f32[16,8,512]{2,1,0:T(8,128)S(1)}, u32[]{:S(2)}, u32[]{:S(2)}) %collective-permute-start.1) | collective-permute-done | bytes 262176 | tf_op jit(solution)/shard_map/ppermute | solution.py:50
  22.7 0.6 collective-permute-start.5
  23.2 1.0 %collective-permute-start.11 = (f32[13,8,256]{2,1,0:T(8,128)S(1)}, f32[13,8,256]{2,1,0:T(8,128)S(1)}, u32[]{:S(2)}, u32[]{:S(2)}) collective-permute-start(f32[13,8,256]{2,1,0:T(8,128)S(1)} %shard_map.58.refs_2_.refs_0_), channel_id=1, source_target_pairs={{0,2},{1,3},{2,0},{3,1},{4,6},{5,7},{6,4},{7,5},{8,10},{9,11},{10,... | collective-permute-start | bytes 319496 | tf_op jit(solution)/shard_map/ppermute | solution.py:34
  24.2 1.6 %collective-permute-start.10 = (f32[13,8,256]{2,1,0:T(8,128)S(1)}, f32[13,8,256]{2,1,0:T(8,128)S(1)}, u32[]{:S(2)}, u32[]{:S(2)}) collective-permute-start(f32[13,8,256]{2,1,0:T(8,128)S(1)} %shard_map.58.refs_2_.refs_0_), channel_id=1, source_target_pairs={{0,1},{1,0},{2,3},{3,2},{4,5},{5,4},{6,7},{7,6},{8,9},{9,8},{10,11... | collective-permute-start | bytes 319496 | tf_op jit(solution)/shard_map/ppermute | solution.py:50
  25.8 1.8 %collective-permute-start.9 = (f32[13,8,256]{2,1,0:T(8,128)S(1)}, f32[13,8,256]{2,1,0:T(8,128)S(1)}, u32[]{:S(2)}, u32[]{:S(2)}) collective-permute-start(f32[13,8,256]{2,1,0:T(8,128)S(1)} %shard_map.58.refs_2_.refs_0_), channel_id=1, source_target_pairs={{1,2},{2,1},{3,0},{0,3},{5,6},{6,5},{7,4},{4,7},{9,10},{10,9},{11,... | collective-permute-start | bytes 319496 | tf_op jit(solution)/shard_map/ppermute | solution.py:50
  27.6 1.0 %collective-permute-done.4.refs_0_ = f32[8,8,512]{2,1,0:T(8,128)S(1)} collective-permute-done((f32[8,8,512]{2,1,0:T(8,128)S(1)}, f32[8,8,512]{2,1,0:T(8,128)S(1)}, u32[]{:S(2)}, u32[]{:S(2)}) %collective-permute-start.4) | collective-permute-done | bytes 131104 | tf_op jit(solution)/shard_map/ppermute | solution.py:50
  28.6 4.0 %shard_map.61 = (f32[5,16,24,512]{3,2,1,0:T(8,128)S(1)}, f32[8,16,512]{2,1,0:T(8,128)S(1)}, f32[4,8,256]{2,1,0:T(8,128)S(1)}, f32[4,8,512]{2,1,0:T(8,128)S(1)}, f32[4,8,512]{2,1,0:T(8,128)S(1)}) custom-call(f32[8,8,512]{2,1,0:T(8,128)S(1)} %collective-permute-done.4.refs_0_, f32[8,8,512]{2,1,0:T(8,128)S(1)} %collective-permute-done.5.refs_1_, ...), custom_call_target="tpu_custom_call" | custom-call | tf_op jit(solution)/shard_map/pallas_call | solution.py:114
  33.0 1.8 %collective-permute-done.9.refs_1_ = f32[13,8,256]{2,1,0:T(8,128)S(1)} collective-permute-done((f32[13,8,256]{2,1,0:T(8,128)S(1)}, f32[13,8,256]{2,1,0:T(8,128)S(1)}, u32[]{:S(2)}, u32[]{:S(2)}) %collective-permute-start.9) | collective-permute-done | bytes 106528 | tf_op jit(solution)/shard_map/ppermute | solution.py:50
  35.1 1.0 %collective-permute-start.14 = (f32[10,32,256]{2,1,0:T(8,128)S(1)}, f32[10,32,256]{2,1,0:T(8,128)S(1)}, u32[]{:S(2)}, u32[]{:S(2)}) collective-permute-start(f32[10,32,256]{2,1,0:T(8,128)S(1)} %get-tuple-element.58), channel_id=1, source_target_pairs={{4,8},{8,4},{12,16},{16,12},{20,24},{24,20},{28,0},{0,28},{5,9},{9... | collective-permute-start | bytes 983048 | tf_op jit(solution)/shard_map/ppermute | solution.py:50
  36.1 0.7 collective-permute-start.15
  36.7 1.6 %collective-permute-start.6 = (f32[4,8,512]{2,1,0:T(8,128)S(1)}, f32[4,8,512]{2,1,0:T(8,128)S(1)}, u32[]{:S(2)}, u32[]{:S(2)}) collective-permute-start(f32[4,8,512]{2,1,0:T(8,128)S(1)} %get-tuple-element.48), channel_id=1, source_target_pairs={{1,2},{2,1},{3,0},{0,3},{5,6},{6,5},{7,4},{4,7},{9,10},{10,9},{11,... | collective-permute-start | bytes 196616 | tf_op jit(solution)/shard_map/ppermute | solution.py:50
  38.3 1.2 %collective-permute-start.7 = (f32[4,8,512]{2,1,0:T(8,128)S(1)}, f32[4,8,512]{2,1,0:T(8,128)S(1)}, u32[]{:S(2)}, u32[]{:S(2)}) collective-permute-start(f32[4,8,512]{2,1,0:T(8,128)S(1)} %get-tuple-element.49), channel_id=1, source_target_pairs={{0,1},{1,0},{2,3},{3,2},{4,5},{5,4},{6,7},{7,6},{8,9},{9,8},{10,11... | collective-permute-start | bytes 196616 | tf_op jit(solution)/shard_map/ppermute | solution.py:50
  39.4 1.7 %collective-permute-start.8 = (f32[4,8,256]{2,1,0:T(8,128)S(1)}, f32[4,8,256]{2,1,0:T(8,128)S(1)}, u32[]{:S(2)}, u32[]{:S(2)}) collective-permute-start(f32[4,8,256]{2,1,0:T(8,128)S(1)} %get-tuple-element.51.refs_4_.refs_2_), channel_id=1, source_target_pairs={{0,2},{1,3},{2,0},{3,1},{4,6},{5,7},{6,4},{7,5},{8,10},{9,11},{10,... | collective-permute-start | bytes 98312 | tf_op jit(solution)/shard_map/ppermute | solution.py:34
  41.1 3.2 %collective-permute-done.8.refs_3_ = f32[4,8,256]{2,1,0:T(8,128)S(1)} collective-permute-done((f32[4,8,256]{2,1,0:T(8,128)S(1)}, f32[4,8,256]{2,1,0:T(8,128)S(1)}, u32[]{:S(2)}, u32[]{:S(2)}) %collective-permute-start.8) | collective-permute-done | bytes 32800 | tf_op jit(solution)/shard_map/ppermute | solution.py:34
  44.4 0.5 collective-permute-start.12
  44.9 1.4 %collective-permute-start.13 = (f32[4,32,256]{2,1,0:T(8,128)S(1)}, f32[4,32,256]{2,1,0:T(8,128)S(1)}, u32[]{:S(2)}, u32[]{:S(2)}) collective-permute-start(f32[4,32,256]{2,1,0:T(8,128)S(1)} %get-tuple-element.56), channel_id=1, source_target_pairs={{0,4},{4,0},{8,12},{12,8},{16,20},{20,16},{24,28},{28,24},{1,5},{5... | collective-permute-start | bytes 393224 | tf_op jit(solution)/shard_map/ppermute | solution.py:50
  46.4 4.5 %collective-permute-done.12.refs_1_ = f32[4,32,256]{2,1,0:T(8,128)S(1)} collective-permute-done((f32[4,32,256]{2,1,0:T(8,128)S(1)}, f32[4,32,256]{2,1,0:T(8,128)S(1)}, u32[]{:S(2)}, u32[]{:S(2)}) %collective-permute-start.12) | collective-permute-done | bytes 131104 | tf_op jit(solution)/shard_map/ppermute | solution.py:50
  51.0 1.0 %shard_map.65 = (f32[7,12,32,256]{3,2,1,0:T(8,128)S(1)}, f32[14,8,512]{2,1,0:T(8,128)S(1)}, f32[14,8,512]{2,1,0:T(8,128)S(1)}) custom-call(f32[4,32,256]{2,1,0:T(8,128)S(1)} %get-tuple-element.54.refs_0_, f32[4,32,256]{2,1,0:T(8,128)S(1)} %collective-permute-done.12.refs_1_, f32[4,32,256]{2,1,0:T(8,128)S(1)} %collective-permute-done.13.refs_2_, ...), custom_call_target="tpu_custom_call" | custom-call | tf_op jit(solution)/shard_map/pallas_call | solution.py:114
  52.0 0.5 collective-permute-start.17
  52.8 9.5 %all_to_all.5.refs_3_ = f32[8,33,128]{2,1,0:T(8,128)S(1)} all-to-all(f32[8,33,128]{2,1,0:T(8,128)S(1)} %shard_map.66), channel_id=1, replica_groups=mesh['gx'=8,'gy'=4] {'gx'}, dimensions={0} | all-to-all | bytes 270336 | tf_op jit(solution)/shard_map/all_to_all | solution.py:652
  62.3 1.8 %shard_map.67 = (f32[4,16,256]{2,1,0:T(8,128)S(1)}, f32[2,16,256]{2,1,0:T(8,128)S(1)}, f32[2,16,256]{2,1,0:T(8,128)S(1)}) custom-call(f32[7,12,32,256]{3,2,1,0:T(8,128)S(1)} %get-tuple-element.64.refs_0_, f32[14,8,512]{2,1,0:T(8,128)S(1)} %collective-permute-done.16.refs_1_, f32[14,8,512]{2,1,0:T(8,128)S(1)} %collective-permute-done.17.refs_2_, ...), custom_call_target="tpu_custom_call" | custom-call | tf_op jit(solution)/shard_map/pallas_call | solution.py:114
  64.4 0.5 collective-permute-start.19
  64.9 1.1 %shard_map.68.refs_0_ = f32[16,24,512]{2,1,0:T(8,128)S(1)} custom-call(f32[8,24,512]{2,1,0:T(8,128)S(1)} %get-tuple-element.50.refs_0_, f32[14,8,512]{2,1,0:T(8,128)S(1)} %collective-permute-done.16.refs_1_, f32[14,8,512]{2,1,0:T(8,128)S(1)} %collective-permute-done.17.refs_2_, f32[4,16,256]{2,1,0:T(8,128)S(1)} %get-tuple-element.66.refs_3_, ...), custom_call_target="tpu_custom_call" | custom-call | tf_op jit(solution)/shard_map/pallas_call | solution.py:114
  66.0 2.4 %collective-permute-done.18.refs_1_ = f32[2,16,256]{2,1,0:T(8,128)S(1)} collective-permute-done((f32[2,16,256]{2,1,0:T(8,128)S(1)}, f32[2,16,256]{2,1,0:T(8,128)S(1)}, u32[]{:S(2)}, u32[]{:S(2)}) %collective-permute-start.18) | collective-permute-done | bytes 32800 | tf_op jit(solution)/shard_map/ppermute | solution.py:50
  68.4 2.4 %shard_map.69 = f32[8,16,512]{2,1,0:T(8,128)} custom-call(f32[16,24,512]{2,1,0:T(8,128)S(1)} %shard_map.68.refs_0_, f32[2,16,256]{2,1,0:T(8,128)S(1)} %collective-permute-done.18.refs_1_, f32[2,16,256]{2,1,0:T(8,128)S(1)} %collective-permute-done.19.refs_2_, f32[5,16,24,512]{3,2,1,0:T(8,128)S(1)} %get-tuple-element.53.refs_5_.refs_8_.refs_4_.refs_3_, ...), custom_call_target="tpu_custom_call" | custom-call | tf_op jit(solution)/shard_map/pallas_call | solution.py:114
  (34 shorter events, 2.5 us)
Async XLA Ops:
  0.0 1.0 %copy-start.2 = (bf16[3,8,16,512]{3,2,1,0:T(8,128)(2,1)S(1)}, bf16[3,8,16,512]{3,2,1,0:T(8,128)(2,1)}, u32[]{:S(2)}) copy-start(bf16[3,8,16,512]{3,2,1,0:T(8,128)(2,1)} %refs_1_.2) | copy-start | bytes 1179652
  1.0 0.9 %copy-start.3 = (f32[8,16,512]{2,1,0:T(8,128)S(1)}, f32[8,16,512]{2,1,0:T(8,128)}, u32[]{:S(2)}) copy-start(f32[8,16,512]{2,1,0:T(8,128)} %refs_0_.1) | copy-start | bytes 786436
  2.5 15.1 %collective-permute-start.2 = (f32[32,8,512]{2,1,0:T(8,128)S(1)}, f32[32,8,512]{2,1,0:T(8,128)S(1)}, u32[]{:S(2)}, u32[]{:S(2)}) collective-permute-start(f32[32,8,512]{2,1,0:T(8,128)S(1)} %get-tuple-element.41), channel_id=1, source_target_pairs={{4,8},{8,4},{12,16},{16,12},{20,24},{24,20},{28,0},{0,28},{5,9},{9... | collective-permute-start | bytes 1572872 | tf_op jit(solution)/shard_map/ppermute | solution.py:50
  5.9 11.7 %collective-permute-start.3 = (f32[32,8,512]{2,1,0:T(8,128)S(1)}, f32[32,8,512]{2,1,0:T(8,128)S(1)}, u32[]{:S(2)}, u32[]{:S(2)}) collective-permute-start(f32[32,8,512]{2,1,0:T(8,128)S(1)} %get-tuple-element.42), channel_id=1, source_target_pairs={{0,4},{4,0},{8,12},{12,8},{16,20},{20,16},{24,28},{28,24},{1,5},{5... | collective-permute-start | bytes 1572872 | tf_op jit(solution)/shard_map/ppermute | solution.py:50
  5.9 13.0 %collective-permute-start = (f32[16,8,512]{2,1,0:T(8,128)S(1)}, f32[16,8,512]{2,1,0:T(8,128)S(1)}, u32[]{:S(2)}, u32[]{:S(2)}) collective-permute-start(f32[16,8,512]{2,1,0:T(8,128)S(1)} %get-tuple-element.37), channel_id=1, source_target_pairs={{1,2},{2,1},{3,0},{0,3},{5,6},{6,5},{7,4},{4,7},{9,10},{10,9},{11,... | collective-permute-start | bytes 786440 | tf_op jit(solution)/shard_map/ppermute | solution.py:50
  9.5 12.7 %collective-permute-start.1 = (f32[16,8,512]{2,1,0:T(8,128)S(1)}, f32[16,8,512]{2,1,0:T(8,128)S(1)}, u32[]{:S(2)}, u32[]{:S(2)}) collective-permute-start(f32[16,8,512]{2,1,0:T(8,128)S(1)} %get-tuple-element.38), channel_id=1, source_target_pairs={{0,1},{1,0},{2,3},{3,2},{4,5},{5,4},{6,7},{7,6},{8,9},{9,8},{10,11... | collective-permute-start | bytes 786440 | tf_op jit(solution)/shard_map/ppermute | solution.py:50
  22.4 6.2 %collective-permute-start.4 = (f32[8,8,512]{2,1,0:T(8,128)S(1)}, f32[8,8,512]{2,1,0:T(8,128)S(1)}, u32[]{:S(2)}, u32[]{:S(2)}) collective-permute-start(f32[8,8,512]{2,1,0:T(8,128)S(1)} %get-tuple-element.45), channel_id=1, source_target_pairs={{4,8},{8,4},{12,16},{16,12},{20,24},{24,20},{28,0},{0,28},{5,9},{9... | collective-permute-start | bytes 393224 | tf_op jit(solution)/shard_map/ppermute | solution.py:50
  22.7 5.9 %collective-permute-start.5 = (f32[8,8,512]{2,1,0:T(8,128)S(1)}, f32[8,8,512]{2,1,0:T(8,128)S(1)}, u32[]{:S(2)}, u32[]{:S(2)}) collective-permute-start(f32[8,8,512]{2,1,0:T(8,128)S(1)} %get-tuple-element.46), channel_id=1, source_target_pairs={{0,4},{4,0},{8,12},{12,8},{16,20},{20,16},{24,28},{28,24},{1,5},{5... | collective-permute-start | bytes 393224 | tf_op jit(solution)/shard_map/ppermute | solution.py:50
  23.2 9.8 %collective-permute-start.11 = (f32[13,8,256]{2,1,0:T(8,128)S(1)}, f32[13,8,256]{2,1,0:T(8,128)S(1)}, u32[]{:S(2)}, u32[]{:S(2)}) collective-permute-start(f32[13,8,256]{2,1,0:T(8,128)S(1)} %shard_map.58.refs_2_.refs_0_), channel_id=1, source_target_pairs={{0,2},{1,3},{2,0},{3,1},{4,6},{5,7},{6,4},{7,5},{8,10},{9,11},{10,... | collective-permute-start | bytes 319496 | tf_op jit(solution)/shard_map/ppermute | solution.py:34
  24.2 8.8 %collective-permute-start.10 = (f32[13,8,256]{2,1,0:T(8,128)S(1)}, f32[13,8,256]{2,1,0:T(8,128)S(1)}, u32[]{:S(2)}, u32[]{:S(2)}) collective-permute-start(f32[13,8,256]{2,1,0:T(8,128)S(1)} %shard_map.58.refs_2_.refs_0_), channel_id=1, source_target_pairs={{0,1},{1,0},{2,3},{3,2},{4,5},{5,4},{6,7},{7,6},{8,9},{9,8},{10,11... | collective-permute-start | bytes 319496 | tf_op jit(solution)/shard_map/ppermute | solution.py:50
  25.8 9.0 %collective-permute-start.9 = (f32[13,8,256]{2,1,0:T(8,128)S(1)}, f32[13,8,256]{2,1,0:T(8,128)S(1)}, u32[]{:S(2)}, u32[]{:S(2)}) collective-permute-start(f32[13,8,256]{2,1,0:T(8,128)S(1)} %shard_map.58.refs_2_.refs_0_), channel_id=1, source_target_pairs={{1,2},{2,1},{3,0},{0,3},{5,6},{6,5},{7,4},{4,7},{9,10},{10,9},{11,... | collective-permute-start | bytes 319496 | tf_op jit(solution)/shard_map/ppermute | solution.py:50
  35.1 15.9 %collective-permute-start.14 = (f32[10,32,256]{2,1,0:T(8,128)S(1)}, f32[10,32,256]{2,1,0:T(8,128)S(1)}, u32[]{:S(2)}, u32[]{:S(2)}) collective-permute-start(f32[10,32,256]{2,1,0:T(8,128)S(1)} %get-tuple-element.58), channel_id=1, source_target_pairs={{4,8},{8,4},{12,16},{16,12},{20,24},{24,20},{28,0},{0,28},{5,9},{9... | collective-permute-start | bytes 983048 | tf_op jit(solution)/shard_map/ppermute | solution.py:50
  36.1 14.9 %collective-permute-start.15 = (f32[10,32,256]{2,1,0:T(8,128)S(1)}, f32[10,32,256]{2,1,0:T(8,128)S(1)}, u32[]{:S(2)}, u32[]{:S(2)}) collective-permute-start(f32[10,32,256]{2,1,0:T(8,128)S(1)} %get-tuple-element.59), channel_id=1, source_target_pairs={{0,4},{4,0},{8,12},{12,8},{16,20},{20,16},{24,28},{28,24},{1,5},{5... | collective-permute-start | bytes 983048 | tf_op jit(solution)/shard_map/ppermute | solution.py:50
  36.7 7.6 %collective-permute-start.6 = (f32[4,8,512]{2,1,0:T(8,128)S(1)}, f32[4,8,512]{2,1,0:T(8,128)S(1)}, u32[]{:S(2)}, u32[]{:S(2)}) collective-permute-start(f32[4,8,512]{2,1,0:T(8,128)S(1)} %get-tuple-element.48), channel_id=1, source_target_pairs={{1,2},{2,1},{3,0},{0,3},{5,6},{6,5},{7,4},{4,7},{9,10},{10,9},{11,... | collective-permute-start | bytes 196616 | tf_op jit(solution)/shard_map/ppermute | solution.py:50
  38.3 6.0 %collective-permute-start.7 = (f32[4,8,512]{2,1,0:T(8,128)S(1)}, f32[4,8,512]{2,1,0:T(8,128)S(1)}, u32[]{:S(2)}, u32[]{:S(2)}) collective-permute-start(f32[4,8,512]{2,1,0:T(8,128)S(1)} %get-tuple-element.49), channel_id=1, source_target_pairs={{0,1},{1,0},{2,3},{3,2},{4,5},{5,4},{6,7},{7,6},{8,9},{9,8},{10,11... | collective-permute-start | bytes 196616 | tf_op jit(solution)/shard_map/ppermute | solution.py:50
  39.4 4.9 %collective-permute-start.8 = (f32[4,8,256]{2,1,0:T(8,128)S(1)}, f32[4,8,256]{2,1,0:T(8,128)S(1)}, u32[]{:S(2)}, u32[]{:S(2)}) collective-permute-start(f32[4,8,256]{2,1,0:T(8,128)S(1)} %get-tuple-element.51.refs_4_.refs_2_), channel_id=1, source_target_pairs={{0,2},{1,3},{2,0},{3,1},{4,6},{5,7},{6,4},{7,5},{8,10},{9,11},{10,... | collective-permute-start | bytes 98312 | tf_op jit(solution)/shard_map/ppermute | solution.py:34
  44.4 8.1 %copy-start.4 = (bf16[256,128]{1,0:T(8,128)(2,1)S(1)}, bf16[256,128]{1,0:T(8,128)(2,1)}, u32[]{:S(2)}) copy-start(bf16[256,128]{1,0:T(8,128)(2,1)} %constant.6.clone.refs_1_) | copy-start | bytes 196612
  44.4 6.6 %collective-permute-start.12 = (f32[4,32,256]{2,1,0:T(8,128)S(1)}, f32[4,32,256]{2,1,0:T(8,128)S(1)}, u32[]{:S(2)}, u32[]{:S(2)}) collective-permute-start(f32[4,32,256]{2,1,0:T(8,128)S(1)} %get-tuple-element.55), channel_id=1, source_target_pairs={{4,8},{8,4},{12,16},{16,12},{20,24},{24,20},{28,0},{0,28},{5,9},{9... | collective-permute-start | bytes 393224 | tf_op jit(solution)/shard_map/ppermute | solution.py:50
  44.9 6.0 %collective-permute-start.13 = (f32[4,32,256]{2,1,0:T(8,128)S(1)}, f32[4,32,256]{2,1,0:T(8,128)S(1)}, u32[]{:S(2)}, u32[]{:S(2)}) collective-permute-start(f32[4,32,256]{2,1,0:T(8,128)S(1)} %get-tuple-element.56), channel_id=1, source_target_pairs={{0,4},{4,0},{8,12},{12,8},{16,20},{20,16},{24,28},{28,24},{1,5},{5... | collective-permute-start | bytes 393224 | tf_op jit(solution)/shard_map/ppermute | solution.py:50
  51.0 11.4 %copy-start.1 = (f32[848,256]{1,0:T(8,128)S(1)}, f32[848,256]{1,0:T(8,128)}, u32[]{:S(2)}) copy-start(f32[848,256]{1,0:T(8,128)} %constant.7.clone.refs_4_) | copy-start | bytes 2605060
  51.9 10.4 %collective-permute-start.16 = (f32[14,8,512]{2,1,0:T(8,128)S(1)}, f32[14,8,512]{2,1,0:T(8,128)S(1)}, u32[]{:S(2)}, u32[]{:S(2)}) collective-permute-start(f32[14,8,512]{2,1,0:T(8,128)S(1)} %get-tuple-element.62), channel_id=1, source_target_pairs={{4,8},{8,4},{12,16},{16,12},{20,24},{24,20},{28,0},{0,28},{5,9},{9... | collective-permute-start | bytes 688136 | tf_op jit(solution)/shard_map/ppermute | solution.py:50
  52.0 10.3 %collective-permute-start.17 = (f32[14,8,512]{2,1,0:T(8,128)S(1)}, f32[14,8,512]{2,1,0:T(8,128)S(1)}, u32[]{:S(2)}, u32[]{:S(2)}) collective-permute-start(f32[14,8,512]{2,1,0:T(8,128)S(1)} %get-tuple-element.63), channel_id=1, source_target_pairs={{0,4},{4,0},{8,12},{12,8},{16,20},{20,16},{24,28},{28,24},{1,5},{5... | collective-permute-start | bytes 688136 | tf_op jit(solution)/shard_map/ppermute | solution.py:50
  52.5 12.4 %copy-start = (bf16[256,512]{1,0:T(8,128)(2,1)S(1)}, bf16[256,512]{1,0:T(8,128)(2,1)}, u32[]{:S(2)}) copy-start(bf16[256,512]{1,0:T(8,128)(2,1)} %constant.8.clone.refs_5_.refs_4_) | copy-start | bytes 786436
  64.1 4.3 %collective-permute-start.18 = (f32[2,16,256]{2,1,0:T(8,128)S(1)}, f32[2,16,256]{2,1,0:T(8,128)S(1)}, u32[]{:S(2)}, u32[]{:S(2)}) collective-permute-start(f32[2,16,256]{2,1,0:T(8,128)S(1)} %get-tuple-element.67), channel_id=1, source_target_pairs={{4,8},{8,4},{12,16},{16,12},{20,24},{24,20},{28,0},{0,28},{5,9},{9... | collective-permute-start | bytes 98312 | tf_op jit(solution)/shard_map/ppermute | solution.py:50
  64.4 4.0 %collective-permute-start.19 = (f32[2,16,256]{2,1,0:T(8,128)S(1)}, f32[2,16,256]{2,1,0:T(8,128)S(1)}, u32[]{:S(2)}, u32[]{:S(2)}) collective-permute-start(f32[2,16,256]{2,1,0:T(8,128)S(1)} %get-tuple-element.68), channel_id=1, source_target_pairs={{0,4},{4,0},{8,12},{12,8},{16,20},{20,16},{24,28},{28,24},{1,5},{5... | collective-permute-start | bytes 98312 | tf_op jit(solution)/shard_map/ppermute | solution.py:50

commit v9 on v7

--- a/solution.py
+++ b/solution.py
@@ -464,11 +464,12 @@
     half_sweep(3, er - 3, 1, parity, v, b, wx, wy, wz, rdiag)
     for out, base, v0 in ((to_up, rows, v0_up), (to_down, H, v0_down)):
         n = 0
-        for k in range(H // 2):
-            value = jnp.concatenate((v[base + 2 * k], v[base + 2 * k + 1]), axis=1)
-            for t in range(wide // 8):
-                out[n] = value[8 * t : 8 * t + 8]
-                n += 1
+        pair_rows = range(base, base + H, 2)
+        value = [jnp.where(parity == ((r + 1) & 1), v[r], v[r + 1]) for r in pair_rows]
+        value = jnp.concatenate(value, axis=1)
+        for t in range(wide // 8):
+            out[n] = value[8 * t : 8 * t + 8]
+            n += 1
         for k in range(H // 2):
             for t in range(v0.shape[1] // 8):
                 out[n] = v0[k, 8 * t : 8 * t + 8]
@@ -546,11 +547,11 @@
     for r in range(rows):
         v[H + r] = before[H + r] + correction[H + r]
     for msg, base in ((up, 0), (down, H + rows)):
+        value = jnp.concatenate([msg[t] for t in range(wide // 8)], axis=0)
         for k in range(H // 2):
-            n = k * (wide // 8)
-            value = jnp.concatenate([msg[n + t] for t in range(wide // 8)], axis=0)
-            v[base + 2 * k] = value[:, :depth] + correction[base + 2 * k]
-            v[base + 2 * k + 1] = value[:, depth:] + correction[base + 2 * k + 1]
+            part = value[:, k * depth : (k + 1) * depth]
+            v[base + 2 * k] = part + correction[base + 2 * k]
+            v[base + 2 * k + 1] = part + correction[base + 2 * k + 1]
     parity = parity2((wide, depth))
     half_sweep(1, er - 1, 0, parity, v, b, wx, wy, wz, rdiag)
     half_sweep(2, er - 2, 1, parity, v, b, wx, wy, wz, rdiag)
@@ -772,7 +773,7 @@
     )
     x_second = x_second.exchanged()
     v0_rows, v0_up, v0_down = call(pack_v_kernel, [(rows, ec, depth)] + [(h, ec, depth)] * 2, v0, y_second)
-    tiles = h * (wide // 8 + ec // 8)
+    tiles = wide // 8 + h * (ec // 8)
     kept1, x_third = call(
         pre1_kernel,
         [(7, er1, wide, depth1), Beside("gx", (tiles, 8, depth))],

time: 71.2 us -> 71.2 us (level)
  no operation moved by 1% of the time
where the time goes in v9:
time: 71.2 us; the launch traced here: 71 us
  waiting for transfers between devices  24.6 us (35%)
  starting transfers between devices  21.5 us (30%)
  Pallas kernels  13 us (18%)
  blocking collectives  9.66 us (14%)
  local copies, waits for them, and re-layouts  1.97 us (3%)
    ppermute x18, waiting for transfers between devices, exchanged(): got.append(lax.ppermute(block, self.axis, route))  21.1 us
    ppermute x18, starting transfers between devices, exchanged(): got.append(lax.ppermute(block, self.axis, route))  18.9 us
    pallas_call x16, Pallas kernels, call(): pl.pallas_call(body, out_shape=[s if hasattr(s, 'dtype') else jax.ShapeDt...  13 us
    all_to_all x1, blocking collectives, coarse_correction(): got = lax.all_to_all(chunks, 'gx', 0, 0)  9.66 us
    ppermute x2, waiting for transfers between devices, moved(): lax.ppermute(block, axis, [(i, (i + distance) % count) for i in range(cou...  3.59 us
    ppermute x2, starting transfers between devices, moved(): lax.ppermute(block, axis, [(i, (i + distance) % count) for i in range(cou...  2.66 us
    unnamed x10, local copies, waits for them, and re-layouts  1.97 us
  transfers between devices with their start and end apart: 20, of which 8 were waited for; matrix products, arithmetic and copies ran while one was open for 0% of the time, Pallas kernels for 11%

profile of v9, /device:TPU:0, one launch (start us, length us, event | category | flops | bytes accessed | tf_op | source)
XLA Modules:
  0.0 71.0 jit_solution(9870083752179673441)
XLA Ops:
  0.0 1.0 %copy-done.2 = bf16[3,8,16,512]{3,2,1,0:T(8,128)(2,1)S(1)} copy-done((bf16[3,8,16,512]{3,2,1,0:T(8,128)(2,1)S(1)}, bf16[3,8,16,512]{3,2,1,0:T(8,128)(2,1)}, u32[]{:S(2)}) %copy-start.2) | copy-done | bytes 393240
  1.0 0.9 %copy-done.3 = f32[8,16,512]{2,1,0:T(8,128)S(1)} copy-done((f32[8,16,512]{2,1,0:T(8,128)S(1)}, f32[8,16,512]{2,1,0:T(8,128)}, u32[]{:S(2)}) %copy-start.3) | copy-done | bytes 262168
  2.5 3.4 %collective-permute-start.2 = (f32[32,8,512]{2,1,0:T(8,128)S(1)}, f32[32,8,512]{2,1,0:T(8,128)S(1)}, u32[]{:S(2)}, u32[]{:S(2)}) collective-permute-start(f32[32,8,512]{2,1,0:T(8,128)S(1)} %get-tuple-element.41), channel_id=1, source_target_pairs={{4,8},{8,4},{12,16},{16,12},{20,24},{24,20},{28,0},{0,28},{5,9},{9... | collective-permute-start | bytes 1572872 | tf_op jit(solution)/shard_map/ppermute | solution.py:50
  5.9 3.6 %collective-permute-start = (f32[16,8,512]{2,1,0:T(8,128)S(1)}, f32[16,8,512]{2,1,0:T(8,128)S(1)}, u32[]{:S(2)}, u32[]{:S(2)}) collective-permute-start(f32[16,8,512]{2,1,0:T(8,128)S(1)} %get-tuple-element.37), channel_id=1, source_target_pairs={{1,2},{2,1},{3,0},{0,3},{5,6},{6,5},{7,4},{4,7},{9,10},{10,9},{11,... | collective-permute-start | bytes 786440 | tf_op jit(solution)/shard_map/ppermute | solution.py:50
  9.5 8.0 %collective-permute-done.2.refs_1_.refs_2_ = f32[32,8,512]{2,1,0:T(8,128)S(1)} collective-permute-done((f32[32,8,512]{2,1,0:T(8,128)S(1)}, f32[32,8,512]{2,1,0:T(8,128)S(1)}, u32[]{:S(2)}, u32[]{:S(2)}) %collective-permute-start.2) | collective-permute-done | bytes 524320 | tf_op jit(solution)/shard_map/ppermute | solution.py:50
  17.6 0.9 %shard_map.57 = (f32[12,8,256]{2,1,0:T(8,128)S(1)}, bf16[512,256]{1,0:T(8,128)(2,1)S(1)}) custom-call(bf16[3,8,16,512]{3,2,1,0:T(8,128)(2,1)S(1)} %get-tuple-element.39.refs_1_.refs_0_, f32[32,8,512]{2,1,0:T(8,128)S(1)} %collective-permute-done.2.refs_1_.refs_2_, f32[32,8,512]{2,1,0:T(8,128)S(1)} %collective-permute-done.3.refs_2_.refs_3_), custom_call_target="tpu_custom_call" | custom-call | tf_op jit(solution)/shard_map/pallas_call | solution.py:114
  18.9 3.3 %collective-permute-done.1.refs_1_.refs_3_ = f32[16,8,512]{2,1,0:T(8,128)S(1)} collective-permute-done((f32[16,8,512]{2,1,0:T(8,128)S(1)}, f32[16,8,512]{2,1,0:T(8,128)S(1)}, u32[]{:S(2)}, u32[]{:S(2)}) %collective-permute-start.1) | collective-permute-done | bytes 262176 | tf_op jit(solution)/shard_map/ppermute | solution.py:50
  22.7 0.6 collective-permute-start.5
  23.2 1.0 %collective-permute-start.11 = (f32[13,8,256]{2,1,0:T(8,128)S(1)}, f32[13,8,256]{2,1,0:T(8,128)S(1)}, u32[]{:S(2)}, u32[]{:S(2)}) collective-permute-start(f32[13,8,256]{2,1,0:T(8,128)S(1)} %shard_map.58.refs_2_.refs_0_), channel_id=1, source_target_pairs={{0,2},{1,3},{2,0},{3,1},{4,6},{5,7},{6,4},{7,5},{8,10},{9,11},{10,... | collective-permute-start | bytes 319496 | tf_op jit(solution)/shard_map/ppermute | solution.py:34
  24.2 1.6 %collective-permute-start.10 = (f32[13,8,256]{2,1,0:T(8,128)S(1)}, f32[13,8,256]{2,1,0:T(8,128)S(1)}, u32[]{:S(2)}, u32[]{:S(2)}) collective-permute-start(f32[13,8,256]{2,1,0:T(8,128)S(1)} %shard_map.58.refs_2_.refs_0_), channel_id=1, source_target_pairs={{0,1},{1,0},{2,3},{3,2},{4,5},{5,4},{6,7},{7,6},{8,9},{9,8},{10,11... | collective-permute-start | bytes 319496 | tf_op jit(solution)/shard_map/ppermute | solution.py:50
  25.8 1.8 %collective-permute-start.9 = (f32[13,8,256]{2,1,0:T(8,128)S(1)}, f32[13,8,256]{2,1,0:T(8,128)S(1)}, u32[]{:S(2)}, u32[]{:S(2)}) collective-permute-start(f32[13,8,256]{2,1,0:T(8,128)S(1)} %shard_map.58.refs_2_.refs_0_), channel_id=1, source_target_pairs={{1,2},{2,1},{3,0},{0,3},{5,6},{6,5},{7,4},{4,7},{9,10},{10,9},{11,... | collective-permute-start | bytes 319496 | tf_op jit(solution)/shard_map/ppermute | solution.py:50
  27.6 1.0 %collective-permute-done.4.refs_0_ = f32[8,8,512]{2,1,0:T(8,128)S(1)} collective-permute-done((f32[8,8,512]{2,1,0:T(8,128)S(1)}, f32[8,8,512]{2,1,0:T(8,128)S(1)}, u32[]{:S(2)}, u32[]{:S(2)}) %collective-permute-start.4) | collective-permute-done | bytes 131104 | tf_op jit(solution)/shard_map/ppermute | solution.py:50
  28.6 4.0 %shard_map.61 = (f32[5,16,24,512]{3,2,1,0:T(8,128)S(1)}, f32[8,16,512]{2,1,0:T(8,128)S(1)}, f32[4,8,256]{2,1,0:T(8,128)S(1)}, f32[4,8,512]{2,1,0:T(8,128)S(1)}, f32[4,8,512]{2,1,0:T(8,128)S(1)}) custom-call(f32[8,8,512]{2,1,0:T(8,128)S(1)} %collective-permute-done.4.refs_0_, f32[8,8,512]{2,1,0:T(8,128)S(1)} %collective-permute-done.5.refs_1_, ...), custom_call_target="tpu_custom_call" | custom-call | tf_op jit(solution)/shard_map/pallas_call | solution.py:114
  33.0 1.8 %collective-permute-done.9.refs_1_ = f32[13,8,256]{2,1,0:T(8,128)S(1)} collective-permute-done((f32[13,8,256]{2,1,0:T(8,128)S(1)}, f32[13,8,256]{2,1,0:T(8,128)S(1)}, u32[]{:S(2)}, u32[]{:S(2)}) %collective-permute-start.9) | collective-permute-done | bytes 106528 | tf_op jit(solution)/shard_map/ppermute | solution.py:50
  35.1 1.0 %collective-permute-start.14 = (f32[10,32,256]{2,1,0:T(8,128)S(1)}, f32[10,32,256]{2,1,0:T(8,128)S(1)}, u32[]{:S(2)}, u32[]{:S(2)}) collective-permute-start(f32[10,32,256]{2,1,0:T(8,128)S(1)} %get-tuple-element.58), channel_id=1, source_target_pairs={{4,8},{8,4},{12,16},{16,12},{20,24},{24,20},{28,0},{0,28},{5,9},{9... | collective-permute-start | bytes 983048 | tf_op jit(solution)/shard_map/ppermute | solution.py:50
  36.1 0.7 collective-permute-start.15
  36.7 1.6 %collective-permute-start.6 = (f32[4,8,512]{2,1,0:T(8,128)S(1)}, f32[4,8,512]{2,1,0:T(8,128)S(1)}, u32[]{:S(2)}, u32[]{:S(2)}) collective-permute-start(f32[4,8,512]{2,1,0:T(8,128)S(1)} %get-tuple-element.48), channel_id=1, source_target_pairs={{1,2},{2,1},{3,0},{0,3},{5,6},{6,5},{7,4},{4,7},{9,10},{10,9},{11,... | collective-permute-start | bytes 196616 | tf_op jit(solution)/shard_map/ppermute | solution.py:50
  38.3 1.2 %collective-permute-start.7 = (f32[4,8,512]{2,1,0:T(8,128)S(1)}, f32[4,8,512]{2,1,0:T(8,128)S(1)}, u32[]{:S(2)}, u32[]{:S(2)}) collective-permute-start(f32[4,8,512]{2,1,0:T(8,128)S(1)} %get-tuple-element.49), channel_id=1, source_target_pairs={{0,1},{1,0},{2,3},{3,2},{4,5},{5,4},{6,7},{7,6},{8,9},{9,8},{10,11... | collective-permute-start | bytes 196616 | tf_op jit(solution)/shard_map/ppermute | solution.py:50
  39.4 1.7 %collective-permute-start.8 = (f32[4,8,256]{2,1,0:T(8,128)S(1)}, f32[4,8,256]{2,1,0:T(8,128)S(1)}, u32[]{:S(2)}, u32[]{:S(2)}) collective-permute-start(f32[4,8,256]{2,1,0:T(8,128)S(1)} %get-tuple-element.51.refs_4_.refs_2_), channel_id=1, source_target_pairs={{0,2},{1,3},{2,0},{3,1},{4,6},{5,7},{6,4},{7,5},{8,10},{9,11},{10,... | collective-permute-start | bytes 98312 | tf_op jit(solution)/shard_map/ppermute | solution.py:34
  41.1 3.2 %collective-permute-done.8.refs_3_ = f32[4,8,256]{2,1,0:T(8,128)S(1)} collective-permute-done((f32[4,8,256]{2,1,0:T(8,128)S(1)}, f32[4,8,256]{2,1,0:T(8,128)S(1)}, u32[]{:S(2)}, u32[]{:S(2)}) %collective-permute-start.8) | collective-permute-done | bytes 32800 | tf_op jit(solution)/shard_map/ppermute | solution.py:34
  44.4 0.5 collective-permute-start.12
  44.9 1.4 %collective-permute-start.13 = (f32[4,32,256]{2,1,0:T(8,128)S(1)}, f32[4,32,256]{2,1,0:T(8,128)S(1)}, u32[]{:S(2)}, u32[]{:S(2)}) collective-permute-start(f32[4,32,256]{2,1,0:T(8,128)S(1)} %get-tuple-element.56), channel_id=1, source_target_pairs={{0,4},{4,0},{8,12},{12,8},{16,20},{20,16},{24,28},{28,24},{1,5},{5... | collective-permute-start | bytes 393224 | tf_op jit(solution)/shard_map/ppermute | solution.py:50
  46.4 4.5 %collective-permute-done.12.refs_1_ = f32[4,32,256]{2,1,0:T(8,128)S(1)} collective-permute-done((f32[4,32,256]{2,1,0:T(8,128)S(1)}, f32[4,32,256]{2,1,0:T(8,128)S(1)}, u32[]{:S(2)}, u32[]{:S(2)}) %collective-permute-start.12) | collective-permute-done | bytes 131104 | tf_op jit(solution)/shard_map/ppermute | solution.py:50
  51.0 1.0 %shard_map.65 = (f32[7,12,32,256]{3,2,1,0:T(8,128)S(1)}, f32[10,8,512]{2,1,0:T(8,128)S(1)}, f32[10,8,512]{2,1,0:T(8,128)S(1)}) custom-call(f32[4,32,256]{2,1,0:T(8,128)S(1)} %get-tuple-element.54.refs_0_, f32[4,32,256]{2,1,0:T(8,128)S(1)} %collective-permute-done.12.refs_1_, f32[4,32,256]{2,1,0:T(8,128)S(1)} %collective-permute-done.13.refs_2_, ...), custom_call_target="tpu_custom_call" | custom-call | tf_op jit(solution)/shard_map/pallas_call | solution.py:114
  52.0 0.5 collective-permute-start.17
  52.8 9.7 %all_to_all.5.refs_0_ = f32[8,33,128]{2,1,0:T(8,128)S(1)} all-to-all(f32[8,33,128]{2,1,0:T(8,128)S(1)} %shard_map.66), channel_id=1, replica_groups=mesh['gx'=8,'gy'=4] {'gx'}, dimensions={0} | all-to-all | bytes 270336 | tf_op jit(solution)/shard_map/all_to_all | solution.py:648
  62.4 1.0 %shard_map.67.refs_3_ = f32[12,32,256]{2,1,0:T(8,128)S(1)} custom-call(f32[8,33,128]{2,1,0:T(8,128)S(1)} %all_to_all.5.refs_0_, f32[848,256]{1,0:T(8,128)S(1)} %copy-done.1), custom_call_target="tpu_custom_call" | custom-call | tf_op jit(solution)/shard_map/pallas_call | solution.py:114
  63.5 0.7 %shard_map.68 = (f32[4,16,256]{2,1,0:T(8,128)S(1)}, f32[2,16,256]{2,1,0:T(8,128)S(1)}, f32[2,16,256]{2,1,0:T(8,128)S(1)}) custom-call(f32[7,12,32,256]{3,2,1,0:T(8,128)S(1)} %get-tuple-element.64.refs_0_, f32[10,8,512]{2,1,0:T(8,128)S(1)} %collective-permute-done.16.refs_1_, f32[10,8,512]{2,1,0:T(8,128)S(1)} %collective-permute-done.17.refs_2_, ...), custom_call_target="tpu_custom_call" | custom-call | tf_op jit(solution)/shard_map/pallas_call | solution.py:114
  64.3 0.7 collective-permute-start.19
  65.0 1.1 %shard_map.69.refs_0_ = f32[16,24,512]{2,1,0:T(8,128)S(1)} custom-call(f32[8,24,512]{2,1,0:T(8,128)S(1)} %get-tuple-element.50.refs_0_, f32[10,8,512]{2,1,0:T(8,128)S(1)} %collective-permute-done.16.refs_1_, f32[10,8,512]{2,1,0:T(8,128)S(1)} %collective-permute-done.17.refs_2_, f32[4,16,256]{2,1,0:T(8,128)S(1)} %get-tuple-element.66.refs_3_, ...), custom_call_target="tpu_custom_call" | custom-call | tf_op jit(solution)/shard_map/pallas_call | solution.py:114
  66.1 2.4 %collective-permute-done.18.refs_1_ = f32[2,16,256]{2,1,0:T(8,128)S(1)} collective-permute-done((f32[2,16,256]{2,1,0:T(8,128)S(1)}, f32[2,16,256]{2,1,0:T(8,128)S(1)}, u32[]{:S(2)}, u32[]{:S(2)}) %collective-permute-start.18) | collective-permute-done | bytes 32800 | tf_op jit(solution)/shard_map/ppermute | solution.py:50
  68.6 2.4 %shard_map.70 = f32[8,16,512]{2,1,0:T(8,128)} custom-call(f32[16,24,512]{2,1,0:T(8,128)S(1)} %shard_map.69.refs_0_, f32[2,16,256]{2,1,0:T(8,128)S(1)} %collective-permute-done.18.refs_1_, f32[2,16,256]{2,1,0:T(8,128)S(1)} %collective-permute-done.19.refs_2_, f32[5,16,24,512]{3,2,1,0:T(8,128)S(1)} %get-tuple-element.53.refs_5_.refs_8_.refs_4_.refs_3_, ...), custom_call_target="tpu_custom_call" | custom-call | tf_op jit(solution)/shard_map/pallas_call | solution.py:114
  (35 shorter events, 2.7 us)
Async XLA Ops:
  0.0 1.0 %copy-start.2 = (bf16[3,8,16,512]{3,2,1,0:T(8,128)(2,1)S(1)}, bf16[3,8,16,512]{3,2,1,0:T(8,128)(2,1)}, u32[]{:S(2)}) copy-start(bf16[3,8,16,512]{3,2,1,0:T(8,128)(2,1)} %refs_1_.3) | copy-start | bytes 1179652
  1.0 0.9 %copy-start.3 = (f32[8,16,512]{2,1,0:T(8,128)S(1)}, f32[8,16,512]{2,1,0:T(8,128)}, u32[]{:S(2)}) copy-start(f32[8,16,512]{2,1,0:T(8,128)} %refs_0_.1) | copy-start | bytes 786436
  2.5 15.1 %collective-permute-start.2 = (f32[32,8,512]{2,1,0:T(8,128)S(1)}, f32[32,8,512]{2,1,0:T(8,128)S(1)}, u32[]{:S(2)}, u32[]{:S(2)}) collective-permute-start(f32[32,8,512]{2,1,0:T(8,128)S(1)} %get-tuple-element.41), channel_id=1, source_target_pairs={{4,8},{8,4},{12,16},{16,12},{20,24},{24,20},{28,0},{0,28},{5,9},{9... | collective-permute-start | bytes 1572872 | tf_op jit(solution)/shard_map/ppermute | solution.py:50
  5.9 11.7 %collective-permute-start.3 = (f32[32,8,512]{2,1,0:T(8,128)S(1)}, f32[32,8,512]{2,1,0:T(8,128)S(1)}, u32[]{:S(2)}, u32[]{:S(2)}) collective-permute-start(f32[32,8,512]{2,1,0:T(8,128)S(1)} %get-tuple-element.42), channel_id=1, source_target_pairs={{0,4},{4,0},{8,12},{12,8},{16,20},{20,16},{24,28},{28,24},{1,5},{5... | collective-permute-start | bytes 1572872 | tf_op jit(solution)/shard_map/ppermute | solution.py:50
  5.9 13.0 %collective-permute-start = (f32[16,8,512]{2,1,0:T(8,128)S(1)}, f32[16,8,512]{2,1,0:T(8,128)S(1)}, u32[]{:S(2)}, u32[]{:S(2)}) collective-permute-start(f32[16,8,512]{2,1,0:T(8,128)S(1)} %get-tuple-element.37), channel_id=1, source_target_pairs={{1,2},{2,1},{3,0},{0,3},{5,6},{6,5},{7,4},{4,7},{9,10},{10,9},{11,... | collective-permute-start | bytes 786440 | tf_op jit(solution)/shard_map/ppermute | solution.py:50
  9.5 12.7 %collective-permute-start.1 = (f32[16,8,512]{2,1,0:T(8,128)S(1)}, f32[16,8,512]{2,1,0:T(8,128)S(1)}, u32[]{:S(2)}, u32[]{:S(2)}) collective-permute-start(f32[16,8,512]{2,1,0:T(8,128)S(1)} %get-tuple-element.38), channel_id=1, source_target_pairs={{0,1},{1,0},{2,3},{3,2},{4,5},{5,4},{6,7},{7,6},{8,9},{9,8},{10,11... | collective-permute-start | bytes 786440 | tf_op jit(solution)/shard_map/ppermute | solution.py:50
  22.4 6.2 %collective-permute-start.4 = (f32[8,8,512]{2,1,0:T(8,128)S(1)}, f32[8,8,512]{2,1,0:T(8,128)S(1)}, u32[]{:S(2)}, u32[]{:S(2)}) collective-permute-start(f32[8,8,512]{2,1,0:T(8,128)S(1)} %get-tuple-element.45), channel_id=1, source_target_pairs={{4,8},{8,4},{12,16},{16,12},{20,24},{24,20},{28,0},{0,28},{5,9},{9... | collective-permute-start | bytes 393224 | tf_op jit(solution)/shard_map/ppermute | solution.py:50
  22.7 5.9 %collective-permute-start.5 = (f32[8,8,512]{2,1,0:T(8,128)S(1)}, f32[8,8,512]{2,1,0:T(8,128)S(1)}, u32[]{:S(2)}, u32[]{:S(2)}) collective-permute-start(f32[8,8,512]{2,1,0:T(8,128)S(1)} %get-tuple-element.46), channel_id=1, source_target_pairs={{0,4},{4,0},{8,12},{12,8},{16,20},{20,16},{24,28},{28,24},{1,5},{5... | collective-permute-start | bytes 393224 | tf_op jit(solution)/shard_map/ppermute | solution.py:50
  23.2 9.8 %collective-permute-start.11 = (f32[13,8,256]{2,1,0:T(8,128)S(1)}, f32[13,8,256]{2,1,0:T(8,128)S(1)}, u32[]{:S(2)}, u32[]{:S(2)}) collective-permute-start(f32[13,8,256]{2,1,0:T(8,128)S(1)} %shard_map.58.refs_2_.refs_0_), channel_id=1, source_target_pairs={{0,2},{1,3},{2,0},{3,1},{4,6},{5,7},{6,4},{7,5},{8,10},{9,11},{10,... | collective-permute-start | bytes 319496 | tf_op jit(solution)/shard_map/ppermute | solution.py:34
  24.2 8.8 %collective-permute-start.10 = (f32[13,8,256]{2,1,0:T(8,128)S(1)}, f32[13,8,256]{2,1,0:T(8,128)S(1)}, u32[]{:S(2)}, u32[]{:S(2)}) collective-permute-start(f32[13,8,256]{2,1,0:T(8,128)S(1)} %shard_map.58.refs_2_.refs_0_), channel_id=1, source_target_pairs={{0,1},{1,0},{2,3},{3,2},{4,5},{5,4},{6,7},{7,6},{8,9},{9,8},{10,11... | collective-permute-start | bytes 319496 | tf_op jit(solution)/shard_map/ppermute | solution.py:50
  25.8 9.0 %collective-permute-start.9 = (f32[13,8,256]{2,1,0:T(8,128)S(1)}, f32[13,8,256]{2,1,0:T(8,128)S(1)}, u32[]{:S(2)}, u32[]{:S(2)}) collective-permute-start(f32[13,8,256]{2,1,0:T(8,128)S(1)} %shard_map.58.refs_2_.refs_0_), channel_id=1, source_target_pairs={{1,2},{2,1},{3,0},{0,3},{5,6},{6,5},{7,4},{4,7},{9,10},{10,9},{11,... | collective-permute-start | bytes 319496 | tf_op jit(solution)/shard_map/ppermute | solution.py:50
  35.1 15.9 %collective-permute-start.14 = (f32[10,32,256]{2,1,0:T(8,128)S(1)}, f32[10,32,256]{2,1,0:T(8,128)S(1)}, u32[]{:S(2)}, u32[]{:S(2)}) collective-permute-start(f32[10,32,256]{2,1,0:T(8,128)S(1)} %get-tuple-element.58), channel_id=1, source_target_pairs={{4,8},{8,4},{12,16},{16,12},{20,24},{24,20},{28,0},{0,28},{5,9},{9... | collective-permute-start | bytes 983048 | tf_op jit(solution)/shard_map/ppermute | solution.py:50
  36.1 14.9 %collective-permute-start.15 = (f32[10,32,256]{2,1,0:T(8,128)S(1)}, f32[10,32,256]{2,1,0:T(8,128)S(1)}, u32[]{:S(2)}, u32[]{:S(2)}) collective-permute-start(f32[10,32,256]{2,1,0:T(8,128)S(1)} %get-tuple-element.59), channel_id=1, source_target_pairs={{0,4},{4,0},{8,12},{12,8},{16,20},{20,16},{24,28},{28,24},{1,5},{5... | collective-permute-start | bytes 983048 | tf_op jit(solution)/shard_map/ppermute | solution.py:50
  36.7 7.6 %collective-permute-start.6 = (f32[4,8,512]{2,1,0:T(8,128)S(1)}, f32[4,8,512]{2,1,0:T(8,128)S(1)}, u32[]{:S(2)}, u32[]{:S(2)}) collective-permute-start(f32[4,8,512]{2,1,0:T(8,128)S(1)} %get-tuple-element.48), channel_id=1, source_target_pairs={{1,2},{2,1},{3,0},{0,3},{5,6},{6,5},{7,4},{4,7},{9,10},{10,9},{11,... | collective-permute-start | bytes 196616 | tf_op jit(solution)/shard_map/ppermute | solution.py:50
  38.3 6.0 %collective-permute-start.7 = (f32[4,8,512]{2,1,0:T(8,128)S(1)}, f32[4,8,512]{2,1,0:T(8,128)S(1)}, u32[]{:S(2)}, u32[]{:S(2)}) collective-permute-start(f32[4,8,512]{2,1,0:T(8,128)S(1)} %get-tuple-element.49), channel_id=1, source_target_pairs={{0,1},{1,0},{2,3},{3,2},{4,5},{5,4},{6,7},{7,6},{8,9},{9,8},{10,11... | collective-permute-start | bytes 196616 | tf_op jit(solution)/shard_map/ppermute | solution.py:50
  39.4 4.9 %collective-permute-start.8 = (f32[4,8,256]{2,1,0:T(8,128)S(1)}, f32[4,8,256]{2,1,0:T(8,128)S(1)}, u32[]{:S(2)}, u32[]{:S(2)}) collective-permute-start(f32[4,8,256]{2,1,0:T(8,128)S(1)} %get-tuple-element.51.refs_4_.refs_2_), channel_id=1, source_target_pairs={{0,2},{1,3},{2,0},{3,1},{4,6},{5,7},{6,4},{7,5},{8,10},{9,11},{10,... | collective-permute-start | bytes 98312 | tf_op jit(solution)/shard_map/ppermute | solution.py:34
  44.4 8.1 %copy-start.4 = (bf16[256,128]{1,0:T(8,128)(2,1)S(1)}, bf16[256,128]{1,0:T(8,128)(2,1)}, u32[]{:S(2)}) copy-start(bf16[256,128]{1,0:T(8,128)(2,1)} %constant.6.clone.refs_1_) | copy-start | bytes 196612
  44.4 6.6 %collective-permute-start.12 = (f32[4,32,256]{2,1,0:T(8,128)S(1)}, f32[4,32,256]{2,1,0:T(8,128)S(1)}, u32[]{:S(2)}, u32[]{:S(2)}) collective-permute-start(f32[4,32,256]{2,1,0:T(8,128)S(1)} %get-tuple-element.55), channel_id=1, source_target_pairs={{4,8},{8,4},{12,16},{16,12},{20,24},{24,20},{28,0},{0,28},{5,9},{9... | collective-permute-start | bytes 393224 | tf_op jit(solution)/shard_map/ppermute | solution.py:50
  44.9 6.0 %collective-permute-start.13 = (f32[4,32,256]{2,1,0:T(8,128)S(1)}, f32[4,32,256]{2,1,0:T(8,128)S(1)}, u32[]{:S(2)}, u32[]{:S(2)}) collective-permute-start(f32[4,32,256]{2,1,0:T(8,128)S(1)} %get-tuple-element.56), channel_id=1, source_target_pairs={{0,4},{4,0},{8,12},{12,8},{16,20},{20,16},{24,28},{28,24},{1,5},{5... | collective-permute-start | bytes 393224 | tf_op jit(solution)/shard_map/ppermute | solution.py:50
  51.0 11.5 %copy-start.1 = (f32[848,256]{1,0:T(8,128)S(1)}, f32[848,256]{1,0:T(8,128)}, u32[]{:S(2)}) copy-start(f32[848,256]{1,0:T(8,128)} %constant.7.clone.refs_1_) | copy-start | bytes 2605060
  51.9 11.5 %collective-permute-start.16 = (f32[10,8,512]{2,1,0:T(8,128)S(1)}, f32[10,8,512]{2,1,0:T(8,128)S(1)}, u32[]{:S(2)}, u32[]{:S(2)}) collective-permute-start(f32[10,8,512]{2,1,0:T(8,128)S(1)} %get-tuple-element.62), channel_id=1, source_target_pairs={{4,8},{8,4},{12,16},{16,12},{20,24},{24,20},{28,0},{0,28},{5,9},{9... | collective-permute-start | bytes 491528 | tf_op jit(solution)/shard_map/ppermute | solution.py:50
  52.0 11.5 %collective-permute-start.17 = (f32[10,8,512]{2,1,0:T(8,128)S(1)}, f32[10,8,512]{2,1,0:T(8,128)S(1)}, u32[]{:S(2)}, u32[]{:S(2)}) collective-permute-start(f32[10,8,512]{2,1,0:T(8,128)S(1)} %get-tuple-element.63), channel_id=1, source_target_pairs={{0,4},{4,0},{8,12},{12,8},{16,20},{20,16},{24,28},{28,24},{1,5},{5... | collective-permute-start | bytes 491528 | tf_op jit(solution)/shard_map/ppermute | solution.py:50
  52.8 12.2 %copy-start = (bf16[256,512]{1,0:T(8,128)(2,1)S(1)}, bf16[256,512]{1,0:T(8,128)(2,1)}, u32[]{:S(2)}) copy-start(bf16[256,512]{1,0:T(8,128)(2,1)} %constant.8.clone.refs_5_.refs_4_) | copy-start | bytes 786436
  64.2 4.3 %collective-permute-start.18 = (f32[2,16,256]{2,1,0:T(8,128)S(1)}, f32[2,16,256]{2,1,0:T(8,128)S(1)}, u32[]{:S(2)}, u32[]{:S(2)}) collective-permute-start(f32[2,16,256]{2,1,0:T(8,128)S(1)} %get-tuple-element.67), channel_id=1, source_target_pairs={{4,8},{8,4},{12,16},{16,12},{20,24},{24,20},{28,0},{0,28},{5,9},{9... | collective-permute-start | bytes 98312 | tf_op jit(solution)/shard_map/ppermute | solution.py:50
  64.3 4.2 %collective-permute-start.19 = (f32[2,16,256]{2,1,0:T(8,128)S(1)}, f32[2,16,256]{2,1,0:T(8,128)S(1)}, u32[]{:S(2)}, u32[]{:S(2)}) collective-permute-start(f32[2,16,256]{2,1,0:T(8,128)S(1)} %get-tuple-element.68), channel_id=1, source_target_pairs={{0,4},{4,0},{8,12},{12,8},{16,20},{20,16},{24,28},{28,24},{1,5},{5... | collective-permute-start | bytes 98312 | tf_op jit(solution)/shard_map/ppermute | solution.py:50
